TPU v7x, 32 devices: a whole 2x2x4 slice. The times are simulated.
32 devices in a mesh: rep: 2 (over y), grp: 4 (over x, core), ing: 4 (over z).
Axes of the slice: x: 2, y: 2, z: 4, core: 2. Of those that a mesh axis runs over, the one named last changes fastest.
Arguments:
- tokens: bfloat16 [8192, 3584], P(('rep', 'grp', 'ing')), parts along dimension 0, may hold values from -6 to 6
- router_logits: float32 [8192, 96], P(('rep', 'grp', 'ing')), parts along dimension 0, may hold values from -8 to 8
- expert_ids: int32 [8192, 8], P(('rep', 'grp', 'ing')), parts along dimension 0, may hold values from 0 to 95, as said below
- w_gate: bfloat16 [4, 3584, 2048], P('grp', None, 'ing'), may hold values from -0.09375 to 0.09375
- w_up: bfloat16 [4, 3584, 2048], P('grp', None, 'ing'), may hold values from -0.09375 to 0.09375
- w_down: bfloat16 [4, 2048, 3584], P('grp', None, 'ing'), may hold values from -0.125 to 0.125
Outputs:
- mixed_out: bfloat16 [8192, 3584], P(('rep', 'grp', 'ing')), parts along dimension 0
There are 2 independent parts, one for each index of `rep`. A program takes and returns all parts, laid end to end along the dimension named above; an argument that names none is the same for every part. Nothing has to cross between parts.
Inputs may be any that keep to these rules, and one draw needn't show every extreme that they name: `expert_ids`: each row names 8 different experts, two in each of exactly 4 groups, expert e lying in group e // 24. Among the tokens of one device at most 8 name the first expert of any one group; among the tokens of the 4 devices that share one ing index at most 16 name the first expert of any one group; both bounds are reached in every draw.
All inputs are finite; a program needn't handle non-finite values.
Results may differ from a plain program's by a relative error of at most 0.0067.
Values may be sent and summed in bfloat16 or wider, within the bound.
No kernel may reach another device: no remote copies, remote signals or barrier semaphores. Data moves between devices by JAX's collectives and lax.ppermute only.
A program may use at most 64 MiB of HBM per device.

v0:
```python
import functools

import jax
import jax.numpy as jnp
from jax import lax
from jax.experimental import pallas as pl
from jax.experimental.pallas import tpu as pltpu
from jax.sharding import PartitionSpec as P

GROUP_EXPERTS = 24
CAP = 8
LANES = 128
ROUTE_SCALE = 2.827
MIB = 1024 * 1024

BF16 = jnp.bfloat16
F32 = jnp.float32
VMEM = pl.BlockSpec(memory_space=pltpu.VMEM)
ANY = pl.BlockSpec(memory_space=pl.ANY)


def params(nbytes):
    return pltpu.CompilerParams(vmem_limit_bytes=2 * nbytes + 4 * MIB)


def named(ids, expert):
    hit = jnp.zeros(expert.shape, F32)
    for k in range(ids.shape[0]):
        hit = jnp.where(ids[k : k + 1, :] == expert, 1.0, hit)
    return hit


def placing(ids, groups, me):
    rows, count = groups * CAP, ids.shape[1]
    row = lax.broadcasted_iota(jnp.int32, (rows, count), 0)
    group = (row // CAP) ^ me
    hit = named(ids, group * GROUP_EXPERTS)
    before = (
        lax.broadcasted_iota(jnp.int32, (count, count), 0)
        <= lax.broadcasted_iota(jnp.int32, (count, count), 1)
    ).astype(BF16)
    rank = jnp.dot(hit.astype(BF16), before, preferred_element_type=F32)
    slot = lax.rem(row, CAP).astype(F32)
    return jnp.where((hit > 0.5) & (rank == slot + 1.0), 1.0, 0.0), group


def dispatch_kernel(groups, width, ids_ref, tokens_ref, *refs):
    outs, (ids_held, staged, sems) = refs[:groups], refs[groups:]
    me = lax.axis_index("grp")
    features = tokens_ref.shape[1]
    first = pltpu.make_async_copy(ids_ref, ids_held, sems.at[features // width])
    first.start()
    copies = []
    for c in range(features // width):
        part = pl.ds(c * width, width)
        copies.append(pltpu.make_async_copy(tokens_ref.at[:, part], staged.at[:, part], sems.at[c]))
        copies[-1].start()
    first.wait()
    place, _ = placing(ids_held[...], groups, me)
    live = jnp.sum(place, axis=1, keepdims=True)
    place = place.astype(BF16)
    for d in range(groups):
        outs[d][:, features:] = jnp.broadcast_to(live[d * CAP : (d + 1) * CAP], (CAP, LANES)).astype(BF16)
    for c in range(features // width):
        copies[c].wait()
        part = slice(c * width, (c + 1) * width)
        rows = jnp.dot(place, staged[:, part], preferred_element_type=F32)
        for d in range(groups):
            outs[d][:, part] = rows[d * CAP : (d + 1) * CAP].astype(BF16)


def prepare_kernel(groups, after_ref, ids_ref, logits_ref, *refs):
    del after_ref
    weights, loaded, (out_ref, ids_held, logits_held, sems) = refs[:3], refs[3:6], refs[6:]
    small = [
        pltpu.make_async_copy(ids_ref, ids_held, sems.at[12]),
        pltpu.make_async_copy(logits_ref, logits_held, sems.at[13]),
    ]
    for copy in small:
        copy.start()
    copies = []
    for k in range(3):
        depth = weights[k].shape[0]
        for c in range(4):
            part = pl.ds(c * (depth // 4), depth // 4)
            copies.append(pltpu.make_async_copy(weights[k].at[part], loaded[k].at[part], sems.at[4 * k + c]))
            copies[-1].start()
    for copy in small:
        copy.wait()
    me = lax.axis_index("grp")
    ids = ids_held[...]
    place, group = placing(ids, groups, me)
    scores = 1.0 / (1.0 + jnp.exp(-logits_held[...]))
    expert = lax.broadcasted_iota(jnp.int32, scores.shape, 0)
    chosen = jnp.sum(jnp.where(named(ids, expert) > 0.5, scores, 0.0), axis=0, keepdims=True)
    leading = jnp.zeros(place.shape, F32)
    for g in range(groups):
        leading = jnp.where(group == g, scores[g * GROUP_EXPERTS : g * GROUP_EXPERTS + 1, :], leading)
    weight = (ROUTE_SCALE * leading / chosen).astype(BF16).astype(F32)
    out_ref[...] = jnp.where(place > 0.5, weight, 0.0).astype(BF16)
    for copy in copies:
        copy.wait()


def compact_kernel(groups, slots, after_ref, *refs):
    del after_ref
    arrived, out_ref = refs[:groups], refs[groups]
    rows, features = groups * CAP, out_ref.shape[1] - LANES
    live = jnp.concatenate([a[:, features:].astype(F32) for a in arrived], axis=0)
    row = lax.broadcasted_iota(jnp.int32, (rows, rows), 0)
    column = lax.broadcasted_iota(jnp.int32, (rows, rows), 1)
    before = (column <= row).astype(BF16)
    rank = jnp.dot(before, live.astype(BF16), preferred_element_type=F32)
    rank = jnp.broadcast_to(rank[:, :1], (rows, LANES))
    lane = lax.broadcasted_iota(jnp.int32, (rows, LANES), 1).astype(F32)
    pick = jnp.where((live > 0.5) & (rank == lane + 1.0), 1.0, 0.0).astype(BF16)[:, :slots]
    origin = (lax.broadcasted_iota(jnp.int32, (rows, LANES), 0) + 1).astype(BF16)
    contract = (((0,), (0,)), ((), ()))
    out_ref[:, features:] = lax.dot_general(pick, origin, contract, preferred_element_type=F32).astype(BF16)
    step = 512
    for c in range(features // step):
        part = slice(c * step, (c + 1) * step)
        whole = jnp.concatenate([a[:, part].astype(F32) for a in arrived], axis=0).astype(BF16)
        out_ref[:, part] = lax.dot_general(pick, whole, contract, preferred_element_type=F32).astype(BF16)


def hidden_kernel(columns, *refs):
    blocks, (gate_ref, up_ref, hidden_ref, tag_ref, held) = refs[:columns], refs[columns:]
    slots = blocks[0].shape[0]
    features, units = gate_ref.shape
    for e in range(columns):
        held[e * slots : (e + 1) * slots, :] = blocks[e][:, :features]
        tag_ref[e * slots : (e + 1) * slots, :] = blocks[e][:, features:].astype(F32)
    step = min(256, units)
    for c in range(units // step):
        part = slice(c * step, (c + 1) * step)
        gate = jnp.dot(held[...], gate_ref[:, part], preferred_element_type=F32)
        up = jnp.dot(held[...], up_ref[:, part], preferred_element_type=F32)
        hidden_ref[:, part] = (gate / (1.0 + jnp.exp(-gate)) * up).astype(BF16)


def down_kernel(groups, columns, *refs):
    hiddens, (tag_ref, down_ref, out_ref) = refs[:columns], refs[columns:]
    me, group = lax.axis_index("ing"), lax.axis_index("grp")
    rows, units = hiddens[0].shape
    slots = rows // columns
    total = jnp.zeros((rows, down_ref.shape[1]), F32)
    for f in range(columns):
        block = jnp.concatenate(
            [hiddens[f][slots * (e ^ f) : slots * ((e ^ f) + 1), :] for e in range(columns)], axis=0
        )
        at = pl.multiple_of((me ^ f) * units, units)
        total += jnp.dot(block, down_ref[pl.ds(at, units), :], preferred_element_type=F32)
    result = total.astype(BF16)
    wide = groups * CAP
    for e in range(columns):
        mine = slice(e * slots, (e + 1) * slots)
        origin = tag_ref[mine, :][:, :1] - 1.0
        lane = lax.broadcasted_iota(jnp.int32, (slots, wide), 1).astype(F32)
        spread = jnp.where(origin == lane, 1.0, 0.0).astype(BF16)
        back = lax.dot_general(spread, result[mine], (((0,), (0,)), ((), ())), preferred_element_type=F32)
        for d in range(groups):
            out_ref[(group ^ d) * columns + (me ^ e)] = back[d * CAP : (d + 1) * CAP].astype(BF16)


def combine_kernel(groups, columns, mixing_ref, back_ref, out_ref, held, sems):
    group = lax.axis_index("grp")
    width = back_ref.shape[2]
    copies = []
    for i in range(columns):
        rows = jnp.concatenate(
            [back_ref[(group ^ d) * columns + i].astype(F32) for d in range(groups)], axis=0
        )
        value = lax.dot_general(
            mixing_ref[...], rows.astype(BF16), (((0,), (0,)), ((), ())), preferred_element_type=F32
        )
        part = pl.ds(i * width, width)
        held[:, part] = value.astype(BF16)
        copies.append(pltpu.make_async_copy(held.at[:, part], out_ref.at[:, part], sems.at[i]))
        copies[-1].start()
    for copy in copies:
        copy.wait()


def swap(x, name, step):
    if step == 0:
        return x
    return lax.ppermute(x, name, [(a, a ^ step) for a in range(lax.axis_size(name))])


def local(tokens, router_logits, expert_ids, w_gate, w_up, w_down):
    groups = lax.axis_size("grp")
    columns = lax.axis_size("ing")
    count, features = tokens.shape
    units, share = w_gate.shape[2], w_down.shape[2]
    slots = groups * CAP // 2
    wide = features + LANES
    ids = pltpu.with_memory_space_constraint(expert_ids.T, pltpu.HBM)
    logits = pltpu.with_memory_space_constraint(router_logits.T, pltpu.HBM)

    outbound = pl.pallas_call(
        functools.partial(dispatch_kernel, groups, 512),
        out_shape=[jax.ShapeDtypeStruct((CAP, wide), BF16)] * groups,
        in_specs=[ANY, ANY],
        out_specs=[VMEM] * groups,
        scratch_shapes=[
            pltpu.VMEM(ids.shape, jnp.int32),
            pltpu.VMEM((count, features), BF16),
            pltpu.SemaphoreType.DMA((features // 512 + 1,)),
        ],
        compiler_params=params(2 * count * features),
        name="dispatch",
    )(ids, pltpu.with_memory_space_constraint(tokens, pltpu.HBM))
    arrived = [swap(outbound[d], "grp", d) for d in range(groups)]

    weights = [w_gate[0], w_up[0], w_down[0]]
    gate, up, down, mixing = pl.pallas_call(
        functools.partial(prepare_kernel, groups),
        out_shape=[pltpu.VMEM(w.shape, BF16) for w in weights]
        + [jax.ShapeDtypeStruct((groups * CAP, count), BF16)],
        in_specs=[ANY] * 6,
        out_specs=[VMEM] * 4,
        scratch_shapes=[
            pltpu.VMEM(ids.shape, jnp.int32),
            pltpu.VMEM(logits.shape, F32),
            pltpu.SemaphoreType.DMA((14,)),
        ],
        compiler_params=params(0),
        name="prepare",
    )(
        outbound[0],
        ids,
        logits,
        *[pltpu.with_memory_space_constraint(w, pltpu.HBM) for w in weights],
    )

    compacted = pl.pallas_call(
        functools.partial(compact_kernel, groups, slots),
        out_shape=jax.ShapeDtypeStruct((slots, wide), BF16),
        in_specs=[ANY] + [VMEM] * groups,
        out_specs=VMEM,
        compiler_params=params(2 * (groups * CAP + slots) * wide),
        name="compact",
    )(mixing, *arrived)
    blocks = [swap(compacted, "ing", e) for e in range(columns)]

    hidden, tags = pl.pallas_call(
        functools.partial(hidden_kernel, columns),
        out_shape=[
            jax.ShapeDtypeStruct((columns * slots, units), BF16),
            jax.ShapeDtypeStruct((columns * slots, LANES), F32),
        ],
        in_specs=[VMEM] * (columns + 2),
        out_specs=[VMEM, VMEM],
        scratch_shapes=[pltpu.VMEM((columns * slots, features), BF16)],
        compiler_params=params(2 * columns * slots * (2 * features + units)),
        name="hidden",
    )(*blocks, gate, up)
    hiddens = [swap(hidden, "ing", f) for f in range(columns)]

    results = pl.pallas_call(
        functools.partial(down_kernel, groups, columns),
        out_shape=jax.ShapeDtypeStruct((groups * columns, CAP, share), BF16),
        in_specs=[VMEM] * (columns + 2),
        out_specs=VMEM,
        compiler_params=params(2 * columns * slots * (columns * units + 4 * share)),
        name="down",
    )(*hiddens, tags, down)
    returned = lax.all_to_all(results, ("grp", "ing"), split_axis=0, concat_axis=0, tiled=True)

    if share % LANES:
        me = lax.axis_index("grp")
        rows = returned.reshape(groups, columns, CAP, share)[jnp.arange(groups) ^ me]
        rows = rows.transpose(0, 2, 1, 3).reshape(groups * CAP, features)
        return jnp.dot(mixing.T, rows, preferred_element_type=F32).astype(BF16)
    return pl.pallas_call(
        functools.partial(combine_kernel, groups, columns),
        out_shape=jax.ShapeDtypeStruct((count, features), BF16),
        in_specs=[VMEM, VMEM],
        out_specs=ANY,
        scratch_shapes=[pltpu.VMEM((count, features), BF16), pltpu.SemaphoreType.DMA((columns,))],
        compiler_params=params(2 * (count + groups * CAP) * features),
        name="combine",
    )(mixing, returned)


def solution(mesh):
    placed = (
        P(("rep", "grp", "ing"), None),
        P(("rep", "grp", "ing"), None),
        P(("rep", "grp", "ing"), None),
        P("grp", None, "ing"),
        P("grp", None, "ing"),
        P("grp", None, "ing"),
    )
    return jax.shard_map(
        local, mesh=mesh, in_specs=placed, out_specs=P(("rep", "grp", "ing"), None), check_vma=False
    )
```

profile of v0, /device:TPU:0, one launch (start us, length us, event | category | flops | bytes accessed | tf_op | source)
XLA Modules:
  0.0 50.6 jit_solution(16967791877764207834)
XLA Ops:
  0.0 2.2 %dispatch.1 = (bf16[8,3712]{1,0:T(8,128)(2,1)S(1)}, bf16[8,3712]{1,0:T(8,128)(2,1)S(1)}, bf16[8,3712]{1,0:T(8,128)(2,1)S(1)}, bf16[8,3712]{1,0:T(8,128)(2,1)S(1)}) custom-call(s32[8,256]{1,0:T(8,128)} %bitcast.9, bf16[256,3584]{1,0:T(8,128)(2,1)} %tokens_ref.1), custom_call_target="tpu_custom_call" | custom-call | tf_op jit(solution)/shard_map/dispatch/pallas_call | solution.py:201
  2.2 0.5 %collective-permute-start = (bf16[8,3712]{1,0:T(8,128)(2,1)S(1)}, bf16[8,3712]{1,0:T(8,128)(2,1)S(1)}, u32[]{:S(2)}, u32[]{:S(2)}) collective-permute-start(bf16[8,3712]{1,0:T(8,128)(2,1)S(1)} %get-tuple-element.17), channel_id=1, source_target_pairs={{0,4},{4,0},{8,12},{12,8},{1,5},{5,1},{9,13},{13,9},{2,6},{6,2},{1... | collective-permute-start | bytes 178184 | tf_op jit(solution)/shard_map/ppermute | solution.py:188
  2.7 2.6 %collective-permute-start.1 = (bf16[8,3712]{1,0:T(8,128)(2,1)S(1)}, bf16[8,3712]{1,0:T(8,128)(2,1)S(1)}, u32[]{:S(2)}, u32[]{:S(2)}) collective-permute-start(bf16[8,3712]{1,0:T(8,128)(2,1)S(1)} %get-tuple-element.18), channel_id=1, source_target_pairs={{0,8},{4,12},{8,0},{12,4},{1,9},{5,13},{9,1},{13,5},{2,10},{6,14},... | collective-permute-start | bytes 178184 | tf_op jit(solution)/shard_map/ppermute | solution.py:188
  5.2 0.1 collective-permute-start.2
  5.3 4.3 %prepare.1 = (bf16[3584,512]{1,0:T(8,128)(2,1)S(1)}, bf16[3584,512]{1,0:T(8,128)(2,1)S(1)}, bf16[2048,896]{1,0:T(8,128)(2,1)S(1)}, bf16[32,256]{1,0:T(8,128)(2,1)S(1)}) custom-call(bf16[8,3712]{1,0:T(8,128)(2,1)S(1)} %get-tuple-element.15.after_ref.refs_0_, s32[8,256]{1,0:T(8,128)} %bitcast.10, f32[96,256]{1,0:T(8,128)} %bitcast.8, ...), custom_call_target="tpu_custom_call" | custom-call | tf_op jit(solution)/shard_map/prepare/pallas_call | solution.py:217
  9.7 0.0 collective-permute-done.refs_1_
  9.7 0.0 collective-permute-done.1.refs_2_
  9.7 0.0 collective-permute-done.2.refs_3_
  9.7 0.4 compact.1.refs_0_
  10.1 3.9 %collective-permute-start.5 = (bf16[16,3712]{1,0:T(8,128)(2,1)S(1)}, bf16[16,3712]{1,0:T(8,128)(2,1)S(1)}, u32[]{:S(2)}, u32[]{:S(2)}) collective-permute-start(bf16[16,3712]{1,0:T(8,128)(2,1)S(1)} %compact.1.refs_0_), channel_id=1, source_target_pairs={{0,3},{1,2},{2,1},{3,0},{4,7},{5,6},{6,5},{7,4},{8,11},{9,10},{10,... | collective-permute-start | bytes 356360 | tf_op jit(solution)/shard_map/ppermute | solution.py:188
  14.0 0.0 collective-permute-start.4
  14.0 0.6 %collective-permute-start.3 = (bf16[16,3712]{1,0:T(8,128)(2,1)S(1)}, bf16[16,3712]{1,0:T(8,128)(2,1)S(1)}, u32[]{:S(2)}, u32[]{:S(2)}) collective-permute-start(bf16[16,3712]{1,0:T(8,128)(2,1)S(1)} %compact.1.refs_0_), channel_id=1, source_target_pairs={{0,1},{1,0},{2,3},{3,2},{4,5},{5,4},{6,7},{7,6},{8,9},{9,8},{10,11... | collective-permute-start | bytes 356360 | tf_op jit(solution)/shard_map/ppermute | solution.py:188
  14.6 3.5 %collective-permute-done.5.refs_3_ = bf16[16,3712]{1,0:T(8,128)(2,1)S(1)} collective-permute-done((bf16[16,3712]{1,0:T(8,128)(2,1)S(1)}, bf16[16,3712]{1,0:T(8,128)(2,1)S(1)}, u32[]{:S(2)}, u32[]{:S(2)}) %collective-permute-start.5) | collective-permute-done | bytes 118816 | tf_op jit(solution)/shard_map/ppermute | solution.py:188
  18.2 6.3 %collective-permute-done.4.refs_2_ = bf16[16,3712]{1,0:T(8,128)(2,1)S(1)} collective-permute-done((bf16[16,3712]{1,0:T(8,128)(2,1)S(1)}, bf16[16,3712]{1,0:T(8,128)(2,1)S(1)}, u32[]{:S(2)}, u32[]{:S(2)}) %collective-permute-start.4) | collective-permute-done | bytes 118816 | tf_op jit(solution)/shard_map/ppermute | solution.py:188
  24.5 0.0 collective-permute-done.3.refs_1_
  24.5 1.4 %hidden.1 = (bf16[64,512]{1,0:T(8,128)(2,1)S(1)}, f32[64,128]{1,0:T(8,128)S(1)}) custom-call(bf16[16,3712]{1,0:T(8,128)(2,1)S(1)} %compact.1.refs_0_, bf16[16,3712]{1,0:T(8,128)(2,1)S(1)} %collective-permute-done.3.refs_1_, bf16[16,3712]{1,0:T(8,128)(2,1)S(1)} %collective-permute-done.4.refs_2_, bf16[16,3712]{1,0:T(8,128)(2,1)S(1)} %collective-permute-done.5.refs_3_, ...), custom_call_target="tpu_custom_call" | custom-call | tf_op jit(solution)/shard_map/hidden/pallas_call | solution.py:247
  26.0 2.6 %collective-permute-start.8 = (bf16[64,512]{1,0:T(8,128)(2,1)S(1)}, bf16[64,512]{1,0:T(8,128)(2,1)S(1)}, u32[]{:S(2)}, u32[]{:S(2)}) collective-permute-start(bf16[64,512]{1,0:T(8,128)(2,1)S(1)} %get-tuple-element.22.refs_0_), channel_id=1, source_target_pairs={{0,3},{1,2},{2,1},{3,0},{4,7},{5,6},{6,5},{7,4},{8,11},{9,10},{10,... | collective-permute-start | bytes 196616 | tf_op jit(solution)/shard_map/ppermute | solution.py:188
  28.5 0.0 collective-permute-start.7
  28.5 1.9 %collective-permute-start.6 = (bf16[64,512]{1,0:T(8,128)(2,1)S(1)}, bf16[64,512]{1,0:T(8,128)(2,1)S(1)}, u32[]{:S(2)}, u32[]{:S(2)}) collective-permute-start(bf16[64,512]{1,0:T(8,128)(2,1)S(1)} %get-tuple-element.22.refs_0_), channel_id=1, source_target_pairs={{0,1},{1,0},{2,3},{3,2},{4,5},{5,4},{6,7},{7,6},{8,9},{9,8},{10,11... | collective-permute-start | bytes 196616 | tf_op jit(solution)/shard_map/ppermute | solution.py:188
  30.4 1.8 %collective-permute-done.8.refs_3_ = bf16[64,512]{1,0:T(8,128)(2,1)S(1)} collective-permute-done((bf16[64,512]{1,0:T(8,128)(2,1)S(1)}, bf16[64,512]{1,0:T(8,128)(2,1)S(1)}, u32[]{:S(2)}, u32[]{:S(2)}) %collective-permute-start.8) | collective-permute-done | bytes 65568 | tf_op jit(solution)/shard_map/ppermute | solution.py:188
  32.2 2.0 %collective-permute-done.7.refs_2_ = bf16[64,512]{1,0:T(8,128)(2,1)S(1)} collective-permute-done((bf16[64,512]{1,0:T(8,128)(2,1)S(1)}, bf16[64,512]{1,0:T(8,128)(2,1)S(1)}, u32[]{:S(2)}, u32[]{:S(2)}) %collective-permute-start.7) | collective-permute-done | bytes 65568 | tf_op jit(solution)/shard_map/ppermute | solution.py:188
  34.2 0.0 collective-permute-done.6.refs_1_
  34.2 1.0 %down.1 = bf16[16,8,896]{2,1,0:T(8,128)(2,1)S(1)} custom-call(bf16[64,512]{1,0:T(8,128)(2,1)S(1)} %get-tuple-element.22.refs_0_, bf16[64,512]{1,0:T(8,128)(2,1)S(1)} %collective-permute-done.6.refs_1_, bf16[64,512]{1,0:T(8,128)(2,1)S(1)} %collective-permute-done.7.refs_2_, bf16[64,512]{1,0:T(8,128)(2,1)S(1)} %collective-permute-done.8.refs_3_, ...), custom_call_target="tpu_custom_call" | custom-call | tf_op jit(solution)/shard_map/down/pallas_call | solution.py:261
  35.2 13.8 %all_to_all.5.back_ref = bf16[16,8,896]{2,1,0:T(8,128)(2,1)S(1)} all-to-all(bf16[16,8,896]{2,1,0:T(8,128)(2,1)S(1)} %down.1), channel_id=1, replica_groups=mesh['rep'=2,'grp'=4,'ing'=4] {'grp','ing'}, dimensions={0} | all-to-all | bytes 458752 | tf_op jit(solution)/shard_map/all_to_all | solution.py:269
  49.0 1.6 %combine.1 = bf16[256,3584]{1,0:T(8,128)(2,1)} custom-call(bf16[32,256]{1,0:T(8,128)(2,1)S(1)} %get-tuple-element.16.after_ref.mixing_ref, bf16[16,8,896]{2,1,0:T(8,128)(2,1)S(1)} %all_to_all.5.back_ref), custom_call_target="tpu_custom_call" | custom-call | tf_op jit(solution)/shard_map/combine/pallas_call | solution.py:276
Async XLA Ops:
  2.2 7.5 %collective-permute-start = (bf16[8,3712]{1,0:T(8,128)(2,1)S(1)}, bf16[8,3712]{1,0:T(8,128)(2,1)S(1)}, u32[]{:S(2)}, u32[]{:S(2)}) collective-permute-start(bf16[8,3712]{1,0:T(8,128)(2,1)S(1)} %get-tuple-element.17), channel_id=1, source_target_pairs={{0,4},{4,0},{8,12},{12,8},{1,5},{5,1},{9,13},{13,9},{2,6},{6,2},{1... | collective-permute-start | bytes 178184 | tf_op jit(solution)/shard_map/ppermute | solution.py:188
  2.7 7.0 %collective-permute-start.1 = (bf16[8,3712]{1,0:T(8,128)(2,1)S(1)}, bf16[8,3712]{1,0:T(8,128)(2,1)S(1)}, u32[]{:S(2)}, u32[]{:S(2)}) collective-permute-start(bf16[8,3712]{1,0:T(8,128)(2,1)S(1)} %get-tuple-element.18), channel_id=1, source_target_pairs={{0,8},{4,12},{8,0},{12,4},{1,9},{5,13},{9,1},{13,5},{2,10},{6,14},... | collective-permute-start | bytes 178184 | tf_op jit(solution)/shard_map/ppermute | solution.py:188
  5.2 4.4 %collective-permute-start.2 = (bf16[8,3712]{1,0:T(8,128)(2,1)S(1)}, bf16[8,3712]{1,0:T(8,128)(2,1)S(1)}, u32[]{:S(2)}, u32[]{:S(2)}) collective-permute-start(bf16[8,3712]{1,0:T(8,128)(2,1)S(1)} %get-tuple-element.19), channel_id=1, source_target_pairs={{0,12},{4,8},{8,4},{12,0},{1,13},{5,9},{9,5},{13,1},{2,14},{6,10},... | collective-permute-start | bytes 178184 | tf_op jit(solution)/shard_map/ppermute | solution.py:188
  10.1 8.1 %collective-permute-start.5 = (bf16[16,3712]{1,0:T(8,128)(2,1)S(1)}, bf16[16,3712]{1,0:T(8,128)(2,1)S(1)}, u32[]{:S(2)}, u32[]{:S(2)}) collective-permute-start(bf16[16,3712]{1,0:T(8,128)(2,1)S(1)} %compact.1.refs_0_), channel_id=1, source_target_pairs={{0,3},{1,2},{2,1},{3,0},{4,7},{5,6},{6,5},{7,4},{8,11},{9,10},{10,... | collective-permute-start | bytes 356360 | tf_op jit(solution)/shard_map/ppermute | solution.py:188
  14.0 10.5 %collective-permute-start.4 = (bf16[16,3712]{1,0:T(8,128)(2,1)S(1)}, bf16[16,3712]{1,0:T(8,128)(2,1)S(1)}, u32[]{:S(2)}, u32[]{:S(2)}) collective-permute-start(bf16[16,3712]{1,0:T(8,128)(2,1)S(1)} %compact.1.refs_0_), channel_id=1, source_target_pairs={{0,2},{1,3},{2,0},{3,1},{4,6},{5,7},{6,4},{7,5},{8,10},{9,11},{10,... | collective-permute-start | bytes 356360 | tf_op jit(solution)/shard_map/ppermute | solution.py:188
  14.0 10.5 %collective-permute-start.3 = (bf16[16,3712]{1,0:T(8,128)(2,1)S(1)}, bf16[16,3712]{1,0:T(8,128)(2,1)S(1)}, u32[]{:S(2)}, u32[]{:S(2)}) collective-permute-start(bf16[16,3712]{1,0:T(8,128)(2,1)S(1)} %compact.1.refs_0_), channel_id=1, source_target_pairs={{0,1},{1,0},{2,3},{3,2},{4,5},{5,4},{6,7},{7,6},{8,9},{9,8},{10,11... | collective-permute-start | bytes 356360 | tf_op jit(solution)/shard_map/ppermute | solution.py:188
  26.0 6.2 %collective-permute-start.8 = (bf16[64,512]{1,0:T(8,128)(2,1)S(1)}, bf16[64,512]{1,0:T(8,128)(2,1)S(1)}, u32[]{:S(2)}, u32[]{:S(2)}) collective-permute-start(bf16[64,512]{1,0:T(8,128)(2,1)S(1)} %get-tuple-element.22.refs_0_), channel_id=1, source_target_pairs={{0,3},{1,2},{2,1},{3,0},{4,7},{5,6},{6,5},{7,4},{8,11},{9,10},{10,... | collective-permute-start | bytes 196616 | tf_op jit(solution)/shard_map/ppermute | solution.py:188
  28.5 5.6 %collective-permute-start.7 = (bf16[64,512]{1,0:T(8,128)(2,1)S(1)}, bf16[64,512]{1,0:T(8,128)(2,1)S(1)}, u32[]{:S(2)}, u32[]{:S(2)}) collective-permute-start(bf16[64,512]{1,0:T(8,128)(2,1)S(1)} %get-tuple-element.22.refs_0_), channel_id=1, source_target_pairs={{0,2},{1,3},{2,0},{3,1},{4,6},{5,7},{6,4},{7,5},{8,10},{9,11},{10,... | collective-permute-start | bytes 196616 | tf_op jit(solution)/shard_map/ppermute | solution.py:188
  28.5 5.6 %collective-permute-start.6 = (bf16[64,512]{1,0:T(8,128)(2,1)S(1)}, bf16[64,512]{1,0:T(8,128)(2,1)S(1)}, u32[]{:S(2)}, u32[]{:S(2)}) collective-permute-start(bf16[64,512]{1,0:T(8,128)(2,1)S(1)} %get-tuple-element.22.refs_0_), channel_id=1, source_target_pairs={{0,1},{1,0},{2,3},{3,2},{4,5},{5,4},{6,7},{7,6},{8,9},{9,8},{10,11... | collective-permute-start | bytes 196616 | tf_op jit(solution)/shard_map/ppermute | solution.py:188
where the time goes:
time: 50.9 us; the launch traced here: 50.6 us
  blocking collectives  13.8 us (27%)
  waiting for transfers between devices  13.7 us (27%)
  starting transfers between devices  12.1 us (24%)
  Pallas kernels  10.9 us (21%)
    all_to_all x1, blocking collectives, local(): lax.all_to_all(results, ('grp', 'ing'), split_axis=0, concat_axis=0, tile...  13.8 us
    ppermute x9, waiting for transfers between devices, swap(): lax.ppermute(x, name, [(a, a ^ step) for a in range(lax.axis_size(name))])  13.7 us
    ppermute x9, starting transfers between devices, swap(): lax.ppermute(x, name, [(a, a ^ step) for a in range(lax.axis_size(name))])  12.1 us
    pallas_call x1, Pallas kernels, local(): pl.pallas_call(functools.partial(prepare_kernel, groups), out_shape=[pltp...  4.33 us
    pallas_call x1, Pallas kernels, local(): pl.pallas_call(functools.partial(dispatch_kernel, groups, 512), out_shape...  2.16 us
    pallas_call x1, Pallas kernels, local(): pl.pallas_call(functools.partial(combine_kernel, groups, columns), out_sh...  1.57 us
    pallas_call x1, Pallas kernels, local(): pl.pallas_call(functools.partial(hidden_kernel, columns), out_shape=[jax....  1.43 us
  transfers between devices with their start and end apart: 9, of which 4 were waited for; matrix products, arithmetic and copies ran while one was open for 0% of the time, Pallas kernels for 9%

commit v1 on v0

v1 whole, which is shorter than its diff:
```python
import functools

import jax
import jax.numpy as jnp
from jax import lax
from jax.experimental import pallas as pl
from jax.experimental.pallas import tpu as pltpu
from jax.sharding import PartitionSpec as P

GROUP_EXPERTS = 24
CAP = 8
LANES = 128
ROUTE_SCALE = 2.827
MIB = 1024 * 1024

BF16 = jnp.bfloat16
F32 = jnp.float32
VMEM = pl.BlockSpec(memory_space=pltpu.VMEM)
ANY = pl.BlockSpec(memory_space=pl.ANY)


def params(nbytes):
    return pltpu.CompilerParams(vmem_limit_bytes=2 * nbytes + 4 * MIB)


def named(ids, expert):
    hit = jnp.zeros(expert.shape, F32)
    for k in range(ids.shape[0]):
        hit = jnp.where(ids[k : k + 1, :] == expert, 1.0, hit)
    return hit


def upto(count):
    return (
        lax.broadcasted_iota(jnp.int32, (count, count), 0)
        <= lax.broadcasted_iota(jnp.int32, (count, count), 1)
    ).astype(BF16)


def placing(ids, groups, me, before):
    rows, count = groups * CAP, ids.shape[1]
    row = lax.broadcasted_iota(jnp.int32, (rows, count), 0)
    group = (row // CAP) ^ me
    hit = named(ids, group * GROUP_EXPERTS)
    rank = jnp.dot(hit.astype(BF16), before, preferred_element_type=F32)
    slot = lax.rem(row, CAP).astype(F32)
    return jnp.where((hit > 0.5) & (rank == slot + 1.0), 1.0, 0.0), group


def dispatch_kernel(groups, width, ids_ref, tokens_ref, *refs):
    outs, (ids_held, staged, before_ref, sems) = refs[:groups], refs[groups:]
    me = lax.axis_index("grp")
    features = tokens_ref.shape[1]
    first = pltpu.make_async_copy(ids_ref, ids_held, sems.at[features // width])
    first.start()
    copies = []
    for c in range(features // width):
        part = pl.ds(c * width, width)
        copies.append(pltpu.make_async_copy(tokens_ref.at[:, part], staged.at[:, part], sems.at[c]))
        copies[-1].start()
    before_ref[...] = upto(tokens_ref.shape[0])
    first.wait()
    place, _ = placing(ids_held[...], groups, me, before_ref[...])
    live = jnp.sum(place, axis=1, keepdims=True)
    place = place.astype(BF16)
    for d in range(groups):
        outs[d][:, features:] = jnp.broadcast_to(live[d * CAP : (d + 1) * CAP], (CAP, LANES)).astype(BF16)
    for c in range(features // width):
        copies[c].wait()
        part = slice(c * width, (c + 1) * width)
        rows = jnp.dot(place, staged[:, part], preferred_element_type=F32)
        for d in range(groups):
            outs[d][:, part] = rows[d * CAP : (d + 1) * CAP].astype(BF16)


def prepare_kernel(groups, after_ref, ids_ref, logits_ref, *refs):
    del after_ref
    weights, loaded, (out_ref, ids_held, logits_held, sems) = refs[:3], refs[3:6], refs[6:]
    small = [
        pltpu.make_async_copy(ids_ref, ids_held, sems.at[12]),
        pltpu.make_async_copy(logits_ref, logits_held, sems.at[13]),
    ]
    for copy in small:
        copy.start()
    copies = []
    for k in range(3):
        depth = weights[k].shape[0]
        for c in range(4):
            part = pl.ds(c * (depth // 4), depth // 4)
            copies.append(pltpu.make_async_copy(weights[k].at[part], loaded[k].at[part], sems.at[4 * k + c]))
            copies[-1].start()
    for copy in small:
        copy.wait()
    me = lax.axis_index("grp")
    ids = ids_held[...]
    place, group = placing(ids, groups, me, upto(ids.shape[1]))
    scores = 1.0 / (1.0 + jnp.exp(-logits_held[...]))
    expert = lax.broadcasted_iota(jnp.int32, scores.shape, 0)
    chosen = jnp.sum(jnp.where(named(ids, expert) > 0.5, scores, 0.0), axis=0, keepdims=True)
    leading = jnp.zeros(place.shape, F32)
    for g in range(groups):
        leading = jnp.where(group == g, scores[g * GROUP_EXPERTS : g * GROUP_EXPERTS + 1, :], leading)
    weight = (ROUTE_SCALE * leading / chosen).astype(BF16).astype(F32)
    out_ref[...] = jnp.where(place > 0.5, weight, 0.0).astype(BF16)
    for copy in copies:
        copy.wait()


def compact_kernel(groups, slots, *refs):
    arrived, (out_ref, pick_ref) = refs[:groups], refs[groups:]
    rows, features = groups * CAP, out_ref.shape[1]
    live = jnp.concatenate([a[:, features:].astype(F32) for a in arrived], axis=0)
    row = lax.broadcasted_iota(jnp.int32, (rows, rows), 0)
    column = lax.broadcasted_iota(jnp.int32, (rows, rows), 1)
    rank = jnp.dot((column <= row).astype(BF16), live.astype(BF16), preferred_element_type=F32)
    lane = lax.broadcasted_iota(jnp.int32, (rows, LANES), 1).astype(F32)
    pick = jnp.where((live > 0.5) & (rank == lane + 1.0), 1.0, 0.0).astype(BF16)
    pick_ref[...] = pick
    step = 512
    for c in range(features // step):
        part = slice(c * step, (c + 1) * step)
        whole = jnp.concatenate([a[:, part].astype(F32) for a in arrived], axis=0).astype(BF16)
        out_ref[:, part] = lax.dot_general(
            pick[:, :slots], whole, (((0,), (0,)), ((), ())), preferred_element_type=F32
        ).astype(BF16)


def hidden_kernel(columns, *refs):
    blocks, (gate_ref, up_ref, hidden_ref, held) = refs[:columns], refs[columns:]
    slots = blocks[0].shape[0]
    units = gate_ref.shape[1]
    for e in range(columns):
        held[e * slots : (e + 1) * slots, :] = blocks[e][...]
    step = min(256, units)
    for c in range(units // step):
        part = slice(c * step, (c + 1) * step)
        gate = jnp.dot(held[...], gate_ref[:, part], preferred_element_type=F32)
        up = jnp.dot(held[...], up_ref[:, part], preferred_element_type=F32)
        hidden_ref[:, part] = (gate / (1.0 + jnp.exp(-gate)) * up).astype(BF16)


def down_kernel(columns, *refs):
    hiddens, down_ref, outs = refs[:columns], refs[columns], refs[columns + 1 :]
    me = lax.axis_index("ing")
    rows, units = hiddens[0].shape
    slots = rows // columns
    total = jnp.zeros((rows, down_ref.shape[1]), F32)
    for f in range(columns):
        block = jnp.concatenate(
            [hiddens[f][slots * (e ^ f) : slots * ((e ^ f) + 1), :] for e in range(columns)], axis=0
        )
        at = pl.multiple_of((me ^ f) * units, units)
        total += jnp.dot(block, down_ref[pl.ds(at, units), :], preferred_element_type=F32)
    for e in range(columns):
        outs[e][...] = total[e * slots : (e + 1) * slots].astype(BF16)


def spread_kernel(groups, columns, pick_ref, *refs):
    blocks, outs = refs[:columns], refs[columns:]
    for e in range(columns):
        block = blocks[e][...]
        back = jnp.dot(pick_ref[:, : block.shape[0]], block, preferred_element_type=F32)
        for d in range(groups):
            outs[d][e] = back[d * CAP : (d + 1) * CAP].astype(BF16)


def combine_kernel(groups, columns, mixing_ref, *refs):
    backs, (out_ref, held, sems) = refs[:groups], refs[groups:]
    me = lax.axis_index("ing")
    width = backs[0].shape[2]
    copies = []
    for e in range(columns):
        rows = jnp.concatenate([backs[d][e].astype(F32) for d in range(groups)], axis=0)
        value = lax.dot_general(
            mixing_ref[...], rows.astype(BF16), (((0,), (0,)), ((), ())), preferred_element_type=F32
        )
        part = pl.ds(e * width, width)
        held[:, part] = value.astype(BF16)
        there = pl.ds(pl.multiple_of((me ^ e) * width, width), width)
        copies.append(pltpu.make_async_copy(held.at[:, part], out_ref.at[:, there], sems.at[e]))
        copies[-1].start()
    for copy in copies:
        copy.wait()


def swap(x, name, step):
    if step == 0:
        return x
    return lax.ppermute(x, name, [(a, a ^ step) for a in range(lax.axis_size(name))])


def local(tokens, router_logits, expert_ids, w_gate, w_up, w_down):
    groups = lax.axis_size("grp")
    columns = lax.axis_size("ing")
    count, features = tokens.shape
    units, share = w_gate.shape[2], w_down.shape[2]
    slots = groups * CAP // 2
    wide = features + LANES
    ids = pltpu.with_memory_space_constraint(expert_ids.T, pltpu.HBM)
    logits = pltpu.with_memory_space_constraint(router_logits.T, pltpu.HBM)

    outbound = pl.pallas_call(
        functools.partial(dispatch_kernel, groups, 512),
        out_shape=[jax.ShapeDtypeStruct((CAP, wide), BF16)] * groups,
        in_specs=[ANY, ANY],
        out_specs=[VMEM] * groups,
        scratch_shapes=[
            pltpu.VMEM(ids.shape, jnp.int32),
            pltpu.VMEM((count, features), BF16),
            pltpu.VMEM((count, count), BF16),
            pltpu.SemaphoreType.DMA((features // 512 + 1,)),
        ],
        compiler_params=params(2 * count * features),
        name="dispatch",
    )(ids, pltpu.with_memory_space_constraint(tokens, pltpu.HBM))
    arrived = [swap(outbound[d], "grp", d) for d in range(groups)]

    compacted, pick = pl.pallas_call(
        functools.partial(compact_kernel, groups, slots),
        out_shape=[
            jax.ShapeDtypeStruct((slots, features), BF16),
            jax.ShapeDtypeStruct((groups * CAP, LANES), BF16),
        ],
        in_specs=[VMEM] * groups,
        out_specs=[VMEM, VMEM],
        compiler_params=params(2 * (groups * CAP + slots) * wide),
        name="compact",
    )(*arrived)
    blocks = [swap(compacted, "ing", e) for e in range(columns)]

    weights = [w_gate[0], w_up[0], w_down[0]]
    gate, up, down, mixing = pl.pallas_call(
        functools.partial(prepare_kernel, groups),
        out_shape=[pltpu.VMEM(w.shape, BF16) for w in weights]
        + [jax.ShapeDtypeStruct((groups * CAP, count), BF16)],
        in_specs=[ANY] * 6,
        out_specs=[VMEM] * 4,
        scratch_shapes=[
            pltpu.VMEM(ids.shape, jnp.int32),
            pltpu.VMEM(logits.shape, F32),
            pltpu.SemaphoreType.DMA((14,)),
        ],
        compiler_params=params(0),
        name="prepare",
    )(
        pick,
        ids,
        logits,
        *[pltpu.with_memory_space_constraint(w, pltpu.HBM) for w in weights],
    )

    hidden = pl.pallas_call(
        functools.partial(hidden_kernel, columns),
        out_shape=jax.ShapeDtypeStruct((columns * slots, units), BF16),
        in_specs=[VMEM] * (columns + 2),
        out_specs=VMEM,
        scratch_shapes=[pltpu.VMEM((columns * slots, features), BF16)],
        compiler_params=params(2 * columns * slots * (2 * features + units)),
        name="hidden",
    )(*blocks, gate, up)
    hiddens = [swap(hidden, "ing", f) for f in range(columns)]

    results = pl.pallas_call(
        functools.partial(down_kernel, columns),
        out_shape=[jax.ShapeDtypeStruct((slots, share), BF16)] * columns,
        in_specs=[VMEM] * (columns + 1),
        out_specs=[VMEM] * columns,
        compiler_params=params(2 * columns * slots * (columns * units + 4 * share)),
        name="down",
    )(*hiddens, down)
    results = [swap(results[e], "ing", e) for e in range(columns)]

    backs = pl.pallas_call(
        functools.partial(spread_kernel, groups, columns),
        out_shape=[jax.ShapeDtypeStruct((columns, CAP, share), BF16)] * groups,
        in_specs=[VMEM] * (columns + 1),
        out_specs=[VMEM] * groups,
        compiler_params=params(2 * (groups * CAP + slots) * features),
        name="spread",
    )(pick, *results)
    backs = [swap(backs[d], "grp", d) for d in range(groups)]

    if share % LANES:
        me = lax.axis_index("ing")
        rows = jnp.stack(backs)[:, jnp.arange(columns) ^ me]
        rows = rows.transpose(0, 2, 1, 3).reshape(groups * CAP, features)
        return jnp.dot(mixing.T, rows, preferred_element_type=F32).astype(BF16)
    return pl.pallas_call(
        functools.partial(combine_kernel, groups, columns),
        out_shape=jax.ShapeDtypeStruct((count, features), BF16),
        in_specs=[VMEM] * (1 + groups),
        out_specs=ANY,
        scratch_shapes=[pltpu.VMEM((count, features), BF16), pltpu.SemaphoreType.DMA((columns,))],
        compiler_params=params(2 * (count + groups * CAP) * features),
        name="combine",
    )(mixing, *backs)


def solution(mesh):
    placed = (
        P(("rep", "grp", "ing"), None),
        P(("rep", "grp", "ing"), None),
        P(("rep", "grp", "ing"), None),
        P("grp", None, "ing"),
        P("grp", None, "ing"),
        P("grp", None, "ing"),
    )
    return jax.shard_map(
        local, mesh=mesh, in_specs=placed, out_specs=P(("rep", "grp", "ing"), None), check_vma=False
    )
```

time: 50.9 us -> 49.6 us (0.974)
  blocking collectives: 13.8 us -> 0 us
  waiting for transfers between devices: 13.7 us -> 20.1 us
  starting transfers between devices: 12.1 us -> 18.4 us
    all_to_all x1 -> x0, blocking collectives: 13.8 us -> none  [local(): lax.all_to_all(results, ('grp', 'ing'), split_axis=0, concat_axis=0, tile...]
    ppermute x9 -> x15, waiting for transfers between devices: 13.7 us -> 20.1 us  [swap(): lax.ppermute(x, name, [(a, a ^ step) for a in range(lax.axis_size(name))])]
    ppermute x9 -> x15, starting transfers between devices: 12.1 us -> 18.4 us  [swap(): lax.ppermute(x, name, [(a, a ^ step) for a in range(lax.axis_size(name))])]
    pallas_call x2 -> x3, Pallas kernels: 2.43 us -> 2.3 us  [the longest x1 1.39 us: local(): pl.pallas_call(functools.partial(hidden_kernel, columns), out_shape=jax.S...]
  transfers between devices with their start and end apart: 9 -> 15, of which waited for: 4 -> 9; matrix products, arithmetic and copies ran while one was open for 0% -> 0% of each run, Pallas kernels for 9% -> 9%
where the time goes in v1:
time: 49.6 us; the launch traced here: 49.3 us
  waiting for transfers between devices  20.1 us (41%)
  starting transfers between devices  18.4 us (37%)
  Pallas kernels  10.7 us (22%)
    ppermute x15, waiting for transfers between devices, swap(): lax.ppermute(x, name, [(a, a ^ step) for a in range(lax.axis_size(name))])  20.1 us
    ppermute x15, starting transfers between devices, swap(): lax.ppermute(x, name, [(a, a ^ step) for a in range(lax.axis_size(name))])  18.4 us
    pallas_call x1, Pallas kernels, local(): pl.pallas_call(functools.partial(prepare_kernel, groups), out_shape=[pltp...  4.33 us
    pallas_call x1, Pallas kernels, local(): pl.pallas_call(functools.partial(dispatch_kernel, groups, 512), out_shape...  2.16 us
    pallas_call x1, Pallas kernels, local(): pl.pallas_call(functools.partial(combine_kernel, groups, columns), out_sh...  1.57 us
    pallas_call x1, Pallas kernels, local(): pl.pallas_call(functools.partial(hidden_kernel, columns), out_shape=jax.S...  1.39 us
  transfers between devices with their start and end apart: 15, of which 9 were waited for; matrix products, arithmetic and copies ran while one was open for 0% of the time, Pallas kernels for 9%

profile of v1, /device:TPU:0, one launch (start us, length us, event | category | flops | bytes accessed | tf_op | source)
XLA Modules:
  0.0 49.3 jit_solution(14021366068474035561)
XLA Ops:
  0.0 2.2 %dispatch.1 = (bf16[8,3712]{1,0:T(8,128)(2,1)S(1)}, bf16[8,3712]{1,0:T(8,128)(2,1)S(1)}, bf16[8,3712]{1,0:T(8,128)(2,1)S(1)}, bf16[8,3712]{1,0:T(8,128)(2,1)S(1)}) custom-call(s32[8,256]{1,0:T(8,128)} %bitcast.9, bf16[256,3584]{1,0:T(8,128)(2,1)} %tokens_ref.1), custom_call_target="tpu_custom_call" | custom-call | tf_op jit(solution)/shard_map/dispatch/pallas_call | solution.py:202
  2.2 0.5 %collective-permute-start = (bf16[8,3712]{1,0:T(8,128)(2,1)S(1)}, bf16[8,3712]{1,0:T(8,128)(2,1)S(1)}, u32[]{:S(2)}, u32[]{:S(2)}) collective-permute-start(bf16[8,3712]{1,0:T(8,128)(2,1)S(1)} %get-tuple-element.24), channel_id=1, source_target_pairs={{0,4},{4,0},{8,12},{12,8},{1,5},{5,1},{9,13},{13,9},{2,6},{6,2},{1... | collective-permute-start | bytes 178184 | tf_op jit(solution)/shard_map/ppermute | solution.py:189
  2.7 2.6 %collective-permute-start.1 = (bf16[8,3712]{1,0:T(8,128)(2,1)S(1)}, bf16[8,3712]{1,0:T(8,128)(2,1)S(1)}, u32[]{:S(2)}, u32[]{:S(2)}) collective-permute-start(bf16[8,3712]{1,0:T(8,128)(2,1)S(1)} %get-tuple-element.25), channel_id=1, source_target_pairs={{0,8},{4,12},{8,0},{12,4},{1,9},{5,13},{9,1},{13,5},{2,10},{6,14},... | collective-permute-start | bytes 178184 | tf_op jit(solution)/shard_map/ppermute | solution.py:189
  5.2 0.1 collective-permute-start.2
  5.3 0.0 collective-permute-done.refs_1_
  5.3 2.5 %collective-permute-done.1.refs_2_ = bf16[8,3712]{1,0:T(8,128)(2,1)S(1)} collective-permute-done((bf16[8,3712]{1,0:T(8,128)(2,1)S(1)}, bf16[8,3712]{1,0:T(8,128)(2,1)S(1)}, u32[]{:S(2)}, u32[]{:S(2)}) %collective-permute-start.1) | collective-permute-done | bytes 59424 | tf_op jit(solution)/shard_map/ppermute | solution.py:189
  7.8 1.4 %collective-permute-done.2.refs_3_ = bf16[8,3712]{1,0:T(8,128)(2,1)S(1)} collective-permute-done((bf16[8,3712]{1,0:T(8,128)(2,1)S(1)}, bf16[8,3712]{1,0:T(8,128)(2,1)S(1)}, u32[]{:S(2)}, u32[]{:S(2)}) %collective-permute-start.2) | collective-permute-done | bytes 59424 | tf_op jit(solution)/shard_map/ppermute | solution.py:189
  9.2 0.3 compact.1
  9.5 3.7 %collective-permute-start.5 = (bf16[16,3584]{1,0:T(8,128)(2,1)S(1)}, bf16[16,3584]{1,0:T(8,128)(2,1)S(1)}, u32[]{:S(2)}, u32[]{:S(2)}) collective-permute-start(bf16[16,3584]{1,0:T(8,128)(2,1)S(1)} %get-tuple-element.29.refs_0_), channel_id=1, source_target_pairs={{0,3},{1,2},{2,1},{3,0},{4,7},{5,6},{6,5},{7,4},{8,11},{9,10},{10,... | collective-permute-start | bytes 344072 | tf_op jit(solution)/shard_map/ppermute | solution.py:189
  13.2 0.0 collective-permute-start.4
  13.2 0.8 %collective-permute-start.3 = (bf16[16,3584]{1,0:T(8,128)(2,1)S(1)}, bf16[16,3584]{1,0:T(8,128)(2,1)S(1)}, u32[]{:S(2)}, u32[]{:S(2)}) collective-permute-start(bf16[16,3584]{1,0:T(8,128)(2,1)S(1)} %get-tuple-element.29.refs_0_), channel_id=1, source_target_pairs={{0,1},{1,0},{2,3},{3,2},{4,5},{5,4},{6,7},{7,6},{8,9},{9,8},{10,11... | collective-permute-start | bytes 344072 | tf_op jit(solution)/shard_map/ppermute | solution.py:189
  14.0 4.3 %prepare.1 = (bf16[3584,512]{1,0:T(8,128)(2,1)S(1)}, bf16[3584,512]{1,0:T(8,128)(2,1)S(1)}, bf16[2048,896]{1,0:T(8,128)(2,1)S(1)}, bf16[32,256]{1,0:T(8,128)(2,1)S(1)}) custom-call(bf16[32,128]{1,0:T(8,128)(2,1)S(1)} %get-tuple-element.27.after_ref.pick_ref, s32[8,256]{1,0:T(8,128)} %bitcast.10, f32[96,256]{1,0:T(8,128)} %bitcast.8, ...), custom_call_target="tpu_custom_call" | custom-call | tf_op jit(solution)/shard_map/prepare/pallas_call | solution.py:232
  18.3 0.0 collective-permute-done.5.refs_3_
  18.3 4.9 %collective-permute-done.4.refs_2_ = bf16[16,3584]{1,0:T(8,128)(2,1)S(1)} collective-permute-done((bf16[16,3584]{1,0:T(8,128)(2,1)S(1)}, bf16[16,3584]{1,0:T(8,128)(2,1)S(1)}, u32[]{:S(2)}, u32[]{:S(2)}) %collective-permute-start.4) | collective-permute-done | bytes 114720 | tf_op jit(solution)/shard_map/ppermute | solution.py:189
  23.2 1.4 %hidden.1.refs_0_ = bf16[64,512]{1,0:T(8,128)(2,1)S(1)} custom-call(bf16[16,3584]{1,0:T(8,128)(2,1)S(1)} %get-tuple-element.29.refs_0_, bf16[16,3584]{1,0:T(8,128)(2,1)S(1)} %collective-permute-done.3.refs_1_, bf16[16,3584]{1,0:T(8,128)(2,1)S(1)} %collective-permute-done.4.refs_2_, bf16[16,3584]{1,0:T(8,128)(2,1)S(1)} %collective-permute-done.5.refs_3_, ...), custom_call_target="tpu_custom_call" | custom-call | tf_op jit(solution)/shard_map/hidden/pallas_call | solution.py:252
  24.6 2.5 %collective-permute-start.8 = (bf16[64,512]{1,0:T(8,128)(2,1)S(1)}, bf16[64,512]{1,0:T(8,128)(2,1)S(1)}, u32[]{:S(2)}, u32[]{:S(2)}) collective-permute-start(bf16[64,512]{1,0:T(8,128)(2,1)S(1)} %hidden.1.refs_0_), channel_id=1, source_target_pairs={{0,3},{1,2},{2,1},{3,0},{4,7},{5,6},{6,5},{7,4},{8,11},{9,10},{10,... | collective-permute-start | bytes 196616 | tf_op jit(solution)/shard_map/ppermute | solution.py:189
  27.1 1.9 %collective-permute-start.6 = (bf16[64,512]{1,0:T(8,128)(2,1)S(1)}, bf16[64,512]{1,0:T(8,128)(2,1)S(1)}, u32[]{:S(2)}, u32[]{:S(2)}) collective-permute-start(bf16[64,512]{1,0:T(8,128)(2,1)S(1)} %hidden.1.refs_0_), channel_id=1, source_target_pairs={{0,1},{1,0},{2,3},{3,2},{4,5},{5,4},{6,7},{7,6},{8,9},{9,8},{10,11... | collective-permute-start | bytes 196616 | tf_op jit(solution)/shard_map/ppermute | solution.py:189
  29.0 1.7 %collective-permute-done.8.refs_3_ = bf16[64,512]{1,0:T(8,128)(2,1)S(1)} collective-permute-done((bf16[64,512]{1,0:T(8,128)(2,1)S(1)}, bf16[64,512]{1,0:T(8,128)(2,1)S(1)}, u32[]{:S(2)}, u32[]{:S(2)}) %collective-permute-start.8) | collective-permute-done | bytes 65568 | tf_op jit(solution)/shard_map/ppermute | solution.py:189
  30.7 2.0 %collective-permute-done.7.refs_2_ = bf16[64,512]{1,0:T(8,128)(2,1)S(1)} collective-permute-done((bf16[64,512]{1,0:T(8,128)(2,1)S(1)}, bf16[64,512]{1,0:T(8,128)(2,1)S(1)}, u32[]{:S(2)}, u32[]{:S(2)}) %collective-permute-start.7) | collective-permute-done | bytes 65568 | tf_op jit(solution)/shard_map/ppermute | solution.py:189
  32.7 0.7 %down.1 = (bf16[16,896]{1,0:T(8,128)(2,1)S(1)}, bf16[16,896]{1,0:T(8,128)(2,1)S(1)}, bf16[16,896]{1,0:T(8,128)(2,1)S(1)}, bf16[16,896]{1,0:T(8,128)(2,1)S(1)}) custom-call(bf16[64,512]{1,0:T(8,128)(2,1)S(1)} %hidden.1.refs_0_, bf16[64,512]{1,0:T(8,128)(2,1)S(1)} %collective-permute-done.6.refs_1_, bf16[64,512]{1,0:T(8,128)(2,1)S(1)} %collective-permute-done.7.refs_2_, ...), custom_call_target="tpu_custom_call" | custom-call | tf_op jit(solution)/shard_map/down/pallas_call | solution.py:263
  33.5 0.6 %collective-permute-start.9 = (bf16[16,896]{1,0:T(8,128)(2,1)S(1)}, bf16[16,896]{1,0:T(8,128)(2,1)S(1)}, u32[]{:S(2)}, u32[]{:S(2)}) collective-permute-start(bf16[16,896]{1,0:T(8,128)(2,1)S(1)} %get-tuple-element.34), channel_id=1, source_target_pairs={{0,1},{1,0},{2,3},{3,2},{4,5},{5,4},{6,7},{7,6},{8,9},{9,8},{10,11... | collective-permute-start | bytes 86024 | tf_op jit(solution)/shard_map/ppermute | solution.py:189
  34.1 2.3 %collective-permute-start.10 = (bf16[16,896]{1,0:T(8,128)(2,1)S(1)}, bf16[16,896]{1,0:T(8,128)(2,1)S(1)}, u32[]{:S(2)}, u32[]{:S(2)}) collective-permute-start(bf16[16,896]{1,0:T(8,128)(2,1)S(1)} %get-tuple-element.35), channel_id=1, source_target_pairs={{0,2},{1,3},{2,0},{3,1},{4,6},{5,7},{6,4},{7,5},{8,10},{9,11},{10,... | collective-permute-start | bytes 86024 | tf_op jit(solution)/shard_map/ppermute | solution.py:189
  36.4 1.5 %collective-permute-start.11 = (bf16[16,896]{1,0:T(8,128)(2,1)S(1)}, bf16[16,896]{1,0:T(8,128)(2,1)S(1)}, u32[]{:S(2)}, u32[]{:S(2)}) collective-permute-start(bf16[16,896]{1,0:T(8,128)(2,1)S(1)} %get-tuple-element.36), channel_id=1, source_target_pairs={{0,3},{1,2},{2,1},{3,0},{4,7},{5,6},{6,5},{7,4},{8,11},{9,10},{10,... | collective-permute-start | bytes 86024 | tf_op jit(solution)/shard_map/ppermute | solution.py:189
  37.9 0.9 %collective-permute-done.10.refs_2_ = bf16[16,896]{1,0:T(8,128)(2,1)S(1)} collective-permute-done((bf16[16,896]{1,0:T(8,128)(2,1)S(1)}, bf16[16,896]{1,0:T(8,128)(2,1)S(1)}, u32[]{:S(2)}, u32[]{:S(2)}) %collective-permute-start.10) | collective-permute-done | bytes 28704 | tf_op jit(solution)/shard_map/ppermute | solution.py:189
  38.9 3.2 %collective-permute-done.11.refs_3_ = bf16[16,896]{1,0:T(8,128)(2,1)S(1)} collective-permute-done((bf16[16,896]{1,0:T(8,128)(2,1)S(1)}, bf16[16,896]{1,0:T(8,128)(2,1)S(1)}, u32[]{:S(2)}, u32[]{:S(2)}) %collective-permute-start.11) | collective-permute-done | bytes 28704 | tf_op jit(solution)/shard_map/ppermute | solution.py:189
  42.1 0.2 spread.1
  42.3 0.1 collective-permute-start.12
  42.4 1.5 %collective-permute-start.13 = (bf16[4,8,896]{2,1,0:T(8,128)(2,1)S(1)}, bf16[4,8,896]{2,1,0:T(8,128)(2,1)S(1)}, u32[]{:S(2)}, u32[]{:S(2)}) collective-permute-start(bf16[4,8,896]{2,1,0:T(8,128)(2,1)S(1)} %get-tuple-element.39), channel_id=1, source_target_pairs={{0,8},{4,12},{8,0},{12,4},{1,9},{5,13},{9,1},{13,5},{2,10},{6,14},... | collective-permute-start | bytes 172040 | tf_op jit(solution)/shard_map/ppermute | solution.py:189
  43.9 0.3 collective-permute-start.14
  44.2 2.5 %collective-permute-done.13.refs_2_ = bf16[4,8,896]{2,1,0:T(8,128)(2,1)S(1)} collective-permute-done((bf16[4,8,896]{2,1,0:T(8,128)(2,1)S(1)}, bf16[4,8,896]{2,1,0:T(8,128)(2,1)S(1)}, u32[]{:S(2)}, u32[]{:S(2)}) %collective-permute-start.13) | collective-permute-done | bytes 57376 | tf_op jit(solution)/shard_map/ppermute | solution.py:189
  46.7 1.1 %collective-permute-done.14.refs_3_ = bf16[4,8,896]{2,1,0:T(8,128)(2,1)S(1)} collective-permute-done((bf16[4,8,896]{2,1,0:T(8,128)(2,1)S(1)}, bf16[4,8,896]{2,1,0:T(8,128)(2,1)S(1)}, u32[]{:S(2)}, u32[]{:S(2)}) %collective-permute-start.14) | collective-permute-done | bytes 57376 | tf_op jit(solution)/shard_map/ppermute | solution.py:189
  47.8 1.6 %combine.1 = bf16[256,3584]{1,0:T(8,128)(2,1)} custom-call(bf16[32,256]{1,0:T(8,128)(2,1)S(1)} %get-tuple-element.28.mixing_ref, bf16[4,8,896]{2,1,0:T(8,128)(2,1)S(1)} %get-tuple-element.37.refs_0_, bf16[4,8,896]{2,1,0:T(8,128)(2,1)S(1)} %collective-permute-done.12.refs_1_, bf16[4,8,896]{2,1,0:T(8,128)(2,1)S(1)} %collective-permute-done.13.refs_2_, ...), custom_call_target="tpu_custom_call" | custom-call | tf_op jit(solution)/shard_map/combine/pallas_call | solution.py:288
  (5 shorter events, 0.0 us)
Async XLA Ops:
  2.2 3.2 %collective-permute-start = (bf16[8,3712]{1,0:T(8,128)(2,1)S(1)}, bf16[8,3712]{1,0:T(8,128)(2,1)S(1)}, u32[]{:S(2)}, u32[]{:S(2)}) collective-permute-start(bf16[8,3712]{1,0:T(8,128)(2,1)S(1)} %get-tuple-element.24), channel_id=1, source_target_pairs={{0,4},{4,0},{8,12},{12,8},{1,5},{5,1},{9,13},{13,9},{2,6},{6,2},{1... | collective-permute-start | bytes 178184 | tf_op jit(solution)/shard_map/ppermute | solution.py:189
  2.7 5.1 %collective-permute-start.1 = (bf16[8,3712]{1,0:T(8,128)(2,1)S(1)}, bf16[8,3712]{1,0:T(8,128)(2,1)S(1)}, u32[]{:S(2)}, u32[]{:S(2)}) collective-permute-start(bf16[8,3712]{1,0:T(8,128)(2,1)S(1)} %get-tuple-element.25), channel_id=1, source_target_pairs={{0,8},{4,12},{8,0},{12,4},{1,9},{5,13},{9,1},{13,5},{2,10},{6,14},... | collective-permute-start | bytes 178184 | tf_op jit(solution)/shard_map/ppermute | solution.py:189
  5.2 3.9 %collective-permute-start.2 = (bf16[8,3712]{1,0:T(8,128)(2,1)S(1)}, bf16[8,3712]{1,0:T(8,128)(2,1)S(1)}, u32[]{:S(2)}, u32[]{:S(2)}) collective-permute-start(bf16[8,3712]{1,0:T(8,128)(2,1)S(1)} %get-tuple-element.26), channel_id=1, source_target_pairs={{0,12},{4,8},{8,4},{12,0},{1,13},{5,9},{9,5},{13,1},{2,14},{6,10},... | collective-permute-start | bytes 178184 | tf_op jit(solution)/shard_map/ppermute | solution.py:189
  9.5 8.8 %collective-permute-start.5 = (bf16[16,3584]{1,0:T(8,128)(2,1)S(1)}, bf16[16,3584]{1,0:T(8,128)(2,1)S(1)}, u32[]{:S(2)}, u32[]{:S(2)}) collective-permute-start(bf16[16,3584]{1,0:T(8,128)(2,1)S(1)} %get-tuple-element.29.refs_0_), channel_id=1, source_target_pairs={{0,3},{1,2},{2,1},{3,0},{4,7},{5,6},{6,5},{7,4},{8,11},{9,10},{10,... | collective-permute-start | bytes 344072 | tf_op jit(solution)/shard_map/ppermute | solution.py:189
  13.2 10.0 %collective-permute-start.4 = (bf16[16,3584]{1,0:T(8,128)(2,1)S(1)}, bf16[16,3584]{1,0:T(8,128)(2,1)S(1)}, u32[]{:S(2)}, u32[]{:S(2)}) collective-permute-start(bf16[16,3584]{1,0:T(8,128)(2,1)S(1)} %get-tuple-element.29.refs_0_), channel_id=1, source_target_pairs={{0,2},{1,3},{2,0},{3,1},{4,6},{5,7},{6,4},{7,5},{8,10},{9,11},{10,... | collective-permute-start | bytes 344072 | tf_op jit(solution)/shard_map/ppermute | solution.py:189
  13.2 10.0 %collective-permute-start.3 = (bf16[16,3584]{1,0:T(8,128)(2,1)S(1)}, bf16[16,3584]{1,0:T(8,128)(2,1)S(1)}, u32[]{:S(2)}, u32[]{:S(2)}) collective-permute-start(bf16[16,3584]{1,0:T(8,128)(2,1)S(1)} %get-tuple-element.29.refs_0_), channel_id=1, source_target_pairs={{0,1},{1,0},{2,3},{3,2},{4,5},{5,4},{6,7},{7,6},{8,9},{9,8},{10,11... | collective-permute-start | bytes 344072 | tf_op jit(solution)/shard_map/ppermute | solution.py:189
  24.6 6.1 %collective-permute-start.8 = (bf16[64,512]{1,0:T(8,128)(2,1)S(1)}, bf16[64,512]{1,0:T(8,128)(2,1)S(1)}, u32[]{:S(2)}, u32[]{:S(2)}) collective-permute-start(bf16[64,512]{1,0:T(8,128)(2,1)S(1)} %hidden.1.refs_0_), channel_id=1, source_target_pairs={{0,3},{1,2},{2,1},{3,0},{4,7},{5,6},{6,5},{7,4},{8,11},{9,10},{10,... | collective-permute-start | bytes 196616 | tf_op jit(solution)/shard_map/ppermute | solution.py:189
  27.1 5.6 %collective-permute-start.7 = (bf16[64,512]{1,0:T(8,128)(2,1)S(1)}, bf16[64,512]{1,0:T(8,128)(2,1)S(1)}, u32[]{:S(2)}, u32[]{:S(2)}) collective-permute-start(bf16[64,512]{1,0:T(8,128)(2,1)S(1)} %hidden.1.refs_0_), channel_id=1, source_target_pairs={{0,2},{1,3},{2,0},{3,1},{4,6},{5,7},{6,4},{7,5},{8,10},{9,11},{10,... | collective-permute-start | bytes 196616 | tf_op jit(solution)/shard_map/ppermute | solution.py:189
  27.1 5.6 %collective-permute-start.6 = (bf16[64,512]{1,0:T(8,128)(2,1)S(1)}, bf16[64,512]{1,0:T(8,128)(2,1)S(1)}, u32[]{:S(2)}, u32[]{:S(2)}) collective-permute-start(bf16[64,512]{1,0:T(8,128)(2,1)S(1)} %hidden.1.refs_0_), channel_id=1, source_target_pairs={{0,1},{1,0},{2,3},{3,2},{4,5},{5,4},{6,7},{7,6},{8,9},{9,8},{10,11... | collective-permute-start | bytes 196616 | tf_op jit(solution)/shard_map/ppermute | solution.py:189
  33.5 4.5 %collective-permute-start.9 = (bf16[16,896]{1,0:T(8,128)(2,1)S(1)}, bf16[16,896]{1,0:T(8,128)(2,1)S(1)}, u32[]{:S(2)}, u32[]{:S(2)}) collective-permute-start(bf16[16,896]{1,0:T(8,128)(2,1)S(1)} %get-tuple-element.34), channel_id=1, source_target_pairs={{0,1},{1,0},{2,3},{3,2},{4,5},{5,4},{6,7},{7,6},{8,9},{9,8},{10,11... | collective-permute-start | bytes 86024 | tf_op jit(solution)/shard_map/ppermute | solution.py:189
  34.1 4.8 %collective-permute-start.10 = (bf16[16,896]{1,0:T(8,128)(2,1)S(1)}, bf16[16,896]{1,0:T(8,128)(2,1)S(1)}, u32[]{:S(2)}, u32[]{:S(2)}) collective-permute-start(bf16[16,896]{1,0:T(8,128)(2,1)S(1)} %get-tuple-element.35), channel_id=1, source_target_pairs={{0,2},{1,3},{2,0},{3,1},{4,6},{5,7},{6,4},{7,5},{8,10},{9,11},{10,... | collective-permute-start | bytes 86024 | tf_op jit(solution)/shard_map/ppermute | solution.py:189
  36.4 5.7 %collective-permute-start.11 = (bf16[16,896]{1,0:T(8,128)(2,1)S(1)}, bf16[16,896]{1,0:T(8,128)(2,1)S(1)}, u32[]{:S(2)}, u32[]{:S(2)}) collective-permute-start(bf16[16,896]{1,0:T(8,128)(2,1)S(1)} %get-tuple-element.36), channel_id=1, source_target_pairs={{0,3},{1,2},{2,1},{3,0},{4,7},{5,6},{6,5},{7,4},{8,11},{9,10},{10,... | collective-permute-start | bytes 86024 | tf_op jit(solution)/shard_map/ppermute | solution.py:189
  42.3 1.9 %collective-permute-start.12 = (bf16[4,8,896]{2,1,0:T(8,128)(2,1)S(1)}, bf16[4,8,896]{2,1,0:T(8,128)(2,1)S(1)}, u32[]{:S(2)}, u32[]{:S(2)}) collective-permute-start(bf16[4,8,896]{2,1,0:T(8,128)(2,1)S(1)} %get-tuple-element.38), channel_id=1, source_target_pairs={{0,4},{4,0},{8,12},{12,8},{1,5},{5,1},{9,13},{13,9},{2,6},{6,2},{1... | collective-permute-start | bytes 172040 | tf_op jit(solution)/shard_map/ppermute | solution.py:189
  42.4 4.3 %collective-permute-start.13 = (bf16[4,8,896]{2,1,0:T(8,128)(2,1)S(1)}, bf16[4,8,896]{2,1,0:T(8,128)(2,1)S(1)}, u32[]{:S(2)}, u32[]{:S(2)}) collective-permute-start(bf16[4,8,896]{2,1,0:T(8,128)(2,1)S(1)} %get-tuple-element.39), channel_id=1, source_target_pairs={{0,8},{4,12},{8,0},{12,4},{1,9},{5,13},{9,1},{13,5},{2,10},{6,14},... | collective-permute-start | bytes 172040 | tf_op jit(solution)/shard_map/ppermute | solution.py:189
  43.9 3.9 %collective-permute-start.14 = (bf16[4,8,896]{2,1,0:T(8,128)(2,1)S(1)}, bf16[4,8,896]{2,1,0:T(8,128)(2,1)S(1)}, u32[]{:S(2)}, u32[]{:S(2)}) collective-permute-start(bf16[4,8,896]{2,1,0:T(8,128)(2,1)S(1)} %get-tuple-element.40), channel_id=1, source_target_pairs={{0,12},{4,8},{8,4},{12,0},{1,13},{5,9},{9,5},{13,1},{2,14},{6,10},... | collective-permute-start | bytes 172040 | tf_op jit(solution)/shard_map/ppermute | solution.py:189

commit v2 on v1

--- a/solution.py
+++ b/solution.py
@@ -101,7 +101,7 @@
     for g in range(groups):
         leading = jnp.where(group == g, scores[g * GROUP_EXPERTS : g * GROUP_EXPERTS + 1, :], leading)
     weight = (ROUTE_SCALE * leading / chosen).astype(BF16).astype(F32)
-    out_ref[...] = jnp.where(place > 0.5, weight, 0.0).astype(BF16)
+    out_ref[...] = jnp.where(place > 0.5, weight, 0.0).T.astype(BF16)
     for copy in copies:
         copy.wait()
 
@@ -171,9 +171,7 @@
     copies = []
     for e in range(columns):
         rows = jnp.concatenate([backs[d][e].astype(F32) for d in range(groups)], axis=0)
-        value = lax.dot_general(
-            mixing_ref[...], rows.astype(BF16), (((0,), (0,)), ((), ())), preferred_element_type=F32
-        )
+        value = jnp.dot(mixing_ref[...], rows.astype(BF16), preferred_element_type=F32)
         part = pl.ds(e * width, width)
         held[:, part] = value.astype(BF16)
         there = pl.ds(pl.multiple_of((me ^ e) * width, width), width)
@@ -187,6 +185,11 @@
     if step == 0:
         return x
     return lax.ppermute(x, name, [(a, a ^ step) for a in range(lax.axis_size(name))])
+
+
+def swap_all(parts, name):
+    got = {k: swap(parts[k], name, k) for k in reversed(range(len(parts)))}
+    return [got[k] for k in range(len(parts))]
 
 
 def local(tokens, router_logits, expert_ids, w_gate, w_up, w_down):
@@ -213,7 +216,7 @@
         compiler_params=params(2 * count * features),
         name="dispatch",
     )(ids, pltpu.with_memory_space_constraint(tokens, pltpu.HBM))
-    arrived = [swap(outbound[d], "grp", d) for d in range(groups)]
+    arrived = swap_all(outbound, "grp")
 
     compacted, pick = pl.pallas_call(
         functools.partial(compact_kernel, groups, slots),
@@ -232,7 +235,7 @@
     gate, up, down, mixing = pl.pallas_call(
         functools.partial(prepare_kernel, groups),
         out_shape=[pltpu.VMEM(w.shape, BF16) for w in weights]
-        + [jax.ShapeDtypeStruct((groups * CAP, count), BF16)],
+        + [jax.ShapeDtypeStruct((count, groups * CAP), BF16)],
         in_specs=[ANY] * 6,
         out_specs=[VMEM] * 4,
         scratch_shapes=[
@@ -268,7 +271,7 @@
         compiler_params=params(2 * columns * slots * (columns * units + 4 * share)),
         name="down",
     )(*hiddens, down)
-    results = [swap(results[e], "ing", e) for e in range(columns)]
+    results = swap_all(results, "ing")
 
     backs = pl.pallas_call(
         functools.partial(spread_kernel, groups, columns),
@@ -278,13 +281,13 @@
         compiler_params=params(2 * (groups * CAP + slots) * features),
         name="spread",
     )(pick, *results)
-    backs = [swap(backs[d], "grp", d) for d in range(groups)]
+    backs = swap_all(backs, "grp")
 
     if share % LANES:
         me = lax.axis_index("ing")
         rows = jnp.stack(backs)[:, jnp.arange(columns) ^ me]
         rows = rows.transpose(0, 2, 1, 3).reshape(groups * CAP, features)
-        return jnp.dot(mixing.T, rows, preferred_element_type=F32).astype(BF16)
+        return jnp.dot(mixing, rows, preferred_element_type=F32).astype(BF16)
     return pl.pallas_call(
         functools.partial(combine_kernel, groups, columns),
         out_shape=jax.ShapeDtypeStruct((count, features), BF16),

time: 49.6 us -> 49.5 us (level)
  no operation moved by 1% of the time
where the time goes in v2:
time: 49.5 us; the launch traced here: 49.3 us
  waiting for transfers between devices  20.1 us (41%)
  starting transfers between devices  18.4 us (37%)
  Pallas kernels  10.6 us (21%)
    ppermute x15, waiting for transfers between devices, swap(): lax.ppermute(x, name, [(a, a ^ step) for a in range(lax.axis_size(name))])  20.1 us
    ppermute x15, starting transfers between devices, swap(): lax.ppermute(x, name, [(a, a ^ step) for a in range(lax.axis_size(name))])  18.4 us
    pallas_call x1, Pallas kernels, local(): pl.pallas_call(functools.partial(prepare_kernel, groups), out_shape=[pltp...  4.33 us
    pallas_call x1, Pallas kernels, local(): pl.pallas_call(functools.partial(dispatch_kernel, groups, 512), out_shape...  2.16 us
    pallas_call x1, Pallas kernels, local(): pl.pallas_call(functools.partial(combine_kernel, groups, columns), out_sh...  1.52 us
    pallas_call x1, Pallas kernels, local(): pl.pallas_call(functools.partial(hidden_kernel, columns), out_shape=jax.S...  1.39 us
  transfers between devices with their start and end apart: 15, of which 9 were waited for; matrix products, arithmetic and copies ran while one was open for 0% of the time, Pallas kernels for 9%

profile of v2, /device:TPU:0, one launch (start us, length us, event | category | flops | bytes accessed | tf_op | source)
XLA Modules:
  0.0 49.3 jit_solution(4064761326194634213)
XLA Ops:
  0.0 2.2 %dispatch.1 = (bf16[8,3712]{1,0:T(8,128)(2,1)S(1)}, bf16[8,3712]{1,0:T(8,128)(2,1)S(1)}, bf16[8,3712]{1,0:T(8,128)(2,1)S(1)}, bf16[8,3712]{1,0:T(8,128)(2,1)S(1)}) custom-call(s32[8,256]{1,0:T(8,128)} %bitcast.9, bf16[256,3584]{1,0:T(8,128)(2,1)} %tokens_ref.1), custom_call_target="tpu_custom_call" | custom-call | tf_op jit(solution)/shard_map/dispatch/pallas_call | solution.py:205
  2.2 0.5 %collective-permute-start = (bf16[8,3712]{1,0:T(8,128)(2,1)S(1)}, bf16[8,3712]{1,0:T(8,128)(2,1)S(1)}, u32[]{:S(2)}, u32[]{:S(2)}) collective-permute-start(bf16[8,3712]{1,0:T(8,128)(2,1)S(1)} %get-tuple-element.24), channel_id=1, source_target_pairs={{0,4},{4,0},{8,12},{12,8},{1,5},{5,1},{9,13},{13,9},{2,6},{6,2},{1... | collective-permute-start | bytes 178184 | tf_op jit(solution)/shard_map/ppermute | solution.py:187
  2.7 2.6 %collective-permute-start.1 = (bf16[8,3712]{1,0:T(8,128)(2,1)S(1)}, bf16[8,3712]{1,0:T(8,128)(2,1)S(1)}, u32[]{:S(2)}, u32[]{:S(2)}) collective-permute-start(bf16[8,3712]{1,0:T(8,128)(2,1)S(1)} %get-tuple-element.25), channel_id=1, source_target_pairs={{0,8},{4,12},{8,0},{12,4},{1,9},{5,13},{9,1},{13,5},{2,10},{6,14},... | collective-permute-start | bytes 178184 | tf_op jit(solution)/shard_map/ppermute | solution.py:187
  5.2 0.1 collective-permute-start.2
  5.3 0.0 collective-permute-done.refs_1_
  5.3 2.5 %collective-permute-done.1.refs_2_ = bf16[8,3712]{1,0:T(8,128)(2,1)S(1)} collective-permute-done((bf16[8,3712]{1,0:T(8,128)(2,1)S(1)}, bf16[8,3712]{1,0:T(8,128)(2,1)S(1)}, u32[]{:S(2)}, u32[]{:S(2)}) %collective-permute-start.1) | collective-permute-done | bytes 59424 | tf_op jit(solution)/shard_map/ppermute | solution.py:187
  7.8 1.4 %collective-permute-done.2.refs_3_ = bf16[8,3712]{1,0:T(8,128)(2,1)S(1)} collective-permute-done((bf16[8,3712]{1,0:T(8,128)(2,1)S(1)}, bf16[8,3712]{1,0:T(8,128)(2,1)S(1)}, u32[]{:S(2)}, u32[]{:S(2)}) %collective-permute-start.2) | collective-permute-done | bytes 59424 | tf_op jit(solution)/shard_map/ppermute | solution.py:187
  9.2 0.3 compact.1
  9.5 3.7 %collective-permute-start.5 = (bf16[16,3584]{1,0:T(8,128)(2,1)S(1)}, bf16[16,3584]{1,0:T(8,128)(2,1)S(1)}, u32[]{:S(2)}, u32[]{:S(2)}) collective-permute-start(bf16[16,3584]{1,0:T(8,128)(2,1)S(1)} %get-tuple-element.29.refs_0_), channel_id=1, source_target_pairs={{0,3},{1,2},{2,1},{3,0},{4,7},{5,6},{6,5},{7,4},{8,11},{9,10},{10,... | collective-permute-start | bytes 344072 | tf_op jit(solution)/shard_map/ppermute | solution.py:187
  13.2 0.0 collective-permute-start.4
  13.2 0.8 %collective-permute-start.3 = (bf16[16,3584]{1,0:T(8,128)(2,1)S(1)}, bf16[16,3584]{1,0:T(8,128)(2,1)S(1)}, u32[]{:S(2)}, u32[]{:S(2)}) collective-permute-start(bf16[16,3584]{1,0:T(8,128)(2,1)S(1)} %get-tuple-element.29.refs_0_), channel_id=1, source_target_pairs={{0,1},{1,0},{2,3},{3,2},{4,5},{5,4},{6,7},{7,6},{8,9},{9,8},{10,11... | collective-permute-start | bytes 344072 | tf_op jit(solution)/shard_map/ppermute | solution.py:187
  14.0 4.3 %prepare.1 = (bf16[3584,512]{1,0:T(8,128)(2,1)S(1)}, bf16[3584,512]{1,0:T(8,128)(2,1)S(1)}, bf16[2048,896]{1,0:T(8,128)(2,1)S(1)}, bf16[256,32]{1,0:T(8,128)(2,1)S(1)}) custom-call(bf16[32,128]{1,0:T(8,128)(2,1)S(1)} %get-tuple-element.27.after_ref.pick_ref, s32[8,256]{1,0:T(8,128)} %bitcast.10, f32[96,256]{1,0:T(8,128)} %bitcast.8, ...), custom_call_target="tpu_custom_call" | custom-call | tf_op jit(solution)/shard_map/prepare/pallas_call | solution.py:235
  18.3 4.9 %collective-permute-done.4.refs_2_ = bf16[16,3584]{1,0:T(8,128)(2,1)S(1)} collective-permute-done((bf16[16,3584]{1,0:T(8,128)(2,1)S(1)}, bf16[16,3584]{1,0:T(8,128)(2,1)S(1)}, u32[]{:S(2)}, u32[]{:S(2)}) %collective-permute-start.4) | collective-permute-done | bytes 114720 | tf_op jit(solution)/shard_map/ppermute | solution.py:187
  23.2 1.4 %hidden.1.refs_0_ = bf16[64,512]{1,0:T(8,128)(2,1)S(1)} custom-call(bf16[16,3584]{1,0:T(8,128)(2,1)S(1)} %get-tuple-element.29.refs_0_, bf16[16,3584]{1,0:T(8,128)(2,1)S(1)} %collective-permute-done.3.refs_1_, bf16[16,3584]{1,0:T(8,128)(2,1)S(1)} %collective-permute-done.4.refs_2_, bf16[16,3584]{1,0:T(8,128)(2,1)S(1)} %collective-permute-done.5.refs_3_, ...), custom_call_target="tpu_custom_call" | custom-call | tf_op jit(solution)/shard_map/hidden/pallas_call | solution.py:255
  24.6 2.5 %collective-permute-start.8 = (bf16[64,512]{1,0:T(8,128)(2,1)S(1)}, bf16[64,512]{1,0:T(8,128)(2,1)S(1)}, u32[]{:S(2)}, u32[]{:S(2)}) collective-permute-start(bf16[64,512]{1,0:T(8,128)(2,1)S(1)} %hidden.1.refs_0_), channel_id=1, source_target_pairs={{0,3},{1,2},{2,1},{3,0},{4,7},{5,6},{6,5},{7,4},{8,11},{9,10},{10,... | collective-permute-start | bytes 196616 | tf_op jit(solution)/shard_map/ppermute | solution.py:187
  27.1 0.0 collective-permute-start.7
  27.1 1.9 %collective-permute-start.6 = (bf16[64,512]{1,0:T(8,128)(2,1)S(1)}, bf16[64,512]{1,0:T(8,128)(2,1)S(1)}, u32[]{:S(2)}, u32[]{:S(2)}) collective-permute-start(bf16[64,512]{1,0:T(8,128)(2,1)S(1)} %hidden.1.refs_0_), channel_id=1, source_target_pairs={{0,1},{1,0},{2,3},{3,2},{4,5},{5,4},{6,7},{7,6},{8,9},{9,8},{10,11... | collective-permute-start | bytes 196616 | tf_op jit(solution)/shard_map/ppermute | solution.py:187
  29.0 1.7 %collective-permute-done.8.refs_3_ = bf16[64,512]{1,0:T(8,128)(2,1)S(1)} collective-permute-done((bf16[64,512]{1,0:T(8,128)(2,1)S(1)}, bf16[64,512]{1,0:T(8,128)(2,1)S(1)}, u32[]{:S(2)}, u32[]{:S(2)}) %collective-permute-start.8) | collective-permute-done | bytes 65568 | tf_op jit(solution)/shard_map/ppermute | solution.py:187
  30.7 2.0 %collective-permute-done.7.refs_2_ = bf16[64,512]{1,0:T(8,128)(2,1)S(1)} collective-permute-done((bf16[64,512]{1,0:T(8,128)(2,1)S(1)}, bf16[64,512]{1,0:T(8,128)(2,1)S(1)}, u32[]{:S(2)}, u32[]{:S(2)}) %collective-permute-start.7) | collective-permute-done | bytes 65568 | tf_op jit(solution)/shard_map/ppermute | solution.py:187
  32.7 0.7 %down.1 = (bf16[16,896]{1,0:T(8,128)(2,1)S(1)}, bf16[16,896]{1,0:T(8,128)(2,1)S(1)}, bf16[16,896]{1,0:T(8,128)(2,1)S(1)}, bf16[16,896]{1,0:T(8,128)(2,1)S(1)}) custom-call(bf16[64,512]{1,0:T(8,128)(2,1)S(1)} %hidden.1.refs_0_, bf16[64,512]{1,0:T(8,128)(2,1)S(1)} %collective-permute-done.6.refs_1_, bf16[64,512]{1,0:T(8,128)(2,1)S(1)} %collective-permute-done.7.refs_2_, ...), custom_call_target="tpu_custom_call" | custom-call | tf_op jit(solution)/shard_map/down/pallas_call | solution.py:266
  33.5 0.6 %collective-permute-start.9 = (bf16[16,896]{1,0:T(8,128)(2,1)S(1)}, bf16[16,896]{1,0:T(8,128)(2,1)S(1)}, u32[]{:S(2)}, u32[]{:S(2)}) collective-permute-start(bf16[16,896]{1,0:T(8,128)(2,1)S(1)} %get-tuple-element.34), channel_id=1, source_target_pairs={{0,1},{1,0},{2,3},{3,2},{4,5},{5,4},{6,7},{7,6},{8,9},{9,8},{10,11... | collective-permute-start | bytes 86024 | tf_op jit(solution)/shard_map/ppermute | solution.py:187
  34.1 2.3 %collective-permute-start.10 = (bf16[16,896]{1,0:T(8,128)(2,1)S(1)}, bf16[16,896]{1,0:T(8,128)(2,1)S(1)}, u32[]{:S(2)}, u32[]{:S(2)}) collective-permute-start(bf16[16,896]{1,0:T(8,128)(2,1)S(1)} %get-tuple-element.35), channel_id=1, source_target_pairs={{0,2},{1,3},{2,0},{3,1},{4,6},{5,7},{6,4},{7,5},{8,10},{9,11},{10,... | collective-permute-start | bytes 86024 | tf_op jit(solution)/shard_map/ppermute | solution.py:187
  36.4 1.5 %collective-permute-start.11 = (bf16[16,896]{1,0:T(8,128)(2,1)S(1)}, bf16[16,896]{1,0:T(8,128)(2,1)S(1)}, u32[]{:S(2)}, u32[]{:S(2)}) collective-permute-start(bf16[16,896]{1,0:T(8,128)(2,1)S(1)} %get-tuple-element.36), channel_id=1, source_target_pairs={{0,3},{1,2},{2,1},{3,0},{4,7},{5,6},{6,5},{7,4},{8,11},{9,10},{10,... | collective-permute-start | bytes 86024 | tf_op jit(solution)/shard_map/ppermute | solution.py:187
  37.9 0.9 %collective-permute-done.10.refs_2_ = bf16[16,896]{1,0:T(8,128)(2,1)S(1)} collective-permute-done((bf16[16,896]{1,0:T(8,128)(2,1)S(1)}, bf16[16,896]{1,0:T(8,128)(2,1)S(1)}, u32[]{:S(2)}, u32[]{:S(2)}) %collective-permute-start.10) | collective-permute-done | bytes 28704 | tf_op jit(solution)/shard_map/ppermute | solution.py:187
  38.9 3.2 %collective-permute-done.11.refs_3_ = bf16[16,896]{1,0:T(8,128)(2,1)S(1)} collective-permute-done((bf16[16,896]{1,0:T(8,128)(2,1)S(1)}, bf16[16,896]{1,0:T(8,128)(2,1)S(1)}, u32[]{:S(2)}, u32[]{:S(2)}) %collective-permute-start.11) | collective-permute-done | bytes 28704 | tf_op jit(solution)/shard_map/ppermute | solution.py:187
  42.1 0.2 spread.1
  42.3 0.1 collective-permute-start.12
  42.4 1.5 %collective-permute-start.13 = (bf16[4,8,896]{2,1,0:T(8,128)(2,1)S(1)}, bf16[4,8,896]{2,1,0:T(8,128)(2,1)S(1)}, u32[]{:S(2)}, u32[]{:S(2)}) collective-permute-start(bf16[4,8,896]{2,1,0:T(8,128)(2,1)S(1)} %get-tuple-element.39), channel_id=1, source_target_pairs={{0,8},{4,12},{8,0},{12,4},{1,9},{5,13},{9,1},{13,5},{2,10},{6,14},... | collective-permute-start | bytes 172040 | tf_op jit(solution)/shard_map/ppermute | solution.py:187
  43.9 0.3 collective-permute-start.14
  44.2 2.5 %collective-permute-done.13.refs_2_ = bf16[4,8,896]{2,1,0:T(8,128)(2,1)S(1)} collective-permute-done((bf16[4,8,896]{2,1,0:T(8,128)(2,1)S(1)}, bf16[4,8,896]{2,1,0:T(8,128)(2,1)S(1)}, u32[]{:S(2)}, u32[]{:S(2)}) %collective-permute-start.13) | collective-permute-done | bytes 57376 | tf_op jit(solution)/shard_map/ppermute | solution.py:187
  46.7 1.1 %collective-permute-done.14.refs_3_ = bf16[4,8,896]{2,1,0:T(8,128)(2,1)S(1)} collective-permute-done((bf16[4,8,896]{2,1,0:T(8,128)(2,1)S(1)}, bf16[4,8,896]{2,1,0:T(8,128)(2,1)S(1)}, u32[]{:S(2)}, u32[]{:S(2)}) %collective-permute-start.14) | collective-permute-done | bytes 57376 | tf_op jit(solution)/shard_map/ppermute | solution.py:187
  47.8 1.5 %combine.1 = bf16[256,3584]{1,0:T(8,128)(2,1)} custom-call(bf16[256,32]{1,0:T(8,128)(2,1)S(1)} %get-tuple-element.28.mixing_ref, bf16[4,8,896]{2,1,0:T(8,128)(2,1)S(1)} %get-tuple-element.37.refs_0_, bf16[4,8,896]{2,1,0:T(8,128)(2,1)S(1)} %collective-permute-done.12.refs_1_, bf16[4,8,896]{2,1,0:T(8,128)(2,1)S(1)} %collective-permute-done.13.refs_2_, ...), custom_call_target="tpu_custom_call" | custom-call | tf_op jit(solution)/shard_map/combine/pallas_call | solution.py:291
  (5 shorter events, 0.0 us)
Async XLA Ops:
  2.2 3.2 %collective-permute-start = (bf16[8,3712]{1,0:T(8,128)(2,1)S(1)}, bf16[8,3712]{1,0:T(8,128)(2,1)S(1)}, u32[]{:S(2)}, u32[]{:S(2)}) collective-permute-start(bf16[8,3712]{1,0:T(8,128)(2,1)S(1)} %get-tuple-element.24), channel_id=1, source_target_pairs={{0,4},{4,0},{8,12},{12,8},{1,5},{5,1},{9,13},{13,9},{2,6},{6,2},{1... | collective-permute-start | bytes 178184 | tf_op jit(solution)/shard_map/ppermute | solution.py:187
  2.7 5.1 %collective-permute-start.1 = (bf16[8,3712]{1,0:T(8,128)(2,1)S(1)}, bf16[8,3712]{1,0:T(8,128)(2,1)S(1)}, u32[]{:S(2)}, u32[]{:S(2)}) collective-permute-start(bf16[8,3712]{1,0:T(8,128)(2,1)S(1)} %get-tuple-element.25), channel_id=1, source_target_pairs={{0,8},{4,12},{8,0},{12,4},{1,9},{5,13},{9,1},{13,5},{2,10},{6,14},... | collective-permute-start | bytes 178184 | tf_op jit(solution)/shard_map/ppermute | solution.py:187
  5.2 3.9 %collective-permute-start.2 = (bf16[8,3712]{1,0:T(8,128)(2,1)S(1)}, bf16[8,3712]{1,0:T(8,128)(2,1)S(1)}, u32[]{:S(2)}, u32[]{:S(2)}) collective-permute-start(bf16[8,3712]{1,0:T(8,128)(2,1)S(1)} %get-tuple-element.26), channel_id=1, source_target_pairs={{0,12},{4,8},{8,4},{12,0},{1,13},{5,9},{9,5},{13,1},{2,14},{6,10},... | collective-permute-start | bytes 178184 | tf_op jit(solution)/shard_map/ppermute | solution.py:187
  9.5 8.8 %collective-permute-start.5 = (bf16[16,3584]{1,0:T(8,128)(2,1)S(1)}, bf16[16,3584]{1,0:T(8,128)(2,1)S(1)}, u32[]{:S(2)}, u32[]{:S(2)}) collective-permute-start(bf16[16,3584]{1,0:T(8,128)(2,1)S(1)} %get-tuple-element.29.refs_0_), channel_id=1, source_target_pairs={{0,3},{1,2},{2,1},{3,0},{4,7},{5,6},{6,5},{7,4},{8,11},{9,10},{10,... | collective-permute-start | bytes 344072 | tf_op jit(solution)/shard_map/ppermute | solution.py:187
  13.2 10.0 %collective-permute-start.4 = (bf16[16,3584]{1,0:T(8,128)(2,1)S(1)}, bf16[16,3584]{1,0:T(8,128)(2,1)S(1)}, u32[]{:S(2)}, u32[]{:S(2)}) collective-permute-start(bf16[16,3584]{1,0:T(8,128)(2,1)S(1)} %get-tuple-element.29.refs_0_), channel_id=1, source_target_pairs={{0,2},{1,3},{2,0},{3,1},{4,6},{5,7},{6,4},{7,5},{8,10},{9,11},{10,... | collective-permute-start | bytes 344072 | tf_op jit(solution)/shard_map/ppermute | solution.py:187
  13.2 10.0 %collective-permute-start.3 = (bf16[16,3584]{1,0:T(8,128)(2,1)S(1)}, bf16[16,3584]{1,0:T(8,128)(2,1)S(1)}, u32[]{:S(2)}, u32[]{:S(2)}) collective-permute-start(bf16[16,3584]{1,0:T(8,128)(2,1)S(1)} %get-tuple-element.29.refs_0_), channel_id=1, source_target_pairs={{0,1},{1,0},{2,3},{3,2},{4,5},{5,4},{6,7},{7,6},{8,9},{9,8},{10,11... | collective-permute-start | bytes 344072 | tf_op jit(solution)/shard_map/ppermute | solution.py:187
  24.6 6.1 %collective-permute-start.8 = (bf16[64,512]{1,0:T(8,128)(2,1)S(1)}, bf16[64,512]{1,0:T(8,128)(2,1)S(1)}, u32[]{:S(2)}, u32[]{:S(2)}) collective-permute-start(bf16[64,512]{1,0:T(8,128)(2,1)S(1)} %hidden.1.refs_0_), channel_id=1, source_target_pairs={{0,3},{1,2},{2,1},{3,0},{4,7},{5,6},{6,5},{7,4},{8,11},{9,10},{10,... | collective-permute-start | bytes 196616 | tf_op jit(solution)/shard_map/ppermute | solution.py:187
  27.1 5.6 %collective-permute-start.7 = (bf16[64,512]{1,0:T(8,128)(2,1)S(1)}, bf16[64,512]{1,0:T(8,128)(2,1)S(1)}, u32[]{:S(2)}, u32[]{:S(2)}) collective-permute-start(bf16[64,512]{1,0:T(8,128)(2,1)S(1)} %hidden.1.refs_0_), channel_id=1, source_target_pairs={{0,2},{1,3},{2,0},{3,1},{4,6},{5,7},{6,4},{7,5},{8,10},{9,11},{10,... | collective-permute-start | bytes 196616 | tf_op jit(solution)/shard_map/ppermute | solution.py:187
  27.1 5.6 %collective-permute-start.6 = (bf16[64,512]{1,0:T(8,128)(2,1)S(1)}, bf16[64,512]{1,0:T(8,128)(2,1)S(1)}, u32[]{:S(2)}, u32[]{:S(2)}) collective-permute-start(bf16[64,512]{1,0:T(8,128)(2,1)S(1)} %hidden.1.refs_0_), channel_id=1, source_target_pairs={{0,1},{1,0},{2,3},{3,2},{4,5},{5,4},{6,7},{7,6},{8,9},{9,8},{10,11... | collective-permute-start | bytes 196616 | tf_op jit(solution)/shard_map/ppermute | solution.py:187
  33.5 4.5 %collective-permute-start.9 = (bf16[16,896]{1,0:T(8,128)(2,1)S(1)}, bf16[16,896]{1,0:T(8,128)(2,1)S(1)}, u32[]{:S(2)}, u32[]{:S(2)}) collective-permute-start(bf16[16,896]{1,0:T(8,128)(2,1)S(1)} %get-tuple-element.34), channel_id=1, source_target_pairs={{0,1},{1,0},{2,3},{3,2},{4,5},{5,4},{6,7},{7,6},{8,9},{9,8},{10,11... | collective-permute-start | bytes 86024 | tf_op jit(solution)/shard_map/ppermute | solution.py:187
  34.1 4.8 %collective-permute-start.10 = (bf16[16,896]{1,0:T(8,128)(2,1)S(1)}, bf16[16,896]{1,0:T(8,128)(2,1)S(1)}, u32[]{:S(2)}, u32[]{:S(2)}) collective-permute-start(bf16[16,896]{1,0:T(8,128)(2,1)S(1)} %get-tuple-element.35), channel_id=1, source_target_pairs={{0,2},{1,3},{2,0},{3,1},{4,6},{5,7},{6,4},{7,5},{8,10},{9,11},{10,... | collective-permute-start | bytes 86024 | tf_op jit(solution)/shard_map/ppermute | solution.py:187
  36.4 5.7 %collective-permute-start.11 = (bf16[16,896]{1,0:T(8,128)(2,1)S(1)}, bf16[16,896]{1,0:T(8,128)(2,1)S(1)}, u32[]{:S(2)}, u32[]{:S(2)}) collective-permute-start(bf16[16,896]{1,0:T(8,128)(2,1)S(1)} %get-tuple-element.36), channel_id=1, source_target_pairs={{0,3},{1,2},{2,1},{3,0},{4,7},{5,6},{6,5},{7,4},{8,11},{9,10},{10,... | collective-permute-start | bytes 86024 | tf_op jit(solution)/shard_map/ppermute | solution.py:187
  42.3 1.9 %collective-permute-start.12 = (bf16[4,8,896]{2,1,0:T(8,128)(2,1)S(1)}, bf16[4,8,896]{2,1,0:T(8,128)(2,1)S(1)}, u32[]{:S(2)}, u32[]{:S(2)}) collective-permute-start(bf16[4,8,896]{2,1,0:T(8,128)(2,1)S(1)} %get-tuple-element.38), channel_id=1, source_target_pairs={{0,4},{4,0},{8,12},{12,8},{1,5},{5,1},{9,13},{13,9},{2,6},{6,2},{1... | collective-permute-start | bytes 172040 | tf_op jit(solution)/shard_map/ppermute | solution.py:187
  42.4 4.3 %collective-permute-start.13 = (bf16[4,8,896]{2,1,0:T(8,128)(2,1)S(1)}, bf16[4,8,896]{2,1,0:T(8,128)(2,1)S(1)}, u32[]{:S(2)}, u32[]{:S(2)}) collective-permute-start(bf16[4,8,896]{2,1,0:T(8,128)(2,1)S(1)} %get-tuple-element.39), channel_id=1, source_target_pairs={{0,8},{4,12},{8,0},{12,4},{1,9},{5,13},{9,1},{13,5},{2,10},{6,14},... | collective-permute-start | bytes 172040 | tf_op jit(solution)/shard_map/ppermute | solution.py:187
  43.9 3.9 %collective-permute-start.14 = (bf16[4,8,896]{2,1,0:T(8,128)(2,1)S(1)}, bf16[4,8,896]{2,1,0:T(8,128)(2,1)S(1)}, u32[]{:S(2)}, u32[]{:S(2)}) collective-permute-start(bf16[4,8,896]{2,1,0:T(8,128)(2,1)S(1)} %get-tuple-element.40), channel_id=1, source_target_pairs={{0,12},{4,8},{8,4},{12,0},{1,13},{5,9},{9,5},{13,1},{2,14},{6,10},... | collective-permute-start | bytes 172040 | tf_op jit(solution)/shard_map/ppermute | solution.py:187

commit v3 on v2

--- a/solution.py
+++ b/solution.py
@@ -107,7 +107,7 @@
 
 
 def compact_kernel(groups, slots, *refs):
-    arrived, (out_ref, pick_ref) = refs[:groups], refs[groups:]
+    arrived, (out_ref, pick_ref) = refs[:groups][::-1], refs[groups:]
     rows, features = groups * CAP, out_ref.shape[1]
     live = jnp.concatenate([a[:, features:].astype(F32) for a in arrived], axis=0)
     row = lax.broadcasted_iota(jnp.int32, (rows, rows), 0)
@@ -156,7 +156,7 @@
 
 
 def spread_kernel(groups, columns, pick_ref, *refs):
-    blocks, outs = refs[:columns], refs[columns:]
+    blocks, outs = refs[:columns][::-1], refs[columns:]
     for e in range(columns):
         block = blocks[e][...]
         back = jnp.dot(pick_ref[:, : block.shape[0]], block, preferred_element_type=F32)
@@ -165,7 +165,7 @@
 
 
 def combine_kernel(groups, columns, mixing_ref, *refs):
-    backs, (out_ref, held, sems) = refs[:groups], refs[groups:]
+    backs, (out_ref, held, sems) = refs[:groups][::-1], refs[groups:]
     me = lax.axis_index("ing")
     width = backs[0].shape[2]
     copies = []
@@ -188,8 +188,7 @@
 
 
 def swap_all(parts, name):
-    got = {k: swap(parts[k], name, k) for k in reversed(range(len(parts)))}
-    return [got[k] for k in range(len(parts))]
+    return [swap(part, name, k) for k, part in enumerate(parts)][::-1]
 
 
 def local(tokens, router_logits, expert_ids, w_gate, w_up, w_down):
@@ -285,7 +284,7 @@
 
     if share % LANES:
         me = lax.axis_index("ing")
-        rows = jnp.stack(backs)[:, jnp.arange(columns) ^ me]
+        rows = jnp.stack(backs[::-1])[:, jnp.arange(columns) ^ me]
         rows = rows.transpose(0, 2, 1, 3).reshape(groups * CAP, features)
         return jnp.dot(mixing, rows, preferred_element_type=F32).astype(BF16)
     return pl.pallas_call(

time: 49.5 us -> 47 us (0.949)
  waiting for transfers between devices: 20.1 us -> 17.4 us
    ppermute x15, waiting for transfers between devices: 20.1 us -> 17.4 us  [swap(): lax.ppermute(x, name, [(a, a ^ step) for a in range(lax.axis_size(name))])]
where the time goes in v3:
time: 47 us; the launch traced here: 46.8 us
  starting transfers between devices  18.7 us (40%)
  waiting for transfers between devices  17.4 us (37%)
  Pallas kernels  10.6 us (23%)
    ppermute x15, starting transfers between devices, swap(): lax.ppermute(x, name, [(a, a ^ step) for a in range(lax.axis_size(name))])  18.7 us
    ppermute x15, waiting for transfers between devices, swap(): lax.ppermute(x, name, [(a, a ^ step) for a in range(lax.axis_size(name))])  17.4 us
    pallas_call x1, Pallas kernels, local(): pl.pallas_call(functools.partial(prepare_kernel, groups), out_shape=[pltp...  4.33 us
    pallas_call x1, Pallas kernels, local(): pl.pallas_call(functools.partial(dispatch_kernel, groups, 512), out_shape...  2.16 us
    pallas_call x1, Pallas kernels, local(): pl.pallas_call(functools.partial(combine_kernel, groups, columns), out_sh...  1.53 us
    pallas_call x1, Pallas kernels, local(): pl.pallas_call(functools.partial(hidden_kernel, columns), out_shape=jax.S...  1.4 us
  transfers between devices with their start and end apart: 15, of which 9 were waited for; matrix products, arithmetic and copies ran while one was open for 0% of the time, Pallas kernels for 9%

profile of v3, /device:TPU:0, one launch (start us, length us, event | category | flops | bytes accessed | tf_op | source)
XLA Modules:
  0.0 46.8 jit_solution(16760106722147135929)
XLA Ops:
  0.0 2.2 %dispatch.1 = (bf16[8,3712]{1,0:T(8,128)(2,1)S(1)}, bf16[8,3712]{1,0:T(8,128)(2,1)S(1)}, bf16[8,3712]{1,0:T(8,128)(2,1)S(1)}, bf16[8,3712]{1,0:T(8,128)(2,1)S(1)}) custom-call(s32[8,256]{1,0:T(8,128)} %bitcast.9, bf16[256,3584]{1,0:T(8,128)(2,1)} %tokens_ref.1), custom_call_target="tpu_custom_call" | custom-call | tf_op jit(solution)/shard_map/dispatch/pallas_call | solution.py:204
  2.2 2.4 %collective-permute-start = (bf16[8,3712]{1,0:T(8,128)(2,1)S(1)}, bf16[8,3712]{1,0:T(8,128)(2,1)S(1)}, u32[]{:S(2)}, u32[]{:S(2)}) collective-permute-start(bf16[8,3712]{1,0:T(8,128)(2,1)S(1)} %get-tuple-element.23), channel_id=1, source_target_pairs={{0,12},{4,8},{8,4},{12,0},{1,13},{5,9},{9,5},{13,1},{2,14},{6,10},... | collective-permute-start | bytes 178184 | tf_op jit(solution)/shard_map/ppermute | solution.py:187
  4.6 0.6 %collective-permute-start.1 = (bf16[8,3712]{1,0:T(8,128)(2,1)S(1)}, bf16[8,3712]{1,0:T(8,128)(2,1)S(1)}, u32[]{:S(2)}, u32[]{:S(2)}) collective-permute-start(bf16[8,3712]{1,0:T(8,128)(2,1)S(1)} %get-tuple-element.24), channel_id=1, source_target_pairs={{0,8},{4,12},{8,0},{12,4},{1,9},{5,13},{9,1},{13,5},{2,10},{6,14},... | collective-permute-start | bytes 178184 | tf_op jit(solution)/shard_map/ppermute | solution.py:187
  5.2 0.0 collective-permute-start.2
  5.3 1.7 %collective-permute-done.refs_0_ = bf16[8,3712]{1,0:T(8,128)(2,1)S(1)} collective-permute-done((bf16[8,3712]{1,0:T(8,128)(2,1)S(1)}, bf16[8,3712]{1,0:T(8,128)(2,1)S(1)}, u32[]{:S(2)}, u32[]{:S(2)}) %collective-permute-start) | collective-permute-done | bytes 59424 | tf_op jit(solution)/shard_map/ppermute | solution.py:187
  7.0 2.2 %collective-permute-done.1.refs_1_ = bf16[8,3712]{1,0:T(8,128)(2,1)S(1)} collective-permute-done((bf16[8,3712]{1,0:T(8,128)(2,1)S(1)}, bf16[8,3712]{1,0:T(8,128)(2,1)S(1)}, u32[]{:S(2)}, u32[]{:S(2)}) %collective-permute-start.1) | collective-permute-done | bytes 59424 | tf_op jit(solution)/shard_map/ppermute | solution.py:187
  9.2 0.3 compact.1
  9.5 3.7 %collective-permute-start.5 = (bf16[16,3584]{1,0:T(8,128)(2,1)S(1)}, bf16[16,3584]{1,0:T(8,128)(2,1)S(1)}, u32[]{:S(2)}, u32[]{:S(2)}) collective-permute-start(bf16[16,3584]{1,0:T(8,128)(2,1)S(1)} %get-tuple-element.29.refs_0_), channel_id=1, source_target_pairs={{0,3},{1,2},{2,1},{3,0},{4,7},{5,6},{6,5},{7,4},{8,11},{9,10},{10,... | collective-permute-start | bytes 344072 | tf_op jit(solution)/shard_map/ppermute | solution.py:187
  13.2 0.7 %collective-permute-start.3 = (bf16[16,3584]{1,0:T(8,128)(2,1)S(1)}, bf16[16,3584]{1,0:T(8,128)(2,1)S(1)}, u32[]{:S(2)}, u32[]{:S(2)}) collective-permute-start(bf16[16,3584]{1,0:T(8,128)(2,1)S(1)} %get-tuple-element.29.refs_0_), channel_id=1, source_target_pairs={{0,1},{1,0},{2,3},{3,2},{4,5},{5,4},{6,7},{7,6},{8,9},{9,8},{10,11... | collective-permute-start | bytes 344072 | tf_op jit(solution)/shard_map/ppermute | solution.py:187
  13.9 4.3 %prepare.1 = (bf16[3584,512]{1,0:T(8,128)(2,1)S(1)}, bf16[3584,512]{1,0:T(8,128)(2,1)S(1)}, bf16[2048,896]{1,0:T(8,128)(2,1)S(1)}, bf16[256,32]{1,0:T(8,128)(2,1)S(1)}) custom-call(bf16[32,128]{1,0:T(8,128)(2,1)S(1)} %get-tuple-element.27.after_ref.pick_ref, s32[8,256]{1,0:T(8,128)} %bitcast.10, f32[96,256]{1,0:T(8,128)} %bitcast.8, ...), custom_call_target="tpu_custom_call" | custom-call | tf_op jit(solution)/shard_map/prepare/pallas_call | solution.py:234
  18.3 0.0 collective-permute-done.5.refs_3_
  18.3 4.6 %collective-permute-done.4.refs_2_ = bf16[16,3584]{1,0:T(8,128)(2,1)S(1)} collective-permute-done((bf16[16,3584]{1,0:T(8,128)(2,1)S(1)}, bf16[16,3584]{1,0:T(8,128)(2,1)S(1)}, u32[]{:S(2)}, u32[]{:S(2)}) %collective-permute-start.4) | collective-permute-done | bytes 114720 | tf_op jit(solution)/shard_map/ppermute | solution.py:187
  22.9 0.0 collective-permute-done.3.refs_1_
  22.9 1.4 %hidden.1.refs_0_ = bf16[64,512]{1,0:T(8,128)(2,1)S(1)} custom-call(bf16[16,3584]{1,0:T(8,128)(2,1)S(1)} %get-tuple-element.29.refs_0_, bf16[16,3584]{1,0:T(8,128)(2,1)S(1)} %collective-permute-done.3.refs_1_, bf16[16,3584]{1,0:T(8,128)(2,1)S(1)} %collective-permute-done.4.refs_2_, bf16[16,3584]{1,0:T(8,128)(2,1)S(1)} %collective-permute-done.5.refs_3_, ...), custom_call_target="tpu_custom_call" | custom-call | tf_op jit(solution)/shard_map/hidden/pallas_call | solution.py:254
  24.3 2.5 %collective-permute-start.8 = (bf16[64,512]{1,0:T(8,128)(2,1)S(1)}, bf16[64,512]{1,0:T(8,128)(2,1)S(1)}, u32[]{:S(2)}, u32[]{:S(2)}) collective-permute-start(bf16[64,512]{1,0:T(8,128)(2,1)S(1)} %hidden.1.refs_0_), channel_id=1, source_target_pairs={{0,3},{1,2},{2,1},{3,0},{4,7},{5,6},{6,5},{7,4},{8,11},{9,10},{10,... | collective-permute-start | bytes 196616 | tf_op jit(solution)/shard_map/ppermute | solution.py:187
  26.8 0.0 collective-permute-start.7
  26.8 1.9 %collective-permute-start.6 = (bf16[64,512]{1,0:T(8,128)(2,1)S(1)}, bf16[64,512]{1,0:T(8,128)(2,1)S(1)}, u32[]{:S(2)}, u32[]{:S(2)}) collective-permute-start(bf16[64,512]{1,0:T(8,128)(2,1)S(1)} %hidden.1.refs_0_), channel_id=1, source_target_pairs={{0,1},{1,0},{2,3},{3,2},{4,5},{5,4},{6,7},{7,6},{8,9},{9,8},{10,11... | collective-permute-start | bytes 196616 | tf_op jit(solution)/shard_map/ppermute | solution.py:187
  28.7 2.0 %collective-permute-done.8.refs_3_ = bf16[64,512]{1,0:T(8,128)(2,1)S(1)} collective-permute-done((bf16[64,512]{1,0:T(8,128)(2,1)S(1)}, bf16[64,512]{1,0:T(8,128)(2,1)S(1)}, u32[]{:S(2)}, u32[]{:S(2)}) %collective-permute-start.8) | collective-permute-done | bytes 65568 | tf_op jit(solution)/shard_map/ppermute | solution.py:187
  30.8 1.7 %collective-permute-done.7.refs_2_ = bf16[64,512]{1,0:T(8,128)(2,1)S(1)} collective-permute-done((bf16[64,512]{1,0:T(8,128)(2,1)S(1)}, bf16[64,512]{1,0:T(8,128)(2,1)S(1)}, u32[]{:S(2)}, u32[]{:S(2)}) %collective-permute-start.7) | collective-permute-done | bytes 65568 | tf_op jit(solution)/shard_map/ppermute | solution.py:187
  32.4 0.0 collective-permute-done.6.refs_1_
  32.4 0.7 %down.1 = (bf16[16,896]{1,0:T(8,128)(2,1)S(1)}, bf16[16,896]{1,0:T(8,128)(2,1)S(1)}, bf16[16,896]{1,0:T(8,128)(2,1)S(1)}, bf16[16,896]{1,0:T(8,128)(2,1)S(1)}) custom-call(bf16[64,512]{1,0:T(8,128)(2,1)S(1)} %hidden.1.refs_0_, bf16[64,512]{1,0:T(8,128)(2,1)S(1)} %collective-permute-done.6.refs_1_, bf16[64,512]{1,0:T(8,128)(2,1)S(1)} %collective-permute-done.7.refs_2_, ...), custom_call_target="tpu_custom_call" | custom-call | tf_op jit(solution)/shard_map/down/pallas_call | solution.py:265
  33.2 2.1 %collective-permute-start.9 = (bf16[16,896]{1,0:T(8,128)(2,1)S(1)}, bf16[16,896]{1,0:T(8,128)(2,1)S(1)}, u32[]{:S(2)}, u32[]{:S(2)}) collective-permute-start(bf16[16,896]{1,0:T(8,128)(2,1)S(1)} %get-tuple-element.33), channel_id=1, source_target_pairs={{0,3},{1,2},{2,1},{3,0},{4,7},{5,6},{6,5},{7,4},{8,11},{9,10},{10,... | collective-permute-start | bytes 86024 | tf_op jit(solution)/shard_map/ppermute | solution.py:187
  35.3 2.3 %collective-permute-start.11 = (bf16[16,896]{1,0:T(8,128)(2,1)S(1)}, bf16[16,896]{1,0:T(8,128)(2,1)S(1)}, u32[]{:S(2)}, u32[]{:S(2)}) collective-permute-start(bf16[16,896]{1,0:T(8,128)(2,1)S(1)} %get-tuple-element.35), channel_id=1, source_target_pairs={{0,1},{1,0},{2,3},{3,2},{4,5},{5,4},{6,7},{7,6},{8,9},{9,8},{10,11... | collective-permute-start | bytes 86024 | tf_op jit(solution)/shard_map/ppermute | solution.py:187
  37.6 1.3 %collective-permute-done.9.refs_0_ = bf16[16,896]{1,0:T(8,128)(2,1)S(1)} collective-permute-done((bf16[16,896]{1,0:T(8,128)(2,1)S(1)}, bf16[16,896]{1,0:T(8,128)(2,1)S(1)}, u32[]{:S(2)}, u32[]{:S(2)}) %collective-permute-start.9) | collective-permute-done | bytes 28704 | tf_op jit(solution)/shard_map/ppermute | solution.py:187
  38.9 1.1 %collective-permute-done.10.refs_1_ = bf16[16,896]{1,0:T(8,128)(2,1)S(1)} collective-permute-done((bf16[16,896]{1,0:T(8,128)(2,1)S(1)}, bf16[16,896]{1,0:T(8,128)(2,1)S(1)}, u32[]{:S(2)}, u32[]{:S(2)}) %collective-permute-start.10) | collective-permute-done | bytes 28704 | tf_op jit(solution)/shard_map/ppermute | solution.py:187
  40.0 0.2 spread.1
  40.2 0.1 collective-permute-start.12
  40.3 2.1 %collective-permute-start.13 = (bf16[4,8,896]{2,1,0:T(8,128)(2,1)S(1)}, bf16[4,8,896]{2,1,0:T(8,128)(2,1)S(1)}, u32[]{:S(2)}, u32[]{:S(2)}) collective-permute-start(bf16[4,8,896]{2,1,0:T(8,128)(2,1)S(1)} %get-tuple-element.38), channel_id=1, source_target_pairs={{0,8},{4,12},{8,0},{12,4},{1,9},{5,13},{9,1},{13,5},{2,10},{6,14},... | collective-permute-start | bytes 172040 | tf_op jit(solution)/shard_map/ppermute | solution.py:187
  42.4 0.0 collective-permute-start.14
  42.4 1.6 %collective-permute-done.12.refs_0_ = bf16[4,8,896]{2,1,0:T(8,128)(2,1)S(1)} collective-permute-done((bf16[4,8,896]{2,1,0:T(8,128)(2,1)S(1)}, bf16[4,8,896]{2,1,0:T(8,128)(2,1)S(1)}, u32[]{:S(2)}, u32[]{:S(2)}) %collective-permute-start.12) | collective-permute-done | bytes 57376 | tf_op jit(solution)/shard_map/ppermute | solution.py:187
  44.0 1.2 %collective-permute-done.13.refs_1_ = bf16[4,8,896]{2,1,0:T(8,128)(2,1)S(1)} collective-permute-done((bf16[4,8,896]{2,1,0:T(8,128)(2,1)S(1)}, bf16[4,8,896]{2,1,0:T(8,128)(2,1)S(1)}, u32[]{:S(2)}, u32[]{:S(2)}) %collective-permute-start.13) | collective-permute-done | bytes 57376 | tf_op jit(solution)/shard_map/ppermute | solution.py:187
  45.2 1.5 %combine.1 = bf16[256,3584]{1,0:T(8,128)(2,1)} custom-call(bf16[256,32]{1,0:T(8,128)(2,1)S(1)} %get-tuple-element.28.mixing_ref, bf16[4,8,896]{2,1,0:T(8,128)(2,1)S(1)} %collective-permute-done.12.refs_0_, bf16[4,8,896]{2,1,0:T(8,128)(2,1)S(1)} %collective-permute-done.13.refs_1_, bf16[4,8,896]{2,1,0:T(8,128)(2,1)S(1)} %collective-permute-done.14.refs_2_, ...), custom_call_target="tpu_custom_call" | custom-call | tf_op jit(solution)/shard_map/combine/pallas_call | solution.py:290
  (5 shorter events, 0.0 us)
Async XLA Ops:
  2.2 4.8 %collective-permute-start = (bf16[8,3712]{1,0:T(8,128)(2,1)S(1)}, bf16[8,3712]{1,0:T(8,128)(2,1)S(1)}, u32[]{:S(2)}, u32[]{:S(2)}) collective-permute-start(bf16[8,3712]{1,0:T(8,128)(2,1)S(1)} %get-tuple-element.23), channel_id=1, source_target_pairs={{0,12},{4,8},{8,4},{12,0},{1,13},{5,9},{9,5},{13,1},{2,14},{6,10},... | collective-permute-start | bytes 178184 | tf_op jit(solution)/shard_map/ppermute | solution.py:187
  4.6 4.5 %collective-permute-start.1 = (bf16[8,3712]{1,0:T(8,128)(2,1)S(1)}, bf16[8,3712]{1,0:T(8,128)(2,1)S(1)}, u32[]{:S(2)}, u32[]{:S(2)}) collective-permute-start(bf16[8,3712]{1,0:T(8,128)(2,1)S(1)} %get-tuple-element.24), channel_id=1, source_target_pairs={{0,8},{4,12},{8,0},{12,4},{1,9},{5,13},{9,1},{13,5},{2,10},{6,14},... | collective-permute-start | bytes 178184 | tf_op jit(solution)/shard_map/ppermute | solution.py:187
  5.2 3.9 %collective-permute-start.2 = (bf16[8,3712]{1,0:T(8,128)(2,1)S(1)}, bf16[8,3712]{1,0:T(8,128)(2,1)S(1)}, u32[]{:S(2)}, u32[]{:S(2)}) collective-permute-start(bf16[8,3712]{1,0:T(8,128)(2,1)S(1)} %get-tuple-element.25), channel_id=1, source_target_pairs={{0,4},{4,0},{8,12},{12,8},{1,5},{5,1},{9,13},{13,9},{2,6},{6,2},{1... | collective-permute-start | bytes 178184 | tf_op jit(solution)/shard_map/ppermute | solution.py:187
  9.5 8.8 %collective-permute-start.5 = (bf16[16,3584]{1,0:T(8,128)(2,1)S(1)}, bf16[16,3584]{1,0:T(8,128)(2,1)S(1)}, u32[]{:S(2)}, u32[]{:S(2)}) collective-permute-start(bf16[16,3584]{1,0:T(8,128)(2,1)S(1)} %get-tuple-element.29.refs_0_), channel_id=1, source_target_pairs={{0,3},{1,2},{2,1},{3,0},{4,7},{5,6},{6,5},{7,4},{8,11},{9,10},{10,... | collective-permute-start | bytes 344072 | tf_op jit(solution)/shard_map/ppermute | solution.py:187
  13.2 9.6 %collective-permute-start.4 = (bf16[16,3584]{1,0:T(8,128)(2,1)S(1)}, bf16[16,3584]{1,0:T(8,128)(2,1)S(1)}, u32[]{:S(2)}, u32[]{:S(2)}) collective-permute-start(bf16[16,3584]{1,0:T(8,128)(2,1)S(1)} %get-tuple-element.29.refs_0_), channel_id=1, source_target_pairs={{0,2},{1,3},{2,0},{3,1},{4,6},{5,7},{6,4},{7,5},{8,10},{9,11},{10,... | collective-permute-start | bytes 344072 | tf_op jit(solution)/shard_map/ppermute | solution.py:187
  13.2 9.6 %collective-permute-start.3 = (bf16[16,3584]{1,0:T(8,128)(2,1)S(1)}, bf16[16,3584]{1,0:T(8,128)(2,1)S(1)}, u32[]{:S(2)}, u32[]{:S(2)}) collective-permute-start(bf16[16,3584]{1,0:T(8,128)(2,1)S(1)} %get-tuple-element.29.refs_0_), channel_id=1, source_target_pairs={{0,1},{1,0},{2,3},{3,2},{4,5},{5,4},{6,7},{7,6},{8,9},{9,8},{10,11... | collective-permute-start | bytes 344072 | tf_op jit(solution)/shard_map/ppermute | solution.py:187
  24.3 6.5 %collective-permute-start.8 = (bf16[64,512]{1,0:T(8,128)(2,1)S(1)}, bf16[64,512]{1,0:T(8,128)(2,1)S(1)}, u32[]{:S(2)}, u32[]{:S(2)}) collective-permute-start(bf16[64,512]{1,0:T(8,128)(2,1)S(1)} %hidden.1.refs_0_), channel_id=1, source_target_pairs={{0,3},{1,2},{2,1},{3,0},{4,7},{5,6},{6,5},{7,4},{8,11},{9,10},{10,... | collective-permute-start | bytes 196616 | tf_op jit(solution)/shard_map/ppermute | solution.py:187
  26.8 5.6 %collective-permute-start.7 = (bf16[64,512]{1,0:T(8,128)(2,1)S(1)}, bf16[64,512]{1,0:T(8,128)(2,1)S(1)}, u32[]{:S(2)}, u32[]{:S(2)}) collective-permute-start(bf16[64,512]{1,0:T(8,128)(2,1)S(1)} %hidden.1.refs_0_), channel_id=1, source_target_pairs={{0,2},{1,3},{2,0},{3,1},{4,6},{5,7},{6,4},{7,5},{8,10},{9,11},{10,... | collective-permute-start | bytes 196616 | tf_op jit(solution)/shard_map/ppermute | solution.py:187
  26.8 5.6 %collective-permute-start.6 = (bf16[64,512]{1,0:T(8,128)(2,1)S(1)}, bf16[64,512]{1,0:T(8,128)(2,1)S(1)}, u32[]{:S(2)}, u32[]{:S(2)}) collective-permute-start(bf16[64,512]{1,0:T(8,128)(2,1)S(1)} %hidden.1.refs_0_), channel_id=1, source_target_pairs={{0,1},{1,0},{2,3},{3,2},{4,5},{5,4},{6,7},{7,6},{8,9},{9,8},{10,11... | collective-permute-start | bytes 196616 | tf_op jit(solution)/shard_map/ppermute | solution.py:187
  33.2 5.7 %collective-permute-start.9 = (bf16[16,896]{1,0:T(8,128)(2,1)S(1)}, bf16[16,896]{1,0:T(8,128)(2,1)S(1)}, u32[]{:S(2)}, u32[]{:S(2)}) collective-permute-start(bf16[16,896]{1,0:T(8,128)(2,1)S(1)} %get-tuple-element.33), channel_id=1, source_target_pairs={{0,3},{1,2},{2,1},{3,0},{4,7},{5,6},{6,5},{7,4},{8,11},{9,10},{10,... | collective-permute-start | bytes 86024 | tf_op jit(solution)/shard_map/ppermute | solution.py:187
  35.3 4.8 %collective-permute-start.10 = (bf16[16,896]{1,0:T(8,128)(2,1)S(1)}, bf16[16,896]{1,0:T(8,128)(2,1)S(1)}, u32[]{:S(2)}, u32[]{:S(2)}) collective-permute-start(bf16[16,896]{1,0:T(8,128)(2,1)S(1)} %get-tuple-element.34), channel_id=1, source_target_pairs={{0,2},{1,3},{2,0},{3,1},{4,6},{5,7},{6,4},{7,5},{8,10},{9,11},{10,... | collective-permute-start | bytes 86024 | tf_op jit(solution)/shard_map/ppermute | solution.py:187
  35.3 4.8 %collective-permute-start.11 = (bf16[16,896]{1,0:T(8,128)(2,1)S(1)}, bf16[16,896]{1,0:T(8,128)(2,1)S(1)}, u32[]{:S(2)}, u32[]{:S(2)}) collective-permute-start(bf16[16,896]{1,0:T(8,128)(2,1)S(1)} %get-tuple-element.35), channel_id=1, source_target_pairs={{0,1},{1,0},{2,3},{3,2},{4,5},{5,4},{6,7},{7,6},{8,9},{9,8},{10,11... | collective-permute-start | bytes 86024 | tf_op jit(solution)/shard_map/ppermute | solution.py:187
  40.2 3.8 %collective-permute-start.12 = (bf16[4,8,896]{2,1,0:T(8,128)(2,1)S(1)}, bf16[4,8,896]{2,1,0:T(8,128)(2,1)S(1)}, u32[]{:S(2)}, u32[]{:S(2)}) collective-permute-start(bf16[4,8,896]{2,1,0:T(8,128)(2,1)S(1)} %get-tuple-element.37), channel_id=1, source_target_pairs={{0,12},{4,8},{8,4},{12,0},{1,13},{5,9},{9,5},{13,1},{2,14},{6,10},... | collective-permute-start | bytes 172040 | tf_op jit(solution)/shard_map/ppermute | solution.py:187
  40.3 4.9 %collective-permute-start.13 = (bf16[4,8,896]{2,1,0:T(8,128)(2,1)S(1)}, bf16[4,8,896]{2,1,0:T(8,128)(2,1)S(1)}, u32[]{:S(2)}, u32[]{:S(2)}) collective-permute-start(bf16[4,8,896]{2,1,0:T(8,128)(2,1)S(1)} %get-tuple-element.38), channel_id=1, source_target_pairs={{0,8},{4,12},{8,0},{12,4},{1,9},{5,13},{9,1},{13,5},{2,10},{6,14},... | collective-permute-start | bytes 172040 | tf_op jit(solution)/shard_map/ppermute | solution.py:187
  42.4 2.8 %collective-permute-start.14 = (bf16[4,8,896]{2,1,0:T(8,128)(2,1)S(1)}, bf16[4,8,896]{2,1,0:T(8,128)(2,1)S(1)}, u32[]{:S(2)}, u32[]{:S(2)}) collective-permute-start(bf16[4,8,896]{2,1,0:T(8,128)(2,1)S(1)} %get-tuple-element.39), channel_id=1, source_target_pairs={{0,4},{4,0},{8,12},{12,8},{1,5},{5,1},{9,13},{13,9},{2,6},{6,2},{1... | collective-permute-start | bytes 172040 | tf_op jit(solution)/shard_map/ppermute | solution.py:187

commit v4 on v3

--- a/solution.py
+++ b/solution.py
@@ -73,22 +73,32 @@
             outs[d][:, part] = rows[d * CAP : (d + 1) * CAP].astype(BF16)
 
 
-def prepare_kernel(groups, after_ref, ids_ref, logits_ref, *refs):
-    del after_ref
-    weights, loaded, (out_ref, ids_held, logits_held, sems) = refs[:3], refs[3:6], refs[6:]
-    small = [
-        pltpu.make_async_copy(ids_ref, ids_held, sems.at[12]),
-        pltpu.make_async_copy(logits_ref, logits_held, sems.at[13]),
-    ]
-    for copy in small:
-        copy.start()
+def start_loads(weights, loaded, sems):
     copies = []
-    for k in range(3):
+    for k in range(len(weights)):
         depth = weights[k].shape[0]
         for c in range(4):
             part = pl.ds(c * (depth // 4), depth // 4)
             copies.append(pltpu.make_async_copy(weights[k].at[part], loaded[k].at[part], sems.at[4 * k + c]))
             copies[-1].start()
+    return copies
+
+
+def load_kernel(after_ref, gate_ref, up_ref, gate_out, up_out, sems):
+    del after_ref
+    for copy in start_loads([gate_ref, up_ref], [gate_out, up_out], sems):
+        copy.wait()
+
+
+def prepare_kernel(groups, after_ref, ids_ref, logits_ref, down_ref, down_out, out_ref, ids_held, logits_held, sems):
+    del after_ref
+    small = [
+        pltpu.make_async_copy(ids_ref, ids_held, sems.at[4]),
+        pltpu.make_async_copy(logits_ref, logits_held, sems.at[5]),
+    ]
+    for copy in small:
+        copy.start()
+    copies = start_loads([down_ref], [down_out], sems)
     for copy in small:
         copy.wait()
     me = lax.axis_index("grp")
@@ -106,8 +116,9 @@
         copy.wait()
 
 
-def compact_kernel(groups, slots, *refs):
-    arrived, (out_ref, pick_ref) = refs[:groups][::-1], refs[groups:]
+def compact_kernel(groups, slots, after_ref, *refs):
+    del after_ref
+    arrived, (out_ref, low_ref, high_ref, pick_ref) = refs[:groups][::-1], refs[groups:]
     rows, features = groups * CAP, out_ref.shape[1]
     live = jnp.concatenate([a[:, features:].astype(F32) for a in arrived], axis=0)
     row = lax.broadcasted_iota(jnp.int32, (rows, rows), 0)
@@ -116,21 +127,47 @@
     lane = lax.broadcasted_iota(jnp.int32, (rows, LANES), 1).astype(F32)
     pick = jnp.where((live > 0.5) & (rank == lane + 1.0), 1.0, 0.0).astype(BF16)
     pick_ref[...] = pick
-    step = 512
+    half = features // 2
+    step = 256
     for c in range(features // step):
         part = slice(c * step, (c + 1) * step)
         whole = jnp.concatenate([a[:, part].astype(F32) for a in arrived], axis=0).astype(BF16)
-        out_ref[:, part] = lax.dot_general(
+        moved = lax.dot_general(
             pick[:, :slots], whole, (((0,), (0,)), ((), ())), preferred_element_type=F32
         ).astype(BF16)
-
-
-def hidden_kernel(columns, *refs):
-    blocks, (gate_ref, up_ref, hidden_ref, held) = refs[:columns], refs[columns:]
-    slots = blocks[0].shape[0]
-    units = gate_ref.shape[1]
-    for e in range(columns):
-        held[e * slots : (e + 1) * slots, :] = blocks[e][...]
+        out_ref[:, part] = moved
+        if (c + 1) * step <= half:
+            low_ref[:, part] = moved
+        else:
+            high_ref[:, c * step - half : (c + 1) * step - half] = moved
+
+
+def hidden_kernel(columns, forwarded, *refs):
+    if forwarded:
+        low, high, near, own, middle, far_low, far_high = refs[:7]
+    blocks, (gate_ref, up_ref, hidden_ref, held) = refs[:-4], refs[-4:]
+    slots = held.shape[0] // columns
+    features, units = gate_ref.shape
+    if forwarded:
+        half = features // 2
+        me = lax.axis_index("ing")
+        held[:slots, :] = own[...]
+        held[slots : 2 * slots, :] = near[...]
+        held[2 * slots : 3 * slots, :half] = low[...]
+        held[2 * slots : 3 * slots, half:] = high[...]
+        inner = (me == 1) | (me == 2)
+
+        @pl.when(inner)
+        def _():
+            held[3 * slots :, :] = middle[...]
+
+        @pl.when(jnp.logical_not(inner))
+        def _():
+            held[3 * slots :, :half] = far_low[...]
+            held[3 * slots :, half:] = far_high[...]
+    else:
+        for e in range(columns):
+            held[e * slots : (e + 1) * slots, :] = blocks[e][...]
     step = min(256, units)
     for c in range(units // step):
         part = slice(c * step, (c + 1) * step)
@@ -217,49 +254,67 @@
     )(ids, pltpu.with_memory_space_constraint(tokens, pltpu.HBM))
     arrived = swap_all(outbound, "grp")
 
-    compacted, pick = pl.pallas_call(
+    weights = [w_gate[0], w_up[0], w_down[0]]
+    weights = [pltpu.with_memory_space_constraint(w, pltpu.HBM) for w in weights]
+    gate, up = pl.pallas_call(
+        load_kernel,
+        out_shape=[pltpu.VMEM(w.shape, BF16) for w in weights[:2]],
+        in_specs=[ANY] * 3,
+        out_specs=[VMEM] * 2,
+        scratch_shapes=[pltpu.SemaphoreType.DMA((8,))],
+        compiler_params=params(0),
+        name="load",
+    )(outbound[0], *weights[:2])
+
+    compacted, low, high, pick = pl.pallas_call(
         functools.partial(compact_kernel, groups, slots),
         out_shape=[
             jax.ShapeDtypeStruct((slots, features), BF16),
+            jax.ShapeDtypeStruct((slots, features // 2), BF16),
+            jax.ShapeDtypeStruct((slots, features // 2), BF16),
             jax.ShapeDtypeStruct((groups * CAP, LANES), BF16),
         ],
-        in_specs=[VMEM] * groups,
-        out_specs=[VMEM, VMEM],
-        compiler_params=params(2 * (groups * CAP + slots) * wide),
+        in_specs=[ANY] + [VMEM] * groups,
+        out_specs=[VMEM] * 4,
+        compiler_params=params(2 * (groups * CAP + 2 * slots) * wide),
         name="compact",
-    )(*arrived)
-    blocks = [swap(compacted, "ing", e) for e in range(columns)]
-
-    weights = [w_gate[0], w_up[0], w_down[0]]
-    gate, up, down, mixing = pl.pallas_call(
-        functools.partial(prepare_kernel, groups),
-        out_shape=[pltpu.VMEM(w.shape, BF16) for w in weights]
-        + [jax.ShapeDtypeStruct((count, groups * CAP), BF16)],
-        in_specs=[ANY] * 6,
-        out_specs=[VMEM] * 4,
-        scratch_shapes=[
-            pltpu.VMEM(ids.shape, jnp.int32),
-            pltpu.VMEM(logits.shape, F32),
-            pltpu.SemaphoreType.DMA((14,)),
-        ],
-        compiler_params=params(0),
-        name="prepare",
-    )(
-        pick,
-        ids,
-        logits,
-        *[pltpu.with_memory_space_constraint(w, pltpu.HBM) for w in weights],
-    )
+    )(gate, *arrived)
+    if columns == 4:
+        low, high = swap(low, "ing", 2), swap(high, "ing", 2)
+        near = swap(compacted, "ing", 1)
+        outward = [(1, 0), (2, 3)]
+        far_low = lax.ppermute(low, "ing", outward)
+        middle = lax.ppermute(compacted, "ing", [(1, 2), (2, 1)])
+        far_high = lax.ppermute(high, "ing", outward)
+        blocks = [low, high, near, compacted, middle, far_low, far_high]
+    else:
+        blocks = [swap(compacted, "ing", e) for e in range(columns)]
 
     hidden = pl.pallas_call(
-        functools.partial(hidden_kernel, columns),
+        functools.partial(hidden_kernel, columns, columns == 4),
         out_shape=jax.ShapeDtypeStruct((columns * slots, units), BF16),
-        in_specs=[VMEM] * (columns + 2),
+        in_specs=[VMEM] * (len(blocks) + 2),
         out_specs=VMEM,
         scratch_shapes=[pltpu.VMEM((columns * slots, features), BF16)],
         compiler_params=params(2 * columns * slots * (2 * features + units)),
         name="hidden",
     )(*blocks, gate, up)
+    down, mixing = pl.pallas_call(
+        functools.partial(prepare_kernel, groups),
+        out_shape=[
+            pltpu.VMEM(w_down.shape[1:], BF16),
+            jax.ShapeDtypeStruct((count, groups * CAP), BF16),
+        ],
+        in_specs=[ANY] * 4,
+        out_specs=[VMEM] * 2,
+        scratch_shapes=[
+            pltpu.VMEM(ids.shape, jnp.int32),
+            pltpu.VMEM(logits.shape, F32),
+            pltpu.SemaphoreType.DMA((6,)),
+        ],
+        compiler_params=params(0),
+        name="prepare",
+    )(hidden, ids, logits, weights[2])
     hiddens = [swap(hidden, "ing", f) for f in range(columns)]
 
     results = pl.pallas_call(

time: 47 us -> 49.7 us (1.057)
  starting transfers between devices: 18.7 us -> 24.7 us
  waiting for transfers between devices: 17.4 us -> 13 us
  Pallas kernels: 10.6 us -> 11.6 us
    ppermute x15, waiting for transfers between devices: 17.4 us -> 8.19 us  [swap(): lax.ppermute(x, name, [(a, a ^ step) for a in range(lax.axis_size(name))])]
    ppermute x0 -> x3, waiting for transfers between devices: none -> 4.77 us  [the longest x1 3.46 us: local(): far_low = lax.ppermute(low, 'ing', outward)]
    ppermute x0 -> x3, starting transfers between devices: none -> 3.23 us  [the longest x1 1.29 us: local(): far_high = lax.ppermute(high, 'ing', outward)]
    pallas_call x1 -> x2, Pallas kernels: 1.4 us -> 4.59 us  [the longest x1 3.17 us: local(): pl.pallas_call(load_kernel, out_shape=[pltpu.VMEM(w.shape, BF16) for w in...]
    ppermute x15, starting transfers between devices: 18.7 us -> 21.5 us  [swap(): lax.ppermute(x, name, [(a, a ^ step) for a in range(lax.axis_size(name))])]
    pallas_call x1, Pallas kernels: 4.33 us -> 2.13 us  [local(): pl.pallas_call(functools.partial(prepare_kernel, groups), out_shape=[pltp...]
  transfers between devices with their start and end apart: 15 -> 18, of which waited for: 9 -> 8; matrix products, arithmetic and copies ran while one was open for 0% -> 0% of each run, Pallas kernels for 9% -> 11%
where the time goes in v4:
time: 49.7 us; the launch traced here: 49.4 us
  starting transfers between devices  24.7 us (50%)
  waiting for transfers between devices  13 us (26%)
  Pallas kernels  11.6 us (23%)
    ppermute x15, starting transfers between devices, swap(): lax.ppermute(x, name, [(a, a ^ step) for a in range(lax.axis_size(name))])  21.5 us
    ppermute x15, waiting for transfers between devices, swap(): lax.ppermute(x, name, [(a, a ^ step) for a in range(lax.axis_size(name))])  8.19 us
    ppermute x1, waiting for transfers between devices, local(): far_low = lax.ppermute(low, 'ing', outward)  3.46 us
    pallas_call x1, Pallas kernels, local(): pl.pallas_call(load_kernel, out_shape=[pltpu.VMEM(w.shape, BF16) for w in...  3.17 us
    pallas_call x1, Pallas kernels, local(): pl.pallas_call(functools.partial(dispatch_kernel, groups, 512), out_shape...  2.16 us
    pallas_call x1, Pallas kernels, local(): pl.pallas_call(functools.partial(prepare_kernel, groups), out_shape=[pltp...  2.13 us
    pallas_call x1, Pallas kernels, local(): pl.pallas_call(functools.partial(combine_kernel, groups, columns), out_sh...  1.52 us
    pallas_call x1, Pallas kernels, local(): pl.pallas_call(functools.partial(hidden_kernel, columns, columns == 4), o...  1.43 us
  transfers between devices with their start and end apart: 18, of which 8 were waited for; matrix products, arithmetic and copies ran while one was open for 0% of the time, Pallas kernels for 11%

profile of v4, /device:TPU:0, one launch (start us, length us, event | category | flops | bytes accessed | tf_op | source)
XLA Modules:
  0.0 49.4 jit_solution(772457524999241389)
XLA Ops:
  0.0 2.2 %dispatch.1 = (bf16[8,3712]{1,0:T(8,128)(2,1)S(1)}, bf16[8,3712]{1,0:T(8,128)(2,1)S(1)}, bf16[8,3712]{1,0:T(8,128)(2,1)S(1)}, bf16[8,3712]{1,0:T(8,128)(2,1)S(1)}) custom-call(s32[8,256]{1,0:T(8,128)} %bitcast.9, bf16[256,3584]{1,0:T(8,128)(2,1)} %tokens_ref.1), custom_call_target="tpu_custom_call" | custom-call | tf_op jit(solution)/shard_map/dispatch/pallas_call | solution.py:241
  2.2 2.4 %collective-permute-start = (bf16[8,3712]{1,0:T(8,128)(2,1)S(1)}, bf16[8,3712]{1,0:T(8,128)(2,1)S(1)}, u32[]{:S(2)}, u32[]{:S(2)}) collective-permute-start(bf16[8,3712]{1,0:T(8,128)(2,1)S(1)} %get-tuple-element.27), channel_id=1, source_target_pairs={{0,12},{4,8},{8,4},{12,0},{1,13},{5,9},{9,5},{13,1},{2,14},{6,10},... | collective-permute-start | bytes 178184 | tf_op jit(solution)/shard_map/ppermute | solution.py:224
  4.6 0.6 %collective-permute-start.1 = (bf16[8,3712]{1,0:T(8,128)(2,1)S(1)}, bf16[8,3712]{1,0:T(8,128)(2,1)S(1)}, u32[]{:S(2)}, u32[]{:S(2)}) collective-permute-start(bf16[8,3712]{1,0:T(8,128)(2,1)S(1)} %get-tuple-element.28), channel_id=1, source_target_pairs={{0,8},{4,12},{8,0},{12,4},{1,9},{5,13},{9,1},{13,5},{2,10},{6,14},... | collective-permute-start | bytes 178184 | tf_op jit(solution)/shard_map/ppermute | solution.py:224
  5.2 0.0 collective-permute-start.2
  5.3 3.2 %load.1 = (bf16[3584,512]{1,0:T(8,128)(2,1)S(1)}, bf16[3584,512]{1,0:T(8,128)(2,1)S(1)}) custom-call(bf16[8,3712]{1,0:T(8,128)(2,1)S(1)} %get-tuple-element.25.after_ref.refs_3_, bf16[3584,512]{1,0:T(8,128)(2,1)} %bitcast.5, bf16[3584,512]{1,0:T(8,128)(2,1)} %bitcast.6), custom_call_target="tpu_custom_call" | custom-call | tf_op jit(solution)/shard_map/load/pallas_call | solution.py:259
  8.5 0.7 %collective-permute-done.1.refs_1_ = bf16[8,3712]{1,0:T(8,128)(2,1)S(1)} collective-permute-done((bf16[8,3712]{1,0:T(8,128)(2,1)S(1)}, bf16[8,3712]{1,0:T(8,128)(2,1)S(1)}, u32[]{:S(2)}, u32[]{:S(2)}) %collective-permute-start.1) | collective-permute-done | bytes 59424 | tf_op jit(solution)/shard_map/ppermute | solution.py:224
  9.2 0.3 compact.1
  9.5 2.7 %collective-permute-start.3 = (bf16[16,1792]{1,0:T(8,128)(2,1)S(1)}, bf16[16,1792]{1,0:T(8,128)(2,1)S(1)}, u32[]{:S(2)}, u32[]{:S(2)}) collective-permute-start(bf16[16,1792]{1,0:T(8,128)(2,1)S(1)} %get-tuple-element.30), channel_id=1, source_target_pairs={{0,2},{1,3},{2,0},{3,1},{4,6},{5,7},{6,4},{7,5},{8,10},{9,11},{10,... | collective-permute-start | bytes 172040 | tf_op jit(solution)/shard_map/ppermute | solution.py:224
  12.2 0.3 collective-permute-start.4
  12.5 0.7 %collective-permute-start.6 = (bf16[16,3584]{1,0:T(8,128)(2,1)S(1)}, bf16[16,3584]{1,0:T(8,128)(2,1)S(1)}, u32[]{:S(2)}, u32[]{:S(2)}) collective-permute-start(bf16[16,3584]{1,0:T(8,128)(2,1)S(1)} %get-tuple-element.32.refs_3_), channel_id=1, source_target_pairs={{1,2},{2,1},{5,6},{6,5},{9,10},{10,9},{13,14},{14,13},{17,18},{18,... | collective-permute-start | bytes 344072 | tf_op jit(solution)/shard_map/ppermute | solution.py:287
  13.1 4.5 %collective-permute-start.5 = (bf16[16,3584]{1,0:T(8,128)(2,1)S(1)}, bf16[16,3584]{1,0:T(8,128)(2,1)S(1)}, u32[]{:S(2)}, u32[]{:S(2)}) collective-permute-start(bf16[16,3584]{1,0:T(8,128)(2,1)S(1)} %get-tuple-element.32.refs_3_), channel_id=1, source_target_pairs={{0,1},{1,0},{2,3},{3,2},{4,5},{5,4},{6,7},{7,6},{8,9},{9,8},{10,11... | collective-permute-start | bytes 344072 | tf_op jit(solution)/shard_map/ppermute | solution.py:224
  17.7 1.3 %collective-permute-start.7 = (bf16[16,1792]{1,0:T(8,128)(2,1)S(1)}, bf16[16,1792]{1,0:T(8,128)(2,1)S(1)}, u32[]{:S(2)}, u32[]{:S(2)}) collective-permute-start(bf16[16,1792]{1,0:T(8,128)(2,1)S(1)} %collective-permute-done.3.refs_0_), channel_id=1, source_target_pairs={{1,0},{2,3},{5,4},{6,7},{9,8},{10,11},{13,12},{14,15},{17,16},{18,... | collective-permute-start | bytes 172040 | tf_op jit(solution)/shard_map/ppermute | solution.py:286
  19.0 1.3 %collective-permute-start.8 = (bf16[16,1792]{1,0:T(8,128)(2,1)S(1)}, bf16[16,1792]{1,0:T(8,128)(2,1)S(1)}, u32[]{:S(2)}, u32[]{:S(2)}) collective-permute-start(bf16[16,1792]{1,0:T(8,128)(2,1)S(1)} %collective-permute-done.4.refs_1_), channel_id=1, source_target_pairs={{1,0},{2,3},{5,4},{6,7},{9,8},{10,11},{13,12},{14,15},{17,16},{18,... | collective-permute-start | bytes 172040 | tf_op jit(solution)/shard_map/ppermute | solution.py:288
  20.3 3.5 %collective-permute-done.7.refs_5_ = bf16[16,1792]{1,0:T(8,128)(2,1)S(1)} collective-permute-done((bf16[16,1792]{1,0:T(8,128)(2,1)S(1)}, bf16[16,1792]{1,0:T(8,128)(2,1)S(1)}, u32[]{:S(2)}, u32[]{:S(2)}) %collective-permute-start.7) | collective-permute-done | bytes 57376 | tf_op jit(solution)/shard_map/ppermute | solution.py:286
  23.7 1.3 %collective-permute-done.8.refs_6_ = bf16[16,1792]{1,0:T(8,128)(2,1)S(1)} collective-permute-done((bf16[16,1792]{1,0:T(8,128)(2,1)S(1)}, bf16[16,1792]{1,0:T(8,128)(2,1)S(1)}, u32[]{:S(2)}, u32[]{:S(2)}) %collective-permute-start.8) | collective-permute-done | bytes 57376 | tf_op jit(solution)/shard_map/ppermute | solution.py:288
  25.1 1.4 %hidden.1.after_ref.refs_0_ = bf16[64,512]{1,0:T(8,128)(2,1)S(1)} custom-call(bf16[16,1792]{1,0:T(8,128)(2,1)S(1)} %collective-permute-done.3.refs_0_, bf16[16,1792]{1,0:T(8,128)(2,1)S(1)} %collective-permute-done.4.refs_1_, bf16[16,3584]{1,0:T(8,128)(2,1)S(1)} %collective-permute-done.5.refs_2_, bf16[16,3584]{1,0:T(8,128)(2,1)S(1)} %get-tuple-element.32.refs_3_, ...), custom_call_target="tpu_custom_call" | custom-call | tf_op jit(solution)/shard_map/hidden/pallas_call | solution.py:293
  26.5 2.7 %collective-permute-start.11 = (bf16[64,512]{1,0:T(8,128)(2,1)S(1)}, bf16[64,512]{1,0:T(8,128)(2,1)S(1)}, u32[]{:S(2)}, u32[]{:S(2)}) collective-permute-start(bf16[64,512]{1,0:T(8,128)(2,1)S(1)} %hidden.1.after_ref.refs_0_), channel_id=1, source_target_pairs={{0,3},{1,2},{2,1},{3,0},{4,7},{5,6},{6,5},{7,4},{8,11},{9,10},{10,... | collective-permute-start | bytes 196616 | tf_op jit(solution)/shard_map/ppermute | solution.py:224
  29.2 1.8 %collective-permute-start.9 = (bf16[64,512]{1,0:T(8,128)(2,1)S(1)}, bf16[64,512]{1,0:T(8,128)(2,1)S(1)}, u32[]{:S(2)}, u32[]{:S(2)}) collective-permute-start(bf16[64,512]{1,0:T(8,128)(2,1)S(1)} %hidden.1.after_ref.refs_0_), channel_id=1, source_target_pairs={{0,1},{1,0},{2,3},{3,2},{4,5},{5,4},{6,7},{7,6},{8,9},{9,8},{10,11... | collective-permute-start | bytes 196616 | tf_op jit(solution)/shard_map/ppermute | solution.py:224
  30.9 2.1 %prepare.1 = (bf16[2048,896]{1,0:T(8,128)(2,1)S(1)}, bf16[256,32]{1,0:T(8,128)(2,1)S(1)}) custom-call(bf16[64,512]{1,0:T(8,128)(2,1)S(1)} %hidden.1.after_ref.refs_0_, s32[8,256]{1,0:T(8,128)} %bitcast.10, f32[96,256]{1,0:T(8,128)} %bitcast.8, bf16[2048,896]{1,0:T(8,128)(2,1)} %bitcast.7), custom_call_target="tpu_custom_call" | custom-call | tf_op jit(solution)/shard_map/prepare/pallas_call | solution.py:302
  33.1 1.4 %collective-permute-done.10.refs_2_ = bf16[64,512]{1,0:T(8,128)(2,1)S(1)} collective-permute-done((bf16[64,512]{1,0:T(8,128)(2,1)S(1)}, bf16[64,512]{1,0:T(8,128)(2,1)S(1)}, u32[]{:S(2)}, u32[]{:S(2)}) %collective-permute-start.10) | collective-permute-done | bytes 65568 | tf_op jit(solution)/shard_map/ppermute | solution.py:224
  34.5 0.7 %down.1 = (bf16[16,896]{1,0:T(8,128)(2,1)S(1)}, bf16[16,896]{1,0:T(8,128)(2,1)S(1)}, bf16[16,896]{1,0:T(8,128)(2,1)S(1)}, bf16[16,896]{1,0:T(8,128)(2,1)S(1)}) custom-call(bf16[64,512]{1,0:T(8,128)(2,1)S(1)} %hidden.1.after_ref.refs_0_, bf16[64,512]{1,0:T(8,128)(2,1)S(1)} %collective-permute-done.9.refs_1_, ...), custom_call_target="tpu_custom_call" | custom-call | tf_op jit(solution)/shard_map/down/pallas_call | solution.py:320
  35.2 2.4 %collective-permute-start.12 = (bf16[16,896]{1,0:T(8,128)(2,1)S(1)}, bf16[16,896]{1,0:T(8,128)(2,1)S(1)}, u32[]{:S(2)}, u32[]{:S(2)}) collective-permute-start(bf16[16,896]{1,0:T(8,128)(2,1)S(1)} %get-tuple-element.37), channel_id=1, source_target_pairs={{0,3},{1,2},{2,1},{3,0},{4,7},{5,6},{6,5},{7,4},{8,11},{9,10},{10,... | collective-permute-start | bytes 86024 | tf_op jit(solution)/shard_map/ppermute | solution.py:224
  37.6 2.0 %collective-permute-start.14 = (bf16[16,896]{1,0:T(8,128)(2,1)S(1)}, bf16[16,896]{1,0:T(8,128)(2,1)S(1)}, u32[]{:S(2)}, u32[]{:S(2)}) collective-permute-start(bf16[16,896]{1,0:T(8,128)(2,1)S(1)} %get-tuple-element.39), channel_id=1, source_target_pairs={{0,1},{1,0},{2,3},{3,2},{4,5},{5,4},{6,7},{7,6},{8,9},{9,8},{10,11... | collective-permute-start | bytes 86024 | tf_op jit(solution)/shard_map/ppermute | solution.py:224
  39.7 1.3 %collective-permute-done.12.refs_0_ = bf16[16,896]{1,0:T(8,128)(2,1)S(1)} collective-permute-done((bf16[16,896]{1,0:T(8,128)(2,1)S(1)}, bf16[16,896]{1,0:T(8,128)(2,1)S(1)}, u32[]{:S(2)}, u32[]{:S(2)}) %collective-permute-start.12) | collective-permute-done | bytes 28704 | tf_op jit(solution)/shard_map/ppermute | solution.py:224
  40.9 1.5 %collective-permute-done.13.refs_1_ = bf16[16,896]{1,0:T(8,128)(2,1)S(1)} collective-permute-done((bf16[16,896]{1,0:T(8,128)(2,1)S(1)}, bf16[16,896]{1,0:T(8,128)(2,1)S(1)}, u32[]{:S(2)}, u32[]{:S(2)}) %collective-permute-start.13) | collective-permute-done | bytes 28704 | tf_op jit(solution)/shard_map/ppermute | solution.py:224
  42.4 0.2 spread.1
  42.6 0.1 collective-permute-start.15
  42.7 1.8 %collective-permute-start.16 = (bf16[4,8,896]{2,1,0:T(8,128)(2,1)S(1)}, bf16[4,8,896]{2,1,0:T(8,128)(2,1)S(1)}, u32[]{:S(2)}, u32[]{:S(2)}) collective-permute-start(bf16[4,8,896]{2,1,0:T(8,128)(2,1)S(1)} %get-tuple-element.42), channel_id=1, source_target_pairs={{0,8},{4,12},{8,0},{12,4},{1,9},{5,13},{9,1},{13,5},{2,10},{6,14},... | collective-permute-start | bytes 172040 | tf_op jit(solution)/shard_map/ppermute | solution.py:224
  44.5 0.1 collective-permute-start.17
  44.5 2.1 %collective-permute-done.15.refs_0_ = bf16[4,8,896]{2,1,0:T(8,128)(2,1)S(1)} collective-permute-done((bf16[4,8,896]{2,1,0:T(8,128)(2,1)S(1)}, bf16[4,8,896]{2,1,0:T(8,128)(2,1)S(1)}, u32[]{:S(2)}, u32[]{:S(2)}) %collective-permute-start.15) | collective-permute-done | bytes 57376 | tf_op jit(solution)/shard_map/ppermute | solution.py:224
  46.6 1.3 %collective-permute-done.16.refs_1_ = bf16[4,8,896]{2,1,0:T(8,128)(2,1)S(1)} collective-permute-done((bf16[4,8,896]{2,1,0:T(8,128)(2,1)S(1)}, bf16[4,8,896]{2,1,0:T(8,128)(2,1)S(1)}, u32[]{:S(2)}, u32[]{:S(2)}) %collective-permute-start.16) | collective-permute-done | bytes 57376 | tf_op jit(solution)/shard_map/ppermute | solution.py:224
  47.9 1.5 %combine.1 = bf16[256,3584]{1,0:T(8,128)(2,1)} custom-call(bf16[256,32]{1,0:T(8,128)(2,1)S(1)} %get-tuple-element.34.mixing_ref, bf16[4,8,896]{2,1,0:T(8,128)(2,1)S(1)} %collective-permute-done.15.refs_0_, bf16[4,8,896]{2,1,0:T(8,128)(2,1)S(1)} %collective-permute-done.16.refs_1_, bf16[4,8,896]{2,1,0:T(8,128)(2,1)S(1)} %collective-permute-done.17.refs_2_, ...), custom_call_target="tpu_custom_call" | custom-call | tf_op jit(solution)/shard_map/combine/pallas_call | solution.py:345
  (12 shorter events, 0.0 us)
Async XLA Ops:
  2.2 6.3 %collective-permute-start = (bf16[8,3712]{1,0:T(8,128)(2,1)S(1)}, bf16[8,3712]{1,0:T(8,128)(2,1)S(1)}, u32[]{:S(2)}, u32[]{:S(2)}) collective-permute-start(bf16[8,3712]{1,0:T(8,128)(2,1)S(1)} %get-tuple-element.27), channel_id=1, source_target_pairs={{0,12},{4,8},{8,4},{12,0},{1,13},{5,9},{9,5},{13,1},{2,14},{6,10},... | collective-permute-start | bytes 178184 | tf_op jit(solution)/shard_map/ppermute | solution.py:224
  4.6 4.5 %collective-permute-start.1 = (bf16[8,3712]{1,0:T(8,128)(2,1)S(1)}, bf16[8,3712]{1,0:T(8,128)(2,1)S(1)}, u32[]{:S(2)}, u32[]{:S(2)}) collective-permute-start(bf16[8,3712]{1,0:T(8,128)(2,1)S(1)} %get-tuple-element.28), channel_id=1, source_target_pairs={{0,8},{4,12},{8,0},{12,4},{1,9},{5,13},{9,1},{13,5},{2,10},{6,14},... | collective-permute-start | bytes 178184 | tf_op jit(solution)/shard_map/ppermute | solution.py:224
  5.2 3.9 %collective-permute-start.2 = (bf16[8,3712]{1,0:T(8,128)(2,1)S(1)}, bf16[8,3712]{1,0:T(8,128)(2,1)S(1)}, u32[]{:S(2)}, u32[]{:S(2)}) collective-permute-start(bf16[8,3712]{1,0:T(8,128)(2,1)S(1)} %get-tuple-element.29), channel_id=1, source_target_pairs={{0,4},{4,0},{8,12},{12,8},{1,5},{5,1},{9,13},{13,9},{2,6},{6,2},{1... | collective-permute-start | bytes 178184 | tf_op jit(solution)/shard_map/ppermute | solution.py:224
  9.5 8.2 %collective-permute-start.3 = (bf16[16,1792]{1,0:T(8,128)(2,1)S(1)}, bf16[16,1792]{1,0:T(8,128)(2,1)S(1)}, u32[]{:S(2)}, u32[]{:S(2)}) collective-permute-start(bf16[16,1792]{1,0:T(8,128)(2,1)S(1)} %get-tuple-element.30), channel_id=1, source_target_pairs={{0,2},{1,3},{2,0},{3,1},{4,6},{5,7},{6,4},{7,5},{8,10},{9,11},{10,... | collective-permute-start | bytes 172040 | tf_op jit(solution)/shard_map/ppermute | solution.py:224
  12.2 6.8 %collective-permute-start.4 = (bf16[16,1792]{1,0:T(8,128)(2,1)S(1)}, bf16[16,1792]{1,0:T(8,128)(2,1)S(1)}, u32[]{:S(2)}, u32[]{:S(2)}) collective-permute-start(bf16[16,1792]{1,0:T(8,128)(2,1)S(1)} %get-tuple-element.31), channel_id=1, source_target_pairs={{0,2},{1,3},{2,0},{3,1},{4,6},{5,7},{6,4},{7,5},{8,10},{9,11},{10,... | collective-permute-start | bytes 172040 | tf_op jit(solution)/shard_map/ppermute | solution.py:224
  12.5 12.6 %collective-permute-start.6 = (bf16[16,3584]{1,0:T(8,128)(2,1)S(1)}, bf16[16,3584]{1,0:T(8,128)(2,1)S(1)}, u32[]{:S(2)}, u32[]{:S(2)}) collective-permute-start(bf16[16,3584]{1,0:T(8,128)(2,1)S(1)} %get-tuple-element.32.refs_3_), channel_id=1, source_target_pairs={{1,2},{2,1},{5,6},{6,5},{9,10},{10,9},{13,14},{14,13},{17,18},{18,... | collective-permute-start | bytes 344072 | tf_op jit(solution)/shard_map/ppermute | solution.py:287
  13.1 11.9 %collective-permute-start.5 = (bf16[16,3584]{1,0:T(8,128)(2,1)S(1)}, bf16[16,3584]{1,0:T(8,128)(2,1)S(1)}, u32[]{:S(2)}, u32[]{:S(2)}) collective-permute-start(bf16[16,3584]{1,0:T(8,128)(2,1)S(1)} %get-tuple-element.32.refs_3_), channel_id=1, source_target_pairs={{0,1},{1,0},{2,3},{3,2},{4,5},{5,4},{6,7},{7,6},{8,9},{9,8},{10,11... | collective-permute-start | bytes 344072 | tf_op jit(solution)/shard_map/ppermute | solution.py:224
  17.7 6.1 %collective-permute-start.7 = (bf16[16,1792]{1,0:T(8,128)(2,1)S(1)}, bf16[16,1792]{1,0:T(8,128)(2,1)S(1)}, u32[]{:S(2)}, u32[]{:S(2)}) collective-permute-start(bf16[16,1792]{1,0:T(8,128)(2,1)S(1)} %collective-permute-done.3.refs_0_), channel_id=1, source_target_pairs={{1,0},{2,3},{5,4},{6,7},{9,8},{10,11},{13,12},{14,15},{17,16},{18,... | collective-permute-start | bytes 172040 | tf_op jit(solution)/shard_map/ppermute | solution.py:286
  19.0 6.1 %collective-permute-start.8 = (bf16[16,1792]{1,0:T(8,128)(2,1)S(1)}, bf16[16,1792]{1,0:T(8,128)(2,1)S(1)}, u32[]{:S(2)}, u32[]{:S(2)}) collective-permute-start(bf16[16,1792]{1,0:T(8,128)(2,1)S(1)} %collective-permute-done.4.refs_1_), channel_id=1, source_target_pairs={{1,0},{2,3},{5,4},{6,7},{9,8},{10,11},{13,12},{14,15},{17,16},{18,... | collective-permute-start | bytes 172040 | tf_op jit(solution)/shard_map/ppermute | solution.py:288
  26.5 6.6 %collective-permute-start.11 = (bf16[64,512]{1,0:T(8,128)(2,1)S(1)}, bf16[64,512]{1,0:T(8,128)(2,1)S(1)}, u32[]{:S(2)}, u32[]{:S(2)}) collective-permute-start(bf16[64,512]{1,0:T(8,128)(2,1)S(1)} %hidden.1.after_ref.refs_0_), channel_id=1, source_target_pairs={{0,3},{1,2},{2,1},{3,0},{4,7},{5,6},{6,5},{7,4},{8,11},{9,10},{10,... | collective-permute-start | bytes 196616 | tf_op jit(solution)/shard_map/ppermute | solution.py:224
  29.2 5.3 %collective-permute-start.10 = (bf16[64,512]{1,0:T(8,128)(2,1)S(1)}, bf16[64,512]{1,0:T(8,128)(2,1)S(1)}, u32[]{:S(2)}, u32[]{:S(2)}) collective-permute-start(bf16[64,512]{1,0:T(8,128)(2,1)S(1)} %hidden.1.after_ref.refs_0_), channel_id=1, source_target_pairs={{0,2},{1,3},{2,0},{3,1},{4,6},{5,7},{6,4},{7,5},{8,10},{9,11},{10,... | collective-permute-start | bytes 196616 | tf_op jit(solution)/shard_map/ppermute | solution.py:224
  29.2 5.3 %collective-permute-start.9 = (bf16[64,512]{1,0:T(8,128)(2,1)S(1)}, bf16[64,512]{1,0:T(8,128)(2,1)S(1)}, u32[]{:S(2)}, u32[]{:S(2)}) collective-permute-start(bf16[64,512]{1,0:T(8,128)(2,1)S(1)} %hidden.1.after_ref.refs_0_), channel_id=1, source_target_pairs={{0,1},{1,0},{2,3},{3,2},{4,5},{5,4},{6,7},{7,6},{8,9},{9,8},{10,11... | collective-permute-start | bytes 196616 | tf_op jit(solution)/shard_map/ppermute | solution.py:224
  35.2 5.7 %collective-permute-start.12 = (bf16[16,896]{1,0:T(8,128)(2,1)S(1)}, bf16[16,896]{1,0:T(8,128)(2,1)S(1)}, u32[]{:S(2)}, u32[]{:S(2)}) collective-permute-start(bf16[16,896]{1,0:T(8,128)(2,1)S(1)} %get-tuple-element.37), channel_id=1, source_target_pairs={{0,3},{1,2},{2,1},{3,0},{4,7},{5,6},{6,5},{7,4},{8,11},{9,10},{10,... | collective-permute-start | bytes 86024 | tf_op jit(solution)/shard_map/ppermute | solution.py:224
  37.6 4.8 %collective-permute-start.13 = (bf16[16,896]{1,0:T(8,128)(2,1)S(1)}, bf16[16,896]{1,0:T(8,128)(2,1)S(1)}, u32[]{:S(2)}, u32[]{:S(2)}) collective-permute-start(bf16[16,896]{1,0:T(8,128)(2,1)S(1)} %get-tuple-element.38), channel_id=1, source_target_pairs={{0,2},{1,3},{2,0},{3,1},{4,6},{5,7},{6,4},{7,5},{8,10},{9,11},{10,... | collective-permute-start | bytes 86024 | tf_op jit(solution)/shard_map/ppermute | solution.py:224
  37.6 4.8 %collective-permute-start.14 = (bf16[16,896]{1,0:T(8,128)(2,1)S(1)}, bf16[16,896]{1,0:T(8,128)(2,1)S(1)}, u32[]{:S(2)}, u32[]{:S(2)}) collective-permute-start(bf16[16,896]{1,0:T(8,128)(2,1)S(1)} %get-tuple-element.39), channel_id=1, source_target_pairs={{0,1},{1,0},{2,3},{3,2},{4,5},{5,4},{6,7},{7,6},{8,9},{9,8},{10,11... | collective-permute-start | bytes 86024 | tf_op jit(solution)/shard_map/ppermute | solution.py:224
  42.6 4.0 %collective-permute-start.15 = (bf16[4,8,896]{2,1,0:T(8,128)(2,1)S(1)}, bf16[4,8,896]{2,1,0:T(8,128)(2,1)S(1)}, u32[]{:S(2)}, u32[]{:S(2)}) collective-permute-start(bf16[4,8,896]{2,1,0:T(8,128)(2,1)S(1)} %get-tuple-element.41), channel_id=1, source_target_pairs={{0,12},{4,8},{8,4},{12,0},{1,13},{5,9},{9,5},{13,1},{2,14},{6,10},... | collective-permute-start | bytes 172040 | tf_op jit(solution)/shard_map/ppermute | solution.py:224
  42.7 5.2 %collective-permute-start.16 = (bf16[4,8,896]{2,1,0:T(8,128)(2,1)S(1)}, bf16[4,8,896]{2,1,0:T(8,128)(2,1)S(1)}, u32[]{:S(2)}, u32[]{:S(2)}) collective-permute-start(bf16[4,8,896]{2,1,0:T(8,128)(2,1)S(1)} %get-tuple-element.42), channel_id=1, source_target_pairs={{0,8},{4,12},{8,0},{12,4},{1,9},{5,13},{9,1},{13,5},{2,10},{6,14},... | collective-permute-start | bytes 172040 | tf_op jit(solution)/shard_map/ppermute | solution.py:224
  44.5 3.4 %collective-permute-start.17 = (bf16[4,8,896]{2,1,0:T(8,128)(2,1)S(1)}, bf16[4,8,896]{2,1,0:T(8,128)(2,1)S(1)}, u32[]{:S(2)}, u32[]{:S(2)}) collective-permute-start(bf16[4,8,896]{2,1,0:T(8,128)(2,1)S(1)} %get-tuple-element.43), channel_id=1, source_target_pairs={{0,4},{4,0},{8,12},{12,8},{1,5},{5,1},{9,13},{13,9},{2,6},{6,2},{1... | collective-permute-start | bytes 172040 | tf_op jit(solution)/shard_map/ppermute | solution.py:224

commit v5 on v3

--- a/solution.py
+++ b/solution.py
@@ -126,16 +126,14 @@
 
 
 def hidden_kernel(columns, *refs):
-    blocks, (gate_ref, up_ref, hidden_ref, held) = refs[:columns], refs[columns:]
-    slots = blocks[0].shape[0]
+    blocks, (gate_ref, up_ref, hidden_ref) = refs[:columns], refs[columns:]
     units = gate_ref.shape[1]
-    for e in range(columns):
-        held[e * slots : (e + 1) * slots, :] = blocks[e][...]
+    rows = jnp.concatenate([block[...] for block in blocks], axis=0)
     step = min(256, units)
     for c in range(units // step):
         part = slice(c * step, (c + 1) * step)
-        gate = jnp.dot(held[...], gate_ref[:, part], preferred_element_type=F32)
-        up = jnp.dot(held[...], up_ref[:, part], preferred_element_type=F32)
+        gate = jnp.dot(rows, gate_ref[:, part], preferred_element_type=F32)
+        up = jnp.dot(rows, up_ref[:, part], preferred_element_type=F32)
         hidden_ref[:, part] = (gate / (1.0 + jnp.exp(-gate)) * up).astype(BF16)
 
 
@@ -167,16 +165,21 @@
 def combine_kernel(groups, columns, mixing_ref, *refs):
     backs, (out_ref, held, sems) = refs[:groups][::-1], refs[groups:]
     me = lax.axis_index("ing")
-    width = backs[0].shape[2]
+    width, half = backs[0].shape[2], held.shape[0] // 2
     copies = []
     for e in range(columns):
         rows = jnp.concatenate([backs[d][e].astype(F32) for d in range(groups)], axis=0)
-        value = jnp.dot(mixing_ref[...], rows.astype(BF16), preferred_element_type=F32)
+        rows = rows.astype(BF16)
         part = pl.ds(e * width, width)
-        held[:, part] = value.astype(BF16)
         there = pl.ds(pl.multiple_of((me ^ e) * width, width), width)
-        copies.append(pltpu.make_async_copy(held.at[:, part], out_ref.at[:, there], sems.at[e]))
-        copies[-1].start()
+        for h in range(2):
+            mine = pl.ds(h * half, half)
+            value = jnp.dot(mixing_ref[mine, :], rows, preferred_element_type=F32)
+            held[mine, part] = value.astype(BF16)
+            copies.append(
+                pltpu.make_async_copy(held.at[mine, part], out_ref.at[mine, there], sems.at[2 * e + h])
+            )
+            copies[-1].start()
     for copy in copies:
         copy.wait()
 
@@ -202,7 +205,7 @@
     logits = pltpu.with_memory_space_constraint(router_logits.T, pltpu.HBM)
 
     outbound = pl.pallas_call(
-        functools.partial(dispatch_kernel, groups, 512),
+        functools.partial(dispatch_kernel, groups, features // 2),
         out_shape=[jax.ShapeDtypeStruct((CAP, wide), BF16)] * groups,
         in_specs=[ANY, ANY],
         out_specs=[VMEM] * groups,
@@ -210,7 +213,7 @@
             pltpu.VMEM(ids.shape, jnp.int32),
             pltpu.VMEM((count, features), BF16),
             pltpu.VMEM((count, count), BF16),
-            pltpu.SemaphoreType.DMA((features // 512 + 1,)),
+            pltpu.SemaphoreType.DMA((3,)),
         ],
         compiler_params=params(2 * count * features),
         name="dispatch",
@@ -256,7 +259,6 @@
         out_shape=jax.ShapeDtypeStruct((columns * slots, units), BF16),
         in_specs=[VMEM] * (columns + 2),
         out_specs=VMEM,
-        scratch_shapes=[pltpu.VMEM((columns * slots, features), BF16)],
         compiler_params=params(2 * columns * slots * (2 * features + units)),
         name="hidden",
     )(*blocks, gate, up)
@@ -292,7 +294,7 @@
         out_shape=jax.ShapeDtypeStruct((count, features), BF16),
         in_specs=[VMEM] * (1 + groups),
         out_specs=ANY,
-        scratch_shapes=[pltpu.VMEM((count, features), BF16), pltpu.SemaphoreType.DMA((columns,))],
+        scratch_shapes=[pltpu.VMEM((count, features), BF16), pltpu.SemaphoreType.DMA((2 * columns,))],
         compiler_params=params(2 * (count + groups * CAP) * features),
         name="combine",
     )(mixing, *backs)

time: 47 us -> 46.6 us (level)
  no operation moved by 1% of the time
where the time goes in v5:
time: 46.6 us; the launch traced here: 46.4 us
  starting transfers between devices  18.7 us (40%)
  waiting for transfers between devices  17.4 us (37%)
  Pallas kernels  10.3 us (22%)
    ppermute x15, starting transfers between devices, swap(): lax.ppermute(x, name, [(a, a ^ step) for a in range(lax.axis_size(name))])  18.7 us
    ppermute x15, waiting for transfers between devices, swap(): lax.ppermute(x, name, [(a, a ^ step) for a in range(lax.axis_size(name))])  17.4 us
    pallas_call x1, Pallas kernels, local(): pl.pallas_call(functools.partial(prepare_kernel, groups), out_shape=[pltp...  4.33 us
    pallas_call x1, Pallas kernels, local(): pl.pallas_call(functools.partial(dispatch_kernel, groups, features // 2),...  1.79 us
    pallas_call x1, Pallas kernels, local(): pl.pallas_call(functools.partial(combine_kernel, groups, columns), out_sh...  1.49 us
    pallas_call x1, Pallas kernels, local(): pl.pallas_call(functools.partial(hidden_kernel, columns), out_shape=jax.S...  1.4 us
  transfers between devices with their start and end apart: 15, of which 9 were waited for; matrix products, arithmetic and copies ran while one was open for 0% of the time, Pallas kernels for 9%

profile of v5, /device:TPU:0, one launch (start us, length us, event | category | flops | bytes accessed | tf_op | source)
XLA Modules:
  0.0 46.4 jit_solution(14041878652614987382)
XLA Ops:
  0.0 1.8 %dispatch.1 = (bf16[8,3712]{1,0:T(8,128)(2,1)S(1)}, bf16[8,3712]{1,0:T(8,128)(2,1)S(1)}, bf16[8,3712]{1,0:T(8,128)(2,1)S(1)}, bf16[8,3712]{1,0:T(8,128)(2,1)S(1)}) custom-call(s32[8,256]{1,0:T(8,128)} %bitcast.9, bf16[256,3584]{1,0:T(8,128)(2,1)} %tokens_ref.1), custom_call_target="tpu_custom_call" | custom-call | tf_op jit(solution)/shard_map/dispatch/pallas_call | solution.py:207
  1.8 2.4 %collective-permute-start = (bf16[8,3712]{1,0:T(8,128)(2,1)S(1)}, bf16[8,3712]{1,0:T(8,128)(2,1)S(1)}, u32[]{:S(2)}, u32[]{:S(2)}) collective-permute-start(bf16[8,3712]{1,0:T(8,128)(2,1)S(1)} %get-tuple-element.23), channel_id=1, source_target_pairs={{0,12},{4,8},{8,4},{12,0},{1,13},{5,9},{9,5},{13,1},{2,14},{6,10},... | collective-permute-start | bytes 178184 | tf_op jit(solution)/shard_map/ppermute | solution.py:190
  4.2 0.6 %collective-permute-start.1 = (bf16[8,3712]{1,0:T(8,128)(2,1)S(1)}, bf16[8,3712]{1,0:T(8,128)(2,1)S(1)}, u32[]{:S(2)}, u32[]{:S(2)}) collective-permute-start(bf16[8,3712]{1,0:T(8,128)(2,1)S(1)} %get-tuple-element.24), channel_id=1, source_target_pairs={{0,8},{4,12},{8,0},{12,4},{1,9},{5,13},{9,1},{13,5},{2,10},{6,14},... | collective-permute-start | bytes 178184 | tf_op jit(solution)/shard_map/ppermute | solution.py:190
  4.9 0.0 collective-permute-start.2
  4.9 1.7 %collective-permute-done.refs_0_ = bf16[8,3712]{1,0:T(8,128)(2,1)S(1)} collective-permute-done((bf16[8,3712]{1,0:T(8,128)(2,1)S(1)}, bf16[8,3712]{1,0:T(8,128)(2,1)S(1)}, u32[]{:S(2)}, u32[]{:S(2)}) %collective-permute-start) | collective-permute-done | bytes 59424 | tf_op jit(solution)/shard_map/ppermute | solution.py:190
  6.6 2.2 %collective-permute-done.1.refs_1_ = bf16[8,3712]{1,0:T(8,128)(2,1)S(1)} collective-permute-done((bf16[8,3712]{1,0:T(8,128)(2,1)S(1)}, bf16[8,3712]{1,0:T(8,128)(2,1)S(1)}, u32[]{:S(2)}, u32[]{:S(2)}) %collective-permute-start.1) | collective-permute-done | bytes 59424 | tf_op jit(solution)/shard_map/ppermute | solution.py:190
  8.8 0.3 compact.1
  9.1 3.7 %collective-permute-start.5 = (bf16[16,3584]{1,0:T(8,128)(2,1)S(1)}, bf16[16,3584]{1,0:T(8,128)(2,1)S(1)}, u32[]{:S(2)}, u32[]{:S(2)}) collective-permute-start(bf16[16,3584]{1,0:T(8,128)(2,1)S(1)} %get-tuple-element.29.refs_0_), channel_id=1, source_target_pairs={{0,3},{1,2},{2,1},{3,0},{4,7},{5,6},{6,5},{7,4},{8,11},{9,10},{10,... | collective-permute-start | bytes 344072 | tf_op jit(solution)/shard_map/ppermute | solution.py:190
  12.9 0.0 collective-permute-start.4
  12.9 0.7 %collective-permute-start.3 = (bf16[16,3584]{1,0:T(8,128)(2,1)S(1)}, bf16[16,3584]{1,0:T(8,128)(2,1)S(1)}, u32[]{:S(2)}, u32[]{:S(2)}) collective-permute-start(bf16[16,3584]{1,0:T(8,128)(2,1)S(1)} %get-tuple-element.29.refs_0_), channel_id=1, source_target_pairs={{0,1},{1,0},{2,3},{3,2},{4,5},{5,4},{6,7},{7,6},{8,9},{9,8},{10,11... | collective-permute-start | bytes 344072 | tf_op jit(solution)/shard_map/ppermute | solution.py:190
  13.6 4.3 %prepare.1 = (bf16[3584,512]{1,0:T(8,128)(2,1)S(1)}, bf16[3584,512]{1,0:T(8,128)(2,1)S(1)}, bf16[2048,896]{1,0:T(8,128)(2,1)S(1)}, bf16[256,32]{1,0:T(8,128)(2,1)S(1)}) custom-call(bf16[32,128]{1,0:T(8,128)(2,1)S(1)} %get-tuple-element.27.after_ref.pick_ref, s32[8,256]{1,0:T(8,128)} %bitcast.10, f32[96,256]{1,0:T(8,128)} %bitcast.8, ...), custom_call_target="tpu_custom_call" | custom-call | tf_op jit(solution)/shard_map/prepare/pallas_call | solution.py:237
  17.9 0.0 collective-permute-done.5.refs_3_
  17.9 4.6 %collective-permute-done.4.refs_2_ = bf16[16,3584]{1,0:T(8,128)(2,1)S(1)} collective-permute-done((bf16[16,3584]{1,0:T(8,128)(2,1)S(1)}, bf16[16,3584]{1,0:T(8,128)(2,1)S(1)}, u32[]{:S(2)}, u32[]{:S(2)}) %collective-permute-start.4) | collective-permute-done | bytes 114720 | tf_op jit(solution)/shard_map/ppermute | solution.py:190
  22.5 0.0 collective-permute-done.3.refs_1_
  22.5 1.4 %hidden.1.refs_0_ = bf16[64,512]{1,0:T(8,128)(2,1)S(1)} custom-call(bf16[16,3584]{1,0:T(8,128)(2,1)S(1)} %get-tuple-element.29.refs_0_, bf16[16,3584]{1,0:T(8,128)(2,1)S(1)} %collective-permute-done.3.refs_1_, bf16[16,3584]{1,0:T(8,128)(2,1)S(1)} %collective-permute-done.4.refs_2_, bf16[16,3584]{1,0:T(8,128)(2,1)S(1)} %collective-permute-done.5.refs_3_, ...), custom_call_target="tpu_custom_call" | custom-call | tf_op jit(solution)/shard_map/hidden/pallas_call | solution.py:257
  23.9 2.5 %collective-permute-start.8 = (bf16[64,512]{1,0:T(8,128)(2,1)S(1)}, bf16[64,512]{1,0:T(8,128)(2,1)S(1)}, u32[]{:S(2)}, u32[]{:S(2)}) collective-permute-start(bf16[64,512]{1,0:T(8,128)(2,1)S(1)} %hidden.1.refs_0_), channel_id=1, source_target_pairs={{0,3},{1,2},{2,1},{3,0},{4,7},{5,6},{6,5},{7,4},{8,11},{9,10},{10,... | collective-permute-start | bytes 196616 | tf_op jit(solution)/shard_map/ppermute | solution.py:190
  26.5 0.0 collective-permute-start.7
  26.5 1.9 %collective-permute-start.6 = (bf16[64,512]{1,0:T(8,128)(2,1)S(1)}, bf16[64,512]{1,0:T(8,128)(2,1)S(1)}, u32[]{:S(2)}, u32[]{:S(2)}) collective-permute-start(bf16[64,512]{1,0:T(8,128)(2,1)S(1)} %hidden.1.refs_0_), channel_id=1, source_target_pairs={{0,1},{1,0},{2,3},{3,2},{4,5},{5,4},{6,7},{7,6},{8,9},{9,8},{10,11... | collective-permute-start | bytes 196616 | tf_op jit(solution)/shard_map/ppermute | solution.py:190
  28.4 2.0 %collective-permute-done.8.refs_3_ = bf16[64,512]{1,0:T(8,128)(2,1)S(1)} collective-permute-done((bf16[64,512]{1,0:T(8,128)(2,1)S(1)}, bf16[64,512]{1,0:T(8,128)(2,1)S(1)}, u32[]{:S(2)}, u32[]{:S(2)}) %collective-permute-start.8) | collective-permute-done | bytes 65568 | tf_op jit(solution)/shard_map/ppermute | solution.py:190
  30.4 1.7 %collective-permute-done.7.refs_2_ = bf16[64,512]{1,0:T(8,128)(2,1)S(1)} collective-permute-done((bf16[64,512]{1,0:T(8,128)(2,1)S(1)}, bf16[64,512]{1,0:T(8,128)(2,1)S(1)}, u32[]{:S(2)}, u32[]{:S(2)}) %collective-permute-start.7) | collective-permute-done | bytes 65568 | tf_op jit(solution)/shard_map/ppermute | solution.py:190
  32.1 0.7 %down.1 = (bf16[16,896]{1,0:T(8,128)(2,1)S(1)}, bf16[16,896]{1,0:T(8,128)(2,1)S(1)}, bf16[16,896]{1,0:T(8,128)(2,1)S(1)}, bf16[16,896]{1,0:T(8,128)(2,1)S(1)}) custom-call(bf16[64,512]{1,0:T(8,128)(2,1)S(1)} %hidden.1.refs_0_, bf16[64,512]{1,0:T(8,128)(2,1)S(1)} %collective-permute-done.6.refs_1_, bf16[64,512]{1,0:T(8,128)(2,1)S(1)} %collective-permute-done.7.refs_2_, ...), custom_call_target="tpu_custom_call" | custom-call | tf_op jit(solution)/shard_map/down/pallas_call | solution.py:267
  32.8 2.1 %collective-permute-start.9 = (bf16[16,896]{1,0:T(8,128)(2,1)S(1)}, bf16[16,896]{1,0:T(8,128)(2,1)S(1)}, u32[]{:S(2)}, u32[]{:S(2)}) collective-permute-start(bf16[16,896]{1,0:T(8,128)(2,1)S(1)} %get-tuple-element.33), channel_id=1, source_target_pairs={{0,3},{1,2},{2,1},{3,0},{4,7},{5,6},{6,5},{7,4},{8,11},{9,10},{10,... | collective-permute-start | bytes 86024 | tf_op jit(solution)/shard_map/ppermute | solution.py:190
  34.9 2.3 %collective-permute-start.11 = (bf16[16,896]{1,0:T(8,128)(2,1)S(1)}, bf16[16,896]{1,0:T(8,128)(2,1)S(1)}, u32[]{:S(2)}, u32[]{:S(2)}) collective-permute-start(bf16[16,896]{1,0:T(8,128)(2,1)S(1)} %get-tuple-element.35), channel_id=1, source_target_pairs={{0,1},{1,0},{2,3},{3,2},{4,5},{5,4},{6,7},{7,6},{8,9},{9,8},{10,11... | collective-permute-start | bytes 86024 | tf_op jit(solution)/shard_map/ppermute | solution.py:190
  37.3 1.3 %collective-permute-done.9.refs_0_ = bf16[16,896]{1,0:T(8,128)(2,1)S(1)} collective-permute-done((bf16[16,896]{1,0:T(8,128)(2,1)S(1)}, bf16[16,896]{1,0:T(8,128)(2,1)S(1)}, u32[]{:S(2)}, u32[]{:S(2)}) %collective-permute-start.9) | collective-permute-done | bytes 28704 | tf_op jit(solution)/shard_map/ppermute | solution.py:190
  38.5 1.1 %collective-permute-done.10.refs_1_ = bf16[16,896]{1,0:T(8,128)(2,1)S(1)} collective-permute-done((bf16[16,896]{1,0:T(8,128)(2,1)S(1)}, bf16[16,896]{1,0:T(8,128)(2,1)S(1)}, u32[]{:S(2)}, u32[]{:S(2)}) %collective-permute-start.10) | collective-permute-done | bytes 28704 | tf_op jit(solution)/shard_map/ppermute | solution.py:190
  39.7 0.2 spread.1
  39.9 0.1 collective-permute-start.12
  39.9 2.1 %collective-permute-start.13 = (bf16[4,8,896]{2,1,0:T(8,128)(2,1)S(1)}, bf16[4,8,896]{2,1,0:T(8,128)(2,1)S(1)}, u32[]{:S(2)}, u32[]{:S(2)}) collective-permute-start(bf16[4,8,896]{2,1,0:T(8,128)(2,1)S(1)} %get-tuple-element.38), channel_id=1, source_target_pairs={{0,8},{4,12},{8,0},{12,4},{1,9},{5,13},{9,1},{13,5},{2,10},{6,14},... | collective-permute-start | bytes 172040 | tf_op jit(solution)/shard_map/ppermute | solution.py:190
  42.0 0.0 collective-permute-start.14
  42.1 1.6 %collective-permute-done.12.refs_0_ = bf16[4,8,896]{2,1,0:T(8,128)(2,1)S(1)} collective-permute-done((bf16[4,8,896]{2,1,0:T(8,128)(2,1)S(1)}, bf16[4,8,896]{2,1,0:T(8,128)(2,1)S(1)}, u32[]{:S(2)}, u32[]{:S(2)}) %collective-permute-start.12) | collective-permute-done | bytes 57376 | tf_op jit(solution)/shard_map/ppermute | solution.py:190
  43.7 1.2 %collective-permute-done.13.refs_1_ = bf16[4,8,896]{2,1,0:T(8,128)(2,1)S(1)} collective-permute-done((bf16[4,8,896]{2,1,0:T(8,128)(2,1)S(1)}, bf16[4,8,896]{2,1,0:T(8,128)(2,1)S(1)}, u32[]{:S(2)}, u32[]{:S(2)}) %collective-permute-start.13) | collective-permute-done | bytes 57376 | tf_op jit(solution)/shard_map/ppermute | solution.py:190
  44.9 1.5 %combine.1 = bf16[256,3584]{1,0:T(8,128)(2,1)} custom-call(bf16[256,32]{1,0:T(8,128)(2,1)S(1)} %get-tuple-element.28.mixing_ref, bf16[4,8,896]{2,1,0:T(8,128)(2,1)S(1)} %collective-permute-done.12.refs_0_, bf16[4,8,896]{2,1,0:T(8,128)(2,1)S(1)} %collective-permute-done.13.refs_1_, bf16[4,8,896]{2,1,0:T(8,128)(2,1)S(1)} %collective-permute-done.14.refs_2_, ...), custom_call_target="tpu_custom_call" | custom-call | tf_op jit(solution)/shard_map/combine/pallas_call | solution.py:292
  (5 shorter events, 0.0 us)
Async XLA Ops:
  1.8 4.8 %collective-permute-start = (bf16[8,3712]{1,0:T(8,128)(2,1)S(1)}, bf16[8,3712]{1,0:T(8,128)(2,1)S(1)}, u32[]{:S(2)}, u32[]{:S(2)}) collective-permute-start(bf16[8,3712]{1,0:T(8,128)(2,1)S(1)} %get-tuple-element.23), channel_id=1, source_target_pairs={{0,12},{4,8},{8,4},{12,0},{1,13},{5,9},{9,5},{13,1},{2,14},{6,10},... | collective-permute-start | bytes 178184 | tf_op jit(solution)/shard_map/ppermute | solution.py:190
  4.2 4.5 %collective-permute-start.1 = (bf16[8,3712]{1,0:T(8,128)(2,1)S(1)}, bf16[8,3712]{1,0:T(8,128)(2,1)S(1)}, u32[]{:S(2)}, u32[]{:S(2)}) collective-permute-start(bf16[8,3712]{1,0:T(8,128)(2,1)S(1)} %get-tuple-element.24), channel_id=1, source_target_pairs={{0,8},{4,12},{8,0},{12,4},{1,9},{5,13},{9,1},{13,5},{2,10},{6,14},... | collective-permute-start | bytes 178184 | tf_op jit(solution)/shard_map/ppermute | solution.py:190
  4.9 3.9 %collective-permute-start.2 = (bf16[8,3712]{1,0:T(8,128)(2,1)S(1)}, bf16[8,3712]{1,0:T(8,128)(2,1)S(1)}, u32[]{:S(2)}, u32[]{:S(2)}) collective-permute-start(bf16[8,3712]{1,0:T(8,128)(2,1)S(1)} %get-tuple-element.25), channel_id=1, source_target_pairs={{0,4},{4,0},{8,12},{12,8},{1,5},{5,1},{9,13},{13,9},{2,6},{6,2},{1... | collective-permute-start | bytes 178184 | tf_op jit(solution)/shard_map/ppermute | solution.py:190
  9.1 8.8 %collective-permute-start.5 = (bf16[16,3584]{1,0:T(8,128)(2,1)S(1)}, bf16[16,3584]{1,0:T(8,128)(2,1)S(1)}, u32[]{:S(2)}, u32[]{:S(2)}) collective-permute-start(bf16[16,3584]{1,0:T(8,128)(2,1)S(1)} %get-tuple-element.29.refs_0_), channel_id=1, source_target_pairs={{0,3},{1,2},{2,1},{3,0},{4,7},{5,6},{6,5},{7,4},{8,11},{9,10},{10,... | collective-permute-start | bytes 344072 | tf_op jit(solution)/shard_map/ppermute | solution.py:190
  12.9 9.6 %collective-permute-start.4 = (bf16[16,3584]{1,0:T(8,128)(2,1)S(1)}, bf16[16,3584]{1,0:T(8,128)(2,1)S(1)}, u32[]{:S(2)}, u32[]{:S(2)}) collective-permute-start(bf16[16,3584]{1,0:T(8,128)(2,1)S(1)} %get-tuple-element.29.refs_0_), channel_id=1, source_target_pairs={{0,2},{1,3},{2,0},{3,1},{4,6},{5,7},{6,4},{7,5},{8,10},{9,11},{10,... | collective-permute-start | bytes 344072 | tf_op jit(solution)/shard_map/ppermute | solution.py:190
  12.9 9.6 %collective-permute-start.3 = (bf16[16,3584]{1,0:T(8,128)(2,1)S(1)}, bf16[16,3584]{1,0:T(8,128)(2,1)S(1)}, u32[]{:S(2)}, u32[]{:S(2)}) collective-permute-start(bf16[16,3584]{1,0:T(8,128)(2,1)S(1)} %get-tuple-element.29.refs_0_), channel_id=1, source_target_pairs={{0,1},{1,0},{2,3},{3,2},{4,5},{5,4},{6,7},{7,6},{8,9},{9,8},{10,11... | collective-permute-start | bytes 344072 | tf_op jit(solution)/shard_map/ppermute | solution.py:190
  23.9 6.5 %collective-permute-start.8 = (bf16[64,512]{1,0:T(8,128)(2,1)S(1)}, bf16[64,512]{1,0:T(8,128)(2,1)S(1)}, u32[]{:S(2)}, u32[]{:S(2)}) collective-permute-start(bf16[64,512]{1,0:T(8,128)(2,1)S(1)} %hidden.1.refs_0_), channel_id=1, source_target_pairs={{0,3},{1,2},{2,1},{3,0},{4,7},{5,6},{6,5},{7,4},{8,11},{9,10},{10,... | collective-permute-start | bytes 196616 | tf_op jit(solution)/shard_map/ppermute | solution.py:190
  26.5 5.6 %collective-permute-start.7 = (bf16[64,512]{1,0:T(8,128)(2,1)S(1)}, bf16[64,512]{1,0:T(8,128)(2,1)S(1)}, u32[]{:S(2)}, u32[]{:S(2)}) collective-permute-start(bf16[64,512]{1,0:T(8,128)(2,1)S(1)} %hidden.1.refs_0_), channel_id=1, source_target_pairs={{0,2},{1,3},{2,0},{3,1},{4,6},{5,7},{6,4},{7,5},{8,10},{9,11},{10,... | collective-permute-start | bytes 196616 | tf_op jit(solution)/shard_map/ppermute | solution.py:190
  26.5 5.6 %collective-permute-start.6 = (bf16[64,512]{1,0:T(8,128)(2,1)S(1)}, bf16[64,512]{1,0:T(8,128)(2,1)S(1)}, u32[]{:S(2)}, u32[]{:S(2)}) collective-permute-start(bf16[64,512]{1,0:T(8,128)(2,1)S(1)} %hidden.1.refs_0_), channel_id=1, source_target_pairs={{0,1},{1,0},{2,3},{3,2},{4,5},{5,4},{6,7},{7,6},{8,9},{9,8},{10,11... | collective-permute-start | bytes 196616 | tf_op jit(solution)/shard_map/ppermute | solution.py:190
  32.8 5.7 %collective-permute-start.9 = (bf16[16,896]{1,0:T(8,128)(2,1)S(1)}, bf16[16,896]{1,0:T(8,128)(2,1)S(1)}, u32[]{:S(2)}, u32[]{:S(2)}) collective-permute-start(bf16[16,896]{1,0:T(8,128)(2,1)S(1)} %get-tuple-element.33), channel_id=1, source_target_pairs={{0,3},{1,2},{2,1},{3,0},{4,7},{5,6},{6,5},{7,4},{8,11},{9,10},{10,... | collective-permute-start | bytes 86024 | tf_op jit(solution)/shard_map/ppermute | solution.py:190
  34.9 4.8 %collective-permute-start.10 = (bf16[16,896]{1,0:T(8,128)(2,1)S(1)}, bf16[16,896]{1,0:T(8,128)(2,1)S(1)}, u32[]{:S(2)}, u32[]{:S(2)}) collective-permute-start(bf16[16,896]{1,0:T(8,128)(2,1)S(1)} %get-tuple-element.34), channel_id=1, source_target_pairs={{0,2},{1,3},{2,0},{3,1},{4,6},{5,7},{6,4},{7,5},{8,10},{9,11},{10,... | collective-permute-start | bytes 86024 | tf_op jit(solution)/shard_map/ppermute | solution.py:190
  34.9 4.8 %collective-permute-start.11 = (bf16[16,896]{1,0:T(8,128)(2,1)S(1)}, bf16[16,896]{1,0:T(8,128)(2,1)S(1)}, u32[]{:S(2)}, u32[]{:S(2)}) collective-permute-start(bf16[16,896]{1,0:T(8,128)(2,1)S(1)} %get-tuple-element.35), channel_id=1, source_target_pairs={{0,1},{1,0},{2,3},{3,2},{4,5},{5,4},{6,7},{7,6},{8,9},{9,8},{10,11... | collective-permute-start | bytes 86024 | tf_op jit(solution)/shard_map/ppermute | solution.py:190
  39.9 3.8 %collective-permute-start.12 = (bf16[4,8,896]{2,1,0:T(8,128)(2,1)S(1)}, bf16[4,8,896]{2,1,0:T(8,128)(2,1)S(1)}, u32[]{:S(2)}, u32[]{:S(2)}) collective-permute-start(bf16[4,8,896]{2,1,0:T(8,128)(2,1)S(1)} %get-tuple-element.37), channel_id=1, source_target_pairs={{0,12},{4,8},{8,4},{12,0},{1,13},{5,9},{9,5},{13,1},{2,14},{6,10},... | collective-permute-start | bytes 172040 | tf_op jit(solution)/shard_map/ppermute | solution.py:190
  39.9 4.9 %collective-permute-start.13 = (bf16[4,8,896]{2,1,0:T(8,128)(2,1)S(1)}, bf16[4,8,896]{2,1,0:T(8,128)(2,1)S(1)}, u32[]{:S(2)}, u32[]{:S(2)}) collective-permute-start(bf16[4,8,896]{2,1,0:T(8,128)(2,1)S(1)} %get-tuple-element.38), channel_id=1, source_target_pairs={{0,8},{4,12},{8,0},{12,4},{1,9},{5,13},{9,1},{13,5},{2,10},{6,14},... | collective-permute-start | bytes 172040 | tf_op jit(solution)/shard_map/ppermute | solution.py:190
  42.0 2.9 %collective-permute-start.14 = (bf16[4,8,896]{2,1,0:T(8,128)(2,1)S(1)}, bf16[4,8,896]{2,1,0:T(8,128)(2,1)S(1)}, u32[]{:S(2)}, u32[]{:S(2)}) collective-permute-start(bf16[4,8,896]{2,1,0:T(8,128)(2,1)S(1)} %get-tuple-element.39), channel_id=1, source_target_pairs={{0,4},{4,0},{8,12},{12,8},{1,5},{5,1},{9,13},{13,9},{2,6},{6,2},{1... | collective-permute-start | bytes 172040 | tf_op jit(solution)/shard_map/ppermute | solution.py:190

commit v6 on v5

--- a/solution.py
+++ b/solution.py
@@ -137,8 +137,8 @@
         hidden_ref[:, part] = (gate / (1.0 + jnp.exp(-gate)) * up).astype(BF16)
 
 
-def down_kernel(columns, *refs):
-    hiddens, down_ref, outs = refs[:columns], refs[columns], refs[columns + 1 :]
+def down_kernel(columns, shifts, *refs):
+    hiddens, down_ref, outs, total_ref = refs[:columns], refs[columns], refs[columns + 1 : -1], refs[-1]
     me = lax.axis_index("ing")
     rows, units = hiddens[0].shape
     slots = rows // columns
@@ -149,35 +149,38 @@
         )
         at = pl.multiple_of((me ^ f) * units, units)
         total += jnp.dot(block, down_ref[pl.ds(at, units), :], preferred_element_type=F32)
-    for e in range(columns):
-        outs[e][...] = total[e * slots : (e + 1) * slots].astype(BF16)
-
-
-def spread_kernel(groups, columns, pick_ref, *refs):
-    blocks, outs = refs[:columns][::-1], refs[columns:]
-    for e in range(columns):
-        block = blocks[e][...]
-        back = jnp.dot(pick_ref[:, : block.shape[0]], block, preferred_element_type=F32)
-        for d in range(groups):
-            outs[d][e] = back[d * CAP : (d + 1) * CAP].astype(BF16)
+    total_ref[...] = total
+    for shift, out in zip(shifts, outs):
+        other = jnp.clip(me + shift, 0, columns - 1)
+        out[...] = total_ref[pl.ds(pl.multiple_of((other ^ me) * slots, slots), slots), :].astype(BF16)
+
+
+def spread_kernel(groups, columns, shifts, pick_ref, *refs):
+    blocks, outs = refs[: len(shifts)], refs[len(shifts) :]
+    me = lax.axis_index("ing")
+    for (first, last, shift), block in zip(shifts, blocks):
+
+        @pl.when((me >= first) & (me <= last))
+        def _():
+            back = jnp.dot(pick_ref[:, : block.shape[0]], block[...], preferred_element_type=F32)
+            for d in range(groups):
+                outs[d][me - shift] = back[d * CAP : (d + 1) * CAP].astype(BF16)
 
 
 def combine_kernel(groups, columns, mixing_ref, *refs):
     backs, (out_ref, held, sems) = refs[:groups][::-1], refs[groups:]
-    me = lax.axis_index("ing")
     width, half = backs[0].shape[2], held.shape[0] // 2
     copies = []
     for e in range(columns):
         rows = jnp.concatenate([backs[d][e].astype(F32) for d in range(groups)], axis=0)
         rows = rows.astype(BF16)
         part = pl.ds(e * width, width)
-        there = pl.ds(pl.multiple_of((me ^ e) * width, width), width)
         for h in range(2):
             mine = pl.ds(h * half, half)
             value = jnp.dot(mixing_ref[mine, :], rows, preferred_element_type=F32)
             held[mine, part] = value.astype(BF16)
             copies.append(
-                pltpu.make_async_copy(held.at[mine, part], out_ref.at[mine, there], sems.at[2 * e + h])
+                pltpu.make_async_copy(held.at[mine, part], out_ref.at[mine, part], sems.at[2 * e + h])
             )
             copies[-1].start()
     for copy in copies:
@@ -264,29 +267,35 @@
     )(*blocks, gate, up)
     hiddens = [swap(hidden, "ing", f) for f in range(columns)]
 
+    moves = [(0, columns - 1 + s, s) for s in range(1 - columns, 0)]
+    moves += [(1, 1, 1)] + [(s, columns - 1, s) for s in range(2, columns)]
+    moves += [(2, columns - 1, 1), (0, columns - 1, 0)]
+    shifts = [s for _, _, s in moves]
     results = pl.pallas_call(
-        functools.partial(down_kernel, columns),
-        out_shape=[jax.ShapeDtypeStruct((slots, share), BF16)] * columns,
+        functools.partial(down_kernel, columns, shifts),
+        out_shape=[jax.ShapeDtypeStruct((slots, share), BF16)] * len(shifts),
         in_specs=[VMEM] * (columns + 1),
-        out_specs=[VMEM] * columns,
-        compiler_params=params(2 * columns * slots * (columns * units + 4 * share)),
+        out_specs=[VMEM] * len(shifts),
+        scratch_shapes=[pltpu.VMEM((columns * slots, share), F32)],
+        compiler_params=params(2 * columns * slots * (columns * units + 6 * share)),
         name="down",
     )(*hiddens, down)
-    results = swap_all(results, "ing")
-
+    returned = [
+        lax.ppermute(block, "ing", [(t - s, t) for t in range(first, last + 1)]) if s else block
+        for (first, last, s), block in zip(moves, results)
+    ]
     backs = pl.pallas_call(
-        functools.partial(spread_kernel, groups, columns),
+        functools.partial(spread_kernel, groups, columns, moves),
         out_shape=[jax.ShapeDtypeStruct((columns, CAP, share), BF16)] * groups,
-        in_specs=[VMEM] * (columns + 1),
+        in_specs=[VMEM] * (1 + len(moves)),
         out_specs=[VMEM] * groups,
-        compiler_params=params(2 * (groups * CAP + slots) * features),
+        compiler_params=params(2 * (groups * CAP + 2 * slots) * features),
         name="spread",
-    )(pick, *results)
+    )(pick, *returned)
     backs = swap_all(backs, "grp")
 
     if share % LANES:
-        me = lax.axis_index("ing")
-        rows = jnp.stack(backs[::-1])[:, jnp.arange(columns) ^ me]
+        rows = jnp.stack(backs[::-1])
         rows = rows.transpose(0, 2, 1, 3).reshape(groups * CAP, features)
         return jnp.dot(mixing, rows, preferred_element_type=F32).astype(BF16)
     return pl.pallas_call(

time: 46.6 us -> 55.4 us (1.19)
  starting transfers between devices: 18.7 us -> 28 us
  waiting for transfers between devices: 17.4 us -> 16.2 us
    ppermute x0 -> x7, starting transfers between devices: none -> 14 us  [local(): lax.ppermute(block, 'ing', [(t - s, t) for t in range(first, last + 1)])]
    ppermute x15 -> x12, starting transfers between devices: 18.7 us -> 14 us  [swap(): lax.ppermute(x, name, [(a, a ^ step) for a in range(lax.axis_size(name))])]
    ppermute x15 -> x12, waiting for transfers between devices: 17.4 us -> 15.4 us  [swap(): lax.ppermute(x, name, [(a, a ^ step) for a in range(lax.axis_size(name))])]
    ppermute x0 -> x7, waiting for transfers between devices: none -> 0.84 us  [local(): lax.ppermute(block, 'ing', [(t - s, t) for t in range(first, last + 1)])]
  transfers between devices with their start and end apart: 15 -> 19, of which waited for: 9 -> 8; matrix products, arithmetic and copies ran while one was open for 0% -> 0% of each run, Pallas kernels for 9% -> 8%
where the time goes in v6:
time: 55.4 us; the launch traced here: 55 us
  starting transfers between devices  28 us (51%)
  waiting for transfers between devices  16.2 us (29%)
  Pallas kernels  10.6 us (19%)
    ppermute x12, waiting for transfers between devices, swap(): lax.ppermute(x, name, [(a, a ^ step) for a in range(lax.axis_size(name))])  15.4 us
    ppermute x7, starting transfers between devices, local(): lax.ppermute(block, 'ing', [(t - s, t) for t in range(first, last + 1)])  14 us
    ppermute x12, starting transfers between devices, swap(): lax.ppermute(x, name, [(a, a ^ step) for a in range(lax.axis_size(name))])  14 us
    pallas_call x1, Pallas kernels, local(): pl.pallas_call(functools.partial(prepare_kernel, groups), out_shape=[pltp...  4.33 us
    pallas_call x1, Pallas kernels, local(): pl.pallas_call(functools.partial(dispatch_kernel, groups, features // 2),...  1.79 us
    pallas_call x1, Pallas kernels, local(): pl.pallas_call(functools.partial(combine_kernel, groups, columns), out_sh...  1.48 us
    pallas_call x1, Pallas kernels, local(): pl.pallas_call(functools.partial(hidden_kernel, columns), out_shape=jax.S...  1.4 us
  transfers between devices with their start and end apart: 19, of which 8 were waited for; matrix products, arithmetic and copies ran while one was open for 0% of the time, Pallas kernels for 8%

profile of v6, /device:TPU:0, one launch (start us, length us, event | category | flops | bytes accessed | tf_op | source)
XLA Modules:
  0.0 55.0 jit_solution(2739863502094390818)
XLA Ops:
  0.0 1.8 %dispatch.1 = (bf16[8,3712]{1,0:T(8,128)(2,1)S(1)}, bf16[8,3712]{1,0:T(8,128)(2,1)S(1)}, bf16[8,3712]{1,0:T(8,128)(2,1)S(1)}, bf16[8,3712]{1,0:T(8,128)(2,1)S(1)}) custom-call(s32[8,256]{1,0:T(8,128)} %bitcast.9, bf16[256,3584]{1,0:T(8,128)(2,1)} %tokens_ref.1), custom_call_target="tpu_custom_call" | custom-call | tf_op jit(solution)/shard_map/dispatch/pallas_call | solution.py:210
  1.8 2.4 %collective-permute-start = (bf16[8,3712]{1,0:T(8,128)(2,1)S(1)}, bf16[8,3712]{1,0:T(8,128)(2,1)S(1)}, u32[]{:S(2)}, u32[]{:S(2)}) collective-permute-start(bf16[8,3712]{1,0:T(8,128)(2,1)S(1)} %get-tuple-element.27), channel_id=1, source_target_pairs={{0,12},{4,8},{8,4},{12,0},{1,13},{5,9},{9,5},{13,1},{2,14},{6,10},... | collective-permute-start | bytes 178184 | tf_op jit(solution)/shard_map/ppermute | solution.py:193
  4.2 0.6 %collective-permute-start.1 = (bf16[8,3712]{1,0:T(8,128)(2,1)S(1)}, bf16[8,3712]{1,0:T(8,128)(2,1)S(1)}, u32[]{:S(2)}, u32[]{:S(2)}) collective-permute-start(bf16[8,3712]{1,0:T(8,128)(2,1)S(1)} %get-tuple-element.28), channel_id=1, source_target_pairs={{0,8},{4,12},{8,0},{12,4},{1,9},{5,13},{9,1},{13,5},{2,10},{6,14},... | collective-permute-start | bytes 178184 | tf_op jit(solution)/shard_map/ppermute | solution.py:193
  4.9 0.0 collective-permute-start.2
  4.9 1.7 %collective-permute-done.refs_0_ = bf16[8,3712]{1,0:T(8,128)(2,1)S(1)} collective-permute-done((bf16[8,3712]{1,0:T(8,128)(2,1)S(1)}, bf16[8,3712]{1,0:T(8,128)(2,1)S(1)}, u32[]{:S(2)}, u32[]{:S(2)}) %collective-permute-start) | collective-permute-done | bytes 59424 | tf_op jit(solution)/shard_map/ppermute | solution.py:193
  6.6 2.2 %collective-permute-done.1.refs_1_ = bf16[8,3712]{1,0:T(8,128)(2,1)S(1)} collective-permute-done((bf16[8,3712]{1,0:T(8,128)(2,1)S(1)}, bf16[8,3712]{1,0:T(8,128)(2,1)S(1)}, u32[]{:S(2)}, u32[]{:S(2)}) %collective-permute-start.1) | collective-permute-done | bytes 59424 | tf_op jit(solution)/shard_map/ppermute | solution.py:193
  8.8 0.3 compact.1
  9.1 3.7 %collective-permute-start.5 = (bf16[16,3584]{1,0:T(8,128)(2,1)S(1)}, bf16[16,3584]{1,0:T(8,128)(2,1)S(1)}, u32[]{:S(2)}, u32[]{:S(2)}) collective-permute-start(bf16[16,3584]{1,0:T(8,128)(2,1)S(1)} %get-tuple-element.33.refs_0_), channel_id=1, source_target_pairs={{0,3},{1,2},{2,1},{3,0},{4,7},{5,6},{6,5},{7,4},{8,11},{9,10},{10,... | collective-permute-start | bytes 344072 | tf_op jit(solution)/shard_map/ppermute | solution.py:193
  12.9 0.7 %collective-permute-start.3 = (bf16[16,3584]{1,0:T(8,128)(2,1)S(1)}, bf16[16,3584]{1,0:T(8,128)(2,1)S(1)}, u32[]{:S(2)}, u32[]{:S(2)}) collective-permute-start(bf16[16,3584]{1,0:T(8,128)(2,1)S(1)} %get-tuple-element.33.refs_0_), channel_id=1, source_target_pairs={{0,1},{1,0},{2,3},{3,2},{4,5},{5,4},{6,7},{7,6},{8,9},{9,8},{10,11... | collective-permute-start | bytes 344072 | tf_op jit(solution)/shard_map/ppermute | solution.py:193
  13.6 4.3 %prepare.1 = (bf16[3584,512]{1,0:T(8,128)(2,1)S(1)}, bf16[3584,512]{1,0:T(8,128)(2,1)S(1)}, bf16[2048,896]{1,0:T(8,128)(2,1)S(1)}, bf16[256,32]{1,0:T(8,128)(2,1)S(1)}) custom-call(bf16[32,128]{1,0:T(8,128)(2,1)S(1)} %get-tuple-element.31.after_ref.pick_ref, s32[8,256]{1,0:T(8,128)} %bitcast.10, f32[96,256]{1,0:T(8,128)} %bitcast.8, ...), custom_call_target="tpu_custom_call" | custom-call | tf_op jit(solution)/shard_map/prepare/pallas_call | solution.py:240
  17.9 4.6 %collective-permute-done.4.refs_2_ = bf16[16,3584]{1,0:T(8,128)(2,1)S(1)} collective-permute-done((bf16[16,3584]{1,0:T(8,128)(2,1)S(1)}, bf16[16,3584]{1,0:T(8,128)(2,1)S(1)}, u32[]{:S(2)}, u32[]{:S(2)}) %collective-permute-start.4) | collective-permute-done | bytes 114720 | tf_op jit(solution)/shard_map/ppermute | solution.py:193
  22.5 1.4 %hidden.1.refs_0_ = bf16[64,512]{1,0:T(8,128)(2,1)S(1)} custom-call(bf16[16,3584]{1,0:T(8,128)(2,1)S(1)} %get-tuple-element.33.refs_0_, bf16[16,3584]{1,0:T(8,128)(2,1)S(1)} %collective-permute-done.3.refs_1_, bf16[16,3584]{1,0:T(8,128)(2,1)S(1)} %collective-permute-done.4.refs_2_, bf16[16,3584]{1,0:T(8,128)(2,1)S(1)} %collective-permute-done.5.refs_3_, ...), custom_call_target="tpu_custom_call" | custom-call | tf_op jit(solution)/shard_map/hidden/pallas_call | solution.py:260
  23.9 2.5 %collective-permute-start.8 = (bf16[64,512]{1,0:T(8,128)(2,1)S(1)}, bf16[64,512]{1,0:T(8,128)(2,1)S(1)}, u32[]{:S(2)}, u32[]{:S(2)}) collective-permute-start(bf16[64,512]{1,0:T(8,128)(2,1)S(1)} %hidden.1.refs_0_), channel_id=1, source_target_pairs={{0,3},{1,2},{2,1},{3,0},{4,7},{5,6},{6,5},{7,4},{8,11},{9,10},{10,... | collective-permute-start | bytes 196616 | tf_op jit(solution)/shard_map/ppermute | solution.py:193
  26.5 1.9 %collective-permute-start.6 = (bf16[64,512]{1,0:T(8,128)(2,1)S(1)}, bf16[64,512]{1,0:T(8,128)(2,1)S(1)}, u32[]{:S(2)}, u32[]{:S(2)}) collective-permute-start(bf16[64,512]{1,0:T(8,128)(2,1)S(1)} %hidden.1.refs_0_), channel_id=1, source_target_pairs={{0,1},{1,0},{2,3},{3,2},{4,5},{5,4},{6,7},{7,6},{8,9},{9,8},{10,11... | collective-permute-start | bytes 196616 | tf_op jit(solution)/shard_map/ppermute | solution.py:193
  28.4 2.0 %collective-permute-done.8.refs_3_ = bf16[64,512]{1,0:T(8,128)(2,1)S(1)} collective-permute-done((bf16[64,512]{1,0:T(8,128)(2,1)S(1)}, bf16[64,512]{1,0:T(8,128)(2,1)S(1)}, u32[]{:S(2)}, u32[]{:S(2)}) %collective-permute-start.8) | collective-permute-done | bytes 65568 | tf_op jit(solution)/shard_map/ppermute | solution.py:193
  30.4 1.7 %collective-permute-done.7.refs_2_ = bf16[64,512]{1,0:T(8,128)(2,1)S(1)} collective-permute-done((bf16[64,512]{1,0:T(8,128)(2,1)S(1)}, bf16[64,512]{1,0:T(8,128)(2,1)S(1)}, u32[]{:S(2)}, u32[]{:S(2)}) %collective-permute-start.7) | collective-permute-done | bytes 65568 | tf_op jit(solution)/shard_map/ppermute | solution.py:193
  32.1 0.8 %down.1 = (bf16[16,896]{1,0:T(8,128)(2,1)S(1)}, bf16[16,896]{1,0:T(8,128)(2,1)S(1)}, bf16[16,896]{1,0:T(8,128)(2,1)S(1)}, bf16[16,896]{1,0:T(8,128)(2,1)S(1)}, b...) custom-call(bf16[64,512]{1,0:T(8,128)(2,1)S(1)} %hidden.1.refs_0_, ...), custom_call_target="tpu_custom_call" | custom-call | tf_op jit(solution)/shard_map/down/pallas_call | solution.py:274
  32.8 1.3 %collective-permute-start.9 = (bf16[16,896]{1,0:T(8,128)(2,1)S(1)}, bf16[16,896]{1,0:T(8,128)(2,1)S(1)}, u32[]{:S(2)}, u32[]{:S(2)}) collective-permute-start(bf16[16,896]{1,0:T(8,128)(2,1)S(1)} %get-tuple-element.37), channel_id=1, source_target_pairs={{3,0},{7,4},{11,8},{15,12},{19,16},{23,20},{27,24},{31,28}} | collective-permute-start | bytes 86024 | tf_op jit(solution)/shard_map/ppermute | solution.py:284
  34.1 1.3 %collective-permute-start.10 = (bf16[16,896]{1,0:T(8,128)(2,1)S(1)}, bf16[16,896]{1,0:T(8,128)(2,1)S(1)}, u32[]{:S(2)}, u32[]{:S(2)}) collective-permute-start(bf16[16,896]{1,0:T(8,128)(2,1)S(1)} %get-tuple-element.38), channel_id=1, source_target_pairs={{2,0},{3,1},{6,4},{7,5},{10,8},{11,9},{14,12},{15,13},{18,16},{19,... | collective-permute-start | bytes 86024 | tf_op jit(solution)/shard_map/ppermute | solution.py:284
  35.4 1.3 %collective-permute-start.11 = (bf16[16,896]{1,0:T(8,128)(2,1)S(1)}, bf16[16,896]{1,0:T(8,128)(2,1)S(1)}, u32[]{:S(2)}, u32[]{:S(2)}) collective-permute-start(bf16[16,896]{1,0:T(8,128)(2,1)S(1)} %get-tuple-element.39), channel_id=1, source_target_pairs={{1,0},{2,1},{3,2},{5,4},{6,5},{7,6},{9,8},{10,9},{11,10},{13,12},{... | collective-permute-start | bytes 86024 | tf_op jit(solution)/shard_map/ppermute | solution.py:284
  36.7 4.5 %collective-permute-start.12 = (bf16[16,896]{1,0:T(8,128)(2,1)S(1)}, bf16[16,896]{1,0:T(8,128)(2,1)S(1)}, u32[]{:S(2)}, u32[]{:S(2)}) collective-permute-start(bf16[16,896]{1,0:T(8,128)(2,1)S(1)} %get-tuple-element.40), channel_id=1, source_target_pairs={{0,1},{4,5},{8,9},{12,13},{16,17},{20,21},{24,25},{28,29}} | collective-permute-start | bytes 86024 | tf_op jit(solution)/shard_map/ppermute | solution.py:284
  41.3 2.2 %collective-permute-start.13 = (bf16[16,896]{1,0:T(8,128)(2,1)S(1)}, bf16[16,896]{1,0:T(8,128)(2,1)S(1)}, u32[]{:S(2)}, u32[]{:S(2)}) collective-permute-start(bf16[16,896]{1,0:T(8,128)(2,1)S(1)} %get-tuple-element.41), channel_id=1, source_target_pairs={{0,2},{1,3},{4,6},{5,7},{8,10},{9,11},{12,14},{13,15},{16,18},{17,... | collective-permute-start | bytes 86024 | tf_op jit(solution)/shard_map/ppermute | solution.py:284
  43.5 2.7 %collective-permute-start.14 = (bf16[16,896]{1,0:T(8,128)(2,1)S(1)}, bf16[16,896]{1,0:T(8,128)(2,1)S(1)}, u32[]{:S(2)}, u32[]{:S(2)}) collective-permute-start(bf16[16,896]{1,0:T(8,128)(2,1)S(1)} %get-tuple-element.42), channel_id=1, source_target_pairs={{0,3},{4,7},{8,11},{12,15},{16,19},{20,23},{24,27},{28,31}} | collective-permute-start | bytes 86024 | tf_op jit(solution)/shard_map/ppermute | solution.py:284
  46.2 0.7 %collective-permute-start.15 = (bf16[16,896]{1,0:T(8,128)(2,1)S(1)}, bf16[16,896]{1,0:T(8,128)(2,1)S(1)}, u32[]{:S(2)}, u32[]{:S(2)}) collective-permute-start(bf16[16,896]{1,0:T(8,128)(2,1)S(1)} %get-tuple-element.43), channel_id=1, source_target_pairs={{1,2},{2,3},{5,6},{6,7},{9,10},{10,11},{13,14},{14,15},{17,18},{18... | collective-permute-start | bytes 86024 | tf_op jit(solution)/shard_map/ppermute | solution.py:284
  47.0 0.8 %collective-permute-done.14.refs_5_ = bf16[16,896]{1,0:T(8,128)(2,1)S(1)} collective-permute-done((bf16[16,896]{1,0:T(8,128)(2,1)S(1)}, bf16[16,896]{1,0:T(8,128)(2,1)S(1)}, u32[]{:S(2)}, u32[]{:S(2)}) %collective-permute-start.14) | collective-permute-done | bytes 28704 | tf_op jit(solution)/shard_map/ppermute | solution.py:284
  47.8 0.5 spread.1
  48.3 0.1 collective-permute-start.16
  48.4 1.8 %collective-permute-start.17 = (bf16[4,8,896]{2,1,0:T(8,128)(2,1)S(1)}, bf16[4,8,896]{2,1,0:T(8,128)(2,1)S(1)}, u32[]{:S(2)}, u32[]{:S(2)}) collective-permute-start(bf16[4,8,896]{2,1,0:T(8,128)(2,1)S(1)} %get-tuple-element.46), channel_id=1, source_target_pairs={{0,8},{4,12},{8,0},{12,4},{1,9},{5,13},{9,1},{13,5},{2,10},{6,14},... | collective-permute-start | bytes 172040 | tf_op jit(solution)/shard_map/ppermute | solution.py:193
  50.3 0.1 collective-permute-start.18
  50.3 2.0 %collective-permute-done.16.refs_0_ = bf16[4,8,896]{2,1,0:T(8,128)(2,1)S(1)} collective-permute-done((bf16[4,8,896]{2,1,0:T(8,128)(2,1)S(1)}, bf16[4,8,896]{2,1,0:T(8,128)(2,1)S(1)}, u32[]{:S(2)}, u32[]{:S(2)}) %collective-permute-start.16) | collective-permute-done | bytes 57376 | tf_op jit(solution)/shard_map/ppermute | solution.py:193
  52.3 1.3 %collective-permute-done.17.refs_1_ = bf16[4,8,896]{2,1,0:T(8,128)(2,1)S(1)} collective-permute-done((bf16[4,8,896]{2,1,0:T(8,128)(2,1)S(1)}, bf16[4,8,896]{2,1,0:T(8,128)(2,1)S(1)}, u32[]{:S(2)}, u32[]{:S(2)}) %collective-permute-start.17) | collective-permute-done | bytes 57376 | tf_op jit(solution)/shard_map/ppermute | solution.py:193
  53.5 1.5 %combine.1 = bf16[256,3584]{1,0:T(8,128)(2,1)} custom-call(bf16[256,32]{1,0:T(8,128)(2,1)S(1)} %get-tuple-element.32.mixing_ref, bf16[4,8,896]{2,1,0:T(8,128)(2,1)S(1)} %collective-permute-done.16.refs_0_, bf16[4,8,896]{2,1,0:T(8,128)(2,1)S(1)} %collective-permute-done.17.refs_1_, bf16[4,8,896]{2,1,0:T(8,128)(2,1)S(1)} %collective-permute-done.18.refs_2_, ...), custom_call_target="tpu_custom_call" | custom-call | tf_op jit(solution)/shard_map/combine/pallas_call | solution.py:301
  (13 shorter events, 0.0 us)
Async XLA Ops:
  1.8 4.8 %collective-permute-start = (bf16[8,3712]{1,0:T(8,128)(2,1)S(1)}, bf16[8,3712]{1,0:T(8,128)(2,1)S(1)}, u32[]{:S(2)}, u32[]{:S(2)}) collective-permute-start(bf16[8,3712]{1,0:T(8,128)(2,1)S(1)} %get-tuple-element.27), channel_id=1, source_target_pairs={{0,12},{4,8},{8,4},{12,0},{1,13},{5,9},{9,5},{13,1},{2,14},{6,10},... | collective-permute-start | bytes 178184 | tf_op jit(solution)/shard_map/ppermute | solution.py:193
  4.2 4.5 %collective-permute-start.1 = (bf16[8,3712]{1,0:T(8,128)(2,1)S(1)}, bf16[8,3712]{1,0:T(8,128)(2,1)S(1)}, u32[]{:S(2)}, u32[]{:S(2)}) collective-permute-start(bf16[8,3712]{1,0:T(8,128)(2,1)S(1)} %get-tuple-element.28), channel_id=1, source_target_pairs={{0,8},{4,12},{8,0},{12,4},{1,9},{5,13},{9,1},{13,5},{2,10},{6,14},... | collective-permute-start | bytes 178184 | tf_op jit(solution)/shard_map/ppermute | solution.py:193
  4.9 3.9 %collective-permute-start.2 = (bf16[8,3712]{1,0:T(8,128)(2,1)S(1)}, bf16[8,3712]{1,0:T(8,128)(2,1)S(1)}, u32[]{:S(2)}, u32[]{:S(2)}) collective-permute-start(bf16[8,3712]{1,0:T(8,128)(2,1)S(1)} %get-tuple-element.29), channel_id=1, source_target_pairs={{0,4},{4,0},{8,12},{12,8},{1,5},{5,1},{9,13},{13,9},{2,6},{6,2},{1... | collective-permute-start | bytes 178184 | tf_op jit(solution)/shard_map/ppermute | solution.py:193
  9.1 8.8 %collective-permute-start.5 = (bf16[16,3584]{1,0:T(8,128)(2,1)S(1)}, bf16[16,3584]{1,0:T(8,128)(2,1)S(1)}, u32[]{:S(2)}, u32[]{:S(2)}) collective-permute-start(bf16[16,3584]{1,0:T(8,128)(2,1)S(1)} %get-tuple-element.33.refs_0_), channel_id=1, source_target_pairs={{0,3},{1,2},{2,1},{3,0},{4,7},{5,6},{6,5},{7,4},{8,11},{9,10},{10,... | collective-permute-start | bytes 344072 | tf_op jit(solution)/shard_map/ppermute | solution.py:193
  12.9 9.6 %collective-permute-start.4 = (bf16[16,3584]{1,0:T(8,128)(2,1)S(1)}, bf16[16,3584]{1,0:T(8,128)(2,1)S(1)}, u32[]{:S(2)}, u32[]{:S(2)}) collective-permute-start(bf16[16,3584]{1,0:T(8,128)(2,1)S(1)} %get-tuple-element.33.refs_0_), channel_id=1, source_target_pairs={{0,2},{1,3},{2,0},{3,1},{4,6},{5,7},{6,4},{7,5},{8,10},{9,11},{10,... | collective-permute-start | bytes 344072 | tf_op jit(solution)/shard_map/ppermute | solution.py:193
  12.9 9.6 %collective-permute-start.3 = (bf16[16,3584]{1,0:T(8,128)(2,1)S(1)}, bf16[16,3584]{1,0:T(8,128)(2,1)S(1)}, u32[]{:S(2)}, u32[]{:S(2)}) collective-permute-start(bf16[16,3584]{1,0:T(8,128)(2,1)S(1)} %get-tuple-element.33.refs_0_), channel_id=1, source_target_pairs={{0,1},{1,0},{2,3},{3,2},{4,5},{5,4},{6,7},{7,6},{8,9},{9,8},{10,11... | collective-permute-start | bytes 344072 | tf_op jit(solution)/shard_map/ppermute | solution.py:193
  23.9 6.5 %collective-permute-start.8 = (bf16[64,512]{1,0:T(8,128)(2,1)S(1)}, bf16[64,512]{1,0:T(8,128)(2,1)S(1)}, u32[]{:S(2)}, u32[]{:S(2)}) collective-permute-start(bf16[64,512]{1,0:T(8,128)(2,1)S(1)} %hidden.1.refs_0_), channel_id=1, source_target_pairs={{0,3},{1,2},{2,1},{3,0},{4,7},{5,6},{6,5},{7,4},{8,11},{9,10},{10,... | collective-permute-start | bytes 196616 | tf_op jit(solution)/shard_map/ppermute | solution.py:193
  26.5 5.6 %collective-permute-start.7 = (bf16[64,512]{1,0:T(8,128)(2,1)S(1)}, bf16[64,512]{1,0:T(8,128)(2,1)S(1)}, u32[]{:S(2)}, u32[]{:S(2)}) collective-permute-start(bf16[64,512]{1,0:T(8,128)(2,1)S(1)} %hidden.1.refs_0_), channel_id=1, source_target_pairs={{0,2},{1,3},{2,0},{3,1},{4,6},{5,7},{6,4},{7,5},{8,10},{9,11},{10,... | collective-permute-start | bytes 196616 | tf_op jit(solution)/shard_map/ppermute | solution.py:193
  26.5 5.6 %collective-permute-start.6 = (bf16[64,512]{1,0:T(8,128)(2,1)S(1)}, bf16[64,512]{1,0:T(8,128)(2,1)S(1)}, u32[]{:S(2)}, u32[]{:S(2)}) collective-permute-start(bf16[64,512]{1,0:T(8,128)(2,1)S(1)} %hidden.1.refs_0_), channel_id=1, source_target_pairs={{0,1},{1,0},{2,3},{3,2},{4,5},{5,4},{6,7},{7,6},{8,9},{9,8},{10,11... | collective-permute-start | bytes 196616 | tf_op jit(solution)/shard_map/ppermute | solution.py:193
  32.8 10.7 %collective-permute-start.9 = (bf16[16,896]{1,0:T(8,128)(2,1)S(1)}, bf16[16,896]{1,0:T(8,128)(2,1)S(1)}, u32[]{:S(2)}, u32[]{:S(2)}) collective-permute-start(bf16[16,896]{1,0:T(8,128)(2,1)S(1)} %get-tuple-element.37), channel_id=1, source_target_pairs={{3,0},{7,4},{11,8},{15,12},{19,16},{23,20},{27,24},{31,28}} | collective-permute-start | bytes 86024 | tf_op jit(solution)/shard_map/ppermute | solution.py:284
  34.1 12.1 %collective-permute-start.10 = (bf16[16,896]{1,0:T(8,128)(2,1)S(1)}, bf16[16,896]{1,0:T(8,128)(2,1)S(1)}, u32[]{:S(2)}, u32[]{:S(2)}) collective-permute-start(bf16[16,896]{1,0:T(8,128)(2,1)S(1)} %get-tuple-element.38), channel_id=1, source_target_pairs={{2,0},{3,1},{6,4},{7,5},{10,8},{11,9},{14,12},{15,13},{18,16},{19,... | collective-permute-start | bytes 86024 | tf_op jit(solution)/shard_map/ppermute | solution.py:284
  35.4 11.5 %collective-permute-start.11 = (bf16[16,896]{1,0:T(8,128)(2,1)S(1)}, bf16[16,896]{1,0:T(8,128)(2,1)S(1)}, u32[]{:S(2)}, u32[]{:S(2)}) collective-permute-start(bf16[16,896]{1,0:T(8,128)(2,1)S(1)} %get-tuple-element.39), channel_id=1, source_target_pairs={{1,0},{2,1},{3,2},{5,4},{6,5},{7,6},{9,8},{10,9},{11,10},{13,12},{... | collective-permute-start | bytes 86024 | tf_op jit(solution)/shard_map/ppermute | solution.py:284
  36.7 10.2 %collective-permute-start.12 = (bf16[16,896]{1,0:T(8,128)(2,1)S(1)}, bf16[16,896]{1,0:T(8,128)(2,1)S(1)}, u32[]{:S(2)}, u32[]{:S(2)}) collective-permute-start(bf16[16,896]{1,0:T(8,128)(2,1)S(1)} %get-tuple-element.40), channel_id=1, source_target_pairs={{0,1},{4,5},{8,9},{12,13},{16,17},{20,21},{24,25},{28,29}} | collective-permute-start | bytes 86024 | tf_op jit(solution)/shard_map/ppermute | solution.py:284
  41.3 5.7 %collective-permute-start.13 = (bf16[16,896]{1,0:T(8,128)(2,1)S(1)}, bf16[16,896]{1,0:T(8,128)(2,1)S(1)}, u32[]{:S(2)}, u32[]{:S(2)}) collective-permute-start(bf16[16,896]{1,0:T(8,128)(2,1)S(1)} %get-tuple-element.41), channel_id=1, source_target_pairs={{0,2},{1,3},{4,6},{5,7},{8,10},{9,11},{12,14},{13,15},{16,18},{17,... | collective-permute-start | bytes 86024 | tf_op jit(solution)/shard_map/ppermute | solution.py:284
  43.5 4.3 %collective-permute-start.14 = (bf16[16,896]{1,0:T(8,128)(2,1)S(1)}, bf16[16,896]{1,0:T(8,128)(2,1)S(1)}, u32[]{:S(2)}, u32[]{:S(2)}) collective-permute-start(bf16[16,896]{1,0:T(8,128)(2,1)S(1)} %get-tuple-element.42), channel_id=1, source_target_pairs={{0,3},{4,7},{8,11},{12,15},{16,19},{20,23},{24,27},{28,31}} | collective-permute-start | bytes 86024 | tf_op jit(solution)/shard_map/ppermute | solution.py:284
  46.2 1.5 %collective-permute-start.15 = (bf16[16,896]{1,0:T(8,128)(2,1)S(1)}, bf16[16,896]{1,0:T(8,128)(2,1)S(1)}, u32[]{:S(2)}, u32[]{:S(2)}) collective-permute-start(bf16[16,896]{1,0:T(8,128)(2,1)S(1)} %get-tuple-element.43), channel_id=1, source_target_pairs={{1,2},{2,3},{5,6},{6,7},{9,10},{10,11},{13,14},{14,15},{17,18},{18... | collective-permute-start | bytes 86024 | tf_op jit(solution)/shard_map/ppermute | solution.py:284
  48.3 3.9 %collective-permute-start.16 = (bf16[4,8,896]{2,1,0:T(8,128)(2,1)S(1)}, bf16[4,8,896]{2,1,0:T(8,128)(2,1)S(1)}, u32[]{:S(2)}, u32[]{:S(2)}) collective-permute-start(bf16[4,8,896]{2,1,0:T(8,128)(2,1)S(1)} %get-tuple-element.45), channel_id=1, source_target_pairs={{0,12},{4,8},{8,4},{12,0},{1,13},{5,9},{9,5},{13,1},{2,14},{6,10},... | collective-permute-start | bytes 172040 | tf_op jit(solution)/shard_map/ppermute | solution.py:193
  48.4 5.1 %collective-permute-start.17 = (bf16[4,8,896]{2,1,0:T(8,128)(2,1)S(1)}, bf16[4,8,896]{2,1,0:T(8,128)(2,1)S(1)}, u32[]{:S(2)}, u32[]{:S(2)}) collective-permute-start(bf16[4,8,896]{2,1,0:T(8,128)(2,1)S(1)} %get-tuple-element.46), channel_id=1, source_target_pairs={{0,8},{4,12},{8,0},{12,4},{1,9},{5,13},{9,1},{13,5},{2,10},{6,14},... | collective-permute-start | bytes 172040 | tf_op jit(solution)/shard_map/ppermute | solution.py:193
  50.3 3.3 %collective-permute-start.18 = (bf16[4,8,896]{2,1,0:T(8,128)(2,1)S(1)}, bf16[4,8,896]{2,1,0:T(8,128)(2,1)S(1)}, u32[]{:S(2)}, u32[]{:S(2)}) collective-permute-start(bf16[4,8,896]{2,1,0:T(8,128)(2,1)S(1)} %get-tuple-element.47), channel_id=1, source_target_pairs={{0,4},{4,0},{8,12},{12,8},{1,5},{5,1},{9,13},{13,9},{2,6},{6,2},{1... | collective-permute-start | bytes 172040 | tf_op jit(solution)/shard_map/ppermute | solution.py:193

commit v7 on v4

--- a/solution.py
+++ b/solution.py
@@ -142,37 +142,19 @@
             high_ref[:, c * step - half : (c + 1) * step - half] = moved
 
 
-def hidden_kernel(columns, forwarded, *refs):
-    if forwarded:
-        low, high, near, own, middle, far_low, far_high = refs[:7]
-    blocks, (gate_ref, up_ref, hidden_ref, held) = refs[:-4], refs[-4:]
-    slots = held.shape[0] // columns
-    features, units = gate_ref.shape
-    if forwarded:
-        half = features // 2
-        me = lax.axis_index("ing")
-        held[:slots, :] = own[...]
-        held[slots : 2 * slots, :] = near[...]
-        held[2 * slots : 3 * slots, :half] = low[...]
-        held[2 * slots : 3 * slots, half:] = high[...]
-        inner = (me == 1) | (me == 2)
-
-        @pl.when(inner)
-        def _():
-            held[3 * slots :, :] = middle[...]
-
-        @pl.when(jnp.logical_not(inner))
-        def _():
-            held[3 * slots :, :half] = far_low[...]
-            held[3 * slots :, half:] = far_high[...]
-    else:
-        for e in range(columns):
-            held[e * slots : (e + 1) * slots, :] = blocks[e][...]
+def hidden_kernel(columns, halved, *refs):
+    blocks, (gate_ref, up_ref, hidden_ref) = refs[:-3], refs[-3:]
+    units = gate_ref.shape[1]
+    blocks = [block[...] for block in blocks]
+    if halved:
+        low, high, near, own, far_low, far_high = blocks
+        blocks = [own, near, jnp.concatenate([low, high], axis=1), jnp.concatenate([far_low, far_high], axis=1)]
+    rows = jnp.concatenate(blocks, axis=0)
     step = min(256, units)
     for c in range(units // step):
         part = slice(c * step, (c + 1) * step)
-        gate = jnp.dot(held[...], gate_ref[:, part], preferred_element_type=F32)
-        up = jnp.dot(held[...], up_ref[:, part], preferred_element_type=F32)
+        gate = jnp.dot(rows, gate_ref[:, part], preferred_element_type=F32)
+        up = jnp.dot(rows, up_ref[:, part], preferred_element_type=F32)
         hidden_ref[:, part] = (gate / (1.0 + jnp.exp(-gate)) * up).astype(BF16)
 
 
@@ -204,16 +186,21 @@
 def combine_kernel(groups, columns, mixing_ref, *refs):
     backs, (out_ref, held, sems) = refs[:groups][::-1], refs[groups:]
     me = lax.axis_index("ing")
-    width = backs[0].shape[2]
+    width, half = backs[0].shape[2], held.shape[0] // 2
     copies = []
     for e in range(columns):
         rows = jnp.concatenate([backs[d][e].astype(F32) for d in range(groups)], axis=0)
-        value = jnp.dot(mixing_ref[...], rows.astype(BF16), preferred_element_type=F32)
+        rows = rows.astype(BF16)
         part = pl.ds(e * width, width)
-        held[:, part] = value.astype(BF16)
         there = pl.ds(pl.multiple_of((me ^ e) * width, width), width)
-        copies.append(pltpu.make_async_copy(held.at[:, part], out_ref.at[:, there], sems.at[e]))
-        copies[-1].start()
+        for h in range(2):
+            mine = pl.ds(h * half, half)
+            value = jnp.dot(mixing_ref[mine, :], rows, preferred_element_type=F32)
+            held[mine, part] = value.astype(BF16)
+            copies.append(
+                pltpu.make_async_copy(held.at[mine, part], out_ref.at[mine, there], sems.at[2 * e + h])
+            )
+            copies[-1].start()
     for copy in copies:
         copy.wait()
 
@@ -239,7 +226,7 @@
     logits = pltpu.with_memory_space_constraint(router_logits.T, pltpu.HBM)
 
     outbound = pl.pallas_call(
-        functools.partial(dispatch_kernel, groups, 512),
+        functools.partial(dispatch_kernel, groups, features // 2),
         out_shape=[jax.ShapeDtypeStruct((CAP, wide), BF16)] * groups,
         in_specs=[ANY, ANY],
         out_specs=[VMEM] * groups,
@@ -247,7 +234,7 @@
             pltpu.VMEM(ids.shape, jnp.int32),
             pltpu.VMEM((count, features), BF16),
             pltpu.VMEM((count, count), BF16),
-            pltpu.SemaphoreType.DMA((features // 512 + 1,)),
+            pltpu.SemaphoreType.DMA((3,)),
         ],
         compiler_params=params(2 * count * features),
         name="dispatch",
@@ -282,11 +269,7 @@
     if columns == 4:
         low, high = swap(low, "ing", 2), swap(high, "ing", 2)
         near = swap(compacted, "ing", 1)
-        outward = [(1, 0), (2, 3)]
-        far_low = lax.ppermute(low, "ing", outward)
-        middle = lax.ppermute(compacted, "ing", [(1, 2), (2, 1)])
-        far_high = lax.ppermute(high, "ing", outward)
-        blocks = [low, high, near, compacted, middle, far_low, far_high]
+        blocks = [low, high, near, compacted, swap(low, "ing", 1), swap(high, "ing", 1)]
     else:
         blocks = [swap(compacted, "ing", e) for e in range(columns)]
 
@@ -295,7 +278,6 @@
         out_shape=jax.ShapeDtypeStruct((columns * slots, units), BF16),
         in_specs=[VMEM] * (len(blocks) + 2),
         out_specs=VMEM,
-        scratch_shapes=[pltpu.VMEM((columns * slots, features), BF16)],
         compiler_params=params(2 * columns * slots * (2 * features + units)),
         name="hidden",
     )(*blocks, gate, up)
@@ -347,7 +329,7 @@
         out_shape=jax.ShapeDtypeStruct((count, features), BF16),
         in_specs=[VMEM] * (1 + groups),
         out_specs=ANY,
-        scratch_shapes=[pltpu.VMEM((count, features), BF16), pltpu.SemaphoreType.DMA((columns,))],
+        scratch_shapes=[pltpu.VMEM((count, features), BF16), pltpu.SemaphoreType.DMA((2 * columns,))],
         compiler_params=params(2 * (count + groups * CAP) * features),
         name="combine",
     )(mixing, *backs)

time: 49.7 us -> 47.6 us (0.958)
  starting transfers between devices: 24.7 us -> 22.2 us
  waiting for transfers between devices: 13 us -> 13.9 us
    ppermute x15 -> x17, waiting for transfers between devices: 8.19 us -> 13.9 us  [swap(): lax.ppermute(x, name, [(a, a ^ step) for a in range(lax.axis_size(name))])]
    ppermute x3 -> x0, waiting for transfers between devices: 4.77 us -> none  [the longest x1 3.46 us: local(): far_low = lax.ppermute(low, 'ing', outward)]
    ppermute x3 -> x0, starting transfers between devices: 3.23 us -> none  [the longest x1 1.29 us: local(): far_high = lax.ppermute(high, 'ing', outward)]
    ppermute x15 -> x17, starting transfers between devices: 21.5 us -> 22.2 us  [swap(): lax.ppermute(x, name, [(a, a ^ step) for a in range(lax.axis_size(name))])]
  transfers between devices with their start and end apart: 18 -> 17, of which waited for: 8 -> 10; matrix products, arithmetic and copies ran while one was open for 0% -> 0% of each run, Pallas kernels for 11% -> 11%
where the time goes in v7:
time: 47.6 us; the launch traced here: 47.4 us
  starting transfers between devices  22.2 us (47%)
  waiting for transfers between devices  13.9 us (29%)
  Pallas kernels  11.2 us (24%)
    ppermute x17, starting transfers between devices, swap(): lax.ppermute(x, name, [(a, a ^ step) for a in range(lax.axis_size(name))])  22.2 us
    ppermute x17, waiting for transfers between devices, swap(): lax.ppermute(x, name, [(a, a ^ step) for a in range(lax.axis_size(name))])  13.9 us
    pallas_call x1, Pallas kernels, local(): pl.pallas_call(load_kernel, out_shape=[pltpu.VMEM(w.shape, BF16) for w in...  3.17 us
    pallas_call x1, Pallas kernels, local(): pl.pallas_call(functools.partial(prepare_kernel, groups), out_shape=[pltp...  2.13 us
    pallas_call x1, Pallas kernels, local(): pl.pallas_call(functools.partial(dispatch_kernel, groups, features // 2),...  1.79 us
    pallas_call x1, Pallas kernels, local(): pl.pallas_call(functools.partial(combine_kernel, groups, columns), out_sh...  1.49 us
    pallas_call x1, Pallas kernels, local(): pl.pallas_call(functools.partial(hidden_kernel, columns, columns == 4), o...  1.4 us
  transfers between devices with their start and end apart: 17, of which 10 were waited for; matrix products, arithmetic and copies ran while one was open for 0% of the time, Pallas kernels for 11%

profile of v7, /device:TPU:0, one launch (start us, length us, event | category | flops | bytes accessed | tf_op | source)
XLA Modules:
  0.0 47.4 jit_solution(17263755684754400432)
XLA Ops:
  0.0 1.8 %dispatch.1 = (bf16[8,3712]{1,0:T(8,128)(2,1)S(1)}, bf16[8,3712]{1,0:T(8,128)(2,1)S(1)}, bf16[8,3712]{1,0:T(8,128)(2,1)S(1)}, bf16[8,3712]{1,0:T(8,128)(2,1)S(1)}) custom-call(s32[8,256]{1,0:T(8,128)} %bitcast.9, bf16[256,3584]{1,0:T(8,128)(2,1)} %tokens_ref.1), custom_call_target="tpu_custom_call" | custom-call | tf_op jit(solution)/shard_map/dispatch/pallas_call | solution.py:228
  1.8 2.4 %collective-permute-start = (bf16[8,3712]{1,0:T(8,128)(2,1)S(1)}, bf16[8,3712]{1,0:T(8,128)(2,1)S(1)}, u32[]{:S(2)}, u32[]{:S(2)}) collective-permute-start(bf16[8,3712]{1,0:T(8,128)(2,1)S(1)} %get-tuple-element.27), channel_id=1, source_target_pairs={{0,12},{4,8},{8,4},{12,0},{1,13},{5,9},{9,5},{13,1},{2,14},{6,10},... | collective-permute-start | bytes 178184 | tf_op jit(solution)/shard_map/ppermute | solution.py:211
  4.2 0.6 %collective-permute-start.1 = (bf16[8,3712]{1,0:T(8,128)(2,1)S(1)}, bf16[8,3712]{1,0:T(8,128)(2,1)S(1)}, u32[]{:S(2)}, u32[]{:S(2)}) collective-permute-start(bf16[8,3712]{1,0:T(8,128)(2,1)S(1)} %get-tuple-element.28), channel_id=1, source_target_pairs={{0,8},{4,12},{8,0},{12,4},{1,9},{5,13},{9,1},{13,5},{2,10},{6,14},... | collective-permute-start | bytes 178184 | tf_op jit(solution)/shard_map/ppermute | solution.py:211
  4.9 3.2 %load.1 = (bf16[3584,512]{1,0:T(8,128)(2,1)S(1)}, bf16[3584,512]{1,0:T(8,128)(2,1)S(1)}) custom-call(bf16[8,3712]{1,0:T(8,128)(2,1)S(1)} %get-tuple-element.25.after_ref.refs_3_, bf16[3584,512]{1,0:T(8,128)(2,1)} %bitcast.5, bf16[3584,512]{1,0:T(8,128)(2,1)} %bitcast.6), custom_call_target="tpu_custom_call" | custom-call | tf_op jit(solution)/shard_map/load/pallas_call | solution.py:246
  8.1 0.7 %collective-permute-done.1.refs_1_ = bf16[8,3712]{1,0:T(8,128)(2,1)S(1)} collective-permute-done((bf16[8,3712]{1,0:T(8,128)(2,1)S(1)}, bf16[8,3712]{1,0:T(8,128)(2,1)S(1)}, u32[]{:S(2)}, u32[]{:S(2)}) %collective-permute-start.1) | collective-permute-done | bytes 59424 | tf_op jit(solution)/shard_map/ppermute | solution.py:211
  8.8 0.3 compact.1
  9.1 2.7 %collective-permute-start.3 = (bf16[16,1792]{1,0:T(8,128)(2,1)S(1)}, bf16[16,1792]{1,0:T(8,128)(2,1)S(1)}, u32[]{:S(2)}, u32[]{:S(2)}) collective-permute-start(bf16[16,1792]{1,0:T(8,128)(2,1)S(1)} %get-tuple-element.30), channel_id=1, source_target_pairs={{0,2},{1,3},{2,0},{3,1},{4,6},{5,7},{6,4},{7,5},{8,10},{9,11},{10,... | collective-permute-start | bytes 172040 | tf_op jit(solution)/shard_map/ppermute | solution.py:211
  11.8 0.3 collective-permute-start.4
  12.1 1.6 %collective-permute-start.5 = (bf16[16,3584]{1,0:T(8,128)(2,1)S(1)}, bf16[16,3584]{1,0:T(8,128)(2,1)S(1)}, u32[]{:S(2)}, u32[]{:S(2)}) collective-permute-start(bf16[16,3584]{1,0:T(8,128)(2,1)S(1)} %get-tuple-element.32.refs_3_), channel_id=1, source_target_pairs={{0,1},{1,0},{2,3},{3,2},{4,5},{5,4},{6,7},{7,6},{8,9},{9,8},{10,11... | collective-permute-start | bytes 344072 | tf_op jit(solution)/shard_map/ppermute | solution.py:211
  13.8 1.2 %collective-permute-done.3.refs_0_ = bf16[16,1792]{1,0:T(8,128)(2,1)S(1)} collective-permute-done((bf16[16,1792]{1,0:T(8,128)(2,1)S(1)}, bf16[16,1792]{1,0:T(8,128)(2,1)S(1)}, u32[]{:S(2)}, u32[]{:S(2)}) %collective-permute-start.3) | collective-permute-done | bytes 57376 | tf_op jit(solution)/shard_map/ppermute | solution.py:211
  14.9 2.0 %collective-permute-start.6 = (bf16[16,1792]{1,0:T(8,128)(2,1)S(1)}, bf16[16,1792]{1,0:T(8,128)(2,1)S(1)}, u32[]{:S(2)}, u32[]{:S(2)}) collective-permute-start(bf16[16,1792]{1,0:T(8,128)(2,1)S(1)} %collective-permute-done.3.refs_0_), channel_id=1, source_target_pairs={{0,1},{1,0},{2,3},{3,2},{4,5},{5,4},{6,7},{7,6},{8,9},{9,8},{10,11... | collective-permute-start | bytes 172040 | tf_op jit(solution)/shard_map/ppermute | solution.py:211
  16.9 0.4 collective-permute-done.4.refs_1_
  17.4 1.5 %collective-permute-start.7 = (bf16[16,1792]{1,0:T(8,128)(2,1)S(1)}, bf16[16,1792]{1,0:T(8,128)(2,1)S(1)}, u32[]{:S(2)}, u32[]{:S(2)}) collective-permute-start(bf16[16,1792]{1,0:T(8,128)(2,1)S(1)} %collective-permute-done.4.refs_1_), channel_id=1, source_target_pairs={{0,1},{1,0},{2,3},{3,2},{4,5},{5,4},{6,7},{7,6},{8,9},{9,8},{10,11... | collective-permute-start | bytes 172040 | tf_op jit(solution)/shard_map/ppermute | solution.py:211
  18.9 0.7 %collective-permute-done.6.refs_4_ = bf16[16,1792]{1,0:T(8,128)(2,1)S(1)} collective-permute-done((bf16[16,1792]{1,0:T(8,128)(2,1)S(1)}, bf16[16,1792]{1,0:T(8,128)(2,1)S(1)}, u32[]{:S(2)}, u32[]{:S(2)}) %collective-permute-start.6) | collective-permute-done | bytes 57376 | tf_op jit(solution)/shard_map/ppermute | solution.py:211
  19.6 2.0 %collective-permute-done.7.refs_5_ = bf16[16,1792]{1,0:T(8,128)(2,1)S(1)} collective-permute-done((bf16[16,1792]{1,0:T(8,128)(2,1)S(1)}, bf16[16,1792]{1,0:T(8,128)(2,1)S(1)}, u32[]{:S(2)}, u32[]{:S(2)}) %collective-permute-start.7) | collective-permute-done | bytes 57376 | tf_op jit(solution)/shard_map/ppermute | solution.py:211
  21.6 1.4 %hidden.1.after_ref.refs_0_ = bf16[64,512]{1,0:T(8,128)(2,1)S(1)} custom-call(bf16[16,1792]{1,0:T(8,128)(2,1)S(1)} %collective-permute-done.3.refs_0_, bf16[16,1792]{1,0:T(8,128)(2,1)S(1)} %collective-permute-done.4.refs_1_, bf16[16,3584]{1,0:T(8,128)(2,1)S(1)} %collective-permute-done.5.refs_2_, bf16[16,3584]{1,0:T(8,128)(2,1)S(1)} %get-tuple-element.32.refs_3_, ...), custom_call_target="tpu_custom_call" | custom-call | tf_op jit(solution)/shard_map/hidden/pallas_call | solution.py:276
  23.0 3.9 %collective-permute-start.10 = (bf16[64,512]{1,0:T(8,128)(2,1)S(1)}, bf16[64,512]{1,0:T(8,128)(2,1)S(1)}, u32[]{:S(2)}, u32[]{:S(2)}) collective-permute-start(bf16[64,512]{1,0:T(8,128)(2,1)S(1)} %hidden.1.after_ref.refs_0_), channel_id=1, source_target_pairs={{0,3},{1,2},{2,1},{3,0},{4,7},{5,6},{6,5},{7,4},{8,11},{9,10},{10,... | collective-permute-start | bytes 196616 | tf_op jit(solution)/shard_map/ppermute | solution.py:211
  26.8 0.6 %collective-permute-start.8 = (bf16[64,512]{1,0:T(8,128)(2,1)S(1)}, bf16[64,512]{1,0:T(8,128)(2,1)S(1)}, u32[]{:S(2)}, u32[]{:S(2)}) collective-permute-start(bf16[64,512]{1,0:T(8,128)(2,1)S(1)} %hidden.1.after_ref.refs_0_), channel_id=1, source_target_pairs={{0,1},{1,0},{2,3},{3,2},{4,5},{5,4},{6,7},{7,6},{8,9},{9,8},{10,11... | collective-permute-start | bytes 196616 | tf_op jit(solution)/shard_map/ppermute | solution.py:211
  27.5 2.1 %prepare.1 = (bf16[2048,896]{1,0:T(8,128)(2,1)S(1)}, bf16[256,32]{1,0:T(8,128)(2,1)S(1)}) custom-call(bf16[64,512]{1,0:T(8,128)(2,1)S(1)} %hidden.1.after_ref.refs_0_, s32[8,256]{1,0:T(8,128)} %bitcast.10, f32[96,256]{1,0:T(8,128)} %bitcast.8, bf16[2048,896]{1,0:T(8,128)(2,1)} %bitcast.7), custom_call_target="tpu_custom_call" | custom-call | tf_op jit(solution)/shard_map/prepare/pallas_call | solution.py:284
  29.6 2.7 %collective-permute-done.9.refs_2_ = bf16[64,512]{1,0:T(8,128)(2,1)S(1)} collective-permute-done((bf16[64,512]{1,0:T(8,128)(2,1)S(1)}, bf16[64,512]{1,0:T(8,128)(2,1)S(1)}, u32[]{:S(2)}, u32[]{:S(2)}) %collective-permute-start.9) | collective-permute-done | bytes 65568 | tf_op jit(solution)/shard_map/ppermute | solution.py:211
  32.3 0.7 %down.1 = (bf16[16,896]{1,0:T(8,128)(2,1)S(1)}, bf16[16,896]{1,0:T(8,128)(2,1)S(1)}, bf16[16,896]{1,0:T(8,128)(2,1)S(1)}, bf16[16,896]{1,0:T(8,128)(2,1)S(1)}) custom-call(bf16[64,512]{1,0:T(8,128)(2,1)S(1)} %hidden.1.after_ref.refs_0_, bf16[64,512]{1,0:T(8,128)(2,1)S(1)} %collective-permute-done.8.refs_1_, ...), custom_call_target="tpu_custom_call" | custom-call | tf_op jit(solution)/shard_map/down/pallas_call | solution.py:302
  33.0 2.7 %collective-permute-start.11 = (bf16[16,896]{1,0:T(8,128)(2,1)S(1)}, bf16[16,896]{1,0:T(8,128)(2,1)S(1)}, u32[]{:S(2)}, u32[]{:S(2)}) collective-permute-start(bf16[16,896]{1,0:T(8,128)(2,1)S(1)} %get-tuple-element.37), channel_id=1, source_target_pairs={{0,3},{1,2},{2,1},{3,0},{4,7},{5,6},{6,5},{7,4},{8,11},{9,10},{10,... | collective-permute-start | bytes 86024 | tf_op jit(solution)/shard_map/ppermute | solution.py:211
  35.7 1.8 %collective-permute-start.13 = (bf16[16,896]{1,0:T(8,128)(2,1)S(1)}, bf16[16,896]{1,0:T(8,128)(2,1)S(1)}, u32[]{:S(2)}, u32[]{:S(2)}) collective-permute-start(bf16[16,896]{1,0:T(8,128)(2,1)S(1)} %get-tuple-element.39), channel_id=1, source_target_pairs={{0,1},{1,0},{2,3},{3,2},{4,5},{5,4},{6,7},{7,6},{8,9},{9,8},{10,11... | collective-permute-start | bytes 86024 | tf_op jit(solution)/shard_map/ppermute | solution.py:211
  37.4 1.3 %collective-permute-done.11.refs_0_ = bf16[16,896]{1,0:T(8,128)(2,1)S(1)} collective-permute-done((bf16[16,896]{1,0:T(8,128)(2,1)S(1)}, bf16[16,896]{1,0:T(8,128)(2,1)S(1)}, u32[]{:S(2)}, u32[]{:S(2)}) %collective-permute-start.11) | collective-permute-done | bytes 28704 | tf_op jit(solution)/shard_map/ppermute | solution.py:211
  38.7 1.7 %collective-permute-done.12.refs_1_ = bf16[16,896]{1,0:T(8,128)(2,1)S(1)} collective-permute-done((bf16[16,896]{1,0:T(8,128)(2,1)S(1)}, bf16[16,896]{1,0:T(8,128)(2,1)S(1)}, u32[]{:S(2)}, u32[]{:S(2)}) %collective-permute-start.12) | collective-permute-done | bytes 28704 | tf_op jit(solution)/shard_map/ppermute | solution.py:211
  40.5 0.2 spread.1
  40.6 0.1 collective-permute-start.14
  40.7 1.8 %collective-permute-start.15 = (bf16[4,8,896]{2,1,0:T(8,128)(2,1)S(1)}, bf16[4,8,896]{2,1,0:T(8,128)(2,1)S(1)}, u32[]{:S(2)}, u32[]{:S(2)}) collective-permute-start(bf16[4,8,896]{2,1,0:T(8,128)(2,1)S(1)} %get-tuple-element.42), channel_id=1, source_target_pairs={{0,8},{4,12},{8,0},{12,4},{1,9},{5,13},{9,1},{13,5},{2,10},{6,14},... | collective-permute-start | bytes 172040 | tf_op jit(solution)/shard_map/ppermute | solution.py:211
  42.5 0.1 collective-permute-start.16
  42.6 2.0 %collective-permute-done.14.refs_0_ = bf16[4,8,896]{2,1,0:T(8,128)(2,1)S(1)} collective-permute-done((bf16[4,8,896]{2,1,0:T(8,128)(2,1)S(1)}, bf16[4,8,896]{2,1,0:T(8,128)(2,1)S(1)}, u32[]{:S(2)}, u32[]{:S(2)}) %collective-permute-start.14) | collective-permute-done | bytes 57376 | tf_op jit(solution)/shard_map/ppermute | solution.py:211
  44.6 1.2 %collective-permute-done.15.refs_1_ = bf16[4,8,896]{2,1,0:T(8,128)(2,1)S(1)} collective-permute-done((bf16[4,8,896]{2,1,0:T(8,128)(2,1)S(1)}, bf16[4,8,896]{2,1,0:T(8,128)(2,1)S(1)}, u32[]{:S(2)}, u32[]{:S(2)}) %collective-permute-start.15) | collective-permute-done | bytes 57376 | tf_op jit(solution)/shard_map/ppermute | solution.py:211
  45.9 1.5 %combine.1 = bf16[256,3584]{1,0:T(8,128)(2,1)} custom-call(bf16[256,32]{1,0:T(8,128)(2,1)S(1)} %get-tuple-element.34.mixing_ref, bf16[4,8,896]{2,1,0:T(8,128)(2,1)S(1)} %collective-permute-done.14.refs_0_, bf16[4,8,896]{2,1,0:T(8,128)(2,1)S(1)} %collective-permute-done.15.refs_1_, bf16[4,8,896]{2,1,0:T(8,128)(2,1)S(1)} %collective-permute-done.16.refs_2_, ...), custom_call_target="tpu_custom_call" | custom-call | tf_op jit(solution)/shard_map/combine/pallas_call | solution.py:327
  (10 shorter events, 0.1 us)
Async XLA Ops:
  1.8 6.3 %collective-permute-start = (bf16[8,3712]{1,0:T(8,128)(2,1)S(1)}, bf16[8,3712]{1,0:T(8,128)(2,1)S(1)}, u32[]{:S(2)}, u32[]{:S(2)}) collective-permute-start(bf16[8,3712]{1,0:T(8,128)(2,1)S(1)} %get-tuple-element.27), channel_id=1, source_target_pairs={{0,12},{4,8},{8,4},{12,0},{1,13},{5,9},{9,5},{13,1},{2,14},{6,10},... | collective-permute-start | bytes 178184 | tf_op jit(solution)/shard_map/ppermute | solution.py:211
  4.2 4.5 %collective-permute-start.1 = (bf16[8,3712]{1,0:T(8,128)(2,1)S(1)}, bf16[8,3712]{1,0:T(8,128)(2,1)S(1)}, u32[]{:S(2)}, u32[]{:S(2)}) collective-permute-start(bf16[8,3712]{1,0:T(8,128)(2,1)S(1)} %get-tuple-element.28), channel_id=1, source_target_pairs={{0,8},{4,12},{8,0},{12,4},{1,9},{5,13},{9,1},{13,5},{2,10},{6,14},... | collective-permute-start | bytes 178184 | tf_op jit(solution)/shard_map/ppermute | solution.py:211
  4.9 3.9 %collective-permute-start.2 = (bf16[8,3712]{1,0:T(8,128)(2,1)S(1)}, bf16[8,3712]{1,0:T(8,128)(2,1)S(1)}, u32[]{:S(2)}, u32[]{:S(2)}) collective-permute-start(bf16[8,3712]{1,0:T(8,128)(2,1)S(1)} %get-tuple-element.29), channel_id=1, source_target_pairs={{0,4},{4,0},{8,12},{12,8},{1,5},{5,1},{9,13},{13,9},{2,6},{6,2},{1... | collective-permute-start | bytes 178184 | tf_op jit(solution)/shard_map/ppermute | solution.py:211
  9.1 5.8 %collective-permute-start.3 = (bf16[16,1792]{1,0:T(8,128)(2,1)S(1)}, bf16[16,1792]{1,0:T(8,128)(2,1)S(1)}, u32[]{:S(2)}, u32[]{:S(2)}) collective-permute-start(bf16[16,1792]{1,0:T(8,128)(2,1)S(1)} %get-tuple-element.30), channel_id=1, source_target_pairs={{0,2},{1,3},{2,0},{3,1},{4,6},{5,7},{6,4},{7,5},{8,10},{9,11},{10,... | collective-permute-start | bytes 172040 | tf_op jit(solution)/shard_map/ppermute | solution.py:211
  11.8 5.5 %collective-permute-start.4 = (bf16[16,1792]{1,0:T(8,128)(2,1)S(1)}, bf16[16,1792]{1,0:T(8,128)(2,1)S(1)}, u32[]{:S(2)}, u32[]{:S(2)}) collective-permute-start(bf16[16,1792]{1,0:T(8,128)(2,1)S(1)} %get-tuple-element.31), channel_id=1, source_target_pairs={{0,2},{1,3},{2,0},{3,1},{4,6},{5,7},{6,4},{7,5},{8,10},{9,11},{10,... | collective-permute-start | bytes 172040 | tf_op jit(solution)/shard_map/ppermute | solution.py:211
  12.1 9.4 %collective-permute-start.5 = (bf16[16,3584]{1,0:T(8,128)(2,1)S(1)}, bf16[16,3584]{1,0:T(8,128)(2,1)S(1)}, u32[]{:S(2)}, u32[]{:S(2)}) collective-permute-start(bf16[16,3584]{1,0:T(8,128)(2,1)S(1)} %get-tuple-element.32.refs_3_), channel_id=1, source_target_pairs={{0,1},{1,0},{2,3},{3,2},{4,5},{5,4},{6,7},{7,6},{8,9},{9,8},{10,11... | collective-permute-start | bytes 344072 | tf_op jit(solution)/shard_map/ppermute | solution.py:211
  14.9 4.7 %collective-permute-start.6 = (bf16[16,1792]{1,0:T(8,128)(2,1)S(1)}, bf16[16,1792]{1,0:T(8,128)(2,1)S(1)}, u32[]{:S(2)}, u32[]{:S(2)}) collective-permute-start(bf16[16,1792]{1,0:T(8,128)(2,1)S(1)} %collective-permute-done.3.refs_0_), channel_id=1, source_target_pairs={{0,1},{1,0},{2,3},{3,2},{4,5},{5,4},{6,7},{7,6},{8,9},{9,8},{10,11... | collective-permute-start | bytes 172040 | tf_op jit(solution)/shard_map/ppermute | solution.py:211
  17.4 4.2 %collective-permute-start.7 = (bf16[16,1792]{1,0:T(8,128)(2,1)S(1)}, bf16[16,1792]{1,0:T(8,128)(2,1)S(1)}, u32[]{:S(2)}, u32[]{:S(2)}) collective-permute-start(bf16[16,1792]{1,0:T(8,128)(2,1)S(1)} %collective-permute-done.4.refs_1_), channel_id=1, source_target_pairs={{0,1},{1,0},{2,3},{3,2},{4,5},{5,4},{6,7},{7,6},{8,9},{9,8},{10,11... | collective-permute-start | bytes 172040 | tf_op jit(solution)/shard_map/ppermute | solution.py:211
  23.0 6.6 %collective-permute-start.10 = (bf16[64,512]{1,0:T(8,128)(2,1)S(1)}, bf16[64,512]{1,0:T(8,128)(2,1)S(1)}, u32[]{:S(2)}, u32[]{:S(2)}) collective-permute-start(bf16[64,512]{1,0:T(8,128)(2,1)S(1)} %hidden.1.after_ref.refs_0_), channel_id=1, source_target_pairs={{0,3},{1,2},{2,1},{3,0},{4,7},{5,6},{6,5},{7,4},{8,11},{9,10},{10,... | collective-permute-start | bytes 196616 | tf_op jit(solution)/shard_map/ppermute | solution.py:211
  26.8 5.4 %collective-permute-start.9 = (bf16[64,512]{1,0:T(8,128)(2,1)S(1)}, bf16[64,512]{1,0:T(8,128)(2,1)S(1)}, u32[]{:S(2)}, u32[]{:S(2)}) collective-permute-start(bf16[64,512]{1,0:T(8,128)(2,1)S(1)} %hidden.1.after_ref.refs_0_), channel_id=1, source_target_pairs={{0,2},{1,3},{2,0},{3,1},{4,6},{5,7},{6,4},{7,5},{8,10},{9,11},{10,... | collective-permute-start | bytes 196616 | tf_op jit(solution)/shard_map/ppermute | solution.py:211
  26.8 5.4 %collective-permute-start.8 = (bf16[64,512]{1,0:T(8,128)(2,1)S(1)}, bf16[64,512]{1,0:T(8,128)(2,1)S(1)}, u32[]{:S(2)}, u32[]{:S(2)}) collective-permute-start(bf16[64,512]{1,0:T(8,128)(2,1)S(1)} %hidden.1.after_ref.refs_0_), channel_id=1, source_target_pairs={{0,1},{1,0},{2,3},{3,2},{4,5},{5,4},{6,7},{7,6},{8,9},{9,8},{10,11... | collective-permute-start | bytes 196616 | tf_op jit(solution)/shard_map/ppermute | solution.py:211
  33.0 5.7 %collective-permute-start.11 = (bf16[16,896]{1,0:T(8,128)(2,1)S(1)}, bf16[16,896]{1,0:T(8,128)(2,1)S(1)}, u32[]{:S(2)}, u32[]{:S(2)}) collective-permute-start(bf16[16,896]{1,0:T(8,128)(2,1)S(1)} %get-tuple-element.37), channel_id=1, source_target_pairs={{0,3},{1,2},{2,1},{3,0},{4,7},{5,6},{6,5},{7,4},{8,11},{9,10},{10,... | collective-permute-start | bytes 86024 | tf_op jit(solution)/shard_map/ppermute | solution.py:211
  35.7 4.8 %collective-permute-start.12 = (bf16[16,896]{1,0:T(8,128)(2,1)S(1)}, bf16[16,896]{1,0:T(8,128)(2,1)S(1)}, u32[]{:S(2)}, u32[]{:S(2)}) collective-permute-start(bf16[16,896]{1,0:T(8,128)(2,1)S(1)} %get-tuple-element.38), channel_id=1, source_target_pairs={{0,2},{1,3},{2,0},{3,1},{4,6},{5,7},{6,4},{7,5},{8,10},{9,11},{10,... | collective-permute-start | bytes 86024 | tf_op jit(solution)/shard_map/ppermute | solution.py:211
  35.7 4.8 %collective-permute-start.13 = (bf16[16,896]{1,0:T(8,128)(2,1)S(1)}, bf16[16,896]{1,0:T(8,128)(2,1)S(1)}, u32[]{:S(2)}, u32[]{:S(2)}) collective-permute-start(bf16[16,896]{1,0:T(8,128)(2,1)S(1)} %get-tuple-element.39), channel_id=1, source_target_pairs={{0,1},{1,0},{2,3},{3,2},{4,5},{5,4},{6,7},{7,6},{8,9},{9,8},{10,11... | collective-permute-start | bytes 86024 | tf_op jit(solution)/shard_map/ppermute | solution.py:211
  40.6 4.0 %collective-permute-start.14 = (bf16[4,8,896]{2,1,0:T(8,128)(2,1)S(1)}, bf16[4,8,896]{2,1,0:T(8,128)(2,1)S(1)}, u32[]{:S(2)}, u32[]{:S(2)}) collective-permute-start(bf16[4,8,896]{2,1,0:T(8,128)(2,1)S(1)} %get-tuple-element.41), channel_id=1, source_target_pairs={{0,12},{4,8},{8,4},{12,0},{1,13},{5,9},{9,5},{13,1},{2,14},{6,10},... | collective-permute-start | bytes 172040 | tf_op jit(solution)/shard_map/ppermute | solution.py:211
  40.7 5.1 %collective-permute-start.15 = (bf16[4,8,896]{2,1,0:T(8,128)(2,1)S(1)}, bf16[4,8,896]{2,1,0:T(8,128)(2,1)S(1)}, u32[]{:S(2)}, u32[]{:S(2)}) collective-permute-start(bf16[4,8,896]{2,1,0:T(8,128)(2,1)S(1)} %get-tuple-element.42), channel_id=1, source_target_pairs={{0,8},{4,12},{8,0},{12,4},{1,9},{5,13},{9,1},{13,5},{2,10},{6,14},... | collective-permute-start | bytes 172040 | tf_op jit(solution)/shard_map/ppermute | solution.py:211
  42.5 3.3 %collective-permute-start.16 = (bf16[4,8,896]{2,1,0:T(8,128)(2,1)S(1)}, bf16[4,8,896]{2,1,0:T(8,128)(2,1)S(1)}, u32[]{:S(2)}, u32[]{:S(2)}) collective-permute-start(bf16[4,8,896]{2,1,0:T(8,128)(2,1)S(1)} %get-tuple-element.43), channel_id=1, source_target_pairs={{0,4},{4,0},{8,12},{12,8},{1,5},{5,1},{9,13},{13,9},{2,6},{6,2},{1... | collective-permute-start | bytes 172040 | tf_op jit(solution)/shard_map/ppermute | solution.py:211

commit v8 on v7

--- a/solution.py
+++ b/solution.py
@@ -118,8 +118,9 @@
 
 def compact_kernel(groups, slots, after_ref, *refs):
     del after_ref
-    arrived, (out_ref, low_ref, high_ref, pick_ref) = refs[:groups][::-1], refs[groups:]
-    rows, features = groups * CAP, out_ref.shape[1]
+    arrived, outs, pick_ref = refs[:groups][::-1], refs[groups:-1], refs[-1]
+    rows, part = groups * CAP, outs[0].shape[1]
+    features = part * len(outs)
     live = jnp.concatenate([a[:, features:].astype(F32) for a in arrived], axis=0)
     row = lax.broadcasted_iota(jnp.int32, (rows, rows), 0)
     column = lax.broadcasted_iota(jnp.int32, (rows, rows), 1)
@@ -127,19 +128,13 @@
     lane = lax.broadcasted_iota(jnp.int32, (rows, LANES), 1).astype(F32)
     pick = jnp.where((live > 0.5) & (rank == lane + 1.0), 1.0, 0.0).astype(BF16)
     pick_ref[...] = pick
-    half = features // 2
     step = 256
     for c in range(features // step):
-        part = slice(c * step, (c + 1) * step)
-        whole = jnp.concatenate([a[:, part].astype(F32) for a in arrived], axis=0).astype(BF16)
-        moved = lax.dot_general(
-            pick[:, :slots], whole, (((0,), (0,)), ((), ())), preferred_element_type=F32
-        ).astype(BF16)
-        out_ref[:, part] = moved
-        if (c + 1) * step <= half:
-            low_ref[:, part] = moved
-        else:
-            high_ref[:, c * step - half : (c + 1) * step - half] = moved
+        at = slice(c * step, (c + 1) * step)
+        whole = jnp.concatenate([a[:, at].astype(F32) for a in arrived], axis=0).astype(BF16)
+        moved = lax.dot_general(pick[:, :slots], whole, (((0,), (0,)), ((), ())), preferred_element_type=F32)
+        first = c * step % part
+        outs[c * step // part][:, first : first + step] = moved.astype(BF16)
 
 
 def hidden_kernel(columns, halved, *refs):
@@ -147,8 +142,9 @@
     units = gate_ref.shape[1]
     blocks = [block[...] for block in blocks]
     if halved:
-        low, high, near, own, far_low, far_high = blocks
-        blocks = [own, near, jnp.concatenate([low, high], axis=1), jnp.concatenate([far_low, far_high], axis=1)]
+        low, near_low, near_high, high, far_high, far_low, own_low, own_high = blocks
+        pairs = [(own_low, own_high), (near_low, near_high), (low, high), (far_low, far_high)]
+        blocks = [jnp.concatenate(pair, axis=1) for pair in pairs]
     rows = jnp.concatenate(blocks, axis=0)
     step = min(256, units)
     for c in range(units // step):
@@ -253,25 +249,23 @@
         name="load",
     )(outbound[0], *weights[:2])
 
-    compacted, low, high, pick = pl.pallas_call(
+    parts = 2 if columns == 4 else 1
+    *own, pick = pl.pallas_call(
         functools.partial(compact_kernel, groups, slots),
-        out_shape=[
-            jax.ShapeDtypeStruct((slots, features), BF16),
-            jax.ShapeDtypeStruct((slots, features // 2), BF16),
-            jax.ShapeDtypeStruct((slots, features // 2), BF16),
-            jax.ShapeDtypeStruct((groups * CAP, LANES), BF16),
-        ],
+        out_shape=[jax.ShapeDtypeStruct((slots, features // parts), BF16)] * parts
+        + [jax.ShapeDtypeStruct((groups * CAP, LANES), BF16)],
         in_specs=[ANY] + [VMEM] * groups,
-        out_specs=[VMEM] * 4,
-        compiler_params=params(2 * (groups * CAP + 2 * slots) * wide),
+        out_specs=[VMEM] * (parts + 1),
+        compiler_params=params(2 * (groups * CAP + slots) * wide),
         name="compact",
     )(gate, *arrived)
     if columns == 4:
-        low, high = swap(low, "ing", 2), swap(high, "ing", 2)
-        near = swap(compacted, "ing", 1)
-        blocks = [low, high, near, compacted, swap(low, "ing", 1), swap(high, "ing", 1)]
+        near_low, near_high, high, far_high = [swap(part, "ing", e) for part, e in zip(own + own[1:] * 2, (1, 1, 2, 3))]
+        low = swap(own[0], "ing", 2)
+        far_low = swap(low, "ing", 1)
+        blocks = [low, near_low, near_high, high, far_high, far_low] + own
     else:
-        blocks = [swap(compacted, "ing", e) for e in range(columns)]
+        blocks = [swap(own[0], "ing", e) for e in range(columns)]
 
     hidden = pl.pallas_call(
         functools.partial(hidden_kernel, columns, columns == 4),

time: 47.6 us -> 46.6 us (0.979)
  waiting for transfers between devices: 13.9 us -> 12.3 us
  starting transfers between devices: 22.2 us -> 22.7 us
    ppermute x17 -> x18, waiting for transfers between devices: 13.9 us -> 12.3 us  [swap(): lax.ppermute(x, name, [(a, a ^ step) for a in range(lax.axis_size(name))])]
    ppermute x17 -> x18, starting transfers between devices: 22.2 us -> 22.7 us  [swap(): lax.ppermute(x, name, [(a, a ^ step) for a in range(lax.axis_size(name))])]
  transfers between devices with their start and end apart: 17 -> 18, of which waited for: 10 -> 10; matrix products, arithmetic and copies ran while one was open for 0% -> 0% of each run, Pallas kernels for 11% -> 11%
where the time goes in v8:
time: 46.6 us; the launch traced here: 46.3 us
  starting transfers between devices  22.7 us (49%)
  waiting for transfers between devices  12.3 us (26%)
  Pallas kernels  11.2 us (24%)
    ppermute x18, starting transfers between devices, swap(): lax.ppermute(x, name, [(a, a ^ step) for a in range(lax.axis_size(name))])  22.7 us
    ppermute x18, waiting for transfers between devices, swap(): lax.ppermute(x, name, [(a, a ^ step) for a in range(lax.axis_size(name))])  12.3 us
    pallas_call x1, Pallas kernels, local(): pl.pallas_call(load_kernel, out_shape=[pltpu.VMEM(w.shape, BF16) for w in...  3.17 us
    pallas_call x1, Pallas kernels, local(): pl.pallas_call(functools.partial(prepare_kernel, groups), out_shape=[pltp...  2.13 us
    pallas_call x1, Pallas kernels, local(): pl.pallas_call(functools.partial(dispatch_kernel, groups, features // 2),...  1.79 us
    pallas_call x1, Pallas kernels, local(): pl.pallas_call(functools.partial(combine_kernel, groups, columns), out_sh...  1.49 us
    pallas_call x1, Pallas kernels, local(): pl.pallas_call(functools.partial(hidden_kernel, columns, columns == 4), o...  1.39 us
  transfers between devices with their start and end apart: 18, of which 10 were waited for; matrix products, arithmetic and copies ran while one was open for 0% of the time, Pallas kernels for 11%

profile of v8, /device:TPU:0, one launch (start us, length us, event | category | flops | bytes accessed | tf_op | source)
XLA Modules:
  0.0 46.3 jit_solution(17066171038733366049)
XLA Ops:
  0.0 1.8 %dispatch.1 = (bf16[8,3712]{1,0:T(8,128)(2,1)S(1)}, bf16[8,3712]{1,0:T(8,128)(2,1)S(1)}, bf16[8,3712]{1,0:T(8,128)(2,1)S(1)}, bf16[8,3712]{1,0:T(8,128)(2,1)S(1)}) custom-call(s32[8,256]{1,0:T(8,128)} %bitcast.9, bf16[256,3584]{1,0:T(8,128)(2,1)} %tokens_ref.1), custom_call_target="tpu_custom_call" | custom-call | tf_op jit(solution)/shard_map/dispatch/pallas_call | solution.py:224
  1.8 2.4 %collective-permute-start = (bf16[8,3712]{1,0:T(8,128)(2,1)S(1)}, bf16[8,3712]{1,0:T(8,128)(2,1)S(1)}, u32[]{:S(2)}, u32[]{:S(2)}) collective-permute-start(bf16[8,3712]{1,0:T(8,128)(2,1)S(1)} %get-tuple-element.26), channel_id=1, source_target_pairs={{0,12},{4,8},{8,4},{12,0},{1,13},{5,9},{9,5},{13,1},{2,14},{6,10},... | collective-permute-start | bytes 178184 | tf_op jit(solution)/shard_map/ppermute | solution.py:207
  4.2 0.6 %collective-permute-start.1 = (bf16[8,3712]{1,0:T(8,128)(2,1)S(1)}, bf16[8,3712]{1,0:T(8,128)(2,1)S(1)}, u32[]{:S(2)}, u32[]{:S(2)}) collective-permute-start(bf16[8,3712]{1,0:T(8,128)(2,1)S(1)} %get-tuple-element.27), channel_id=1, source_target_pairs={{0,8},{4,12},{8,0},{12,4},{1,9},{5,13},{9,1},{13,5},{2,10},{6,14},... | collective-permute-start | bytes 178184 | tf_op jit(solution)/shard_map/ppermute | solution.py:207
  4.9 3.2 %load.1 = (bf16[3584,512]{1,0:T(8,128)(2,1)S(1)}, bf16[3584,512]{1,0:T(8,128)(2,1)S(1)}) custom-call(bf16[8,3712]{1,0:T(8,128)(2,1)S(1)} %get-tuple-element.24.after_ref.refs_3_, bf16[3584,512]{1,0:T(8,128)(2,1)} %bitcast.5, bf16[3584,512]{1,0:T(8,128)(2,1)} %bitcast.6), custom_call_target="tpu_custom_call" | custom-call | tf_op jit(solution)/shard_map/load/pallas_call | solution.py:242
  8.1 0.7 %collective-permute-done.1.refs_1_ = bf16[8,3712]{1,0:T(8,128)(2,1)S(1)} collective-permute-done((bf16[8,3712]{1,0:T(8,128)(2,1)S(1)}, bf16[8,3712]{1,0:T(8,128)(2,1)S(1)}, u32[]{:S(2)}, u32[]{:S(2)}) %collective-permute-start.1) | collective-permute-done | bytes 59424 | tf_op jit(solution)/shard_map/ppermute | solution.py:207
  8.8 0.3 compact.1
  9.1 2.7 %collective-permute-start.3 = (bf16[16,1792]{1,0:T(8,128)(2,1)S(1)}, bf16[16,1792]{1,0:T(8,128)(2,1)S(1)}, u32[]{:S(2)}, u32[]{:S(2)}) collective-permute-start(bf16[16,1792]{1,0:T(8,128)(2,1)S(1)} %get-tuple-element.29.refs_6_), channel_id=1, source_target_pairs={{0,2},{1,3},{2,0},{3,1},{4,6},{5,7},{6,4},{7,5},{8,10},{9,11},{10,... | collective-permute-start | bytes 172040 | tf_op jit(solution)/shard_map/ppermute | solution.py:207
  11.8 1.6 %collective-permute-start.4 = (bf16[16,1792]{1,0:T(8,128)(2,1)S(1)}, bf16[16,1792]{1,0:T(8,128)(2,1)S(1)}, u32[]{:S(2)}, u32[]{:S(2)}) collective-permute-start(bf16[16,1792]{1,0:T(8,128)(2,1)S(1)} %get-tuple-element.29.refs_6_), channel_id=1, source_target_pairs={{0,1},{1,0},{2,3},{3,2},{4,5},{5,4},{6,7},{7,6},{8,9},{9,8},{10,11... | collective-permute-start | bytes 172040 | tf_op jit(solution)/shard_map/ppermute | solution.py:207
  13.4 0.2 collective-permute-start.7
  13.6 1.8 %collective-permute-start.6 = (bf16[16,1792]{1,0:T(8,128)(2,1)S(1)}, bf16[16,1792]{1,0:T(8,128)(2,1)S(1)}, u32[]{:S(2)}, u32[]{:S(2)}) collective-permute-start(bf16[16,1792]{1,0:T(8,128)(2,1)S(1)} %get-tuple-element.30.refs_7_), channel_id=1, source_target_pairs={{0,2},{1,3},{2,0},{3,1},{4,6},{5,7},{6,4},{7,5},{8,10},{9,11},{10,... | collective-permute-start | bytes 172040 | tf_op jit(solution)/shard_map/ppermute | solution.py:207
  15.3 2.5 %collective-permute-start.5 = (bf16[16,1792]{1,0:T(8,128)(2,1)S(1)}, bf16[16,1792]{1,0:T(8,128)(2,1)S(1)}, u32[]{:S(2)}, u32[]{:S(2)}) collective-permute-start(bf16[16,1792]{1,0:T(8,128)(2,1)S(1)} %get-tuple-element.30.refs_7_), channel_id=1, source_target_pairs={{0,1},{1,0},{2,3},{3,2},{4,5},{5,4},{6,7},{7,6},{8,9},{9,8},{10,11... | collective-permute-start | bytes 172040 | tf_op jit(solution)/shard_map/ppermute | solution.py:207
  17.8 2.2 %collective-permute-done.7.refs_4_ = bf16[16,1792]{1,0:T(8,128)(2,1)S(1)} collective-permute-done((bf16[16,1792]{1,0:T(8,128)(2,1)S(1)}, bf16[16,1792]{1,0:T(8,128)(2,1)S(1)}, u32[]{:S(2)}, u32[]{:S(2)}) %collective-permute-start.7) | collective-permute-done | bytes 57376 | tf_op jit(solution)/shard_map/ppermute | solution.py:207
  20.1 1.1 %collective-permute-done.5.refs_2_ = bf16[16,1792]{1,0:T(8,128)(2,1)S(1)} collective-permute-done((bf16[16,1792]{1,0:T(8,128)(2,1)S(1)}, bf16[16,1792]{1,0:T(8,128)(2,1)S(1)}, u32[]{:S(2)}, u32[]{:S(2)}) %collective-permute-start.5) | collective-permute-done | bytes 57376 | tf_op jit(solution)/shard_map/ppermute | solution.py:207
  21.2 0.8 %collective-permute-done.8.refs_5_ = bf16[16,1792]{1,0:T(8,128)(2,1)S(1)} collective-permute-done((bf16[16,1792]{1,0:T(8,128)(2,1)S(1)}, bf16[16,1792]{1,0:T(8,128)(2,1)S(1)}, u32[]{:S(2)}, u32[]{:S(2)}) %collective-permute-start.8) | collective-permute-done | bytes 57376 | tf_op jit(solution)/shard_map/ppermute | solution.py:207
  22.0 1.4 %hidden.1.after_ref.refs_0_ = bf16[64,512]{1,0:T(8,128)(2,1)S(1)} custom-call(bf16[16,1792]{1,0:T(8,128)(2,1)S(1)} %collective-permute-done.3.refs_0_, bf16[16,1792]{1,0:T(8,128)(2,1)S(1)} %collective-permute-done.4.refs_1_, bf16[16,1792]{1,0:T(8,128)(2,1)S(1)} %collective-permute-done.5.refs_2_, bf16[16,1792]{1,0:T(8,128)(2,1)S(1)} %collective-permute-done.6.refs_3_, ...), custom_call_target="tpu_custom_call" | custom-call | tf_op jit(solution)/shard_map/hidden/pallas_call | solution.py:270
  23.4 3.4 %collective-permute-start.11 = (bf16[64,512]{1,0:T(8,128)(2,1)S(1)}, bf16[64,512]{1,0:T(8,128)(2,1)S(1)}, u32[]{:S(2)}, u32[]{:S(2)}) collective-permute-start(bf16[64,512]{1,0:T(8,128)(2,1)S(1)} %hidden.1.after_ref.refs_0_), channel_id=1, source_target_pairs={{0,3},{1,2},{2,1},{3,0},{4,7},{5,6},{6,5},{7,4},{8,11},{9,10},{10,... | collective-permute-start | bytes 196616 | tf_op jit(solution)/shard_map/ppermute | solution.py:207
  26.8 1.0 %collective-permute-start.9 = (bf16[64,512]{1,0:T(8,128)(2,1)S(1)}, bf16[64,512]{1,0:T(8,128)(2,1)S(1)}, u32[]{:S(2)}, u32[]{:S(2)}) collective-permute-start(bf16[64,512]{1,0:T(8,128)(2,1)S(1)} %hidden.1.after_ref.refs_0_), channel_id=1, source_target_pairs={{0,1},{1,0},{2,3},{3,2},{4,5},{5,4},{6,7},{7,6},{8,9},{9,8},{10,11... | collective-permute-start | bytes 196616 | tf_op jit(solution)/shard_map/ppermute | solution.py:207
  27.8 2.1 %prepare.1 = (bf16[2048,896]{1,0:T(8,128)(2,1)S(1)}, bf16[256,32]{1,0:T(8,128)(2,1)S(1)}) custom-call(bf16[64,512]{1,0:T(8,128)(2,1)S(1)} %hidden.1.after_ref.refs_0_, s32[8,256]{1,0:T(8,128)} %bitcast.10, f32[96,256]{1,0:T(8,128)} %bitcast.8, bf16[2048,896]{1,0:T(8,128)(2,1)} %bitcast.7), custom_call_target="tpu_custom_call" | custom-call | tf_op jit(solution)/shard_map/prepare/pallas_call | solution.py:278
  30.0 2.1 %collective-permute-done.10.refs_2_ = bf16[64,512]{1,0:T(8,128)(2,1)S(1)} collective-permute-done((bf16[64,512]{1,0:T(8,128)(2,1)S(1)}, bf16[64,512]{1,0:T(8,128)(2,1)S(1)}, u32[]{:S(2)}, u32[]{:S(2)}) %collective-permute-start.10) | collective-permute-done | bytes 65568 | tf_op jit(solution)/shard_map/ppermute | solution.py:207
  32.1 0.1 collective-permute-done.9.refs_1_
  32.2 0.7 %down.1 = (bf16[16,896]{1,0:T(8,128)(2,1)S(1)}, bf16[16,896]{1,0:T(8,128)(2,1)S(1)}, bf16[16,896]{1,0:T(8,128)(2,1)S(1)}, bf16[16,896]{1,0:T(8,128)(2,1)S(1)}) custom-call(bf16[64,512]{1,0:T(8,128)(2,1)S(1)} %hidden.1.after_ref.refs_0_, bf16[64,512]{1,0:T(8,128)(2,1)S(1)} %collective-permute-done.9.refs_1_, ...), custom_call_target="tpu_custom_call" | custom-call | tf_op jit(solution)/shard_map/down/pallas_call | solution.py:296
  32.9 1.7 %collective-permute-start.12 = (bf16[16,896]{1,0:T(8,128)(2,1)S(1)}, bf16[16,896]{1,0:T(8,128)(2,1)S(1)}, u32[]{:S(2)}, u32[]{:S(2)}) collective-permute-start(bf16[16,896]{1,0:T(8,128)(2,1)S(1)} %get-tuple-element.35), channel_id=1, source_target_pairs={{0,3},{1,2},{2,1},{3,0},{4,7},{5,6},{6,5},{7,4},{8,11},{9,10},{10,... | collective-permute-start | bytes 86024 | tf_op jit(solution)/shard_map/ppermute | solution.py:207
  34.7 0.2 collective-permute-start.13
  34.9 2.5 %collective-permute-start.14 = (bf16[16,896]{1,0:T(8,128)(2,1)S(1)}, bf16[16,896]{1,0:T(8,128)(2,1)S(1)}, u32[]{:S(2)}, u32[]{:S(2)}) collective-permute-start(bf16[16,896]{1,0:T(8,128)(2,1)S(1)} %get-tuple-element.37), channel_id=1, source_target_pairs={{0,1},{1,0},{2,3},{3,2},{4,5},{5,4},{6,7},{7,6},{8,9},{9,8},{10,11... | collective-permute-start | bytes 86024 | tf_op jit(solution)/shard_map/ppermute | solution.py:207
  37.4 1.3 %collective-permute-done.12.refs_0_ = bf16[16,896]{1,0:T(8,128)(2,1)S(1)} collective-permute-done((bf16[16,896]{1,0:T(8,128)(2,1)S(1)}, bf16[16,896]{1,0:T(8,128)(2,1)S(1)}, u32[]{:S(2)}, u32[]{:S(2)}) %collective-permute-start.12) | collective-permute-done | bytes 28704 | tf_op jit(solution)/shard_map/ppermute | solution.py:207
  38.6 1.1 %collective-permute-done.13.refs_1_ = bf16[16,896]{1,0:T(8,128)(2,1)S(1)} collective-permute-done((bf16[16,896]{1,0:T(8,128)(2,1)S(1)}, bf16[16,896]{1,0:T(8,128)(2,1)S(1)}, u32[]{:S(2)}, u32[]{:S(2)}) %collective-permute-start.13) | collective-permute-done | bytes 28704 | tf_op jit(solution)/shard_map/ppermute | solution.py:207
  39.7 0.2 spread.1
  40.0 1.2 %collective-permute-start.16 = (bf16[4,8,896]{2,1,0:T(8,128)(2,1)S(1)}, bf16[4,8,896]{2,1,0:T(8,128)(2,1)S(1)}, u32[]{:S(2)}, u32[]{:S(2)}) collective-permute-start(bf16[4,8,896]{2,1,0:T(8,128)(2,1)S(1)} %get-tuple-element.40), channel_id=1, source_target_pairs={{0,8},{4,12},{8,0},{12,4},{1,9},{5,13},{9,1},{13,5},{2,10},{6,14},... | collective-permute-start | bytes 172040 | tf_op jit(solution)/shard_map/ppermute | solution.py:207
  41.2 0.7 %collective-permute-start.17 = (bf16[4,8,896]{2,1,0:T(8,128)(2,1)S(1)}, bf16[4,8,896]{2,1,0:T(8,128)(2,1)S(1)}, u32[]{:S(2)}, u32[]{:S(2)}) collective-permute-start(bf16[4,8,896]{2,1,0:T(8,128)(2,1)S(1)} %get-tuple-element.41), channel_id=1, source_target_pairs={{0,4},{4,0},{8,12},{12,8},{1,5},{5,1},{9,13},{13,9},{2,6},{6,2},{1... | collective-permute-start | bytes 172040 | tf_op jit(solution)/shard_map/ppermute | solution.py:207
  41.8 2.3 %collective-permute-done.15.refs_0_ = bf16[4,8,896]{2,1,0:T(8,128)(2,1)S(1)} collective-permute-done((bf16[4,8,896]{2,1,0:T(8,128)(2,1)S(1)}, bf16[4,8,896]{2,1,0:T(8,128)(2,1)S(1)}, u32[]{:S(2)}, u32[]{:S(2)}) %collective-permute-start.15) | collective-permute-done | bytes 57376 | tf_op jit(solution)/shard_map/ppermute | solution.py:207
  44.1 0.7 %collective-permute-done.16.refs_1_ = bf16[4,8,896]{2,1,0:T(8,128)(2,1)S(1)} collective-permute-done((bf16[4,8,896]{2,1,0:T(8,128)(2,1)S(1)}, bf16[4,8,896]{2,1,0:T(8,128)(2,1)S(1)}, u32[]{:S(2)}, u32[]{:S(2)}) %collective-permute-start.16) | collective-permute-done | bytes 57376 | tf_op jit(solution)/shard_map/ppermute | solution.py:207
  44.8 1.5 %combine.1 = bf16[256,3584]{1,0:T(8,128)(2,1)} custom-call(bf16[256,32]{1,0:T(8,128)(2,1)S(1)} %get-tuple-element.32.mixing_ref, bf16[4,8,896]{2,1,0:T(8,128)(2,1)S(1)} %collective-permute-done.15.refs_0_, bf16[4,8,896]{2,1,0:T(8,128)(2,1)S(1)} %collective-permute-done.16.refs_1_, bf16[4,8,896]{2,1,0:T(8,128)(2,1)S(1)} %collective-permute-done.17.refs_2_, ...), custom_call_target="tpu_custom_call" | custom-call | tf_op jit(solution)/shard_map/combine/pallas_call | solution.py:321
  (12 shorter events, 0.2 us)
Async XLA Ops:
  1.8 6.3 %collective-permute-start = (bf16[8,3712]{1,0:T(8,128)(2,1)S(1)}, bf16[8,3712]{1,0:T(8,128)(2,1)S(1)}, u32[]{:S(2)}, u32[]{:S(2)}) collective-permute-start(bf16[8,3712]{1,0:T(8,128)(2,1)S(1)} %get-tuple-element.26), channel_id=1, source_target_pairs={{0,12},{4,8},{8,4},{12,0},{1,13},{5,9},{9,5},{13,1},{2,14},{6,10},... | collective-permute-start | bytes 178184 | tf_op jit(solution)/shard_map/ppermute | solution.py:207
  4.2 4.5 %collective-permute-start.1 = (bf16[8,3712]{1,0:T(8,128)(2,1)S(1)}, bf16[8,3712]{1,0:T(8,128)(2,1)S(1)}, u32[]{:S(2)}, u32[]{:S(2)}) collective-permute-start(bf16[8,3712]{1,0:T(8,128)(2,1)S(1)} %get-tuple-element.27), channel_id=1, source_target_pairs={{0,8},{4,12},{8,0},{12,4},{1,9},{5,13},{9,1},{13,5},{2,10},{6,14},... | collective-permute-start | bytes 178184 | tf_op jit(solution)/shard_map/ppermute | solution.py:207
  4.9 3.9 %collective-permute-start.2 = (bf16[8,3712]{1,0:T(8,128)(2,1)S(1)}, bf16[8,3712]{1,0:T(8,128)(2,1)S(1)}, u32[]{:S(2)}, u32[]{:S(2)}) collective-permute-start(bf16[8,3712]{1,0:T(8,128)(2,1)S(1)} %get-tuple-element.28), channel_id=1, source_target_pairs={{0,4},{4,0},{8,12},{12,8},{1,5},{5,1},{9,13},{13,9},{2,6},{6,2},{1... | collective-permute-start | bytes 178184 | tf_op jit(solution)/shard_map/ppermute | solution.py:207
  9.1 8.7 %collective-permute-start.3 = (bf16[16,1792]{1,0:T(8,128)(2,1)S(1)}, bf16[16,1792]{1,0:T(8,128)(2,1)S(1)}, u32[]{:S(2)}, u32[]{:S(2)}) collective-permute-start(bf16[16,1792]{1,0:T(8,128)(2,1)S(1)} %get-tuple-element.29.refs_6_), channel_id=1, source_target_pairs={{0,2},{1,3},{2,0},{3,1},{4,6},{5,7},{6,4},{7,5},{8,10},{9,11},{10,... | collective-permute-start | bytes 172040 | tf_op jit(solution)/shard_map/ppermute | solution.py:207
  11.8 6.0 %collective-permute-start.4 = (bf16[16,1792]{1,0:T(8,128)(2,1)S(1)}, bf16[16,1792]{1,0:T(8,128)(2,1)S(1)}, u32[]{:S(2)}, u32[]{:S(2)}) collective-permute-start(bf16[16,1792]{1,0:T(8,128)(2,1)S(1)} %get-tuple-element.29.refs_6_), channel_id=1, source_target_pairs={{0,1},{1,0},{2,3},{3,2},{4,5},{5,4},{6,7},{7,6},{8,9},{9,8},{10,11... | collective-permute-start | bytes 172040 | tf_op jit(solution)/shard_map/ppermute | solution.py:207
  13.4 6.7 %collective-permute-start.7 = (bf16[16,1792]{1,0:T(8,128)(2,1)S(1)}, bf16[16,1792]{1,0:T(8,128)(2,1)S(1)}, u32[]{:S(2)}, u32[]{:S(2)}) collective-permute-start(bf16[16,1792]{1,0:T(8,128)(2,1)S(1)} %get-tuple-element.30.refs_7_), channel_id=1, source_target_pairs={{0,3},{1,2},{2,1},{3,0},{4,7},{5,6},{6,5},{7,4},{8,11},{9,10},{10,... | collective-permute-start | bytes 172040 | tf_op jit(solution)/shard_map/ppermute | solution.py:207
  13.6 6.5 %collective-permute-start.6 = (bf16[16,1792]{1,0:T(8,128)(2,1)S(1)}, bf16[16,1792]{1,0:T(8,128)(2,1)S(1)}, u32[]{:S(2)}, u32[]{:S(2)}) collective-permute-start(bf16[16,1792]{1,0:T(8,128)(2,1)S(1)} %get-tuple-element.30.refs_7_), channel_id=1, source_target_pairs={{0,2},{1,3},{2,0},{3,1},{4,6},{5,7},{6,4},{7,5},{8,10},{9,11},{10,... | collective-permute-start | bytes 172040 | tf_op jit(solution)/shard_map/ppermute | solution.py:207
  15.3 5.8 %collective-permute-start.5 = (bf16[16,1792]{1,0:T(8,128)(2,1)S(1)}, bf16[16,1792]{1,0:T(8,128)(2,1)S(1)}, u32[]{:S(2)}, u32[]{:S(2)}) collective-permute-start(bf16[16,1792]{1,0:T(8,128)(2,1)S(1)} %get-tuple-element.30.refs_7_), channel_id=1, source_target_pairs={{0,1},{1,0},{2,3},{3,2},{4,5},{5,4},{6,7},{7,6},{8,9},{9,8},{10,11... | collective-permute-start | bytes 172040 | tf_op jit(solution)/shard_map/ppermute | solution.py:207
  17.8 4.2 %collective-permute-start.8 = (bf16[16,1792]{1,0:T(8,128)(2,1)S(1)}, bf16[16,1792]{1,0:T(8,128)(2,1)S(1)}, u32[]{:S(2)}, u32[]{:S(2)}) collective-permute-start(bf16[16,1792]{1,0:T(8,128)(2,1)S(1)} %collective-permute-done.3.refs_0_), channel_id=1, source_target_pairs={{0,1},{1,0},{2,3},{3,2},{4,5},{5,4},{6,7},{7,6},{8,9},{9,8},{10,11... | collective-permute-start | bytes 172040 | tf_op jit(solution)/shard_map/ppermute | solution.py:207
  23.4 6.6 %collective-permute-start.11 = (bf16[64,512]{1,0:T(8,128)(2,1)S(1)}, bf16[64,512]{1,0:T(8,128)(2,1)S(1)}, u32[]{:S(2)}, u32[]{:S(2)}) collective-permute-start(bf16[64,512]{1,0:T(8,128)(2,1)S(1)} %hidden.1.after_ref.refs_0_), channel_id=1, source_target_pairs={{0,3},{1,2},{2,1},{3,0},{4,7},{5,6},{6,5},{7,4},{8,11},{9,10},{10,... | collective-permute-start | bytes 196616 | tf_op jit(solution)/shard_map/ppermute | solution.py:207
  26.8 5.3 %collective-permute-start.10 = (bf16[64,512]{1,0:T(8,128)(2,1)S(1)}, bf16[64,512]{1,0:T(8,128)(2,1)S(1)}, u32[]{:S(2)}, u32[]{:S(2)}) collective-permute-start(bf16[64,512]{1,0:T(8,128)(2,1)S(1)} %hidden.1.after_ref.refs_0_), channel_id=1, source_target_pairs={{0,2},{1,3},{2,0},{3,1},{4,6},{5,7},{6,4},{7,5},{8,10},{9,11},{10,... | collective-permute-start | bytes 196616 | tf_op jit(solution)/shard_map/ppermute | solution.py:207
  26.8 5.3 %collective-permute-start.9 = (bf16[64,512]{1,0:T(8,128)(2,1)S(1)}, bf16[64,512]{1,0:T(8,128)(2,1)S(1)}, u32[]{:S(2)}, u32[]{:S(2)}) collective-permute-start(bf16[64,512]{1,0:T(8,128)(2,1)S(1)} %hidden.1.after_ref.refs_0_), channel_id=1, source_target_pairs={{0,1},{1,0},{2,3},{3,2},{4,5},{5,4},{6,7},{7,6},{8,9},{9,8},{10,11... | collective-permute-start | bytes 196616 | tf_op jit(solution)/shard_map/ppermute | solution.py:207
  32.9 5.7 %collective-permute-start.12 = (bf16[16,896]{1,0:T(8,128)(2,1)S(1)}, bf16[16,896]{1,0:T(8,128)(2,1)S(1)}, u32[]{:S(2)}, u32[]{:S(2)}) collective-permute-start(bf16[16,896]{1,0:T(8,128)(2,1)S(1)} %get-tuple-element.35), channel_id=1, source_target_pairs={{0,3},{1,2},{2,1},{3,0},{4,7},{5,6},{6,5},{7,4},{8,11},{9,10},{10,... | collective-permute-start | bytes 86024 | tf_op jit(solution)/shard_map/ppermute | solution.py:207
  34.7 5.1 %collective-permute-start.13 = (bf16[16,896]{1,0:T(8,128)(2,1)S(1)}, bf16[16,896]{1,0:T(8,128)(2,1)S(1)}, u32[]{:S(2)}, u32[]{:S(2)}) collective-permute-start(bf16[16,896]{1,0:T(8,128)(2,1)S(1)} %get-tuple-element.36), channel_id=1, source_target_pairs={{0,2},{1,3},{2,0},{3,1},{4,6},{5,7},{6,4},{7,5},{8,10},{9,11},{10,... | collective-permute-start | bytes 86024 | tf_op jit(solution)/shard_map/ppermute | solution.py:207
  34.9 4.8 %collective-permute-start.14 = (bf16[16,896]{1,0:T(8,128)(2,1)S(1)}, bf16[16,896]{1,0:T(8,128)(2,1)S(1)}, u32[]{:S(2)}, u32[]{:S(2)}) collective-permute-start(bf16[16,896]{1,0:T(8,128)(2,1)S(1)} %get-tuple-element.37), channel_id=1, source_target_pairs={{0,1},{1,0},{2,3},{3,2},{4,5},{5,4},{6,7},{7,6},{8,9},{9,8},{10,11... | collective-permute-start | bytes 86024 | tf_op jit(solution)/shard_map/ppermute | solution.py:207
  39.9 4.2 %collective-permute-start.15 = (bf16[4,8,896]{2,1,0:T(8,128)(2,1)S(1)}, bf16[4,8,896]{2,1,0:T(8,128)(2,1)S(1)}, u32[]{:S(2)}, u32[]{:S(2)}) collective-permute-start(bf16[4,8,896]{2,1,0:T(8,128)(2,1)S(1)} %get-tuple-element.39), channel_id=1, source_target_pairs={{0,12},{4,8},{8,4},{12,0},{1,13},{5,9},{9,5},{13,1},{2,14},{6,10},... | collective-permute-start | bytes 172040 | tf_op jit(solution)/shard_map/ppermute | solution.py:207
  40.0 4.8 %collective-permute-start.16 = (bf16[4,8,896]{2,1,0:T(8,128)(2,1)S(1)}, bf16[4,8,896]{2,1,0:T(8,128)(2,1)S(1)}, u32[]{:S(2)}, u32[]{:S(2)}) collective-permute-start(bf16[4,8,896]{2,1,0:T(8,128)(2,1)S(1)} %get-tuple-element.40), channel_id=1, source_target_pairs={{0,8},{4,12},{8,0},{12,4},{1,9},{5,13},{9,1},{13,5},{2,10},{6,14},... | collective-permute-start | bytes 172040 | tf_op jit(solution)/shard_map/ppermute | solution.py:207
  41.2 3.6 %collective-permute-start.17 = (bf16[4,8,896]{2,1,0:T(8,128)(2,1)S(1)}, bf16[4,8,896]{2,1,0:T(8,128)(2,1)S(1)}, u32[]{:S(2)}, u32[]{:S(2)}) collective-permute-start(bf16[4,8,896]{2,1,0:T(8,128)(2,1)S(1)} %get-tuple-element.41), channel_id=1, source_target_pairs={{0,4},{4,0},{8,12},{12,8},{1,5},{5,1},{9,13},{13,9},{2,6},{6,2},{1... | collective-permute-start | bytes 172040 | tf_op jit(solution)/shard_map/ppermute | solution.py:207

commit v9 on v8

--- a/solution.py
+++ b/solution.py
@@ -116,11 +116,11 @@
         copy.wait()
 
 
-def compact_kernel(groups, slots, after_ref, *refs):
+def compact_kernel(groups, slots, parts, after_ref, *refs):
     del after_ref
     arrived, outs, pick_ref = refs[:groups][::-1], refs[groups:-1], refs[-1]
-    rows, part = groups * CAP, outs[0].shape[1]
-    features = part * len(outs)
+    rows = groups * CAP
+    features = arrived[0].shape[1] - LANES
     live = jnp.concatenate([a[:, features:].astype(F32) for a in arrived], axis=0)
     row = lax.broadcasted_iota(jnp.int32, (rows, rows), 0)
     column = lax.broadcasted_iota(jnp.int32, (rows, rows), 1)
@@ -133,8 +133,9 @@
         at = slice(c * step, (c + 1) * step)
         whole = jnp.concatenate([a[:, at].astype(F32) for a in arrived], axis=0).astype(BF16)
         moved = lax.dot_general(pick[:, :slots], whole, (((0,), (0,)), ((), ())), preferred_element_type=F32)
-        first = c * step % part
-        outs[c * step // part][:, first : first + step] = moved.astype(BF16)
+        for (first, last), out in zip(parts, outs):
+            if first <= c * step < last:
+                out[:, c * step - first : (c + 1) * step - first] = moved.astype(BF16)
 
 
 def hidden_kernel(columns, halved, *refs):
@@ -142,7 +143,7 @@
     units = gate_ref.shape[1]
     blocks = [block[...] for block in blocks]
     if halved:
-        low, near_low, near_high, high, far_high, far_low, own_low, own_high = blocks
+        low, near_high, high, far_high, near_low, far_low, own_low, own_high = blocks
         pairs = [(own_low, own_high), (near_low, near_high), (low, high), (far_low, far_high)]
         blocks = [jnp.concatenate(pair, axis=1) for pair in pairs]
     rows = jnp.concatenate(blocks, axis=0)
@@ -249,21 +250,24 @@
         name="load",
     )(outbound[0], *weights[:2])
 
-    parts = 2 if columns == 4 else 1
+    cut = features * 3 // 7 // 256 * 256
+    parts = [(0, cut), (cut, features), (0, cut)] if columns == 4 else [(0, features)]
     *own, pick = pl.pallas_call(
-        functools.partial(compact_kernel, groups, slots),
-        out_shape=[jax.ShapeDtypeStruct((slots, features // parts), BF16)] * parts
+        functools.partial(compact_kernel, groups, slots, parts),
+        out_shape=[jax.ShapeDtypeStruct((slots, last - first), BF16) for first, last in parts]
         + [jax.ShapeDtypeStruct((groups * CAP, LANES), BF16)],
         in_specs=[ANY] + [VMEM] * groups,
-        out_specs=[VMEM] * (parts + 1),
-        compiler_params=params(2 * (groups * CAP + slots) * wide),
+        out_specs=[VMEM] * (len(parts) + 1),
+        compiler_params=params(2 * (groups * CAP + 2 * slots) * wide),
         name="compact",
     )(gate, *arrived)
     if columns == 4:
-        near_low, near_high, high, far_high = [swap(part, "ing", e) for part, e in zip(own + own[1:] * 2, (1, 1, 2, 3))]
-        low = swap(own[0], "ing", 2)
+        own_low, own_high, own_again = own
+        near_high, high, far_high = [swap(own_high, "ing", e) for e in (1, 2, 3)]
+        low = swap(own_low, "ing", 2)
         far_low = swap(low, "ing", 1)
-        blocks = [low, near_low, near_high, high, far_high, far_low] + own
+        near_low = swap(own_again, "ing", 1)
+        blocks = [low, near_high, high, far_high, near_low, far_low, own_low, own_high]
     else:
         blocks = [swap(own[0], "ing", e) for e in range(columns)]
 

time: 46.6 us -> 47 us (level)
  starting transfers between devices: 22.7 us -> 23.3 us
    ppermute x18, starting transfers between devices: 22.7 us -> 23.3 us  [swap(): lax.ppermute(x, name, [(a, a ^ step) for a in range(lax.axis_size(name))])]
  transfers between devices with their start and end apart: 18 -> 18, of which waited for: 10 -> 9; matrix products, arithmetic and copies ran while one was open for 0% -> 0% of each run, Pallas kernels for 11% -> 11%
where the time goes in v9:
time: 47 us; the launch traced here: 46.8 us
  starting transfers between devices  23.3 us (50%)
  waiting for transfers between devices  12.2 us (26%)
  Pallas kernels  11.2 us (24%)
    ppermute x18, starting transfers between devices, swap(): lax.ppermute(x, name, [(a, a ^ step) for a in range(lax.axis_size(name))])  23.3 us
    ppermute x18, waiting for transfers between devices, swap(): lax.ppermute(x, name, [(a, a ^ step) for a in range(lax.axis_size(name))])  12.2 us
    pallas_call x1, Pallas kernels, local(): pl.pallas_call(load_kernel, out_shape=[pltpu.VMEM(w.shape, BF16) for w in...  3.17 us
    pallas_call x1, Pallas kernels, local(): pl.pallas_call(functools.partial(prepare_kernel, groups), out_shape=[pltp...  2.13 us
    pallas_call x1, Pallas kernels, local(): pl.pallas_call(functools.partial(dispatch_kernel, groups, features // 2),...  1.79 us
    pallas_call x1, Pallas kernels, local(): pl.pallas_call(functools.partial(combine_kernel, groups, columns), out_sh...  1.49 us
    pallas_call x1, Pallas kernels, local(): pl.pallas_call(functools.partial(hidden_kernel, columns, columns == 4), o...  1.4 us
  transfers between devices with their start and end apart: 18, of which 9 were waited for; matrix products, arithmetic and copies ran while one was open for 0% of the time, Pallas kernels for 11%

profile of v9, /device:TPU:0, one launch (start us, length us, event | category | flops | bytes accessed | tf_op | source)
XLA Modules:
  0.0 46.8 jit_solution(3054167473896341217)
XLA Ops:
  0.0 1.8 %dispatch.1 = (bf16[8,3712]{1,0:T(8,128)(2,1)S(1)}, bf16[8,3712]{1,0:T(8,128)(2,1)S(1)}, bf16[8,3712]{1,0:T(8,128)(2,1)S(1)}, bf16[8,3712]{1,0:T(8,128)(2,1)S(1)}) custom-call(s32[8,256]{1,0:T(8,128)} %bitcast.9, bf16[256,3584]{1,0:T(8,128)(2,1)} %tokens_ref.1), custom_call_target="tpu_custom_call" | custom-call | tf_op jit(solution)/shard_map/dispatch/pallas_call | solution.py:225
  1.8 2.4 %collective-permute-start = (bf16[8,3712]{1,0:T(8,128)(2,1)S(1)}, bf16[8,3712]{1,0:T(8,128)(2,1)S(1)}, u32[]{:S(2)}, u32[]{:S(2)}) collective-permute-start(bf16[8,3712]{1,0:T(8,128)(2,1)S(1)} %get-tuple-element.27), channel_id=1, source_target_pairs={{0,12},{4,8},{8,4},{12,0},{1,13},{5,9},{9,5},{13,1},{2,14},{6,10},... | collective-permute-start | bytes 178184 | tf_op jit(solution)/shard_map/ppermute | solution.py:208
  4.2 0.6 %collective-permute-start.1 = (bf16[8,3712]{1,0:T(8,128)(2,1)S(1)}, bf16[8,3712]{1,0:T(8,128)(2,1)S(1)}, u32[]{:S(2)}, u32[]{:S(2)}) collective-permute-start(bf16[8,3712]{1,0:T(8,128)(2,1)S(1)} %get-tuple-element.28), channel_id=1, source_target_pairs={{0,8},{4,12},{8,0},{12,4},{1,9},{5,13},{9,1},{13,5},{2,10},{6,14},... | collective-permute-start | bytes 178184 | tf_op jit(solution)/shard_map/ppermute | solution.py:208
  4.9 3.2 %load.1 = (bf16[3584,512]{1,0:T(8,128)(2,1)S(1)}, bf16[3584,512]{1,0:T(8,128)(2,1)S(1)}) custom-call(bf16[8,3712]{1,0:T(8,128)(2,1)S(1)} %get-tuple-element.25.after_ref.refs_3_, bf16[3584,512]{1,0:T(8,128)(2,1)} %bitcast.5, bf16[3584,512]{1,0:T(8,128)(2,1)} %bitcast.6), custom_call_target="tpu_custom_call" | custom-call | tf_op jit(solution)/shard_map/load/pallas_call | solution.py:243
  8.1 0.7 %collective-permute-done.1.refs_1_ = bf16[8,3712]{1,0:T(8,128)(2,1)S(1)} collective-permute-done((bf16[8,3712]{1,0:T(8,128)(2,1)S(1)}, bf16[8,3712]{1,0:T(8,128)(2,1)S(1)}, u32[]{:S(2)}, u32[]{:S(2)}) %collective-permute-start.1) | collective-permute-done | bytes 59424 | tf_op jit(solution)/shard_map/ppermute | solution.py:208
  8.8 0.3 compact.1
  9.1 2.7 %collective-permute-start.3 = (bf16[16,1536]{1,0:T(8,128)(2,1)S(1)}, bf16[16,1536]{1,0:T(8,128)(2,1)S(1)}, u32[]{:S(2)}, u32[]{:S(2)}) collective-permute-start(bf16[16,1536]{1,0:T(8,128)(2,1)S(1)} %get-tuple-element.30.refs_6_), channel_id=1, source_target_pairs={{0,2},{1,3},{2,0},{3,1},{4,6},{5,7},{6,4},{7,5},{8,10},{9,11},{10,... | collective-permute-start | bytes 147464 | tf_op jit(solution)/shard_map/ppermute | solution.py:208
  11.8 1.3 %collective-permute-start.6 = (bf16[16,2048]{1,0:T(8,128)(2,1)S(1)}, bf16[16,2048]{1,0:T(8,128)(2,1)S(1)}, u32[]{:S(2)}, u32[]{:S(2)}) collective-permute-start(bf16[16,2048]{1,0:T(8,128)(2,1)S(1)} %get-tuple-element.31.refs_7_), channel_id=1, source_target_pairs={{0,3},{1,2},{2,1},{3,0},{4,7},{5,6},{6,5},{7,4},{8,11},{9,10},{10,... | collective-permute-start | bytes 196616 | tf_op jit(solution)/shard_map/ppermute | solution.py:208
  13.2 1.7 %collective-permute-start.5 = (bf16[16,2048]{1,0:T(8,128)(2,1)S(1)}, bf16[16,2048]{1,0:T(8,128)(2,1)S(1)}, u32[]{:S(2)}, u32[]{:S(2)}) collective-permute-start(bf16[16,2048]{1,0:T(8,128)(2,1)S(1)} %get-tuple-element.31.refs_7_), channel_id=1, source_target_pairs={{0,2},{1,3},{2,0},{3,1},{4,6},{5,7},{6,4},{7,5},{8,10},{9,11},{10,... | collective-permute-start | bytes 196616 | tf_op jit(solution)/shard_map/ppermute | solution.py:208
  14.9 1.3 %collective-permute-start.4 = (bf16[16,2048]{1,0:T(8,128)(2,1)S(1)}, bf16[16,2048]{1,0:T(8,128)(2,1)S(1)}, u32[]{:S(2)}, u32[]{:S(2)}) collective-permute-start(bf16[16,2048]{1,0:T(8,128)(2,1)S(1)} %get-tuple-element.31.refs_7_), channel_id=1, source_target_pairs={{0,1},{1,0},{2,3},{3,2},{4,5},{5,4},{6,7},{7,6},{8,9},{9,8},{10,11... | collective-permute-start | bytes 196616 | tf_op jit(solution)/shard_map/ppermute | solution.py:208
  16.2 0.7 %collective-permute-start.7 = (bf16[16,1536]{1,0:T(8,128)(2,1)S(1)}, bf16[16,1536]{1,0:T(8,128)(2,1)S(1)}, u32[]{:S(2)}, u32[]{:S(2)}) collective-permute-start(bf16[16,1536]{1,0:T(8,128)(2,1)S(1)} %get-tuple-element.32), channel_id=1, source_target_pairs={{0,1},{1,0},{2,3},{3,2},{4,5},{5,4},{6,7},{7,6},{8,9},{9,8},{10,11... | collective-permute-start | bytes 147464 | tf_op jit(solution)/shard_map/ppermute | solution.py:208
  16.9 1.4 %collective-permute-start.8 = (bf16[16,1536]{1,0:T(8,128)(2,1)S(1)}, bf16[16,1536]{1,0:T(8,128)(2,1)S(1)}, u32[]{:S(2)}, u32[]{:S(2)}) collective-permute-start(bf16[16,1536]{1,0:T(8,128)(2,1)S(1)} %collective-permute-done.3.refs_0_), channel_id=1, source_target_pairs={{0,1},{1,0},{2,3},{3,2},{4,5},{5,4},{6,7},{7,6},{8,9},{9,8},{10,11... | collective-permute-start | bytes 147464 | tf_op jit(solution)/shard_map/ppermute | solution.py:208
  18.3 3.5 %collective-permute-done.7.refs_4_ = bf16[16,1536]{1,0:T(8,128)(2,1)S(1)} collective-permute-done((bf16[16,1536]{1,0:T(8,128)(2,1)S(1)}, bf16[16,1536]{1,0:T(8,128)(2,1)S(1)}, u32[]{:S(2)}, u32[]{:S(2)}) %collective-permute-start.7) | collective-permute-done | bytes 49184 | tf_op jit(solution)/shard_map/ppermute | solution.py:208
  21.8 0.5 %collective-permute-done.8.refs_5_ = bf16[16,1536]{1,0:T(8,128)(2,1)S(1)} collective-permute-done((bf16[16,1536]{1,0:T(8,128)(2,1)S(1)}, bf16[16,1536]{1,0:T(8,128)(2,1)S(1)}, u32[]{:S(2)}, u32[]{:S(2)}) %collective-permute-start.8) | collective-permute-done | bytes 49184 | tf_op jit(solution)/shard_map/ppermute | solution.py:208
  22.3 1.4 %hidden.1.after_ref.refs_0_ = bf16[64,512]{1,0:T(8,128)(2,1)S(1)} custom-call(bf16[16,1536]{1,0:T(8,128)(2,1)S(1)} %collective-permute-done.3.refs_0_, bf16[16,2048]{1,0:T(8,128)(2,1)S(1)} %collective-permute-done.4.refs_1_, bf16[16,2048]{1,0:T(8,128)(2,1)S(1)} %collective-permute-done.5.refs_2_, bf16[16,2048]{1,0:T(8,128)(2,1)S(1)} %collective-permute-done.6.refs_3_, ...), custom_call_target="tpu_custom_call" | custom-call | tf_op jit(solution)/shard_map/hidden/pallas_call | solution.py:274
  23.7 3.4 %collective-permute-start.11 = (bf16[64,512]{1,0:T(8,128)(2,1)S(1)}, bf16[64,512]{1,0:T(8,128)(2,1)S(1)}, u32[]{:S(2)}, u32[]{:S(2)}) collective-permute-start(bf16[64,512]{1,0:T(8,128)(2,1)S(1)} %hidden.1.after_ref.refs_0_), channel_id=1, source_target_pairs={{0,3},{1,2},{2,1},{3,0},{4,7},{5,6},{6,5},{7,4},{8,11},{9,10},{10,... | collective-permute-start | bytes 196616 | tf_op jit(solution)/shard_map/ppermute | solution.py:208
  27.1 1.0 %collective-permute-start.9 = (bf16[64,512]{1,0:T(8,128)(2,1)S(1)}, bf16[64,512]{1,0:T(8,128)(2,1)S(1)}, u32[]{:S(2)}, u32[]{:S(2)}) collective-permute-start(bf16[64,512]{1,0:T(8,128)(2,1)S(1)} %hidden.1.after_ref.refs_0_), channel_id=1, source_target_pairs={{0,1},{1,0},{2,3},{3,2},{4,5},{5,4},{6,7},{7,6},{8,9},{9,8},{10,11... | collective-permute-start | bytes 196616 | tf_op jit(solution)/shard_map/ppermute | solution.py:208
  28.2 2.1 %prepare.1 = (bf16[2048,896]{1,0:T(8,128)(2,1)S(1)}, bf16[256,32]{1,0:T(8,128)(2,1)S(1)}) custom-call(bf16[64,512]{1,0:T(8,128)(2,1)S(1)} %hidden.1.after_ref.refs_0_, s32[8,256]{1,0:T(8,128)} %bitcast.10, f32[96,256]{1,0:T(8,128)} %bitcast.8, bf16[2048,896]{1,0:T(8,128)(2,1)} %bitcast.7), custom_call_target="tpu_custom_call" | custom-call | tf_op jit(solution)/shard_map/prepare/pallas_call | solution.py:282
  30.3 0.2 collective-permute-done.11.refs_3_
  30.5 1.9 %collective-permute-done.10.refs_2_ = bf16[64,512]{1,0:T(8,128)(2,1)S(1)} collective-permute-done((bf16[64,512]{1,0:T(8,128)(2,1)S(1)}, bf16[64,512]{1,0:T(8,128)(2,1)S(1)}, u32[]{:S(2)}, u32[]{:S(2)}) %collective-permute-start.10) | collective-permute-done | bytes 65568 | tf_op jit(solution)/shard_map/ppermute | solution.py:208
  32.3 0.7 %down.1 = (bf16[16,896]{1,0:T(8,128)(2,1)S(1)}, bf16[16,896]{1,0:T(8,128)(2,1)S(1)}, bf16[16,896]{1,0:T(8,128)(2,1)S(1)}, bf16[16,896]{1,0:T(8,128)(2,1)S(1)}) custom-call(bf16[64,512]{1,0:T(8,128)(2,1)S(1)} %hidden.1.after_ref.refs_0_, bf16[64,512]{1,0:T(8,128)(2,1)S(1)} %collective-permute-done.9.refs_1_, ...), custom_call_target="tpu_custom_call" | custom-call | tf_op jit(solution)/shard_map/down/pallas_call | solution.py:300
  33.1 1.9 %collective-permute-start.12 = (bf16[16,896]{1,0:T(8,128)(2,1)S(1)}, bf16[16,896]{1,0:T(8,128)(2,1)S(1)}, u32[]{:S(2)}, u32[]{:S(2)}) collective-permute-start(bf16[16,896]{1,0:T(8,128)(2,1)S(1)} %get-tuple-element.37), channel_id=1, source_target_pairs={{0,3},{1,2},{2,1},{3,0},{4,7},{5,6},{6,5},{7,4},{8,11},{9,10},{10,... | collective-permute-start | bytes 86024 | tf_op jit(solution)/shard_map/ppermute | solution.py:208
  35.0 0.2 collective-permute-start.13
  35.2 2.3 %collective-permute-start.14 = (bf16[16,896]{1,0:T(8,128)(2,1)S(1)}, bf16[16,896]{1,0:T(8,128)(2,1)S(1)}, u32[]{:S(2)}, u32[]{:S(2)}) collective-permute-start(bf16[16,896]{1,0:T(8,128)(2,1)S(1)} %get-tuple-element.39), channel_id=1, source_target_pairs={{0,1},{1,0},{2,3},{3,2},{4,5},{5,4},{6,7},{7,6},{8,9},{9,8},{10,11... | collective-permute-start | bytes 86024 | tf_op jit(solution)/shard_map/ppermute | solution.py:208
  37.5 1.3 %collective-permute-done.12.refs_0_ = bf16[16,896]{1,0:T(8,128)(2,1)S(1)} collective-permute-done((bf16[16,896]{1,0:T(8,128)(2,1)S(1)}, bf16[16,896]{1,0:T(8,128)(2,1)S(1)}, u32[]{:S(2)}, u32[]{:S(2)}) %collective-permute-start.12) | collective-permute-done | bytes 28704 | tf_op jit(solution)/shard_map/ppermute | solution.py:208
  38.8 1.2 %collective-permute-done.13.refs_1_ = bf16[16,896]{1,0:T(8,128)(2,1)S(1)} collective-permute-done((bf16[16,896]{1,0:T(8,128)(2,1)S(1)}, bf16[16,896]{1,0:T(8,128)(2,1)S(1)}, u32[]{:S(2)}, u32[]{:S(2)}) %collective-permute-start.13) | collective-permute-done | bytes 28704 | tf_op jit(solution)/shard_map/ppermute | solution.py:208
  40.1 0.2 spread.1
  40.2 0.1 collective-permute-start.15
  40.3 2.0 %collective-permute-start.16 = (bf16[4,8,896]{2,1,0:T(8,128)(2,1)S(1)}, bf16[4,8,896]{2,1,0:T(8,128)(2,1)S(1)}, u32[]{:S(2)}, u32[]{:S(2)}) collective-permute-start(bf16[4,8,896]{2,1,0:T(8,128)(2,1)S(1)} %get-tuple-element.42), channel_id=1, source_target_pairs={{0,8},{4,12},{8,0},{12,4},{1,9},{5,13},{9,1},{13,5},{2,10},{6,14},... | collective-permute-start | bytes 172040 | tf_op jit(solution)/shard_map/ppermute | solution.py:208
  42.4 1.7 %collective-permute-done.15.refs_0_ = bf16[4,8,896]{2,1,0:T(8,128)(2,1)S(1)} collective-permute-done((bf16[4,8,896]{2,1,0:T(8,128)(2,1)S(1)}, bf16[4,8,896]{2,1,0:T(8,128)(2,1)S(1)}, u32[]{:S(2)}, u32[]{:S(2)}) %collective-permute-start.15) | collective-permute-done | bytes 57376 | tf_op jit(solution)/shard_map/ppermute | solution.py:208
  44.1 1.2 %collective-permute-done.16.refs_1_ = bf16[4,8,896]{2,1,0:T(8,128)(2,1)S(1)} collective-permute-done((bf16[4,8,896]{2,1,0:T(8,128)(2,1)S(1)}, bf16[4,8,896]{2,1,0:T(8,128)(2,1)S(1)}, u32[]{:S(2)}, u32[]{:S(2)}) %collective-permute-start.16) | collective-permute-done | bytes 57376 | tf_op jit(solution)/shard_map/ppermute | solution.py:208
  45.3 1.5 %combine.1 = bf16[256,3584]{1,0:T(8,128)(2,1)} custom-call(bf16[256,32]{1,0:T(8,128)(2,1)S(1)} %get-tuple-element.34.mixing_ref, bf16[4,8,896]{2,1,0:T(8,128)(2,1)S(1)} %collective-permute-done.15.refs_0_, bf16[4,8,896]{2,1,0:T(8,128)(2,1)S(1)} %collective-permute-done.16.refs_1_, bf16[4,8,896]{2,1,0:T(8,128)(2,1)S(1)} %collective-permute-done.17.refs_2_, ...), custom_call_target="tpu_custom_call" | custom-call | tf_op jit(solution)/shard_map/combine/pallas_call | solution.py:325
  (12 shorter events, 0.1 us)
Async XLA Ops:
  1.8 6.3 %collective-permute-start = (bf16[8,3712]{1,0:T(8,128)(2,1)S(1)}, bf16[8,3712]{1,0:T(8,128)(2,1)S(1)}, u32[]{:S(2)}, u32[]{:S(2)}) collective-permute-start(bf16[8,3712]{1,0:T(8,128)(2,1)S(1)} %get-tuple-element.27), channel_id=1, source_target_pairs={{0,12},{4,8},{8,4},{12,0},{1,13},{5,9},{9,5},{13,1},{2,14},{6,10},... | collective-permute-start | bytes 178184 | tf_op jit(solution)/shard_map/ppermute | solution.py:208
  4.2 4.5 %collective-permute-start.1 = (bf16[8,3712]{1,0:T(8,128)(2,1)S(1)}, bf16[8,3712]{1,0:T(8,128)(2,1)S(1)}, u32[]{:S(2)}, u32[]{:S(2)}) collective-permute-start(bf16[8,3712]{1,0:T(8,128)(2,1)S(1)} %get-tuple-element.28), channel_id=1, source_target_pairs={{0,8},{4,12},{8,0},{12,4},{1,9},{5,13},{9,1},{13,5},{2,10},{6,14},... | collective-permute-start | bytes 178184 | tf_op jit(solution)/shard_map/ppermute | solution.py:208
  4.9 3.9 %collective-permute-start.2 = (bf16[8,3712]{1,0:T(8,128)(2,1)S(1)}, bf16[8,3712]{1,0:T(8,128)(2,1)S(1)}, u32[]{:S(2)}, u32[]{:S(2)}) collective-permute-start(bf16[8,3712]{1,0:T(8,128)(2,1)S(1)} %get-tuple-element.29), channel_id=1, source_target_pairs={{0,4},{4,0},{8,12},{12,8},{1,5},{5,1},{9,13},{13,9},{2,6},{6,2},{1... | collective-permute-start | bytes 178184 | tf_op jit(solution)/shard_map/ppermute | solution.py:208
  9.1 7.8 %collective-permute-start.3 = (bf16[16,1536]{1,0:T(8,128)(2,1)S(1)}, bf16[16,1536]{1,0:T(8,128)(2,1)S(1)}, u32[]{:S(2)}, u32[]{:S(2)}) collective-permute-start(bf16[16,1536]{1,0:T(8,128)(2,1)S(1)} %get-tuple-element.30.refs_6_), channel_id=1, source_target_pairs={{0,2},{1,3},{2,0},{3,1},{4,6},{5,7},{6,4},{7,5},{8,10},{9,11},{10,... | collective-permute-start | bytes 147464 | tf_op jit(solution)/shard_map/ppermute | solution.py:208
  11.8 9.9 %collective-permute-start.6 = (bf16[16,2048]{1,0:T(8,128)(2,1)S(1)}, bf16[16,2048]{1,0:T(8,128)(2,1)S(1)}, u32[]{:S(2)}, u32[]{:S(2)}) collective-permute-start(bf16[16,2048]{1,0:T(8,128)(2,1)S(1)} %get-tuple-element.31.refs_7_), channel_id=1, source_target_pairs={{0,3},{1,2},{2,1},{3,0},{4,7},{5,6},{6,5},{7,4},{8,11},{9,10},{10,... | collective-permute-start | bytes 196616 | tf_op jit(solution)/shard_map/ppermute | solution.py:208
  13.2 8.6 %collective-permute-start.5 = (bf16[16,2048]{1,0:T(8,128)(2,1)S(1)}, bf16[16,2048]{1,0:T(8,128)(2,1)S(1)}, u32[]{:S(2)}, u32[]{:S(2)}) collective-permute-start(bf16[16,2048]{1,0:T(8,128)(2,1)S(1)} %get-tuple-element.31.refs_7_), channel_id=1, source_target_pairs={{0,2},{1,3},{2,0},{3,1},{4,6},{5,7},{6,4},{7,5},{8,10},{9,11},{10,... | collective-permute-start | bytes 196616 | tf_op jit(solution)/shard_map/ppermute | solution.py:208
  14.9 6.9 %collective-permute-start.4 = (bf16[16,2048]{1,0:T(8,128)(2,1)S(1)}, bf16[16,2048]{1,0:T(8,128)(2,1)S(1)}, u32[]{:S(2)}, u32[]{:S(2)}) collective-permute-start(bf16[16,2048]{1,0:T(8,128)(2,1)S(1)} %get-tuple-element.31.refs_7_), channel_id=1, source_target_pairs={{0,1},{1,0},{2,3},{3,2},{4,5},{5,4},{6,7},{7,6},{8,9},{9,8},{10,11... | collective-permute-start | bytes 196616 | tf_op jit(solution)/shard_map/ppermute | solution.py:208
  16.2 5.5 %collective-permute-start.7 = (bf16[16,1536]{1,0:T(8,128)(2,1)S(1)}, bf16[16,1536]{1,0:T(8,128)(2,1)S(1)}, u32[]{:S(2)}, u32[]{:S(2)}) collective-permute-start(bf16[16,1536]{1,0:T(8,128)(2,1)S(1)} %get-tuple-element.32), channel_id=1, source_target_pairs={{0,1},{1,0},{2,3},{3,2},{4,5},{5,4},{6,7},{7,6},{8,9},{9,8},{10,11... | collective-permute-start | bytes 147464 | tf_op jit(solution)/shard_map/ppermute | solution.py:208
  16.9 5.4 %collective-permute-start.8 = (bf16[16,1536]{1,0:T(8,128)(2,1)S(1)}, bf16[16,1536]{1,0:T(8,128)(2,1)S(1)}, u32[]{:S(2)}, u32[]{:S(2)}) collective-permute-start(bf16[16,1536]{1,0:T(8,128)(2,1)S(1)} %collective-permute-done.3.refs_0_), channel_id=1, source_target_pairs={{0,1},{1,0},{2,3},{3,2},{4,5},{5,4},{6,7},{7,6},{8,9},{9,8},{10,11... | collective-permute-start | bytes 147464 | tf_op jit(solution)/shard_map/ppermute | solution.py:208
  23.7 6.8 %collective-permute-start.11 = (bf16[64,512]{1,0:T(8,128)(2,1)S(1)}, bf16[64,512]{1,0:T(8,128)(2,1)S(1)}, u32[]{:S(2)}, u32[]{:S(2)}) collective-permute-start(bf16[64,512]{1,0:T(8,128)(2,1)S(1)} %hidden.1.after_ref.refs_0_), channel_id=1, source_target_pairs={{0,3},{1,2},{2,1},{3,0},{4,7},{5,6},{6,5},{7,4},{8,11},{9,10},{10,... | collective-permute-start | bytes 196616 | tf_op jit(solution)/shard_map/ppermute | solution.py:208
  27.1 5.2 %collective-permute-start.10 = (bf16[64,512]{1,0:T(8,128)(2,1)S(1)}, bf16[64,512]{1,0:T(8,128)(2,1)S(1)}, u32[]{:S(2)}, u32[]{:S(2)}) collective-permute-start(bf16[64,512]{1,0:T(8,128)(2,1)S(1)} %hidden.1.after_ref.refs_0_), channel_id=1, source_target_pairs={{0,2},{1,3},{2,0},{3,1},{4,6},{5,7},{6,4},{7,5},{8,10},{9,11},{10,... | collective-permute-start | bytes 196616 | tf_op jit(solution)/shard_map/ppermute | solution.py:208
  27.1 5.2 %collective-permute-start.9 = (bf16[64,512]{1,0:T(8,128)(2,1)S(1)}, bf16[64,512]{1,0:T(8,128)(2,1)S(1)}, u32[]{:S(2)}, u32[]{:S(2)}) collective-permute-start(bf16[64,512]{1,0:T(8,128)(2,1)S(1)} %hidden.1.after_ref.refs_0_), channel_id=1, source_target_pairs={{0,1},{1,0},{2,3},{3,2},{4,5},{5,4},{6,7},{7,6},{8,9},{9,8},{10,11... | collective-permute-start | bytes 196616 | tf_op jit(solution)/shard_map/ppermute | solution.py:208
  33.1 5.7 %collective-permute-start.12 = (bf16[16,896]{1,0:T(8,128)(2,1)S(1)}, bf16[16,896]{1,0:T(8,128)(2,1)S(1)}, u32[]{:S(2)}, u32[]{:S(2)}) collective-permute-start(bf16[16,896]{1,0:T(8,128)(2,1)S(1)} %get-tuple-element.37), channel_id=1, source_target_pairs={{0,3},{1,2},{2,1},{3,0},{4,7},{5,6},{6,5},{7,4},{8,11},{9,10},{10,... | collective-permute-start | bytes 86024 | tf_op jit(solution)/shard_map/ppermute | solution.py:208
  35.0 5.1 %collective-permute-start.13 = (bf16[16,896]{1,0:T(8,128)(2,1)S(1)}, bf16[16,896]{1,0:T(8,128)(2,1)S(1)}, u32[]{:S(2)}, u32[]{:S(2)}) collective-permute-start(bf16[16,896]{1,0:T(8,128)(2,1)S(1)} %get-tuple-element.38), channel_id=1, source_target_pairs={{0,2},{1,3},{2,0},{3,1},{4,6},{5,7},{6,4},{7,5},{8,10},{9,11},{10,... | collective-permute-start | bytes 86024 | tf_op jit(solution)/shard_map/ppermute | solution.py:208
  35.2 4.9 %collective-permute-start.14 = (bf16[16,896]{1,0:T(8,128)(2,1)S(1)}, bf16[16,896]{1,0:T(8,128)(2,1)S(1)}, u32[]{:S(2)}, u32[]{:S(2)}) collective-permute-start(bf16[16,896]{1,0:T(8,128)(2,1)S(1)} %get-tuple-element.39), channel_id=1, source_target_pairs={{0,1},{1,0},{2,3},{3,2},{4,5},{5,4},{6,7},{7,6},{8,9},{9,8},{10,11... | collective-permute-start | bytes 86024 | tf_op jit(solution)/shard_map/ppermute | solution.py:208
  40.2 3.8 %collective-permute-start.15 = (bf16[4,8,896]{2,1,0:T(8,128)(2,1)S(1)}, bf16[4,8,896]{2,1,0:T(8,128)(2,1)S(1)}, u32[]{:S(2)}, u32[]{:S(2)}) collective-permute-start(bf16[4,8,896]{2,1,0:T(8,128)(2,1)S(1)} %get-tuple-element.41), channel_id=1, source_target_pairs={{0,12},{4,8},{8,4},{12,0},{1,13},{5,9},{9,5},{13,1},{2,14},{6,10},... | collective-permute-start | bytes 172040 | tf_op jit(solution)/shard_map/ppermute | solution.py:208
  40.3 4.9 %collective-permute-start.16 = (bf16[4,8,896]{2,1,0:T(8,128)(2,1)S(1)}, bf16[4,8,896]{2,1,0:T(8,128)(2,1)S(1)}, u32[]{:S(2)}, u32[]{:S(2)}) collective-permute-start(bf16[4,8,896]{2,1,0:T(8,128)(2,1)S(1)} %get-tuple-element.42), channel_id=1, source_target_pairs={{0,8},{4,12},{8,0},{12,4},{1,9},{5,13},{9,1},{13,5},{2,10},{6,14},... | collective-permute-start | bytes 172040 | tf_op jit(solution)/shard_map/ppermute | solution.py:208
  42.3 2.9 %collective-permute-start.17 = (bf16[4,8,896]{2,1,0:T(8,128)(2,1)S(1)}, bf16[4,8,896]{2,1,0:T(8,128)(2,1)S(1)}, u32[]{:S(2)}, u32[]{:S(2)}) collective-permute-start(bf16[4,8,896]{2,1,0:T(8,128)(2,1)S(1)} %get-tuple-element.43), channel_id=1, source_target_pairs={{0,4},{4,0},{8,12},{12,8},{1,5},{5,1},{9,13},{13,9},{2,6},{6,2},{1... | collective-permute-start | bytes 172040 | tf_op jit(solution)/shard_map/ppermute | solution.py:208

commit v10 on v9

--- a/solution.py
+++ b/solution.py
@@ -38,13 +38,14 @@
 
 
 def placing(ids, groups, me, before):
-    rows, count = groups * CAP, ids.shape[1]
+    rows, count = max(groups, 8), ids.shape[1]
     row = lax.broadcasted_iota(jnp.int32, (rows, count), 0)
-    group = (row // CAP) ^ me
-    hit = named(ids, group * GROUP_EXPERTS)
+    hit = named(ids, jnp.where(row < groups, (row ^ me) * GROUP_EXPERTS, -1))
     rank = jnp.dot(hit.astype(BF16), before, preferred_element_type=F32)
-    slot = lax.rem(row, CAP).astype(F32)
-    return jnp.where((hit > 0.5) & (rank == slot + 1.0), 1.0, 0.0), group
+    slot = lax.broadcasted_iota(jnp.int32, (CAP, count), 0).astype(F32) + 1.0
+    seat = jnp.where(hit > 0.5, rank, 0.0)
+    place = [jnp.where(seat[d : d + 1, :] == slot, 1.0, 0.0) for d in range(groups)]
+    return jnp.concatenate(place, axis=0), rank[:, count - 1 :]
 
 
 def dispatch_kernel(groups, width, ids_ref, tokens_ref, *refs):
@@ -60,11 +61,12 @@
         copies[-1].start()
     before_ref[...] = upto(tokens_ref.shape[0])
     first.wait()
-    place, _ = placing(ids_held[...], groups, me, before_ref[...])
-    live = jnp.sum(place, axis=1, keepdims=True)
+    place, counts = placing(ids_held[...], groups, me, before_ref[...])
     place = place.astype(BF16)
+    slot = lax.broadcasted_iota(jnp.int32, (CAP, LANES), 0).astype(F32)
     for d in range(groups):
-        outs[d][:, features:] = jnp.broadcast_to(live[d * CAP : (d + 1) * CAP], (CAP, LANES)).astype(BF16)
+        live = slot < jnp.broadcast_to(counts[d : d + 1, :], (CAP, LANES))
+        outs[d][:, features:] = jnp.where(live, 1.0, 0.0).astype(BF16)
     for c in range(features // width):
         copies[c].wait()
         part = slice(c * width, (c + 1) * width)
@@ -103,7 +105,8 @@
         copy.wait()
     me = lax.axis_index("grp")
     ids = ids_held[...]
-    place, group = placing(ids, groups, me, upto(ids.shape[1]))
+    place, _ = placing(ids, groups, me, upto(ids.shape[1]))
+    group = (lax.broadcasted_iota(jnp.int32, place.shape, 0) // CAP) ^ me
     scores = 1.0 / (1.0 + jnp.exp(-logits_held[...]))
     expert = lax.broadcasted_iota(jnp.int32, scores.shape, 0)
     chosen = jnp.sum(jnp.where(named(ids, expert) > 0.5, scores, 0.0), axis=0, keepdims=True)
@@ -143,7 +146,7 @@
     units = gate_ref.shape[1]
     blocks = [block[...] for block in blocks]
     if halved:
-        low, near_high, high, far_high, near_low, far_low, own_low, own_high = blocks
+        low, near_low, near_high, high, far_high, far_low, own_low, own_high = blocks
         pairs = [(own_low, own_high), (near_low, near_high), (low, high), (far_low, far_high)]
         blocks = [jnp.concatenate(pair, axis=1) for pair in pairs]
     rows = jnp.concatenate(blocks, axis=0)
@@ -250,8 +253,8 @@
         name="load",
     )(outbound[0], *weights[:2])
 
-    cut = features * 3 // 7 // 256 * 256
-    parts = [(0, cut), (cut, features), (0, cut)] if columns == 4 else [(0, features)]
+    cut = features // 2
+    parts = [(0, cut), (cut, features)] if columns == 4 else [(0, features)]
     *own, pick = pl.pallas_call(
         functools.partial(compact_kernel, groups, slots, parts),
         out_shape=[jax.ShapeDtypeStruct((slots, last - first), BF16) for first, last in parts]
@@ -262,12 +265,10 @@
         name="compact",
     )(gate, *arrived)
     if columns == 4:
-        own_low, own_high, own_again = own
-        near_high, high, far_high = [swap(own_high, "ing", e) for e in (1, 2, 3)]
-        low = swap(own_low, "ing", 2)
+        near_low, near_high, high, far_high = [swap(part, "ing", e) for part, e in zip(own + own[1:] * 2, (1, 1, 2, 3))]
+        low = swap(own[0], "ing", 2)
         far_low = swap(low, "ing", 1)
-        near_low = swap(own_again, "ing", 1)
-        blocks = [low, near_high, high, far_high, near_low, far_low, own_low, own_high]
+        blocks = [low, near_low, near_high, high, far_high, far_low] + own
     else:
         blocks = [swap(own[0], "ing", e) for e in range(columns)]
 

time: 47 us -> 46.6 us (level)
  starting transfers between devices: 23.3 us -> 22.7 us
    ppermute x18, starting transfers between devices: 23.3 us -> 22.7 us  [swap(): lax.ppermute(x, name, [(a, a ^ step) for a in range(lax.axis_size(name))])]
  transfers between devices with their start and end apart: 18 -> 18, of which waited for: 9 -> 10; matrix products, arithmetic and copies ran while one was open for 0% -> 0% of each run, Pallas kernels for 11% -> 11%
where the time goes in v10:
time: 46.6 us; the launch traced here: 46.3 us
  starting transfers between devices  22.7 us (49%)
  waiting for transfers between devices  12.3 us (26%)
  Pallas kernels  11.2 us (24%)
    ppermute x18, starting transfers between devices, swap(): lax.ppermute(x, name, [(a, a ^ step) for a in range(lax.axis_size(name))])  22.7 us
    ppermute x18, waiting for transfers between devices, swap(): lax.ppermute(x, name, [(a, a ^ step) for a in range(lax.axis_size(name))])  12.3 us
    pallas_call x1, Pallas kernels, local(): pl.pallas_call(load_kernel, out_shape=[pltpu.VMEM(w.shape, BF16) for w in...  3.17 us
    pallas_call x1, Pallas kernels, local(): pl.pallas_call(functools.partial(prepare_kernel, groups), out_shape=[pltp...  2.13 us
    pallas_call x1, Pallas kernels, local(): pl.pallas_call(functools.partial(dispatch_kernel, groups, features // 2),...  1.79 us
    pallas_call x1, Pallas kernels, local(): pl.pallas_call(functools.partial(combine_kernel, groups, columns), out_sh...  1.49 us
    pallas_call x1, Pallas kernels, local(): pl.pallas_call(functools.partial(hidden_kernel, columns, columns == 4), o...  1.39 us
  transfers between devices with their start and end apart: 18, of which 10 were waited for; matrix products, arithmetic and copies ran while one was open for 0% of the time, Pallas kernels for 11%

profile of v10, /device:TPU:0, one launch (start us, length us, event | category | flops | bytes accessed | tf_op | source)
XLA Modules:
  0.0 46.3 jit_solution(9046109650777114788)
XLA Ops:
  0.0 1.8 %dispatch.1 = (bf16[8,3712]{1,0:T(8,128)(2,1)S(1)}, bf16[8,3712]{1,0:T(8,128)(2,1)S(1)}, bf16[8,3712]{1,0:T(8,128)(2,1)S(1)}, bf16[8,3712]{1,0:T(8,128)(2,1)S(1)}) custom-call(s32[8,256]{1,0:T(8,128)} %bitcast.9, bf16[256,3584]{1,0:T(8,128)(2,1)} %tokens_ref.1), custom_call_target="tpu_custom_call" | custom-call | tf_op jit(solution)/shard_map/dispatch/pallas_call | solution.py:228
  1.8 2.4 %collective-permute-start = (bf16[8,3712]{1,0:T(8,128)(2,1)S(1)}, bf16[8,3712]{1,0:T(8,128)(2,1)S(1)}, u32[]{:S(2)}, u32[]{:S(2)}) collective-permute-start(bf16[8,3712]{1,0:T(8,128)(2,1)S(1)} %get-tuple-element.26), channel_id=1, source_target_pairs={{0,12},{4,8},{8,4},{12,0},{1,13},{5,9},{9,5},{13,1},{2,14},{6,10},... | collective-permute-start | bytes 178184 | tf_op jit(solution)/shard_map/ppermute | solution.py:211
  4.2 0.6 %collective-permute-start.1 = (bf16[8,3712]{1,0:T(8,128)(2,1)S(1)}, bf16[8,3712]{1,0:T(8,128)(2,1)S(1)}, u32[]{:S(2)}, u32[]{:S(2)}) collective-permute-start(bf16[8,3712]{1,0:T(8,128)(2,1)S(1)} %get-tuple-element.27), channel_id=1, source_target_pairs={{0,8},{4,12},{8,0},{12,4},{1,9},{5,13},{9,1},{13,5},{2,10},{6,14},... | collective-permute-start | bytes 178184 | tf_op jit(solution)/shard_map/ppermute | solution.py:211
  4.9 3.2 %load.1 = (bf16[3584,512]{1,0:T(8,128)(2,1)S(1)}, bf16[3584,512]{1,0:T(8,128)(2,1)S(1)}) custom-call(bf16[8,3712]{1,0:T(8,128)(2,1)S(1)} %get-tuple-element.24.after_ref.refs_3_, bf16[3584,512]{1,0:T(8,128)(2,1)} %bitcast.5, bf16[3584,512]{1,0:T(8,128)(2,1)} %bitcast.6), custom_call_target="tpu_custom_call" | custom-call | tf_op jit(solution)/shard_map/load/pallas_call | solution.py:246
  8.1 0.7 %collective-permute-done.1.refs_1_ = bf16[8,3712]{1,0:T(8,128)(2,1)S(1)} collective-permute-done((bf16[8,3712]{1,0:T(8,128)(2,1)S(1)}, bf16[8,3712]{1,0:T(8,128)(2,1)S(1)}, u32[]{:S(2)}, u32[]{:S(2)}) %collective-permute-start.1) | collective-permute-done | bytes 59424 | tf_op jit(solution)/shard_map/ppermute | solution.py:211
  8.8 0.3 compact.1
  9.1 2.7 %collective-permute-start.3 = (bf16[16,1792]{1,0:T(8,128)(2,1)S(1)}, bf16[16,1792]{1,0:T(8,128)(2,1)S(1)}, u32[]{:S(2)}, u32[]{:S(2)}) collective-permute-start(bf16[16,1792]{1,0:T(8,128)(2,1)S(1)} %get-tuple-element.29.refs_6_), channel_id=1, source_target_pairs={{0,2},{1,3},{2,0},{3,1},{4,6},{5,7},{6,4},{7,5},{8,10},{9,11},{10,... | collective-permute-start | bytes 172040 | tf_op jit(solution)/shard_map/ppermute | solution.py:211
  11.8 1.6 %collective-permute-start.4 = (bf16[16,1792]{1,0:T(8,128)(2,1)S(1)}, bf16[16,1792]{1,0:T(8,128)(2,1)S(1)}, u32[]{:S(2)}, u32[]{:S(2)}) collective-permute-start(bf16[16,1792]{1,0:T(8,128)(2,1)S(1)} %get-tuple-element.29.refs_6_), channel_id=1, source_target_pairs={{0,1},{1,0},{2,3},{3,2},{4,5},{5,4},{6,7},{7,6},{8,9},{9,8},{10,11... | collective-permute-start | bytes 172040 | tf_op jit(solution)/shard_map/ppermute | solution.py:211
  13.4 0.2 collective-permute-start.7
  13.6 1.8 %collective-permute-start.6 = (bf16[16,1792]{1,0:T(8,128)(2,1)S(1)}, bf16[16,1792]{1,0:T(8,128)(2,1)S(1)}, u32[]{:S(2)}, u32[]{:S(2)}) collective-permute-start(bf16[16,1792]{1,0:T(8,128)(2,1)S(1)} %get-tuple-element.30.refs_7_), channel_id=1, source_target_pairs={{0,2},{1,3},{2,0},{3,1},{4,6},{5,7},{6,4},{7,5},{8,10},{9,11},{10,... | collective-permute-start | bytes 172040 | tf_op jit(solution)/shard_map/ppermute | solution.py:211
  15.3 2.5 %collective-permute-start.5 = (bf16[16,1792]{1,0:T(8,128)(2,1)S(1)}, bf16[16,1792]{1,0:T(8,128)(2,1)S(1)}, u32[]{:S(2)}, u32[]{:S(2)}) collective-permute-start(bf16[16,1792]{1,0:T(8,128)(2,1)S(1)} %get-tuple-element.30.refs_7_), channel_id=1, source_target_pairs={{0,1},{1,0},{2,3},{3,2},{4,5},{5,4},{6,7},{7,6},{8,9},{9,8},{10,11... | collective-permute-start | bytes 172040 | tf_op jit(solution)/shard_map/ppermute | solution.py:211
  17.8 2.2 %collective-permute-done.7.refs_4_ = bf16[16,1792]{1,0:T(8,128)(2,1)S(1)} collective-permute-done((bf16[16,1792]{1,0:T(8,128)(2,1)S(1)}, bf16[16,1792]{1,0:T(8,128)(2,1)S(1)}, u32[]{:S(2)}, u32[]{:S(2)}) %collective-permute-start.7) | collective-permute-done | bytes 57376 | tf_op jit(solution)/shard_map/ppermute | solution.py:211
  20.1 1.1 %collective-permute-done.5.refs_2_ = bf16[16,1792]{1,0:T(8,128)(2,1)S(1)} collective-permute-done((bf16[16,1792]{1,0:T(8,128)(2,1)S(1)}, bf16[16,1792]{1,0:T(8,128)(2,1)S(1)}, u32[]{:S(2)}, u32[]{:S(2)}) %collective-permute-start.5) | collective-permute-done | bytes 57376 | tf_op jit(solution)/shard_map/ppermute | solution.py:211
  21.2 0.8 %collective-permute-done.8.refs_5_ = bf16[16,1792]{1,0:T(8,128)(2,1)S(1)} collective-permute-done((bf16[16,1792]{1,0:T(8,128)(2,1)S(1)}, bf16[16,1792]{1,0:T(8,128)(2,1)S(1)}, u32[]{:S(2)}, u32[]{:S(2)}) %collective-permute-start.8) | collective-permute-done | bytes 57376 | tf_op jit(solution)/shard_map/ppermute | solution.py:211
  22.0 1.4 %hidden.1.after_ref.refs_0_ = bf16[64,512]{1,0:T(8,128)(2,1)S(1)} custom-call(bf16[16,1792]{1,0:T(8,128)(2,1)S(1)} %collective-permute-done.3.refs_0_, bf16[16,1792]{1,0:T(8,128)(2,1)S(1)} %collective-permute-done.4.refs_1_, bf16[16,1792]{1,0:T(8,128)(2,1)S(1)} %collective-permute-done.5.refs_2_, bf16[16,1792]{1,0:T(8,128)(2,1)S(1)} %collective-permute-done.6.refs_3_, ...), custom_call_target="tpu_custom_call" | custom-call | tf_op jit(solution)/shard_map/hidden/pallas_call | solution.py:275
  23.4 3.4 %collective-permute-start.11 = (bf16[64,512]{1,0:T(8,128)(2,1)S(1)}, bf16[64,512]{1,0:T(8,128)(2,1)S(1)}, u32[]{:S(2)}, u32[]{:S(2)}) collective-permute-start(bf16[64,512]{1,0:T(8,128)(2,1)S(1)} %hidden.1.after_ref.refs_0_), channel_id=1, source_target_pairs={{0,3},{1,2},{2,1},{3,0},{4,7},{5,6},{6,5},{7,4},{8,11},{9,10},{10,... | collective-permute-start | bytes 196616 | tf_op jit(solution)/shard_map/ppermute | solution.py:211
  26.8 1.0 %collective-permute-start.9 = (bf16[64,512]{1,0:T(8,128)(2,1)S(1)}, bf16[64,512]{1,0:T(8,128)(2,1)S(1)}, u32[]{:S(2)}, u32[]{:S(2)}) collective-permute-start(bf16[64,512]{1,0:T(8,128)(2,1)S(1)} %hidden.1.after_ref.refs_0_), channel_id=1, source_target_pairs={{0,1},{1,0},{2,3},{3,2},{4,5},{5,4},{6,7},{7,6},{8,9},{9,8},{10,11... | collective-permute-start | bytes 196616 | tf_op jit(solution)/shard_map/ppermute | solution.py:211
  27.8 2.1 %prepare.1 = (bf16[2048,896]{1,0:T(8,128)(2,1)S(1)}, bf16[256,32]{1,0:T(8,128)(2,1)S(1)}) custom-call(bf16[64,512]{1,0:T(8,128)(2,1)S(1)} %hidden.1.after_ref.refs_0_, s32[8,256]{1,0:T(8,128)} %bitcast.10, f32[96,256]{1,0:T(8,128)} %bitcast.8, bf16[2048,896]{1,0:T(8,128)(2,1)} %bitcast.7), custom_call_target="tpu_custom_call" | custom-call | tf_op jit(solution)/shard_map/prepare/pallas_call | solution.py:283
  30.0 2.1 %collective-permute-done.10.refs_2_ = bf16[64,512]{1,0:T(8,128)(2,1)S(1)} collective-permute-done((bf16[64,512]{1,0:T(8,128)(2,1)S(1)}, bf16[64,512]{1,0:T(8,128)(2,1)S(1)}, u32[]{:S(2)}, u32[]{:S(2)}) %collective-permute-start.10) | collective-permute-done | bytes 65568 | tf_op jit(solution)/shard_map/ppermute | solution.py:211
  32.1 0.1 collective-permute-done.9.refs_1_
  32.2 0.7 %down.1 = (bf16[16,896]{1,0:T(8,128)(2,1)S(1)}, bf16[16,896]{1,0:T(8,128)(2,1)S(1)}, bf16[16,896]{1,0:T(8,128)(2,1)S(1)}, bf16[16,896]{1,0:T(8,128)(2,1)S(1)}) custom-call(bf16[64,512]{1,0:T(8,128)(2,1)S(1)} %hidden.1.after_ref.refs_0_, bf16[64,512]{1,0:T(8,128)(2,1)S(1)} %collective-permute-done.9.refs_1_, ...), custom_call_target="tpu_custom_call" | custom-call | tf_op jit(solution)/shard_map/down/pallas_call | solution.py:301
  32.9 1.7 %collective-permute-start.12 = (bf16[16,896]{1,0:T(8,128)(2,1)S(1)}, bf16[16,896]{1,0:T(8,128)(2,1)S(1)}, u32[]{:S(2)}, u32[]{:S(2)}) collective-permute-start(bf16[16,896]{1,0:T(8,128)(2,1)S(1)} %get-tuple-element.35), channel_id=1, source_target_pairs={{0,3},{1,2},{2,1},{3,0},{4,7},{5,6},{6,5},{7,4},{8,11},{9,10},{10,... | collective-permute-start | bytes 86024 | tf_op jit(solution)/shard_map/ppermute | solution.py:211
  34.7 0.2 collective-permute-start.13
  34.9 2.5 %collective-permute-start.14 = (bf16[16,896]{1,0:T(8,128)(2,1)S(1)}, bf16[16,896]{1,0:T(8,128)(2,1)S(1)}, u32[]{:S(2)}, u32[]{:S(2)}) collective-permute-start(bf16[16,896]{1,0:T(8,128)(2,1)S(1)} %get-tuple-element.37), channel_id=1, source_target_pairs={{0,1},{1,0},{2,3},{3,2},{4,5},{5,4},{6,7},{7,6},{8,9},{9,8},{10,11... | collective-permute-start | bytes 86024 | tf_op jit(solution)/shard_map/ppermute | solution.py:211
  37.4 1.3 %collective-permute-done.12.refs_0_ = bf16[16,896]{1,0:T(8,128)(2,1)S(1)} collective-permute-done((bf16[16,896]{1,0:T(8,128)(2,1)S(1)}, bf16[16,896]{1,0:T(8,128)(2,1)S(1)}, u32[]{:S(2)}, u32[]{:S(2)}) %collective-permute-start.12) | collective-permute-done | bytes 28704 | tf_op jit(solution)/shard_map/ppermute | solution.py:211
  38.6 1.1 %collective-permute-done.13.refs_1_ = bf16[16,896]{1,0:T(8,128)(2,1)S(1)} collective-permute-done((bf16[16,896]{1,0:T(8,128)(2,1)S(1)}, bf16[16,896]{1,0:T(8,128)(2,1)S(1)}, u32[]{:S(2)}, u32[]{:S(2)}) %collective-permute-start.13) | collective-permute-done | bytes 28704 | tf_op jit(solution)/shard_map/ppermute | solution.py:211
  39.7 0.2 spread.1
  40.0 1.2 %collective-permute-start.16 = (bf16[4,8,896]{2,1,0:T(8,128)(2,1)S(1)}, bf16[4,8,896]{2,1,0:T(8,128)(2,1)S(1)}, u32[]{:S(2)}, u32[]{:S(2)}) collective-permute-start(bf16[4,8,896]{2,1,0:T(8,128)(2,1)S(1)} %get-tuple-element.40), channel_id=1, source_target_pairs={{0,8},{4,12},{8,0},{12,4},{1,9},{5,13},{9,1},{13,5},{2,10},{6,14},... | collective-permute-start | bytes 172040 | tf_op jit(solution)/shard_map/ppermute | solution.py:211
  41.2 0.7 %collective-permute-start.17 = (bf16[4,8,896]{2,1,0:T(8,128)(2,1)S(1)}, bf16[4,8,896]{2,1,0:T(8,128)(2,1)S(1)}, u32[]{:S(2)}, u32[]{:S(2)}) collective-permute-start(bf16[4,8,896]{2,1,0:T(8,128)(2,1)S(1)} %get-tuple-element.41), channel_id=1, source_target_pairs={{0,4},{4,0},{8,12},{12,8},{1,5},{5,1},{9,13},{13,9},{2,6},{6,2},{1... | collective-permute-start | bytes 172040 | tf_op jit(solution)/shard_map/ppermute | solution.py:211
  41.8 2.3 %collective-permute-done.15.refs_0_ = bf16[4,8,896]{2,1,0:T(8,128)(2,1)S(1)} collective-permute-done((bf16[4,8,896]{2,1,0:T(8,128)(2,1)S(1)}, bf16[4,8,896]{2,1,0:T(8,128)(2,1)S(1)}, u32[]{:S(2)}, u32[]{:S(2)}) %collective-permute-start.15) | collective-permute-done | bytes 57376 | tf_op jit(solution)/shard_map/ppermute | solution.py:211
  44.1 0.7 %collective-permute-done.16.refs_1_ = bf16[4,8,896]{2,1,0:T(8,128)(2,1)S(1)} collective-permute-done((bf16[4,8,896]{2,1,0:T(8,128)(2,1)S(1)}, bf16[4,8,896]{2,1,0:T(8,128)(2,1)S(1)}, u32[]{:S(2)}, u32[]{:S(2)}) %collective-permute-start.16) | collective-permute-done | bytes 57376 | tf_op jit(solution)/shard_map/ppermute | solution.py:211
  44.8 1.5 %combine.1 = bf16[256,3584]{1,0:T(8,128)(2,1)} custom-call(bf16[256,32]{1,0:T(8,128)(2,1)S(1)} %get-tuple-element.32.mixing_ref, bf16[4,8,896]{2,1,0:T(8,128)(2,1)S(1)} %collective-permute-done.15.refs_0_, bf16[4,8,896]{2,1,0:T(8,128)(2,1)S(1)} %collective-permute-done.16.refs_1_, bf16[4,8,896]{2,1,0:T(8,128)(2,1)S(1)} %collective-permute-done.17.refs_2_, ...), custom_call_target="tpu_custom_call" | custom-call | tf_op jit(solution)/shard_map/combine/pallas_call | solution.py:326
  (12 shorter events, 0.2 us)
Async XLA Ops:
  1.8 6.3 %collective-permute-start = (bf16[8,3712]{1,0:T(8,128)(2,1)S(1)}, bf16[8,3712]{1,0:T(8,128)(2,1)S(1)}, u32[]{:S(2)}, u32[]{:S(2)}) collective-permute-start(bf16[8,3712]{1,0:T(8,128)(2,1)S(1)} %get-tuple-element.26), channel_id=1, source_target_pairs={{0,12},{4,8},{8,4},{12,0},{1,13},{5,9},{9,5},{13,1},{2,14},{6,10},... | collective-permute-start | bytes 178184 | tf_op jit(solution)/shard_map/ppermute | solution.py:211
  4.2 4.5 %collective-permute-start.1 = (bf16[8,3712]{1,0:T(8,128)(2,1)S(1)}, bf16[8,3712]{1,0:T(8,128)(2,1)S(1)}, u32[]{:S(2)}, u32[]{:S(2)}) collective-permute-start(bf16[8,3712]{1,0:T(8,128)(2,1)S(1)} %get-tuple-element.27), channel_id=1, source_target_pairs={{0,8},{4,12},{8,0},{12,4},{1,9},{5,13},{9,1},{13,5},{2,10},{6,14},... | collective-permute-start | bytes 178184 | tf_op jit(solution)/shard_map/ppermute | solution.py:211
  4.9 3.9 %collective-permute-start.2 = (bf16[8,3712]{1,0:T(8,128)(2,1)S(1)}, bf16[8,3712]{1,0:T(8,128)(2,1)S(1)}, u32[]{:S(2)}, u32[]{:S(2)}) collective-permute-start(bf16[8,3712]{1,0:T(8,128)(2,1)S(1)} %get-tuple-element.28), channel_id=1, source_target_pairs={{0,4},{4,0},{8,12},{12,8},{1,5},{5,1},{9,13},{13,9},{2,6},{6,2},{1... | collective-permute-start | bytes 178184 | tf_op jit(solution)/shard_map/ppermute | solution.py:211
  9.1 8.7 %collective-permute-start.3 = (bf16[16,1792]{1,0:T(8,128)(2,1)S(1)}, bf16[16,1792]{1,0:T(8,128)(2,1)S(1)}, u32[]{:S(2)}, u32[]{:S(2)}) collective-permute-start(bf16[16,1792]{1,0:T(8,128)(2,1)S(1)} %get-tuple-element.29.refs_6_), channel_id=1, source_target_pairs={{0,2},{1,3},{2,0},{3,1},{4,6},{5,7},{6,4},{7,5},{8,10},{9,11},{10,... | collective-permute-start | bytes 172040 | tf_op jit(solution)/shard_map/ppermute | solution.py:211
  11.8 6.0 %collective-permute-start.4 = (bf16[16,1792]{1,0:T(8,128)(2,1)S(1)}, bf16[16,1792]{1,0:T(8,128)(2,1)S(1)}, u32[]{:S(2)}, u32[]{:S(2)}) collective-permute-start(bf16[16,1792]{1,0:T(8,128)(2,1)S(1)} %get-tuple-element.29.refs_6_), channel_id=1, source_target_pairs={{0,1},{1,0},{2,3},{3,2},{4,5},{5,4},{6,7},{7,6},{8,9},{9,8},{10,11... | collective-permute-start | bytes 172040 | tf_op jit(solution)/shard_map/ppermute | solution.py:211
  13.4 6.7 %collective-permute-start.7 = (bf16[16,1792]{1,0:T(8,128)(2,1)S(1)}, bf16[16,1792]{1,0:T(8,128)(2,1)S(1)}, u32[]{:S(2)}, u32[]{:S(2)}) collective-permute-start(bf16[16,1792]{1,0:T(8,128)(2,1)S(1)} %get-tuple-element.30.refs_7_), channel_id=1, source_target_pairs={{0,3},{1,2},{2,1},{3,0},{4,7},{5,6},{6,5},{7,4},{8,11},{9,10},{10,... | collective-permute-start | bytes 172040 | tf_op jit(solution)/shard_map/ppermute | solution.py:211
  13.6 6.5 %collective-permute-start.6 = (bf16[16,1792]{1,0:T(8,128)(2,1)S(1)}, bf16[16,1792]{1,0:T(8,128)(2,1)S(1)}, u32[]{:S(2)}, u32[]{:S(2)}) collective-permute-start(bf16[16,1792]{1,0:T(8,128)(2,1)S(1)} %get-tuple-element.30.refs_7_), channel_id=1, source_target_pairs={{0,2},{1,3},{2,0},{3,1},{4,6},{5,7},{6,4},{7,5},{8,10},{9,11},{10,... | collective-permute-start | bytes 172040 | tf_op jit(solution)/shard_map/ppermute | solution.py:211
  15.3 5.8 %collective-permute-start.5 = (bf16[16,1792]{1,0:T(8,128)(2,1)S(1)}, bf16[16,1792]{1,0:T(8,128)(2,1)S(1)}, u32[]{:S(2)}, u32[]{:S(2)}) collective-permute-start(bf16[16,1792]{1,0:T(8,128)(2,1)S(1)} %get-tuple-element.30.refs_7_), channel_id=1, source_target_pairs={{0,1},{1,0},{2,3},{3,2},{4,5},{5,4},{6,7},{7,6},{8,9},{9,8},{10,11... | collective-permute-start | bytes 172040 | tf_op jit(solution)/shard_map/ppermute | solution.py:211
  17.8 4.2 %collective-permute-start.8 = (bf16[16,1792]{1,0:T(8,128)(2,1)S(1)}, bf16[16,1792]{1,0:T(8,128)(2,1)S(1)}, u32[]{:S(2)}, u32[]{:S(2)}) collective-permute-start(bf16[16,1792]{1,0:T(8,128)(2,1)S(1)} %collective-permute-done.3.refs_0_), channel_id=1, source_target_pairs={{0,1},{1,0},{2,3},{3,2},{4,5},{5,4},{6,7},{7,6},{8,9},{9,8},{10,11... | collective-permute-start | bytes 172040 | tf_op jit(solution)/shard_map/ppermute | solution.py:211
  23.4 6.6 %collective-permute-start.11 = (bf16[64,512]{1,0:T(8,128)(2,1)S(1)}, bf16[64,512]{1,0:T(8,128)(2,1)S(1)}, u32[]{:S(2)}, u32[]{:S(2)}) collective-permute-start(bf16[64,512]{1,0:T(8,128)(2,1)S(1)} %hidden.1.after_ref.refs_0_), channel_id=1, source_target_pairs={{0,3},{1,2},{2,1},{3,0},{4,7},{5,6},{6,5},{7,4},{8,11},{9,10},{10,... | collective-permute-start | bytes 196616 | tf_op jit(solution)/shard_map/ppermute | solution.py:211
  26.8 5.3 %collective-permute-start.10 = (bf16[64,512]{1,0:T(8,128)(2,1)S(1)}, bf16[64,512]{1,0:T(8,128)(2,1)S(1)}, u32[]{:S(2)}, u32[]{:S(2)}) collective-permute-start(bf16[64,512]{1,0:T(8,128)(2,1)S(1)} %hidden.1.after_ref.refs_0_), channel_id=1, source_target_pairs={{0,2},{1,3},{2,0},{3,1},{4,6},{5,7},{6,4},{7,5},{8,10},{9,11},{10,... | collective-permute-start | bytes 196616 | tf_op jit(solution)/shard_map/ppermute | solution.py:211
  26.8 5.3 %collective-permute-start.9 = (bf16[64,512]{1,0:T(8,128)(2,1)S(1)}, bf16[64,512]{1,0:T(8,128)(2,1)S(1)}, u32[]{:S(2)}, u32[]{:S(2)}) collective-permute-start(bf16[64,512]{1,0:T(8,128)(2,1)S(1)} %hidden.1.after_ref.refs_0_), channel_id=1, source_target_pairs={{0,1},{1,0},{2,3},{3,2},{4,5},{5,4},{6,7},{7,6},{8,9},{9,8},{10,11... | collective-permute-start | bytes 196616 | tf_op jit(solution)/shard_map/ppermute | solution.py:211
  32.9 5.7 %collective-permute-start.12 = (bf16[16,896]{1,0:T(8,128)(2,1)S(1)}, bf16[16,896]{1,0:T(8,128)(2,1)S(1)}, u32[]{:S(2)}, u32[]{:S(2)}) collective-permute-start(bf16[16,896]{1,0:T(8,128)(2,1)S(1)} %get-tuple-element.35), channel_id=1, source_target_pairs={{0,3},{1,2},{2,1},{3,0},{4,7},{5,6},{6,5},{7,4},{8,11},{9,10},{10,... | collective-permute-start | bytes 86024 | tf_op jit(solution)/shard_map/ppermute | solution.py:211
  34.7 5.1 %collective-permute-start.13 = (bf16[16,896]{1,0:T(8,128)(2,1)S(1)}, bf16[16,896]{1,0:T(8,128)(2,1)S(1)}, u32[]{:S(2)}, u32[]{:S(2)}) collective-permute-start(bf16[16,896]{1,0:T(8,128)(2,1)S(1)} %get-tuple-element.36), channel_id=1, source_target_pairs={{0,2},{1,3},{2,0},{3,1},{4,6},{5,7},{6,4},{7,5},{8,10},{9,11},{10,... | collective-permute-start | bytes 86024 | tf_op jit(solution)/shard_map/ppermute | solution.py:211
  34.9 4.8 %collective-permute-start.14 = (bf16[16,896]{1,0:T(8,128)(2,1)S(1)}, bf16[16,896]{1,0:T(8,128)(2,1)S(1)}, u32[]{:S(2)}, u32[]{:S(2)}) collective-permute-start(bf16[16,896]{1,0:T(8,128)(2,1)S(1)} %get-tuple-element.37), channel_id=1, source_target_pairs={{0,1},{1,0},{2,3},{3,2},{4,5},{5,4},{6,7},{7,6},{8,9},{9,8},{10,11... | collective-permute-start | bytes 86024 | tf_op jit(solution)/shard_map/ppermute | solution.py:211
  39.9 4.2 %collective-permute-start.15 = (bf16[4,8,896]{2,1,0:T(8,128)(2,1)S(1)}, bf16[4,8,896]{2,1,0:T(8,128)(2,1)S(1)}, u32[]{:S(2)}, u32[]{:S(2)}) collective-permute-start(bf16[4,8,896]{2,1,0:T(8,128)(2,1)S(1)} %get-tuple-element.39), channel_id=1, source_target_pairs={{0,12},{4,8},{8,4},{12,0},{1,13},{5,9},{9,5},{13,1},{2,14},{6,10},... | collective-permute-start | bytes 172040 | tf_op jit(solution)/shard_map/ppermute | solution.py:211
  40.0 4.8 %collective-permute-start.16 = (bf16[4,8,896]{2,1,0:T(8,128)(2,1)S(1)}, bf16[4,8,896]{2,1,0:T(8,128)(2,1)S(1)}, u32[]{:S(2)}, u32[]{:S(2)}) collective-permute-start(bf16[4,8,896]{2,1,0:T(8,128)(2,1)S(1)} %get-tuple-element.40), channel_id=1, source_target_pairs={{0,8},{4,12},{8,0},{12,4},{1,9},{5,13},{9,1},{13,5},{2,10},{6,14},... | collective-permute-start | bytes 172040 | tf_op jit(solution)/shard_map/ppermute | solution.py:211
  41.2 3.6 %collective-permute-start.17 = (bf16[4,8,896]{2,1,0:T(8,128)(2,1)S(1)}, bf16[4,8,896]{2,1,0:T(8,128)(2,1)S(1)}, u32[]{:S(2)}, u32[]{:S(2)}) collective-permute-start(bf16[4,8,896]{2,1,0:T(8,128)(2,1)S(1)} %get-tuple-element.41), channel_id=1, source_target_pairs={{0,4},{4,0},{8,12},{12,8},{1,5},{5,1},{9,13},{13,9},{2,6},{6,2},{1... | collective-permute-start | bytes 172040 | tf_op jit(solution)/shard_map/ppermute | solution.py:211

commit v11 on v10

--- a/solution.py
+++ b/solution.py
@@ -141,35 +141,53 @@
                 out[:, c * step - first : (c + 1) * step - first] = moved.astype(BF16)
 
 
-def hidden_kernel(columns, halved, *refs):
-    blocks, (gate_ref, up_ref, hidden_ref) = refs[:-3], refs[-3:]
+def ahead_kernel(first, order, *refs):
+    blocks, (gate_ref, up_ref, gate_sum, up_sum) = [refs[k] for k in order], refs[len(order) :]
+    rows = jnp.concatenate([block[...] for block in blocks], axis=0)
+    step = min(256, gate_ref.shape[1])
+    for c in range(gate_ref.shape[1] // step):
+        part = slice(c * step, (c + 1) * step)
+        gate_sum[:, part] = jnp.dot(rows, gate_ref[first:, part], preferred_element_type=F32)
+        up_sum[:, part] = jnp.dot(rows, up_ref[first:, part], preferred_element_type=F32)
+
+
+def hidden_kernel(last, count, *refs):
+    blocks, sums, (gate_ref, up_ref, hidden_ref) = refs[:count], refs[count:-3], refs[-3:]
     units = gate_ref.shape[1]
-    blocks = [block[...] for block in blocks]
-    if halved:
-        low, near_low, near_high, high, far_high, far_low, own_low, own_high = blocks
-        pairs = [(own_low, own_high), (near_low, near_high), (low, high), (far_low, far_high)]
-        blocks = [jnp.concatenate(pair, axis=1) for pair in pairs]
-    rows = jnp.concatenate(blocks, axis=0)
+    rows = jnp.concatenate([block[...] for block in blocks], axis=0)
     step = min(256, units)
     for c in range(units // step):
         part = slice(c * step, (c + 1) * step)
-        gate = jnp.dot(rows, gate_ref[:, part], preferred_element_type=F32)
-        up = jnp.dot(rows, up_ref[:, part], preferred_element_type=F32)
+        gate = jnp.dot(rows, gate_ref[:last, part], preferred_element_type=F32)
+        up = jnp.dot(rows, up_ref[:last, part], preferred_element_type=F32)
+        if sums:
+            gate, up = gate + sums[0][:, part], up + sums[1][:, part]
         hidden_ref[:, part] = (gate / (1.0 + jnp.exp(-gate)) * up).astype(BF16)
 
 
-def down_kernel(columns, *refs):
-    hiddens, down_ref, outs = refs[:columns], refs[columns], refs[columns + 1 :]
+def down_sum(columns, which, hiddens, down_ref):
     me = lax.axis_index("ing")
     rows, units = hiddens[0].shape
     slots = rows // columns
     total = jnp.zeros((rows, down_ref.shape[1]), F32)
-    for f in range(columns):
+    for f, hidden in zip(which, hiddens):
         block = jnp.concatenate(
-            [hiddens[f][slots * (e ^ f) : slots * ((e ^ f) + 1), :] for e in range(columns)], axis=0
+            [hidden[slots * (e ^ f) : slots * ((e ^ f) + 1), :] for e in range(columns)], axis=0
         )
         at = pl.multiple_of((me ^ f) * units, units)
         total += jnp.dot(block, down_ref[pl.ds(at, units), :], preferred_element_type=F32)
+    return total
+
+
+def begin_kernel(columns, which, *refs):
+    refs[-1][...] = down_sum(columns, which, refs[:-2], refs[-2])
+
+
+def down_kernel(columns, which, *refs):
+    count = len(which)
+    hiddens, (sum_ref, down_ref), outs = refs[:count], refs[count : count + 2], refs[count + 2 :]
+    total = sum_ref[...] + down_sum(columns, which, hiddens, down_ref)
+    slots = total.shape[0] // columns
     for e in range(columns):
         outs[e][...] = total[e * slots : (e + 1) * slots].astype(BF16)
 
@@ -268,18 +286,27 @@
         near_low, near_high, high, far_high = [swap(part, "ing", e) for part, e in zip(own + own[1:] * 2, (1, 1, 2, 3))]
         low = swap(own[0], "ing", 2)
         far_low = swap(low, "ing", 1)
-        blocks = [low, near_low, near_high, high, far_high, far_low] + own
+        sums = pl.pallas_call(
+            functools.partial(ahead_kernel, cut, (0, 1, 3, 2)),
+            out_shape=[jax.ShapeDtypeStruct((columns * slots, units), F32)] * 2,
+            in_specs=[VMEM] * (columns + 2),
+            out_specs=[VMEM] * 2,
+            compiler_params=params(2 * columns * slots * (features + 4 * units)),
+            name="ahead",
+        )(own[1], near_high, far_high, high, gate, up)
+        blocks = [own[0], near_low, low, far_low]
     else:
+        sums, cut = [], features
         blocks = [swap(own[0], "ing", e) for e in range(columns)]
 
     hidden = pl.pallas_call(
-        functools.partial(hidden_kernel, columns, columns == 4),
+        functools.partial(hidden_kernel, cut, columns),
         out_shape=jax.ShapeDtypeStruct((columns * slots, units), BF16),
-        in_specs=[VMEM] * (len(blocks) + 2),
+        in_specs=[VMEM] * (columns + len(sums) + 2),
         out_specs=VMEM,
-        compiler_params=params(2 * columns * slots * (2 * features + units)),
+        compiler_params=params(2 * columns * slots * (2 * features + 5 * units)),
         name="hidden",
-    )(*blocks, gate, up)
+    )(*blocks, *sums, gate, up)
     down, mixing = pl.pallas_call(
         functools.partial(prepare_kernel, groups),
         out_shape=[
@@ -298,14 +325,23 @@
     )(hidden, ids, logits, weights[2])
     hiddens = [swap(hidden, "ing", f) for f in range(columns)]
 
+    early, late = (0, columns - 1), tuple(range(1, columns - 1))
+    begun = pl.pallas_call(
+        functools.partial(begin_kernel, columns, early),
+        out_shape=jax.ShapeDtypeStruct((columns * slots, share), F32),
+        in_specs=[VMEM] * (len(early) + 1),
+        out_specs=VMEM,
+        compiler_params=params(2 * columns * slots * (2 * units + 4 * share)),
+        name="begin",
+    )(*[hiddens[f] for f in early], down)
     results = pl.pallas_call(
-        functools.partial(down_kernel, columns),
+        functools.partial(down_kernel, columns, late),
         out_shape=[jax.ShapeDtypeStruct((slots, share), BF16)] * columns,
-        in_specs=[VMEM] * (columns + 1),
+        in_specs=[VMEM] * (len(late) + 2),
         out_specs=[VMEM] * columns,
-        compiler_params=params(2 * columns * slots * (columns * units + 4 * share)),
+        compiler_params=params(2 * columns * slots * (columns * units + 6 * share)),
         name="down",
-    )(*hiddens, down)
+    )(*[hiddens[f] for f in late], begun, down)
     results = swap_all(results, "ing")
 
     backs = pl.pallas_call(

time: 46.6 us -> 46.2 us (level)
  waiting for transfers between devices: 12.3 us -> 11.7 us
    ppermute x18, waiting for transfers between devices: 12.3 us -> 11.7 us  [swap(): lax.ppermute(x, name, [(a, a ^ step) for a in range(lax.axis_size(name))])]
    pallas_call x2 -> x4, Pallas kernels: 2.12 us -> 2.37 us  [the longest x1 0.77 us: local(): pl.pallas_call(functools.partial(hidden_kernel, cut, columns), out_shape=...]
  transfers between devices with their start and end apart: 18 -> 18, of which waited for: 10 -> 9; matrix products, arithmetic and copies ran while one was open for 0% -> 0% of each run, Pallas kernels for 11% -> 14%
where the time goes in v11:
time: 46.2 us; the launch traced here: 46 us
  starting transfers between devices  22.7 us (49%)
  waiting for transfers between devices  11.7 us (25%)
  Pallas kernels  11.5 us (25%)
    ppermute x18, starting transfers between devices, swap(): lax.ppermute(x, name, [(a, a ^ step) for a in range(lax.axis_size(name))])  22.7 us
    ppermute x18, waiting for transfers between devices, swap(): lax.ppermute(x, name, [(a, a ^ step) for a in range(lax.axis_size(name))])  11.7 us
    pallas_call x1, Pallas kernels, local(): pl.pallas_call(load_kernel, out_shape=[pltpu.VMEM(w.shape, BF16) for w in...  3.17 us
    pallas_call x1, Pallas kernels, local(): pl.pallas_call(functools.partial(prepare_kernel, groups), out_shape=[pltp...  2.13 us
    pallas_call x1, Pallas kernels, local(): pl.pallas_call(functools.partial(dispatch_kernel, groups, features // 2),...  1.79 us
    pallas_call x1, Pallas kernels, local(): pl.pallas_call(functools.partial(combine_kernel, groups, columns), out_sh...  1.49 us
  transfers between devices with their start and end apart: 18, of which 9 were waited for; matrix products, arithmetic and copies ran while one was open for 0% of the time, Pallas kernels for 14%

profile of v11, /device:TPU:0, one launch (start us, length us, event | category | flops | bytes accessed | tf_op | source)
XLA Modules:
  0.0 46.0 jit_solution(716140668234583121)
XLA Ops:
  0.0 1.8 %dispatch.1 = (bf16[8,3712]{1,0:T(8,128)(2,1)S(1)}, bf16[8,3712]{1,0:T(8,128)(2,1)S(1)}, bf16[8,3712]{1,0:T(8,128)(2,1)S(1)}, bf16[8,3712]{1,0:T(8,128)(2,1)S(1)}) custom-call(s32[8,256]{1,0:T(8,128)} %bitcast.9, bf16[256,3584]{1,0:T(8,128)(2,1)} %tokens_ref.1), custom_call_target="tpu_custom_call" | custom-call | tf_op jit(solution)/shard_map/dispatch/pallas_call | solution.py:246
  1.8 2.4 %collective-permute-start = (bf16[8,3712]{1,0:T(8,128)(2,1)S(1)}, bf16[8,3712]{1,0:T(8,128)(2,1)S(1)}, u32[]{:S(2)}, u32[]{:S(2)}) collective-permute-start(bf16[8,3712]{1,0:T(8,128)(2,1)S(1)} %get-tuple-element.28), channel_id=1, source_target_pairs={{0,12},{4,8},{8,4},{12,0},{1,13},{5,9},{9,5},{13,1},{2,14},{6,10},... | collective-permute-start | bytes 178184 | tf_op jit(solution)/shard_map/ppermute | solution.py:229
  4.2 0.6 %collective-permute-start.1 = (bf16[8,3712]{1,0:T(8,128)(2,1)S(1)}, bf16[8,3712]{1,0:T(8,128)(2,1)S(1)}, u32[]{:S(2)}, u32[]{:S(2)}) collective-permute-start(bf16[8,3712]{1,0:T(8,128)(2,1)S(1)} %get-tuple-element.29), channel_id=1, source_target_pairs={{0,8},{4,12},{8,0},{12,4},{1,9},{5,13},{9,1},{13,5},{2,10},{6,14},... | collective-permute-start | bytes 178184 | tf_op jit(solution)/shard_map/ppermute | solution.py:229
  4.9 3.2 %load.1 = (bf16[3584,512]{1,0:T(8,128)(2,1)S(1)}, bf16[3584,512]{1,0:T(8,128)(2,1)S(1)}) custom-call(bf16[8,3712]{1,0:T(8,128)(2,1)S(1)} %get-tuple-element.26.after_ref.refs_3_, bf16[3584,512]{1,0:T(8,128)(2,1)} %bitcast.5, bf16[3584,512]{1,0:T(8,128)(2,1)} %bitcast.6), custom_call_target="tpu_custom_call" | custom-call | tf_op jit(solution)/shard_map/load/pallas_call | solution.py:264
  8.1 0.7 %collective-permute-done.1.refs_1_ = bf16[8,3712]{1,0:T(8,128)(2,1)S(1)} collective-permute-done((bf16[8,3712]{1,0:T(8,128)(2,1)S(1)}, bf16[8,3712]{1,0:T(8,128)(2,1)S(1)}, u32[]{:S(2)}, u32[]{:S(2)}) %collective-permute-start.1) | collective-permute-done | bytes 59424 | tf_op jit(solution)/shard_map/ppermute | solution.py:229
  8.8 0.3 compact.1
  9.1 2.7 %collective-permute-start.4 = (bf16[16,1792]{1,0:T(8,128)(2,1)S(1)}, bf16[16,1792]{1,0:T(8,128)(2,1)S(1)}, u32[]{:S(2)}, u32[]{:S(2)}) collective-permute-start(bf16[16,1792]{1,0:T(8,128)(2,1)S(1)} %get-tuple-element.31.refs_0_), channel_id=1, source_target_pairs={{0,2},{1,3},{2,0},{3,1},{4,6},{5,7},{6,4},{7,5},{8,10},{9,11},{10,... | collective-permute-start | bytes 172040 | tf_op jit(solution)/shard_map/ppermute | solution.py:229
  11.8 1.6 %collective-permute-start.6 = (bf16[16,1792]{1,0:T(8,128)(2,1)S(1)}, bf16[16,1792]{1,0:T(8,128)(2,1)S(1)}, u32[]{:S(2)}, u32[]{:S(2)}) collective-permute-start(bf16[16,1792]{1,0:T(8,128)(2,1)S(1)} %get-tuple-element.32.refs_0_), channel_id=1, source_target_pairs={{0,1},{1,0},{2,3},{3,2},{4,5},{5,4},{6,7},{7,6},{8,9},{9,8},{10,11... | collective-permute-start | bytes 172040 | tf_op jit(solution)/shard_map/ppermute | solution.py:229
  13.4 0.2 collective-permute-start.7
  13.6 1.8 %collective-permute-start.8 = (bf16[16,1792]{1,0:T(8,128)(2,1)S(1)}, bf16[16,1792]{1,0:T(8,128)(2,1)S(1)}, u32[]{:S(2)}, u32[]{:S(2)}) collective-permute-start(bf16[16,1792]{1,0:T(8,128)(2,1)S(1)} %get-tuple-element.32.refs_0_), channel_id=1, source_target_pairs={{0,2},{1,3},{2,0},{3,1},{4,6},{5,7},{6,4},{7,5},{8,10},{9,11},{10,... | collective-permute-start | bytes 172040 | tf_op jit(solution)/shard_map/ppermute | solution.py:229
  15.3 2.5 %collective-permute-start.3 = (bf16[16,1792]{1,0:T(8,128)(2,1)S(1)}, bf16[16,1792]{1,0:T(8,128)(2,1)S(1)}, u32[]{:S(2)}, u32[]{:S(2)}) collective-permute-start(bf16[16,1792]{1,0:T(8,128)(2,1)S(1)} %get-tuple-element.31.refs_0_), channel_id=1, source_target_pairs={{0,1},{1,0},{2,3},{3,2},{4,5},{5,4},{6,7},{7,6},{8,9},{9,8},{10,11... | collective-permute-start | bytes 172040 | tf_op jit(solution)/shard_map/ppermute | solution.py:229
  17.8 2.2 %collective-permute-done.7.refs_2_ = bf16[16,1792]{1,0:T(8,128)(2,1)S(1)} collective-permute-done((bf16[16,1792]{1,0:T(8,128)(2,1)S(1)}, bf16[16,1792]{1,0:T(8,128)(2,1)S(1)}, u32[]{:S(2)}, u32[]{:S(2)}) %collective-permute-start.7) | collective-permute-done | bytes 57376 | tf_op jit(solution)/shard_map/ppermute | solution.py:229
  20.1 0.7 %ahead.1 = (f32[64,512]{1,0:T(8,128)S(1)}, f32[64,512]{1,0:T(8,128)S(1)}) custom-call(bf16[16,1792]{1,0:T(8,128)(2,1)S(1)} %get-tuple-element.32.refs_0_, bf16[16,1792]{1,0:T(8,128)(2,1)S(1)} %collective-permute-done.6.refs_1_, bf16[16,1792]{1,0:T(8,128)(2,1)S(1)} %collective-permute-done.7.refs_2_, bf16[16,1792]{1,0:T(8,128)(2,1)S(1)} %collective-permute-done.8.refs_3_, ...), custom_call_target="tpu_custom_call" | custom-call | tf_op jit(solution)/shard_map/ahead/pallas_call | solution.py:289
  20.8 0.3 collective-permute-done.3.refs_1_
  21.2 0.8 %collective-permute-done.5.refs_3_ = bf16[16,1792]{1,0:T(8,128)(2,1)S(1)} collective-permute-done((bf16[16,1792]{1,0:T(8,128)(2,1)S(1)}, bf16[16,1792]{1,0:T(8,128)(2,1)S(1)}, u32[]{:S(2)}, u32[]{:S(2)}) %collective-permute-start.5) | collective-permute-done | bytes 57376 | tf_op jit(solution)/shard_map/ppermute | solution.py:229
  22.0 0.8 %hidden.1.after_ref.refs_0_ = bf16[64,512]{1,0:T(8,128)(2,1)S(1)} custom-call(bf16[16,1792]{1,0:T(8,128)(2,1)S(1)} %get-tuple-element.31.refs_0_, bf16[16,1792]{1,0:T(8,128)(2,1)S(1)} %collective-permute-done.3.refs_1_, bf16[16,1792]{1,0:T(8,128)(2,1)S(1)} %collective-permute-done.4.refs_2_, bf16[16,1792]{1,0:T(8,128)(2,1)S(1)} %collective-permute-done.5.refs_3_, ...), custom_call_target="tpu_custom_call" | custom-call | tf_op jit(solution)/shard_map/hidden/pallas_call | solution.py:302
  22.8 3.4 %collective-permute-start.11 = (bf16[64,512]{1,0:T(8,128)(2,1)S(1)}, bf16[64,512]{1,0:T(8,128)(2,1)S(1)}, u32[]{:S(2)}, u32[]{:S(2)}) collective-permute-start(bf16[64,512]{1,0:T(8,128)(2,1)S(1)} %hidden.1.after_ref.refs_0_), channel_id=1, source_target_pairs={{0,3},{1,2},{2,1},{3,0},{4,7},{5,6},{6,5},{7,4},{8,11},{9,10},{10,... | collective-permute-start | bytes 196616 | tf_op jit(solution)/shard_map/ppermute | solution.py:229
  26.2 1.0 %collective-permute-start.9 = (bf16[64,512]{1,0:T(8,128)(2,1)S(1)}, bf16[64,512]{1,0:T(8,128)(2,1)S(1)}, u32[]{:S(2)}, u32[]{:S(2)}) collective-permute-start(bf16[64,512]{1,0:T(8,128)(2,1)S(1)} %hidden.1.after_ref.refs_0_), channel_id=1, source_target_pairs={{0,1},{1,0},{2,3},{3,2},{4,5},{5,4},{6,7},{7,6},{8,9},{9,8},{10,11... | collective-permute-start | bytes 196616 | tf_op jit(solution)/shard_map/ppermute | solution.py:229
  27.2 2.1 %prepare.1 = (bf16[2048,896]{1,0:T(8,128)(2,1)S(1)}, bf16[256,32]{1,0:T(8,128)(2,1)S(1)}) custom-call(bf16[64,512]{1,0:T(8,128)(2,1)S(1)} %hidden.1.after_ref.refs_0_, s32[8,256]{1,0:T(8,128)} %bitcast.10, f32[96,256]{1,0:T(8,128)} %bitcast.8, bf16[2048,896]{1,0:T(8,128)(2,1)} %bitcast.7), custom_call_target="tpu_custom_call" | custom-call | tf_op jit(solution)/shard_map/prepare/pallas_call | solution.py:310
  29.4 0.4 begin.1.refs_2_
  29.8 1.6 %collective-permute-done.10.refs_1_ = bf16[64,512]{1,0:T(8,128)(2,1)S(1)} collective-permute-done((bf16[64,512]{1,0:T(8,128)(2,1)S(1)}, bf16[64,512]{1,0:T(8,128)(2,1)S(1)}, u32[]{:S(2)}, u32[]{:S(2)}) %collective-permute-start.10) | collective-permute-done | bytes 65568 | tf_op jit(solution)/shard_map/ppermute | solution.py:229
  31.5 0.4 down.1
  31.9 2.1 %collective-permute-start.12 = (bf16[16,896]{1,0:T(8,128)(2,1)S(1)}, bf16[16,896]{1,0:T(8,128)(2,1)S(1)}, u32[]{:S(2)}, u32[]{:S(2)}) collective-permute-start(bf16[16,896]{1,0:T(8,128)(2,1)S(1)} %get-tuple-element.39), channel_id=1, source_target_pairs={{0,3},{1,2},{2,1},{3,0},{4,7},{5,6},{6,5},{7,4},{8,11},{9,10},{10,... | collective-permute-start | bytes 86024 | tf_op jit(solution)/shard_map/ppermute | solution.py:229
  34.0 2.3 %collective-permute-start.14 = (bf16[16,896]{1,0:T(8,128)(2,1)S(1)}, bf16[16,896]{1,0:T(8,128)(2,1)S(1)}, u32[]{:S(2)}, u32[]{:S(2)}) collective-permute-start(bf16[16,896]{1,0:T(8,128)(2,1)S(1)} %get-tuple-element.41), channel_id=1, source_target_pairs={{0,1},{1,0},{2,3},{3,2},{4,5},{5,4},{6,7},{7,6},{8,9},{9,8},{10,11... | collective-permute-start | bytes 86024 | tf_op jit(solution)/shard_map/ppermute | solution.py:229
  36.3 1.3 %collective-permute-done.12.refs_0_ = bf16[16,896]{1,0:T(8,128)(2,1)S(1)} collective-permute-done((bf16[16,896]{1,0:T(8,128)(2,1)S(1)}, bf16[16,896]{1,0:T(8,128)(2,1)S(1)}, u32[]{:S(2)}, u32[]{:S(2)}) %collective-permute-start.12) | collective-permute-done | bytes 28704 | tf_op jit(solution)/shard_map/ppermute | solution.py:229
  37.6 1.4 %collective-permute-done.13.refs_1_ = bf16[16,896]{1,0:T(8,128)(2,1)S(1)} collective-permute-done((bf16[16,896]{1,0:T(8,128)(2,1)S(1)}, bf16[16,896]{1,0:T(8,128)(2,1)S(1)}, u32[]{:S(2)}, u32[]{:S(2)}) %collective-permute-start.13) | collective-permute-done | bytes 28704 | tf_op jit(solution)/shard_map/ppermute | solution.py:229
  39.0 0.2 spread.1
  39.3 1.4 %collective-permute-start.16 = (bf16[4,8,896]{2,1,0:T(8,128)(2,1)S(1)}, bf16[4,8,896]{2,1,0:T(8,128)(2,1)S(1)}, u32[]{:S(2)}, u32[]{:S(2)}) collective-permute-start(bf16[4,8,896]{2,1,0:T(8,128)(2,1)S(1)} %get-tuple-element.44), channel_id=1, source_target_pairs={{0,8},{4,12},{8,0},{12,4},{1,9},{5,13},{9,1},{13,5},{2,10},{6,14},... | collective-permute-start | bytes 172040 | tf_op jit(solution)/shard_map/ppermute | solution.py:229
  40.7 0.4 collective-permute-start.17
  41.1 2.4 %collective-permute-done.15.refs_0_ = bf16[4,8,896]{2,1,0:T(8,128)(2,1)S(1)} collective-permute-done((bf16[4,8,896]{2,1,0:T(8,128)(2,1)S(1)}, bf16[4,8,896]{2,1,0:T(8,128)(2,1)S(1)}, u32[]{:S(2)}, u32[]{:S(2)}) %collective-permute-start.15) | collective-permute-done | bytes 57376 | tf_op jit(solution)/shard_map/ppermute | solution.py:229
  43.5 1.0 %collective-permute-done.16.refs_1_ = bf16[4,8,896]{2,1,0:T(8,128)(2,1)S(1)} collective-permute-done((bf16[4,8,896]{2,1,0:T(8,128)(2,1)S(1)}, bf16[4,8,896]{2,1,0:T(8,128)(2,1)S(1)}, u32[]{:S(2)}, u32[]{:S(2)}) %collective-permute-start.16) | collective-permute-done | bytes 57376 | tf_op jit(solution)/shard_map/ppermute | solution.py:229
  44.5 1.5 %combine.1 = bf16[256,3584]{1,0:T(8,128)(2,1)} custom-call(bf16[256,32]{1,0:T(8,128)(2,1)S(1)} %get-tuple-element.36.mixing_ref, bf16[4,8,896]{2,1,0:T(8,128)(2,1)S(1)} %collective-permute-done.15.refs_0_, bf16[4,8,896]{2,1,0:T(8,128)(2,1)S(1)} %collective-permute-done.16.refs_1_, bf16[4,8,896]{2,1,0:T(8,128)(2,1)S(1)} %collective-permute-done.17.refs_2_, ...), custom_call_target="tpu_custom_call" | custom-call | tf_op jit(solution)/shard_map/combine/pallas_call | solution.py:362
  (14 shorter events, 0.2 us)
Async XLA Ops:
  1.8 6.3 %collective-permute-start = (bf16[8,3712]{1,0:T(8,128)(2,1)S(1)}, bf16[8,3712]{1,0:T(8,128)(2,1)S(1)}, u32[]{:S(2)}, u32[]{:S(2)}) collective-permute-start(bf16[8,3712]{1,0:T(8,128)(2,1)S(1)} %get-tuple-element.28), channel_id=1, source_target_pairs={{0,12},{4,8},{8,4},{12,0},{1,13},{5,9},{9,5},{13,1},{2,14},{6,10},... | collective-permute-start | bytes 178184 | tf_op jit(solution)/shard_map/ppermute | solution.py:229
  4.2 4.5 %collective-permute-start.1 = (bf16[8,3712]{1,0:T(8,128)(2,1)S(1)}, bf16[8,3712]{1,0:T(8,128)(2,1)S(1)}, u32[]{:S(2)}, u32[]{:S(2)}) collective-permute-start(bf16[8,3712]{1,0:T(8,128)(2,1)S(1)} %get-tuple-element.29), channel_id=1, source_target_pairs={{0,8},{4,12},{8,0},{12,4},{1,9},{5,13},{9,1},{13,5},{2,10},{6,14},... | collective-permute-start | bytes 178184 | tf_op jit(solution)/shard_map/ppermute | solution.py:229
  4.9 3.9 %collective-permute-start.2 = (bf16[8,3712]{1,0:T(8,128)(2,1)S(1)}, bf16[8,3712]{1,0:T(8,128)(2,1)S(1)}, u32[]{:S(2)}, u32[]{:S(2)}) collective-permute-start(bf16[8,3712]{1,0:T(8,128)(2,1)S(1)} %get-tuple-element.30), channel_id=1, source_target_pairs={{0,4},{4,0},{8,12},{12,8},{1,5},{5,1},{9,13},{13,9},{2,6},{6,2},{1... | collective-permute-start | bytes 178184 | tf_op jit(solution)/shard_map/ppermute | solution.py:229
  9.1 8.7 %collective-permute-start.4 = (bf16[16,1792]{1,0:T(8,128)(2,1)S(1)}, bf16[16,1792]{1,0:T(8,128)(2,1)S(1)}, u32[]{:S(2)}, u32[]{:S(2)}) collective-permute-start(bf16[16,1792]{1,0:T(8,128)(2,1)S(1)} %get-tuple-element.31.refs_0_), channel_id=1, source_target_pairs={{0,2},{1,3},{2,0},{3,1},{4,6},{5,7},{6,4},{7,5},{8,10},{9,11},{10,... | collective-permute-start | bytes 172040 | tf_op jit(solution)/shard_map/ppermute | solution.py:229
  11.8 6.0 %collective-permute-start.6 = (bf16[16,1792]{1,0:T(8,128)(2,1)S(1)}, bf16[16,1792]{1,0:T(8,128)(2,1)S(1)}, u32[]{:S(2)}, u32[]{:S(2)}) collective-permute-start(bf16[16,1792]{1,0:T(8,128)(2,1)S(1)} %get-tuple-element.32.refs_0_), channel_id=1, source_target_pairs={{0,1},{1,0},{2,3},{3,2},{4,5},{5,4},{6,7},{7,6},{8,9},{9,8},{10,11... | collective-permute-start | bytes 172040 | tf_op jit(solution)/shard_map/ppermute | solution.py:229
  13.4 6.7 %collective-permute-start.7 = (bf16[16,1792]{1,0:T(8,128)(2,1)S(1)}, bf16[16,1792]{1,0:T(8,128)(2,1)S(1)}, u32[]{:S(2)}, u32[]{:S(2)}) collective-permute-start(bf16[16,1792]{1,0:T(8,128)(2,1)S(1)} %get-tuple-element.32.refs_0_), channel_id=1, source_target_pairs={{0,3},{1,2},{2,1},{3,0},{4,7},{5,6},{6,5},{7,4},{8,11},{9,10},{10,... | collective-permute-start | bytes 172040 | tf_op jit(solution)/shard_map/ppermute | solution.py:229
  13.6 6.5 %collective-permute-start.8 = (bf16[16,1792]{1,0:T(8,128)(2,1)S(1)}, bf16[16,1792]{1,0:T(8,128)(2,1)S(1)}, u32[]{:S(2)}, u32[]{:S(2)}) collective-permute-start(bf16[16,1792]{1,0:T(8,128)(2,1)S(1)} %get-tuple-element.32.refs_0_), channel_id=1, source_target_pairs={{0,2},{1,3},{2,0},{3,1},{4,6},{5,7},{6,4},{7,5},{8,10},{9,11},{10,... | collective-permute-start | bytes 172040 | tf_op jit(solution)/shard_map/ppermute | solution.py:229
  15.3 5.8 %collective-permute-start.3 = (bf16[16,1792]{1,0:T(8,128)(2,1)S(1)}, bf16[16,1792]{1,0:T(8,128)(2,1)S(1)}, u32[]{:S(2)}, u32[]{:S(2)}) collective-permute-start(bf16[16,1792]{1,0:T(8,128)(2,1)S(1)} %get-tuple-element.31.refs_0_), channel_id=1, source_target_pairs={{0,1},{1,0},{2,3},{3,2},{4,5},{5,4},{6,7},{7,6},{8,9},{9,8},{10,11... | collective-permute-start | bytes 172040 | tf_op jit(solution)/shard_map/ppermute | solution.py:229
  17.8 4.2 %collective-permute-start.5 = (bf16[16,1792]{1,0:T(8,128)(2,1)S(1)}, bf16[16,1792]{1,0:T(8,128)(2,1)S(1)}, u32[]{:S(2)}, u32[]{:S(2)}) collective-permute-start(bf16[16,1792]{1,0:T(8,128)(2,1)S(1)} %collective-permute-done.4.refs_2_), channel_id=1, source_target_pairs={{0,1},{1,0},{2,3},{3,2},{4,5},{5,4},{6,7},{7,6},{8,9},{9,8},{10,11... | collective-permute-start | bytes 172040 | tf_op jit(solution)/shard_map/ppermute | solution.py:229
  22.8 6.6 %collective-permute-start.11 = (bf16[64,512]{1,0:T(8,128)(2,1)S(1)}, bf16[64,512]{1,0:T(8,128)(2,1)S(1)}, u32[]{:S(2)}, u32[]{:S(2)}) collective-permute-start(bf16[64,512]{1,0:T(8,128)(2,1)S(1)} %hidden.1.after_ref.refs_0_), channel_id=1, source_target_pairs={{0,3},{1,2},{2,1},{3,0},{4,7},{5,6},{6,5},{7,4},{8,11},{9,10},{10,... | collective-permute-start | bytes 196616 | tf_op jit(solution)/shard_map/ppermute | solution.py:229
  26.2 5.2 %collective-permute-start.10 = (bf16[64,512]{1,0:T(8,128)(2,1)S(1)}, bf16[64,512]{1,0:T(8,128)(2,1)S(1)}, u32[]{:S(2)}, u32[]{:S(2)}) collective-permute-start(bf16[64,512]{1,0:T(8,128)(2,1)S(1)} %hidden.1.after_ref.refs_0_), channel_id=1, source_target_pairs={{0,2},{1,3},{2,0},{3,1},{4,6},{5,7},{6,4},{7,5},{8,10},{9,11},{10,... | collective-permute-start | bytes 196616 | tf_op jit(solution)/shard_map/ppermute | solution.py:229
  26.2 5.2 %collective-permute-start.9 = (bf16[64,512]{1,0:T(8,128)(2,1)S(1)}, bf16[64,512]{1,0:T(8,128)(2,1)S(1)}, u32[]{:S(2)}, u32[]{:S(2)}) collective-permute-start(bf16[64,512]{1,0:T(8,128)(2,1)S(1)} %hidden.1.after_ref.refs_0_), channel_id=1, source_target_pairs={{0,1},{1,0},{2,3},{3,2},{4,5},{5,4},{6,7},{7,6},{8,9},{9,8},{10,11... | collective-permute-start | bytes 196616 | tf_op jit(solution)/shard_map/ppermute | solution.py:229
  31.9 5.7 %collective-permute-start.12 = (bf16[16,896]{1,0:T(8,128)(2,1)S(1)}, bf16[16,896]{1,0:T(8,128)(2,1)S(1)}, u32[]{:S(2)}, u32[]{:S(2)}) collective-permute-start(bf16[16,896]{1,0:T(8,128)(2,1)S(1)} %get-tuple-element.39), channel_id=1, source_target_pairs={{0,3},{1,2},{2,1},{3,0},{4,7},{5,6},{6,5},{7,4},{8,11},{9,10},{10,... | collective-permute-start | bytes 86024 | tf_op jit(solution)/shard_map/ppermute | solution.py:229
  34.0 5.0 %collective-permute-start.13 = (bf16[16,896]{1,0:T(8,128)(2,1)S(1)}, bf16[16,896]{1,0:T(8,128)(2,1)S(1)}, u32[]{:S(2)}, u32[]{:S(2)}) collective-permute-start(bf16[16,896]{1,0:T(8,128)(2,1)S(1)} %get-tuple-element.40), channel_id=1, source_target_pairs={{0,2},{1,3},{2,0},{3,1},{4,6},{5,7},{6,4},{7,5},{8,10},{9,11},{10,... | collective-permute-start | bytes 86024 | tf_op jit(solution)/shard_map/ppermute | solution.py:229
  34.0 5.0 %collective-permute-start.14 = (bf16[16,896]{1,0:T(8,128)(2,1)S(1)}, bf16[16,896]{1,0:T(8,128)(2,1)S(1)}, u32[]{:S(2)}, u32[]{:S(2)}) collective-permute-start(bf16[16,896]{1,0:T(8,128)(2,1)S(1)} %get-tuple-element.41), channel_id=1, source_target_pairs={{0,1},{1,0},{2,3},{3,2},{4,5},{5,4},{6,7},{7,6},{8,9},{9,8},{10,11... | collective-permute-start | bytes 86024 | tf_op jit(solution)/shard_map/ppermute | solution.py:229
  39.2 4.3 %collective-permute-start.15 = (bf16[4,8,896]{2,1,0:T(8,128)(2,1)S(1)}, bf16[4,8,896]{2,1,0:T(8,128)(2,1)S(1)}, u32[]{:S(2)}, u32[]{:S(2)}) collective-permute-start(bf16[4,8,896]{2,1,0:T(8,128)(2,1)S(1)} %get-tuple-element.43), channel_id=1, source_target_pairs={{0,12},{4,8},{8,4},{12,0},{1,13},{5,9},{9,5},{13,1},{2,14},{6,10},... | collective-permute-start | bytes 172040 | tf_op jit(solution)/shard_map/ppermute | solution.py:229
  39.3 5.2 %collective-permute-start.16 = (bf16[4,8,896]{2,1,0:T(8,128)(2,1)S(1)}, bf16[4,8,896]{2,1,0:T(8,128)(2,1)S(1)}, u32[]{:S(2)}, u32[]{:S(2)}) collective-permute-start(bf16[4,8,896]{2,1,0:T(8,128)(2,1)S(1)} %get-tuple-element.44), channel_id=1, source_target_pairs={{0,8},{4,12},{8,0},{12,4},{1,9},{5,13},{9,1},{13,5},{2,10},{6,14},... | collective-permute-start | bytes 172040 | tf_op jit(solution)/shard_map/ppermute | solution.py:229
  40.7 3.8 %collective-permute-start.17 = (bf16[4,8,896]{2,1,0:T(8,128)(2,1)S(1)}, bf16[4,8,896]{2,1,0:T(8,128)(2,1)S(1)}, u32[]{:S(2)}, u32[]{:S(2)}) collective-permute-start(bf16[4,8,896]{2,1,0:T(8,128)(2,1)S(1)} %get-tuple-element.45), channel_id=1, source_target_pairs={{0,4},{4,0},{8,12},{12,8},{1,5},{5,1},{9,13},{13,9},{2,6},{6,2},{1... | collective-permute-start | bytes 172040 | tf_op jit(solution)/shard_map/ppermute | solution.py:229

commit v12 on v11

--- a/solution.py
+++ b/solution.py
@@ -52,13 +52,15 @@
     outs, (ids_held, staged, before_ref, sems) = refs[:groups], refs[groups:]
     me = lax.axis_index("grp")
     features = tokens_ref.shape[1]
-    first = pltpu.make_async_copy(ids_ref, ids_held, sems.at[features // width])
+    first = pltpu.make_async_copy(ids_ref, ids_held, sems.at[4 * (features // width)])
     first.start()
+    quarter = tokens_ref.shape[0] // 4
     copies = []
     for c in range(features // width):
-        part = pl.ds(c * width, width)
-        copies.append(pltpu.make_async_copy(tokens_ref.at[:, part], staged.at[:, part], sems.at[c]))
-        copies[-1].start()
+        for q in range(4):
+            part = pl.ds(q * quarter, quarter), pl.ds(c * width, width)
+            copies.append(pltpu.make_async_copy(tokens_ref.at[part], staged.at[part], sems.at[4 * c + q]))
+            copies[-1].start()
     before_ref[...] = upto(tokens_ref.shape[0])
     first.wait()
     place, counts = placing(ids_held[...], groups, me, before_ref[...])
@@ -68,7 +70,8 @@
         live = slot < jnp.broadcast_to(counts[d : d + 1, :], (CAP, LANES))
         outs[d][:, features:] = jnp.where(live, 1.0, 0.0).astype(BF16)
     for c in range(features // width):
-        copies[c].wait()
+        for q in range(4):
+            copies[4 * c + q].wait()
         part = slice(c * width, (c + 1) * width)
         rows = jnp.dot(place, staged[:, part], preferred_element_type=F32)
         for d in range(groups):
@@ -252,7 +255,7 @@
             pltpu.VMEM(ids.shape, jnp.int32),
             pltpu.VMEM((count, features), BF16),
             pltpu.VMEM((count, count), BF16),
-            pltpu.SemaphoreType.DMA((3,)),
+            pltpu.SemaphoreType.DMA((9,)),
         ],
         compiler_params=params(2 * count * features),
         name="dispatch",

time: 46.2 us -> 46.4 us (level)
  no operation moved by 1% of the time
where the time goes in v12:
time: 46.4 us; the launch traced here: 46.1 us
  starting transfers between devices  22.7 us (49%)
  waiting for transfers between devices  11.7 us (25%)
  Pallas kernels  11.6 us (25%)
    ppermute x18, starting transfers between devices, swap(): lax.ppermute(x, name, [(a, a ^ step) for a in range(lax.axis_size(name))])  22.7 us
    ppermute x18, waiting for transfers between devices, swap(): lax.ppermute(x, name, [(a, a ^ step) for a in range(lax.axis_size(name))])  11.7 us
    pallas_call x1, Pallas kernels, local(): pl.pallas_call(load_kernel, out_shape=[pltpu.VMEM(w.shape, BF16) for w in...  3.17 us
    pallas_call x1, Pallas kernels, local(): pl.pallas_call(functools.partial(prepare_kernel, groups), out_shape=[pltp...  2.13 us
    pallas_call x1, Pallas kernels, local(): pl.pallas_call(functools.partial(dispatch_kernel, groups, features // 2),...  1.95 us
    pallas_call x1, Pallas kernels, local(): pl.pallas_call(functools.partial(combine_kernel, groups, columns), out_sh...  1.49 us
  transfers between devices with their start and end apart: 18, of which 9 were waited for; matrix products, arithmetic and copies ran while one was open for 0% of the time, Pallas kernels for 14%

profile of v12, /device:TPU:0, one launch (start us, length us, event | category | flops | bytes accessed | tf_op | source)
XLA Modules:
  0.0 46.1 jit_solution(9984293288163755001)
XLA Ops:
  0.0 1.9 %dispatch.1 = (bf16[8,3712]{1,0:T(8,128)(2,1)S(1)}, bf16[8,3712]{1,0:T(8,128)(2,1)S(1)}, bf16[8,3712]{1,0:T(8,128)(2,1)S(1)}, bf16[8,3712]{1,0:T(8,128)(2,1)S(1)}) custom-call(s32[8,256]{1,0:T(8,128)} %bitcast.9, bf16[256,3584]{1,0:T(8,128)(2,1)} %tokens_ref.1), custom_call_target="tpu_custom_call" | custom-call | tf_op jit(solution)/shard_map/dispatch/pallas_call | solution.py:249
  2.0 2.4 %collective-permute-start = (bf16[8,3712]{1,0:T(8,128)(2,1)S(1)}, bf16[8,3712]{1,0:T(8,128)(2,1)S(1)}, u32[]{:S(2)}, u32[]{:S(2)}) collective-permute-start(bf16[8,3712]{1,0:T(8,128)(2,1)S(1)} %get-tuple-element.28), channel_id=1, source_target_pairs={{0,12},{4,8},{8,4},{12,0},{1,13},{5,9},{9,5},{13,1},{2,14},{6,10},... | collective-permute-start | bytes 178184 | tf_op jit(solution)/shard_map/ppermute | solution.py:232
  4.4 0.6 %collective-permute-start.1 = (bf16[8,3712]{1,0:T(8,128)(2,1)S(1)}, bf16[8,3712]{1,0:T(8,128)(2,1)S(1)}, u32[]{:S(2)}, u32[]{:S(2)}) collective-permute-start(bf16[8,3712]{1,0:T(8,128)(2,1)S(1)} %get-tuple-element.29), channel_id=1, source_target_pairs={{0,8},{4,12},{8,0},{12,4},{1,9},{5,13},{9,1},{13,5},{2,10},{6,14},... | collective-permute-start | bytes 178184 | tf_op jit(solution)/shard_map/ppermute | solution.py:232
  5.1 3.2 %load.1 = (bf16[3584,512]{1,0:T(8,128)(2,1)S(1)}, bf16[3584,512]{1,0:T(8,128)(2,1)S(1)}) custom-call(bf16[8,3712]{1,0:T(8,128)(2,1)S(1)} %get-tuple-element.26.after_ref.refs_3_, bf16[3584,512]{1,0:T(8,128)(2,1)} %bitcast.5, bf16[3584,512]{1,0:T(8,128)(2,1)} %bitcast.6), custom_call_target="tpu_custom_call" | custom-call | tf_op jit(solution)/shard_map/load/pallas_call | solution.py:267
  8.3 0.7 %collective-permute-done.1.refs_1_ = bf16[8,3712]{1,0:T(8,128)(2,1)S(1)} collective-permute-done((bf16[8,3712]{1,0:T(8,128)(2,1)S(1)}, bf16[8,3712]{1,0:T(8,128)(2,1)S(1)}, u32[]{:S(2)}, u32[]{:S(2)}) %collective-permute-start.1) | collective-permute-done | bytes 59424 | tf_op jit(solution)/shard_map/ppermute | solution.py:232
  8.9 0.3 compact.1
  9.3 2.7 %collective-permute-start.4 = (bf16[16,1792]{1,0:T(8,128)(2,1)S(1)}, bf16[16,1792]{1,0:T(8,128)(2,1)S(1)}, u32[]{:S(2)}, u32[]{:S(2)}) collective-permute-start(bf16[16,1792]{1,0:T(8,128)(2,1)S(1)} %get-tuple-element.31.refs_0_), channel_id=1, source_target_pairs={{0,2},{1,3},{2,0},{3,1},{4,6},{5,7},{6,4},{7,5},{8,10},{9,11},{10,... | collective-permute-start | bytes 172040 | tf_op jit(solution)/shard_map/ppermute | solution.py:232
  12.0 1.6 %collective-permute-start.6 = (bf16[16,1792]{1,0:T(8,128)(2,1)S(1)}, bf16[16,1792]{1,0:T(8,128)(2,1)S(1)}, u32[]{:S(2)}, u32[]{:S(2)}) collective-permute-start(bf16[16,1792]{1,0:T(8,128)(2,1)S(1)} %get-tuple-element.32.refs_0_), channel_id=1, source_target_pairs={{0,1},{1,0},{2,3},{3,2},{4,5},{5,4},{6,7},{7,6},{8,9},{9,8},{10,11... | collective-permute-start | bytes 172040 | tf_op jit(solution)/shard_map/ppermute | solution.py:232
  13.6 0.2 collective-permute-start.7
  13.7 1.8 %collective-permute-start.8 = (bf16[16,1792]{1,0:T(8,128)(2,1)S(1)}, bf16[16,1792]{1,0:T(8,128)(2,1)S(1)}, u32[]{:S(2)}, u32[]{:S(2)}) collective-permute-start(bf16[16,1792]{1,0:T(8,128)(2,1)S(1)} %get-tuple-element.32.refs_0_), channel_id=1, source_target_pairs={{0,2},{1,3},{2,0},{3,1},{4,6},{5,7},{6,4},{7,5},{8,10},{9,11},{10,... | collective-permute-start | bytes 172040 | tf_op jit(solution)/shard_map/ppermute | solution.py:232
  15.5 2.5 %collective-permute-start.3 = (bf16[16,1792]{1,0:T(8,128)(2,1)S(1)}, bf16[16,1792]{1,0:T(8,128)(2,1)S(1)}, u32[]{:S(2)}, u32[]{:S(2)}) collective-permute-start(bf16[16,1792]{1,0:T(8,128)(2,1)S(1)} %get-tuple-element.31.refs_0_), channel_id=1, source_target_pairs={{0,1},{1,0},{2,3},{3,2},{4,5},{5,4},{6,7},{7,6},{8,9},{9,8},{10,11... | collective-permute-start | bytes 172040 | tf_op jit(solution)/shard_map/ppermute | solution.py:232
  18.0 2.2 %collective-permute-done.7.refs_2_ = bf16[16,1792]{1,0:T(8,128)(2,1)S(1)} collective-permute-done((bf16[16,1792]{1,0:T(8,128)(2,1)S(1)}, bf16[16,1792]{1,0:T(8,128)(2,1)S(1)}, u32[]{:S(2)}, u32[]{:S(2)}) %collective-permute-start.7) | collective-permute-done | bytes 57376 | tf_op jit(solution)/shard_map/ppermute | solution.py:232
  20.2 0.7 %ahead.1 = (f32[64,512]{1,0:T(8,128)S(1)}, f32[64,512]{1,0:T(8,128)S(1)}) custom-call(bf16[16,1792]{1,0:T(8,128)(2,1)S(1)} %get-tuple-element.32.refs_0_, bf16[16,1792]{1,0:T(8,128)(2,1)S(1)} %collective-permute-done.6.refs_1_, bf16[16,1792]{1,0:T(8,128)(2,1)S(1)} %collective-permute-done.7.refs_2_, bf16[16,1792]{1,0:T(8,128)(2,1)S(1)} %collective-permute-done.8.refs_3_, ...), custom_call_target="tpu_custom_call" | custom-call | tf_op jit(solution)/shard_map/ahead/pallas_call | solution.py:292
  21.0 0.3 collective-permute-done.3.refs_1_
  21.3 0.8 %collective-permute-done.5.refs_3_ = bf16[16,1792]{1,0:T(8,128)(2,1)S(1)} collective-permute-done((bf16[16,1792]{1,0:T(8,128)(2,1)S(1)}, bf16[16,1792]{1,0:T(8,128)(2,1)S(1)}, u32[]{:S(2)}, u32[]{:S(2)}) %collective-permute-start.5) | collective-permute-done | bytes 57376 | tf_op jit(solution)/shard_map/ppermute | solution.py:232
  22.1 0.8 %hidden.1.after_ref.refs_0_ = bf16[64,512]{1,0:T(8,128)(2,1)S(1)} custom-call(bf16[16,1792]{1,0:T(8,128)(2,1)S(1)} %get-tuple-element.31.refs_0_, bf16[16,1792]{1,0:T(8,128)(2,1)S(1)} %collective-permute-done.3.refs_1_, bf16[16,1792]{1,0:T(8,128)(2,1)S(1)} %collective-permute-done.4.refs_2_, bf16[16,1792]{1,0:T(8,128)(2,1)S(1)} %collective-permute-done.5.refs_3_, ...), custom_call_target="tpu_custom_call" | custom-call | tf_op jit(solution)/shard_map/hidden/pallas_call | solution.py:305
  22.9 3.4 %collective-permute-start.11 = (bf16[64,512]{1,0:T(8,128)(2,1)S(1)}, bf16[64,512]{1,0:T(8,128)(2,1)S(1)}, u32[]{:S(2)}, u32[]{:S(2)}) collective-permute-start(bf16[64,512]{1,0:T(8,128)(2,1)S(1)} %hidden.1.after_ref.refs_0_), channel_id=1, source_target_pairs={{0,3},{1,2},{2,1},{3,0},{4,7},{5,6},{6,5},{7,4},{8,11},{9,10},{10,... | collective-permute-start | bytes 196616 | tf_op jit(solution)/shard_map/ppermute | solution.py:232
  26.4 1.0 %collective-permute-start.9 = (bf16[64,512]{1,0:T(8,128)(2,1)S(1)}, bf16[64,512]{1,0:T(8,128)(2,1)S(1)}, u32[]{:S(2)}, u32[]{:S(2)}) collective-permute-start(bf16[64,512]{1,0:T(8,128)(2,1)S(1)} %hidden.1.after_ref.refs_0_), channel_id=1, source_target_pairs={{0,1},{1,0},{2,3},{3,2},{4,5},{5,4},{6,7},{7,6},{8,9},{9,8},{10,11... | collective-permute-start | bytes 196616 | tf_op jit(solution)/shard_map/ppermute | solution.py:232
  27.4 2.1 %prepare.1 = (bf16[2048,896]{1,0:T(8,128)(2,1)S(1)}, bf16[256,32]{1,0:T(8,128)(2,1)S(1)}) custom-call(bf16[64,512]{1,0:T(8,128)(2,1)S(1)} %hidden.1.after_ref.refs_0_, s32[8,256]{1,0:T(8,128)} %bitcast.10, f32[96,256]{1,0:T(8,128)} %bitcast.8, bf16[2048,896]{1,0:T(8,128)(2,1)} %bitcast.7), custom_call_target="tpu_custom_call" | custom-call | tf_op jit(solution)/shard_map/prepare/pallas_call | solution.py:313
  29.5 0.4 begin.1.refs_2_
  30.0 1.6 %collective-permute-done.10.refs_1_ = bf16[64,512]{1,0:T(8,128)(2,1)S(1)} collective-permute-done((bf16[64,512]{1,0:T(8,128)(2,1)S(1)}, bf16[64,512]{1,0:T(8,128)(2,1)S(1)}, u32[]{:S(2)}, u32[]{:S(2)}) %collective-permute-start.10) | collective-permute-done | bytes 65568 | tf_op jit(solution)/shard_map/ppermute | solution.py:232
  31.6 0.4 down.1
  32.0 2.1 %collective-permute-start.12 = (bf16[16,896]{1,0:T(8,128)(2,1)S(1)}, bf16[16,896]{1,0:T(8,128)(2,1)S(1)}, u32[]{:S(2)}, u32[]{:S(2)}) collective-permute-start(bf16[16,896]{1,0:T(8,128)(2,1)S(1)} %get-tuple-element.39), channel_id=1, source_target_pairs={{0,3},{1,2},{2,1},{3,0},{4,7},{5,6},{6,5},{7,4},{8,11},{9,10},{10,... | collective-permute-start | bytes 86024 | tf_op jit(solution)/shard_map/ppermute | solution.py:232
  34.2 2.3 %collective-permute-start.14 = (bf16[16,896]{1,0:T(8,128)(2,1)S(1)}, bf16[16,896]{1,0:T(8,128)(2,1)S(1)}, u32[]{:S(2)}, u32[]{:S(2)}) collective-permute-start(bf16[16,896]{1,0:T(8,128)(2,1)S(1)} %get-tuple-element.41), channel_id=1, source_target_pairs={{0,1},{1,0},{2,3},{3,2},{4,5},{5,4},{6,7},{7,6},{8,9},{9,8},{10,11... | collective-permute-start | bytes 86024 | tf_op jit(solution)/shard_map/ppermute | solution.py:232
  36.5 1.3 %collective-permute-done.12.refs_0_ = bf16[16,896]{1,0:T(8,128)(2,1)S(1)} collective-permute-done((bf16[16,896]{1,0:T(8,128)(2,1)S(1)}, bf16[16,896]{1,0:T(8,128)(2,1)S(1)}, u32[]{:S(2)}, u32[]{:S(2)}) %collective-permute-start.12) | collective-permute-done | bytes 28704 | tf_op jit(solution)/shard_map/ppermute | solution.py:232
  37.8 1.3 %collective-permute-done.13.refs_1_ = bf16[16,896]{1,0:T(8,128)(2,1)S(1)} collective-permute-done((bf16[16,896]{1,0:T(8,128)(2,1)S(1)}, bf16[16,896]{1,0:T(8,128)(2,1)S(1)}, u32[]{:S(2)}, u32[]{:S(2)}) %collective-permute-start.13) | collective-permute-done | bytes 28704 | tf_op jit(solution)/shard_map/ppermute | solution.py:232
  39.1 0.2 spread.1
  39.4 1.4 %collective-permute-start.16 = (bf16[4,8,896]{2,1,0:T(8,128)(2,1)S(1)}, bf16[4,8,896]{2,1,0:T(8,128)(2,1)S(1)}, u32[]{:S(2)}, u32[]{:S(2)}) collective-permute-start(bf16[4,8,896]{2,1,0:T(8,128)(2,1)S(1)} %get-tuple-element.44), channel_id=1, source_target_pairs={{0,8},{4,12},{8,0},{12,4},{1,9},{5,13},{9,1},{13,5},{2,10},{6,14},... | collective-permute-start | bytes 172040 | tf_op jit(solution)/shard_map/ppermute | solution.py:232
  40.8 0.4 collective-permute-start.17
  41.3 2.4 %collective-permute-done.15.refs_0_ = bf16[4,8,896]{2,1,0:T(8,128)(2,1)S(1)} collective-permute-done((bf16[4,8,896]{2,1,0:T(8,128)(2,1)S(1)}, bf16[4,8,896]{2,1,0:T(8,128)(2,1)S(1)}, u32[]{:S(2)}, u32[]{:S(2)}) %collective-permute-start.15) | collective-permute-done | bytes 57376 | tf_op jit(solution)/shard_map/ppermute | solution.py:232
  43.6 1.0 %collective-permute-done.16.refs_1_ = bf16[4,8,896]{2,1,0:T(8,128)(2,1)S(1)} collective-permute-done((bf16[4,8,896]{2,1,0:T(8,128)(2,1)S(1)}, bf16[4,8,896]{2,1,0:T(8,128)(2,1)S(1)}, u32[]{:S(2)}, u32[]{:S(2)}) %collective-permute-start.16) | collective-permute-done | bytes 57376 | tf_op jit(solution)/shard_map/ppermute | solution.py:232
  44.6 1.5 %combine.1 = bf16[256,3584]{1,0:T(8,128)(2,1)} custom-call(bf16[256,32]{1,0:T(8,128)(2,1)S(1)} %get-tuple-element.36.mixing_ref, bf16[4,8,896]{2,1,0:T(8,128)(2,1)S(1)} %collective-permute-done.15.refs_0_, bf16[4,8,896]{2,1,0:T(8,128)(2,1)S(1)} %collective-permute-done.16.refs_1_, bf16[4,8,896]{2,1,0:T(8,128)(2,1)S(1)} %collective-permute-done.17.refs_2_, ...), custom_call_target="tpu_custom_call" | custom-call | tf_op jit(solution)/shard_map/combine/pallas_call | solution.py:365
  (14 shorter events, 0.2 us)
Async XLA Ops:
  2.0 6.3 %collective-permute-start = (bf16[8,3712]{1,0:T(8,128)(2,1)S(1)}, bf16[8,3712]{1,0:T(8,128)(2,1)S(1)}, u32[]{:S(2)}, u32[]{:S(2)}) collective-permute-start(bf16[8,3712]{1,0:T(8,128)(2,1)S(1)} %get-tuple-element.28), channel_id=1, source_target_pairs={{0,12},{4,8},{8,4},{12,0},{1,13},{5,9},{9,5},{13,1},{2,14},{6,10},... | collective-permute-start | bytes 178184 | tf_op jit(solution)/shard_map/ppermute | solution.py:232
  4.4 4.5 %collective-permute-start.1 = (bf16[8,3712]{1,0:T(8,128)(2,1)S(1)}, bf16[8,3712]{1,0:T(8,128)(2,1)S(1)}, u32[]{:S(2)}, u32[]{:S(2)}) collective-permute-start(bf16[8,3712]{1,0:T(8,128)(2,1)S(1)} %get-tuple-element.29), channel_id=1, source_target_pairs={{0,8},{4,12},{8,0},{12,4},{1,9},{5,13},{9,1},{13,5},{2,10},{6,14},... | collective-permute-start | bytes 178184 | tf_op jit(solution)/shard_map/ppermute | solution.py:232
  5.0 3.9 %collective-permute-start.2 = (bf16[8,3712]{1,0:T(8,128)(2,1)S(1)}, bf16[8,3712]{1,0:T(8,128)(2,1)S(1)}, u32[]{:S(2)}, u32[]{:S(2)}) collective-permute-start(bf16[8,3712]{1,0:T(8,128)(2,1)S(1)} %get-tuple-element.30), channel_id=1, source_target_pairs={{0,4},{4,0},{8,12},{12,8},{1,5},{5,1},{9,13},{13,9},{2,6},{6,2},{1... | collective-permute-start | bytes 178184 | tf_op jit(solution)/shard_map/ppermute | solution.py:232
  9.3 8.7 %collective-permute-start.4 = (bf16[16,1792]{1,0:T(8,128)(2,1)S(1)}, bf16[16,1792]{1,0:T(8,128)(2,1)S(1)}, u32[]{:S(2)}, u32[]{:S(2)}) collective-permute-start(bf16[16,1792]{1,0:T(8,128)(2,1)S(1)} %get-tuple-element.31.refs_0_), channel_id=1, source_target_pairs={{0,2},{1,3},{2,0},{3,1},{4,6},{5,7},{6,4},{7,5},{8,10},{9,11},{10,... | collective-permute-start | bytes 172040 | tf_op jit(solution)/shard_map/ppermute | solution.py:232
  12.0 6.0 %collective-permute-start.6 = (bf16[16,1792]{1,0:T(8,128)(2,1)S(1)}, bf16[16,1792]{1,0:T(8,128)(2,1)S(1)}, u32[]{:S(2)}, u32[]{:S(2)}) collective-permute-start(bf16[16,1792]{1,0:T(8,128)(2,1)S(1)} %get-tuple-element.32.refs_0_), channel_id=1, source_target_pairs={{0,1},{1,0},{2,3},{3,2},{4,5},{5,4},{6,7},{7,6},{8,9},{9,8},{10,11... | collective-permute-start | bytes 172040 | tf_op jit(solution)/shard_map/ppermute | solution.py:232
  13.6 6.7 %collective-permute-start.7 = (bf16[16,1792]{1,0:T(8,128)(2,1)S(1)}, bf16[16,1792]{1,0:T(8,128)(2,1)S(1)}, u32[]{:S(2)}, u32[]{:S(2)}) collective-permute-start(bf16[16,1792]{1,0:T(8,128)(2,1)S(1)} %get-tuple-element.32.refs_0_), channel_id=1, source_target_pairs={{0,3},{1,2},{2,1},{3,0},{4,7},{5,6},{6,5},{7,4},{8,11},{9,10},{10,... | collective-permute-start | bytes 172040 | tf_op jit(solution)/shard_map/ppermute | solution.py:232
  13.7 6.5 %collective-permute-start.8 = (bf16[16,1792]{1,0:T(8,128)(2,1)S(1)}, bf16[16,1792]{1,0:T(8,128)(2,1)S(1)}, u32[]{:S(2)}, u32[]{:S(2)}) collective-permute-start(bf16[16,1792]{1,0:T(8,128)(2,1)S(1)} %get-tuple-element.32.refs_0_), channel_id=1, source_target_pairs={{0,2},{1,3},{2,0},{3,1},{4,6},{5,7},{6,4},{7,5},{8,10},{9,11},{10,... | collective-permute-start | bytes 172040 | tf_op jit(solution)/shard_map/ppermute | solution.py:232
  15.5 5.8 %collective-permute-start.3 = (bf16[16,1792]{1,0:T(8,128)(2,1)S(1)}, bf16[16,1792]{1,0:T(8,128)(2,1)S(1)}, u32[]{:S(2)}, u32[]{:S(2)}) collective-permute-start(bf16[16,1792]{1,0:T(8,128)(2,1)S(1)} %get-tuple-element.31.refs_0_), channel_id=1, source_target_pairs={{0,1},{1,0},{2,3},{3,2},{4,5},{5,4},{6,7},{7,6},{8,9},{9,8},{10,11... | collective-permute-start | bytes 172040 | tf_op jit(solution)/shard_map/ppermute | solution.py:232
  18.0 4.2 %collective-permute-start.5 = (bf16[16,1792]{1,0:T(8,128)(2,1)S(1)}, bf16[16,1792]{1,0:T(8,128)(2,1)S(1)}, u32[]{:S(2)}, u32[]{:S(2)}) collective-permute-start(bf16[16,1792]{1,0:T(8,128)(2,1)S(1)} %collective-permute-done.4.refs_2_), channel_id=1, source_target_pairs={{0,1},{1,0},{2,3},{3,2},{4,5},{5,4},{6,7},{7,6},{8,9},{9,8},{10,11... | collective-permute-start | bytes 172040 | tf_op jit(solution)/shard_map/ppermute | solution.py:232
  22.9 6.6 %collective-permute-start.11 = (bf16[64,512]{1,0:T(8,128)(2,1)S(1)}, bf16[64,512]{1,0:T(8,128)(2,1)S(1)}, u32[]{:S(2)}, u32[]{:S(2)}) collective-permute-start(bf16[64,512]{1,0:T(8,128)(2,1)S(1)} %hidden.1.after_ref.refs_0_), channel_id=1, source_target_pairs={{0,3},{1,2},{2,1},{3,0},{4,7},{5,6},{6,5},{7,4},{8,11},{9,10},{10,... | collective-permute-start | bytes 196616 | tf_op jit(solution)/shard_map/ppermute | solution.py:232
  26.4 5.2 %collective-permute-start.10 = (bf16[64,512]{1,0:T(8,128)(2,1)S(1)}, bf16[64,512]{1,0:T(8,128)(2,1)S(1)}, u32[]{:S(2)}, u32[]{:S(2)}) collective-permute-start(bf16[64,512]{1,0:T(8,128)(2,1)S(1)} %hidden.1.after_ref.refs_0_), channel_id=1, source_target_pairs={{0,2},{1,3},{2,0},{3,1},{4,6},{5,7},{6,4},{7,5},{8,10},{9,11},{10,... | collective-permute-start | bytes 196616 | tf_op jit(solution)/shard_map/ppermute | solution.py:232
  26.4 5.2 %collective-permute-start.9 = (bf16[64,512]{1,0:T(8,128)(2,1)S(1)}, bf16[64,512]{1,0:T(8,128)(2,1)S(1)}, u32[]{:S(2)}, u32[]{:S(2)}) collective-permute-start(bf16[64,512]{1,0:T(8,128)(2,1)S(1)} %hidden.1.after_ref.refs_0_), channel_id=1, source_target_pairs={{0,1},{1,0},{2,3},{3,2},{4,5},{5,4},{6,7},{7,6},{8,9},{9,8},{10,11... | collective-permute-start | bytes 196616 | tf_op jit(solution)/shard_map/ppermute | solution.py:232
  32.0 5.7 %collective-permute-start.12 = (bf16[16,896]{1,0:T(8,128)(2,1)S(1)}, bf16[16,896]{1,0:T(8,128)(2,1)S(1)}, u32[]{:S(2)}, u32[]{:S(2)}) collective-permute-start(bf16[16,896]{1,0:T(8,128)(2,1)S(1)} %get-tuple-element.39), channel_id=1, source_target_pairs={{0,3},{1,2},{2,1},{3,0},{4,7},{5,6},{6,5},{7,4},{8,11},{9,10},{10,... | collective-permute-start | bytes 86024 | tf_op jit(solution)/shard_map/ppermute | solution.py:232
  34.2 5.0 %collective-permute-start.13 = (bf16[16,896]{1,0:T(8,128)(2,1)S(1)}, bf16[16,896]{1,0:T(8,128)(2,1)S(1)}, u32[]{:S(2)}, u32[]{:S(2)}) collective-permute-start(bf16[16,896]{1,0:T(8,128)(2,1)S(1)} %get-tuple-element.40), channel_id=1, source_target_pairs={{0,2},{1,3},{2,0},{3,1},{4,6},{5,7},{6,4},{7,5},{8,10},{9,11},{10,... | collective-permute-start | bytes 86024 | tf_op jit(solution)/shard_map/ppermute | solution.py:232
  34.2 5.0 %collective-permute-start.14 = (bf16[16,896]{1,0:T(8,128)(2,1)S(1)}, bf16[16,896]{1,0:T(8,128)(2,1)S(1)}, u32[]{:S(2)}, u32[]{:S(2)}) collective-permute-start(bf16[16,896]{1,0:T(8,128)(2,1)S(1)} %get-tuple-element.41), channel_id=1, source_target_pairs={{0,1},{1,0},{2,3},{3,2},{4,5},{5,4},{6,7},{7,6},{8,9},{9,8},{10,11... | collective-permute-start | bytes 86024 | tf_op jit(solution)/shard_map/ppermute | solution.py:232
  39.3 4.3 %collective-permute-start.15 = (bf16[4,8,896]{2,1,0:T(8,128)(2,1)S(1)}, bf16[4,8,896]{2,1,0:T(8,128)(2,1)S(1)}, u32[]{:S(2)}, u32[]{:S(2)}) collective-permute-start(bf16[4,8,896]{2,1,0:T(8,128)(2,1)S(1)} %get-tuple-element.43), channel_id=1, source_target_pairs={{0,12},{4,8},{8,4},{12,0},{1,13},{5,9},{9,5},{13,1},{2,14},{6,10},... | collective-permute-start | bytes 172040 | tf_op jit(solution)/shard_map/ppermute | solution.py:232
  39.4 5.2 %collective-permute-start.16 = (bf16[4,8,896]{2,1,0:T(8,128)(2,1)S(1)}, bf16[4,8,896]{2,1,0:T(8,128)(2,1)S(1)}, u32[]{:S(2)}, u32[]{:S(2)}) collective-permute-start(bf16[4,8,896]{2,1,0:T(8,128)(2,1)S(1)} %get-tuple-element.44), channel_id=1, source_target_pairs={{0,8},{4,12},{8,0},{12,4},{1,9},{5,13},{9,1},{13,5},{2,10},{6,14},... | collective-permute-start | bytes 172040 | tf_op jit(solution)/shard_map/ppermute | solution.py:232
  40.8 3.8 %collective-permute-start.17 = (bf16[4,8,896]{2,1,0:T(8,128)(2,1)S(1)}, bf16[4,8,896]{2,1,0:T(8,128)(2,1)S(1)}, u32[]{:S(2)}, u32[]{:S(2)}) collective-permute-start(bf16[4,8,896]{2,1,0:T(8,128)(2,1)S(1)} %get-tuple-element.45), channel_id=1, source_target_pairs={{0,4},{4,0},{8,12},{12,8},{1,5},{5,1},{9,13},{13,9},{2,6},{6,2},{1... | collective-permute-start | bytes 172040 | tf_op jit(solution)/shard_map/ppermute | solution.py:232

commit v13 on v11

--- a/solution.py
+++ b/solution.py
@@ -202,23 +202,18 @@
 
 
 def combine_kernel(groups, columns, mixing_ref, *refs):
-    backs, (out_ref, held, sems) = refs[:groups][::-1], refs[groups:]
+    backs, (out_ref, rows_ref, held, sems) = refs[:groups][::-1], refs[groups:]
     me = lax.axis_index("ing")
-    width, half = backs[0].shape[2], held.shape[0] // 2
-    copies = []
+    width, quarter = backs[0].shape[2], held.shape[0] // 4
     for e in range(columns):
         rows = jnp.concatenate([backs[d][e].astype(F32) for d in range(groups)], axis=0)
-        rows = rows.astype(BF16)
-        part = pl.ds(e * width, width)
-        there = pl.ds(pl.multiple_of((me ^ e) * width, width), width)
-        for h in range(2):
-            mine = pl.ds(h * half, half)
-            value = jnp.dot(mixing_ref[mine, :], rows, preferred_element_type=F32)
-            held[mine, part] = value.astype(BF16)
-            copies.append(
-                pltpu.make_async_copy(held.at[mine, part], out_ref.at[mine, there], sems.at[2 * e + h])
-            )
-            copies[-1].start()
+        rows_ref[:, pl.ds(pl.multiple_of((me ^ e) * width, width), width)] = rows.astype(BF16)
+    copies = []
+    for q in range(4):
+        mine = pl.ds(q * quarter, quarter)
+        held[mine, :] = jnp.dot(mixing_ref[mine, :], rows_ref[...], preferred_element_type=F32).astype(BF16)
+        copies.append(pltpu.make_async_copy(held.at[mine], out_ref.at[mine], sems.at[q]))
+        copies[-1].start()
     for copy in copies:
         copy.wait()
 
@@ -244,7 +239,7 @@
     logits = pltpu.with_memory_space_constraint(router_logits.T, pltpu.HBM)
 
     outbound = pl.pallas_call(
-        functools.partial(dispatch_kernel, groups, features // 2),
+        functools.partial(dispatch_kernel, groups, features),
         out_shape=[jax.ShapeDtypeStruct((CAP, wide), BF16)] * groups,
         in_specs=[ANY, ANY],
         out_specs=[VMEM] * groups,
@@ -252,7 +247,7 @@
             pltpu.VMEM(ids.shape, jnp.int32),
             pltpu.VMEM((count, features), BF16),
             pltpu.VMEM((count, count), BF16),
-            pltpu.SemaphoreType.DMA((3,)),
+            pltpu.SemaphoreType.DMA((2,)),
         ],
         compiler_params=params(2 * count * features),
         name="dispatch",
@@ -364,7 +359,11 @@
         out_shape=jax.ShapeDtypeStruct((count, features), BF16),
         in_specs=[VMEM] * (1 + groups),
         out_specs=ANY,
-        scratch_shapes=[pltpu.VMEM((count, features), BF16), pltpu.SemaphoreType.DMA((2 * columns,))],
+        scratch_shapes=[
+            pltpu.VMEM((groups * CAP, features), BF16),
+            pltpu.VMEM((count, features), BF16),
+            pltpu.SemaphoreType.DMA((4,)),
+        ],
         compiler_params=params(2 * (count + groups * CAP) * features),
         name="combine",
     )(mixing, *backs)

time: 46.2 us -> 46.5 us (level)
  no operation moved by 1% of the time
where the time goes in v13:
time: 46.5 us; the launch traced here: 46.2 us
  starting transfers between devices  22.7 us (49%)
  Pallas kernels  11.7 us (25%)
  waiting for transfers between devices  11.7 us (25%)
    ppermute x18, starting transfers between devices, swap(): lax.ppermute(x, name, [(a, a ^ step) for a in range(lax.axis_size(name))])  22.7 us
    ppermute x18, waiting for transfers between devices, swap(): lax.ppermute(x, name, [(a, a ^ step) for a in range(lax.axis_size(name))])  11.7 us
    pallas_call x1, Pallas kernels, local(): pl.pallas_call(load_kernel, out_shape=[pltpu.VMEM(w.shape, BF16) for w in...  3.17 us
    pallas_call x1, Pallas kernels, local(): pl.pallas_call(functools.partial(prepare_kernel, groups), out_shape=[pltp...  2.13 us
    pallas_call x1, Pallas kernels, local(): pl.pallas_call(functools.partial(dispatch_kernel, groups, features), out_...  1.99 us
    pallas_call x1, Pallas kernels, local(): pl.pallas_call(functools.partial(combine_kernel, groups, columns), out_sh...  1.54 us
  transfers between devices with their start and end apart: 18, of which 9 were waited for; matrix products, arithmetic and copies ran while one was open for 0% of the time, Pallas kernels for 14%

profile of v13, /device:TPU:0, one launch (start us, length us, event | category | flops | bytes accessed | tf_op | source)
XLA Modules:
  0.0 46.2 jit_solution(5474785765570155782)
XLA Ops:
  0.0 2.0 %dispatch.1 = (bf16[8,3712]{1,0:T(8,128)(2,1)S(1)}, bf16[8,3712]{1,0:T(8,128)(2,1)S(1)}, bf16[8,3712]{1,0:T(8,128)(2,1)S(1)}, bf16[8,3712]{1,0:T(8,128)(2,1)S(1)}) custom-call(s32[8,256]{1,0:T(8,128)} %bitcast.9, bf16[256,3584]{1,0:T(8,128)(2,1)} %tokens_ref.1), custom_call_target="tpu_custom_call" | custom-call | tf_op jit(solution)/shard_map/dispatch/pallas_call | solution.py:241
  2.0 2.4 %collective-permute-start = (bf16[8,3712]{1,0:T(8,128)(2,1)S(1)}, bf16[8,3712]{1,0:T(8,128)(2,1)S(1)}, u32[]{:S(2)}, u32[]{:S(2)}) collective-permute-start(bf16[8,3712]{1,0:T(8,128)(2,1)S(1)} %get-tuple-element.28), channel_id=1, source_target_pairs={{0,12},{4,8},{8,4},{12,0},{1,13},{5,9},{9,5},{13,1},{2,14},{6,10},... | collective-permute-start | bytes 178184 | tf_op jit(solution)/shard_map/ppermute | solution.py:224
  4.4 0.6 %collective-permute-start.1 = (bf16[8,3712]{1,0:T(8,128)(2,1)S(1)}, bf16[8,3712]{1,0:T(8,128)(2,1)S(1)}, u32[]{:S(2)}, u32[]{:S(2)}) collective-permute-start(bf16[8,3712]{1,0:T(8,128)(2,1)S(1)} %get-tuple-element.29), channel_id=1, source_target_pairs={{0,8},{4,12},{8,0},{12,4},{1,9},{5,13},{9,1},{13,5},{2,10},{6,14},... | collective-permute-start | bytes 178184 | tf_op jit(solution)/shard_map/ppermute | solution.py:224
  5.1 3.2 %load.1 = (bf16[3584,512]{1,0:T(8,128)(2,1)S(1)}, bf16[3584,512]{1,0:T(8,128)(2,1)S(1)}) custom-call(bf16[8,3712]{1,0:T(8,128)(2,1)S(1)} %get-tuple-element.26.after_ref.refs_3_, bf16[3584,512]{1,0:T(8,128)(2,1)} %bitcast.5, bf16[3584,512]{1,0:T(8,128)(2,1)} %bitcast.6), custom_call_target="tpu_custom_call" | custom-call | tf_op jit(solution)/shard_map/load/pallas_call | solution.py:259
  8.3 0.7 %collective-permute-done.1.refs_1_ = bf16[8,3712]{1,0:T(8,128)(2,1)S(1)} collective-permute-done((bf16[8,3712]{1,0:T(8,128)(2,1)S(1)}, bf16[8,3712]{1,0:T(8,128)(2,1)S(1)}, u32[]{:S(2)}, u32[]{:S(2)}) %collective-permute-start.1) | collective-permute-done | bytes 59424 | tf_op jit(solution)/shard_map/ppermute | solution.py:224
  9.0 0.3 compact.1
  9.3 2.7 %collective-permute-start.4 = (bf16[16,1792]{1,0:T(8,128)(2,1)S(1)}, bf16[16,1792]{1,0:T(8,128)(2,1)S(1)}, u32[]{:S(2)}, u32[]{:S(2)}) collective-permute-start(bf16[16,1792]{1,0:T(8,128)(2,1)S(1)} %get-tuple-element.31.refs_0_), channel_id=1, source_target_pairs={{0,2},{1,3},{2,0},{3,1},{4,6},{5,7},{6,4},{7,5},{8,10},{9,11},{10,... | collective-permute-start | bytes 172040 | tf_op jit(solution)/shard_map/ppermute | solution.py:224
  12.0 1.6 %collective-permute-start.6 = (bf16[16,1792]{1,0:T(8,128)(2,1)S(1)}, bf16[16,1792]{1,0:T(8,128)(2,1)S(1)}, u32[]{:S(2)}, u32[]{:S(2)}) collective-permute-start(bf16[16,1792]{1,0:T(8,128)(2,1)S(1)} %get-tuple-element.32.refs_0_), channel_id=1, source_target_pairs={{0,1},{1,0},{2,3},{3,2},{4,5},{5,4},{6,7},{7,6},{8,9},{9,8},{10,11... | collective-permute-start | bytes 172040 | tf_op jit(solution)/shard_map/ppermute | solution.py:224
  13.6 0.2 collective-permute-start.7
  13.8 1.8 %collective-permute-start.8 = (bf16[16,1792]{1,0:T(8,128)(2,1)S(1)}, bf16[16,1792]{1,0:T(8,128)(2,1)S(1)}, u32[]{:S(2)}, u32[]{:S(2)}) collective-permute-start(bf16[16,1792]{1,0:T(8,128)(2,1)S(1)} %get-tuple-element.32.refs_0_), channel_id=1, source_target_pairs={{0,2},{1,3},{2,0},{3,1},{4,6},{5,7},{6,4},{7,5},{8,10},{9,11},{10,... | collective-permute-start | bytes 172040 | tf_op jit(solution)/shard_map/ppermute | solution.py:224
  15.5 2.5 %collective-permute-start.3 = (bf16[16,1792]{1,0:T(8,128)(2,1)S(1)}, bf16[16,1792]{1,0:T(8,128)(2,1)S(1)}, u32[]{:S(2)}, u32[]{:S(2)}) collective-permute-start(bf16[16,1792]{1,0:T(8,128)(2,1)S(1)} %get-tuple-element.31.refs_0_), channel_id=1, source_target_pairs={{0,1},{1,0},{2,3},{3,2},{4,5},{5,4},{6,7},{7,6},{8,9},{9,8},{10,11... | collective-permute-start | bytes 172040 | tf_op jit(solution)/shard_map/ppermute | solution.py:224
  18.0 2.2 %collective-permute-done.7.refs_2_ = bf16[16,1792]{1,0:T(8,128)(2,1)S(1)} collective-permute-done((bf16[16,1792]{1,0:T(8,128)(2,1)S(1)}, bf16[16,1792]{1,0:T(8,128)(2,1)S(1)}, u32[]{:S(2)}, u32[]{:S(2)}) %collective-permute-start.7) | collective-permute-done | bytes 57376 | tf_op jit(solution)/shard_map/ppermute | solution.py:224
  20.3 0.7 %ahead.1 = (f32[64,512]{1,0:T(8,128)S(1)}, f32[64,512]{1,0:T(8,128)S(1)}) custom-call(bf16[16,1792]{1,0:T(8,128)(2,1)S(1)} %get-tuple-element.32.refs_0_, bf16[16,1792]{1,0:T(8,128)(2,1)S(1)} %collective-permute-done.6.refs_1_, bf16[16,1792]{1,0:T(8,128)(2,1)S(1)} %collective-permute-done.7.refs_2_, bf16[16,1792]{1,0:T(8,128)(2,1)S(1)} %collective-permute-done.8.refs_3_, ...), custom_call_target="tpu_custom_call" | custom-call | tf_op jit(solution)/shard_map/ahead/pallas_call | solution.py:284
  21.0 0.3 collective-permute-done.3.refs_1_
  21.4 0.8 %collective-permute-done.5.refs_3_ = bf16[16,1792]{1,0:T(8,128)(2,1)S(1)} collective-permute-done((bf16[16,1792]{1,0:T(8,128)(2,1)S(1)}, bf16[16,1792]{1,0:T(8,128)(2,1)S(1)}, u32[]{:S(2)}, u32[]{:S(2)}) %collective-permute-start.5) | collective-permute-done | bytes 57376 | tf_op jit(solution)/shard_map/ppermute | solution.py:224
  22.2 0.8 %hidden.1.after_ref.refs_0_ = bf16[64,512]{1,0:T(8,128)(2,1)S(1)} custom-call(bf16[16,1792]{1,0:T(8,128)(2,1)S(1)} %get-tuple-element.31.refs_0_, bf16[16,1792]{1,0:T(8,128)(2,1)S(1)} %collective-permute-done.3.refs_1_, bf16[16,1792]{1,0:T(8,128)(2,1)S(1)} %collective-permute-done.4.refs_2_, bf16[16,1792]{1,0:T(8,128)(2,1)S(1)} %collective-permute-done.5.refs_3_, ...), custom_call_target="tpu_custom_call" | custom-call | tf_op jit(solution)/shard_map/hidden/pallas_call | solution.py:297
  23.0 3.4 %collective-permute-start.11 = (bf16[64,512]{1,0:T(8,128)(2,1)S(1)}, bf16[64,512]{1,0:T(8,128)(2,1)S(1)}, u32[]{:S(2)}, u32[]{:S(2)}) collective-permute-start(bf16[64,512]{1,0:T(8,128)(2,1)S(1)} %hidden.1.after_ref.refs_0_), channel_id=1, source_target_pairs={{0,3},{1,2},{2,1},{3,0},{4,7},{5,6},{6,5},{7,4},{8,11},{9,10},{10,... | collective-permute-start | bytes 196616 | tf_op jit(solution)/shard_map/ppermute | solution.py:224
  26.4 1.0 %collective-permute-start.9 = (bf16[64,512]{1,0:T(8,128)(2,1)S(1)}, bf16[64,512]{1,0:T(8,128)(2,1)S(1)}, u32[]{:S(2)}, u32[]{:S(2)}) collective-permute-start(bf16[64,512]{1,0:T(8,128)(2,1)S(1)} %hidden.1.after_ref.refs_0_), channel_id=1, source_target_pairs={{0,1},{1,0},{2,3},{3,2},{4,5},{5,4},{6,7},{7,6},{8,9},{9,8},{10,11... | collective-permute-start | bytes 196616 | tf_op jit(solution)/shard_map/ppermute | solution.py:224
  27.4 2.1 %prepare.1 = (bf16[2048,896]{1,0:T(8,128)(2,1)S(1)}, bf16[256,32]{1,0:T(8,128)(2,1)S(1)}) custom-call(bf16[64,512]{1,0:T(8,128)(2,1)S(1)} %hidden.1.after_ref.refs_0_, s32[8,256]{1,0:T(8,128)} %bitcast.10, f32[96,256]{1,0:T(8,128)} %bitcast.8, bf16[2048,896]{1,0:T(8,128)(2,1)} %bitcast.7), custom_call_target="tpu_custom_call" | custom-call | tf_op jit(solution)/shard_map/prepare/pallas_call | solution.py:305
  29.6 0.4 begin.1.refs_2_
  30.0 1.6 %collective-permute-done.10.refs_1_ = bf16[64,512]{1,0:T(8,128)(2,1)S(1)} collective-permute-done((bf16[64,512]{1,0:T(8,128)(2,1)S(1)}, bf16[64,512]{1,0:T(8,128)(2,1)S(1)}, u32[]{:S(2)}, u32[]{:S(2)}) %collective-permute-start.10) | collective-permute-done | bytes 65568 | tf_op jit(solution)/shard_map/ppermute | solution.py:224
  31.6 0.4 down.1
  32.1 2.1 %collective-permute-start.12 = (bf16[16,896]{1,0:T(8,128)(2,1)S(1)}, bf16[16,896]{1,0:T(8,128)(2,1)S(1)}, u32[]{:S(2)}, u32[]{:S(2)}) collective-permute-start(bf16[16,896]{1,0:T(8,128)(2,1)S(1)} %get-tuple-element.39), channel_id=1, source_target_pairs={{0,3},{1,2},{2,1},{3,0},{4,7},{5,6},{6,5},{7,4},{8,11},{9,10},{10,... | collective-permute-start | bytes 86024 | tf_op jit(solution)/shard_map/ppermute | solution.py:224
  34.2 2.3 %collective-permute-start.14 = (bf16[16,896]{1,0:T(8,128)(2,1)S(1)}, bf16[16,896]{1,0:T(8,128)(2,1)S(1)}, u32[]{:S(2)}, u32[]{:S(2)}) collective-permute-start(bf16[16,896]{1,0:T(8,128)(2,1)S(1)} %get-tuple-element.41), channel_id=1, source_target_pairs={{0,1},{1,0},{2,3},{3,2},{4,5},{5,4},{6,7},{7,6},{8,9},{9,8},{10,11... | collective-permute-start | bytes 86024 | tf_op jit(solution)/shard_map/ppermute | solution.py:224
  36.5 1.3 %collective-permute-done.12.refs_0_ = bf16[16,896]{1,0:T(8,128)(2,1)S(1)} collective-permute-done((bf16[16,896]{1,0:T(8,128)(2,1)S(1)}, bf16[16,896]{1,0:T(8,128)(2,1)S(1)}, u32[]{:S(2)}, u32[]{:S(2)}) %collective-permute-start.12) | collective-permute-done | bytes 28704 | tf_op jit(solution)/shard_map/ppermute | solution.py:224
  37.8 1.4 %collective-permute-done.13.refs_1_ = bf16[16,896]{1,0:T(8,128)(2,1)S(1)} collective-permute-done((bf16[16,896]{1,0:T(8,128)(2,1)S(1)}, bf16[16,896]{1,0:T(8,128)(2,1)S(1)}, u32[]{:S(2)}, u32[]{:S(2)}) %collective-permute-start.13) | collective-permute-done | bytes 28704 | tf_op jit(solution)/shard_map/ppermute | solution.py:224
  39.2 0.2 spread.1
  39.5 1.4 %collective-permute-start.16 = (bf16[4,8,896]{2,1,0:T(8,128)(2,1)S(1)}, bf16[4,8,896]{2,1,0:T(8,128)(2,1)S(1)}, u32[]{:S(2)}, u32[]{:S(2)}) collective-permute-start(bf16[4,8,896]{2,1,0:T(8,128)(2,1)S(1)} %get-tuple-element.44), channel_id=1, source_target_pairs={{0,8},{4,12},{8,0},{12,4},{1,9},{5,13},{9,1},{13,5},{2,10},{6,14},... | collective-permute-start | bytes 172040 | tf_op jit(solution)/shard_map/ppermute | solution.py:224
  40.8 0.4 collective-permute-start.17
  41.3 2.4 %collective-permute-done.15.refs_0_ = bf16[4,8,896]{2,1,0:T(8,128)(2,1)S(1)} collective-permute-done((bf16[4,8,896]{2,1,0:T(8,128)(2,1)S(1)}, bf16[4,8,896]{2,1,0:T(8,128)(2,1)S(1)}, u32[]{:S(2)}, u32[]{:S(2)}) %collective-permute-start.15) | collective-permute-done | bytes 57376 | tf_op jit(solution)/shard_map/ppermute | solution.py:224
  43.6 1.0 %collective-permute-done.16.refs_1_ = bf16[4,8,896]{2,1,0:T(8,128)(2,1)S(1)} collective-permute-done((bf16[4,8,896]{2,1,0:T(8,128)(2,1)S(1)}, bf16[4,8,896]{2,1,0:T(8,128)(2,1)S(1)}, u32[]{:S(2)}, u32[]{:S(2)}) %collective-permute-start.16) | collective-permute-done | bytes 57376 | tf_op jit(solution)/shard_map/ppermute | solution.py:224
  44.7 1.5 %combine.1 = bf16[256,3584]{1,0:T(8,128)(2,1)} custom-call(bf16[256,32]{1,0:T(8,128)(2,1)S(1)} %get-tuple-element.36.mixing_ref, bf16[4,8,896]{2,1,0:T(8,128)(2,1)S(1)} %collective-permute-done.15.refs_0_, bf16[4,8,896]{2,1,0:T(8,128)(2,1)S(1)} %collective-permute-done.16.refs_1_, bf16[4,8,896]{2,1,0:T(8,128)(2,1)S(1)} %collective-permute-done.17.refs_2_, ...), custom_call_target="tpu_custom_call" | custom-call | tf_op jit(solution)/shard_map/combine/pallas_call | solution.py:357
  (14 shorter events, 0.2 us)
Async XLA Ops:
  2.0 6.3 %collective-permute-start = (bf16[8,3712]{1,0:T(8,128)(2,1)S(1)}, bf16[8,3712]{1,0:T(8,128)(2,1)S(1)}, u32[]{:S(2)}, u32[]{:S(2)}) collective-permute-start(bf16[8,3712]{1,0:T(8,128)(2,1)S(1)} %get-tuple-element.28), channel_id=1, source_target_pairs={{0,12},{4,8},{8,4},{12,0},{1,13},{5,9},{9,5},{13,1},{2,14},{6,10},... | collective-permute-start | bytes 178184 | tf_op jit(solution)/shard_map/ppermute | solution.py:224
  4.4 4.5 %collective-permute-start.1 = (bf16[8,3712]{1,0:T(8,128)(2,1)S(1)}, bf16[8,3712]{1,0:T(8,128)(2,1)S(1)}, u32[]{:S(2)}, u32[]{:S(2)}) collective-permute-start(bf16[8,3712]{1,0:T(8,128)(2,1)S(1)} %get-tuple-element.29), channel_id=1, source_target_pairs={{0,8},{4,12},{8,0},{12,4},{1,9},{5,13},{9,1},{13,5},{2,10},{6,14},... | collective-permute-start | bytes 178184 | tf_op jit(solution)/shard_map/ppermute | solution.py:224
  5.1 3.9 %collective-permute-start.2 = (bf16[8,3712]{1,0:T(8,128)(2,1)S(1)}, bf16[8,3712]{1,0:T(8,128)(2,1)S(1)}, u32[]{:S(2)}, u32[]{:S(2)}) collective-permute-start(bf16[8,3712]{1,0:T(8,128)(2,1)S(1)} %get-tuple-element.30), channel_id=1, source_target_pairs={{0,4},{4,0},{8,12},{12,8},{1,5},{5,1},{9,13},{13,9},{2,6},{6,2},{1... | collective-permute-start | bytes 178184 | tf_op jit(solution)/shard_map/ppermute | solution.py:224
  9.3 8.7 %collective-permute-start.4 = (bf16[16,1792]{1,0:T(8,128)(2,1)S(1)}, bf16[16,1792]{1,0:T(8,128)(2,1)S(1)}, u32[]{:S(2)}, u32[]{:S(2)}) collective-permute-start(bf16[16,1792]{1,0:T(8,128)(2,1)S(1)} %get-tuple-element.31.refs_0_), channel_id=1, source_target_pairs={{0,2},{1,3},{2,0},{3,1},{4,6},{5,7},{6,4},{7,5},{8,10},{9,11},{10,... | collective-permute-start | bytes 172040 | tf_op jit(solution)/shard_map/ppermute | solution.py:224
  12.0 6.0 %collective-permute-start.6 = (bf16[16,1792]{1,0:T(8,128)(2,1)S(1)}, bf16[16,1792]{1,0:T(8,128)(2,1)S(1)}, u32[]{:S(2)}, u32[]{:S(2)}) collective-permute-start(bf16[16,1792]{1,0:T(8,128)(2,1)S(1)} %get-tuple-element.32.refs_0_), channel_id=1, source_target_pairs={{0,1},{1,0},{2,3},{3,2},{4,5},{5,4},{6,7},{7,6},{8,9},{9,8},{10,11... | collective-permute-start | bytes 172040 | tf_op jit(solution)/shard_map/ppermute | solution.py:224
  13.6 6.7 %collective-permute-start.7 = (bf16[16,1792]{1,0:T(8,128)(2,1)S(1)}, bf16[16,1792]{1,0:T(8,128)(2,1)S(1)}, u32[]{:S(2)}, u32[]{:S(2)}) collective-permute-start(bf16[16,1792]{1,0:T(8,128)(2,1)S(1)} %get-tuple-element.32.refs_0_), channel_id=1, source_target_pairs={{0,3},{1,2},{2,1},{3,0},{4,7},{5,6},{6,5},{7,4},{8,11},{9,10},{10,... | collective-permute-start | bytes 172040 | tf_op jit(solution)/shard_map/ppermute | solution.py:224
  13.8 6.5 %collective-permute-start.8 = (bf16[16,1792]{1,0:T(8,128)(2,1)S(1)}, bf16[16,1792]{1,0:T(8,128)(2,1)S(1)}, u32[]{:S(2)}, u32[]{:S(2)}) collective-permute-start(bf16[16,1792]{1,0:T(8,128)(2,1)S(1)} %get-tuple-element.32.refs_0_), channel_id=1, source_target_pairs={{0,2},{1,3},{2,0},{3,1},{4,6},{5,7},{6,4},{7,5},{8,10},{9,11},{10,... | collective-permute-start | bytes 172040 | tf_op jit(solution)/shard_map/ppermute | solution.py:224
  15.5 5.8 %collective-permute-start.3 = (bf16[16,1792]{1,0:T(8,128)(2,1)S(1)}, bf16[16,1792]{1,0:T(8,128)(2,1)S(1)}, u32[]{:S(2)}, u32[]{:S(2)}) collective-permute-start(bf16[16,1792]{1,0:T(8,128)(2,1)S(1)} %get-tuple-element.31.refs_0_), channel_id=1, source_target_pairs={{0,1},{1,0},{2,3},{3,2},{4,5},{5,4},{6,7},{7,6},{8,9},{9,8},{10,11... | collective-permute-start | bytes 172040 | tf_op jit(solution)/shard_map/ppermute | solution.py:224
  18.0 4.2 %collective-permute-start.5 = (bf16[16,1792]{1,0:T(8,128)(2,1)S(1)}, bf16[16,1792]{1,0:T(8,128)(2,1)S(1)}, u32[]{:S(2)}, u32[]{:S(2)}) collective-permute-start(bf16[16,1792]{1,0:T(8,128)(2,1)S(1)} %collective-permute-done.4.refs_2_), channel_id=1, source_target_pairs={{0,1},{1,0},{2,3},{3,2},{4,5},{5,4},{6,7},{7,6},{8,9},{9,8},{10,11... | collective-permute-start | bytes 172040 | tf_op jit(solution)/shard_map/ppermute | solution.py:224
  23.0 6.6 %collective-permute-start.11 = (bf16[64,512]{1,0:T(8,128)(2,1)S(1)}, bf16[64,512]{1,0:T(8,128)(2,1)S(1)}, u32[]{:S(2)}, u32[]{:S(2)}) collective-permute-start(bf16[64,512]{1,0:T(8,128)(2,1)S(1)} %hidden.1.after_ref.refs_0_), channel_id=1, source_target_pairs={{0,3},{1,2},{2,1},{3,0},{4,7},{5,6},{6,5},{7,4},{8,11},{9,10},{10,... | collective-permute-start | bytes 196616 | tf_op jit(solution)/shard_map/ppermute | solution.py:224
  26.4 5.2 %collective-permute-start.10 = (bf16[64,512]{1,0:T(8,128)(2,1)S(1)}, bf16[64,512]{1,0:T(8,128)(2,1)S(1)}, u32[]{:S(2)}, u32[]{:S(2)}) collective-permute-start(bf16[64,512]{1,0:T(8,128)(2,1)S(1)} %hidden.1.after_ref.refs_0_), channel_id=1, source_target_pairs={{0,2},{1,3},{2,0},{3,1},{4,6},{5,7},{6,4},{7,5},{8,10},{9,11},{10,... | collective-permute-start | bytes 196616 | tf_op jit(solution)/shard_map/ppermute | solution.py:224
  26.4 5.2 %collective-permute-start.9 = (bf16[64,512]{1,0:T(8,128)(2,1)S(1)}, bf16[64,512]{1,0:T(8,128)(2,1)S(1)}, u32[]{:S(2)}, u32[]{:S(2)}) collective-permute-start(bf16[64,512]{1,0:T(8,128)(2,1)S(1)} %hidden.1.after_ref.refs_0_), channel_id=1, source_target_pairs={{0,1},{1,0},{2,3},{3,2},{4,5},{5,4},{6,7},{7,6},{8,9},{9,8},{10,11... | collective-permute-start | bytes 196616 | tf_op jit(solution)/shard_map/ppermute | solution.py:224
  32.1 5.7 %collective-permute-start.12 = (bf16[16,896]{1,0:T(8,128)(2,1)S(1)}, bf16[16,896]{1,0:T(8,128)(2,1)S(1)}, u32[]{:S(2)}, u32[]{:S(2)}) collective-permute-start(bf16[16,896]{1,0:T(8,128)(2,1)S(1)} %get-tuple-element.39), channel_id=1, source_target_pairs={{0,3},{1,2},{2,1},{3,0},{4,7},{5,6},{6,5},{7,4},{8,11},{9,10},{10,... | collective-permute-start | bytes 86024 | tf_op jit(solution)/shard_map/ppermute | solution.py:224
  34.2 5.0 %collective-permute-start.13 = (bf16[16,896]{1,0:T(8,128)(2,1)S(1)}, bf16[16,896]{1,0:T(8,128)(2,1)S(1)}, u32[]{:S(2)}, u32[]{:S(2)}) collective-permute-start(bf16[16,896]{1,0:T(8,128)(2,1)S(1)} %get-tuple-element.40), channel_id=1, source_target_pairs={{0,2},{1,3},{2,0},{3,1},{4,6},{5,7},{6,4},{7,5},{8,10},{9,11},{10,... | collective-permute-start | bytes 86024 | tf_op jit(solution)/shard_map/ppermute | solution.py:224
  34.2 5.0 %collective-permute-start.14 = (bf16[16,896]{1,0:T(8,128)(2,1)S(1)}, bf16[16,896]{1,0:T(8,128)(2,1)S(1)}, u32[]{:S(2)}, u32[]{:S(2)}) collective-permute-start(bf16[16,896]{1,0:T(8,128)(2,1)S(1)} %get-tuple-element.41), channel_id=1, source_target_pairs={{0,1},{1,0},{2,3},{3,2},{4,5},{5,4},{6,7},{7,6},{8,9},{9,8},{10,11... | collective-permute-start | bytes 86024 | tf_op jit(solution)/shard_map/ppermute | solution.py:224
  39.4 4.3 %collective-permute-start.15 = (bf16[4,8,896]{2,1,0:T(8,128)(2,1)S(1)}, bf16[4,8,896]{2,1,0:T(8,128)(2,1)S(1)}, u32[]{:S(2)}, u32[]{:S(2)}) collective-permute-start(bf16[4,8,896]{2,1,0:T(8,128)(2,1)S(1)} %get-tuple-element.43), channel_id=1, source_target_pairs={{0,12},{4,8},{8,4},{12,0},{1,13},{5,9},{9,5},{13,1},{2,14},{6,10},... | collective-permute-start | bytes 172040 | tf_op jit(solution)/shard_map/ppermute | solution.py:224
  39.5 5.2 %collective-permute-start.16 = (bf16[4,8,896]{2,1,0:T(8,128)(2,1)S(1)}, bf16[4,8,896]{2,1,0:T(8,128)(2,1)S(1)}, u32[]{:S(2)}, u32[]{:S(2)}) collective-permute-start(bf16[4,8,896]{2,1,0:T(8,128)(2,1)S(1)} %get-tuple-element.44), channel_id=1, source_target_pairs={{0,8},{4,12},{8,0},{12,4},{1,9},{5,13},{9,1},{13,5},{2,10},{6,14},... | collective-permute-start | bytes 172040 | tf_op jit(solution)/shard_map/ppermute | solution.py:224
  40.8 3.8 %collective-permute-start.17 = (bf16[4,8,896]{2,1,0:T(8,128)(2,1)S(1)}, bf16[4,8,896]{2,1,0:T(8,128)(2,1)S(1)}, u32[]{:S(2)}, u32[]{:S(2)}) collective-permute-start(bf16[4,8,896]{2,1,0:T(8,128)(2,1)S(1)} %get-tuple-element.45), channel_id=1, source_target_pairs={{0,4},{4,0},{8,12},{12,8},{1,5},{5,1},{9,13},{13,9},{2,6},{6,2},{1... | collective-permute-start | bytes 172040 | tf_op jit(solution)/shard_map/ppermute | solution.py:224

commit v14 on v11

--- a/solution.py
+++ b/solution.py
@@ -185,20 +185,25 @@
 
 def down_kernel(columns, which, *refs):
     count = len(which)
-    hiddens, (sum_ref, down_ref), outs = refs[:count], refs[count : count + 2], refs[count + 2 :]
-    total = sum_ref[...] + down_sum(columns, which, hiddens, down_ref)
-    slots = total.shape[0] // columns
-    for e in range(columns):
-        outs[e][...] = total[e * slots : (e + 1) * slots].astype(BF16)
+    hiddens, (sum_ref, down_ref) = refs[:count], refs[count : count + 2]
+    outs, total_ref = refs[count + 2 : -1], refs[-1]
+    me = lax.axis_index("ing")
+    total_ref[...] = sum_ref[...] + down_sum(columns, which, hiddens, down_ref)
+    slots = total_ref.shape[0] // columns
+    for s in range(columns):
+        at = pl.multiple_of((lax.rem(me + s, columns) ^ me) * slots, slots)
+        outs[s][...] = total_ref[pl.ds(at, slots), :].astype(BF16)
 
 
 def spread_kernel(groups, columns, pick_ref, *refs):
-    blocks, outs = refs[:columns][::-1], refs[columns:]
-    for e in range(columns):
-        block = blocks[e][...]
+    blocks, outs = refs[:columns], refs[columns:]
+    me = lax.axis_index("ing")
+    for k in range(columns):
+        block = blocks[k][...]
+        place = lax.rem(me + columns - (k + 1), columns) ^ me
         back = jnp.dot(pick_ref[:, : block.shape[0]], block, preferred_element_type=F32)
         for d in range(groups):
-            outs[d][e] = back[d * CAP : (d + 1) * CAP].astype(BF16)
+            outs[d][place] = back[d * CAP : (d + 1) * CAP].astype(BF16)
 
 
 def combine_kernel(groups, columns, mixing_ref, *refs):
@@ -339,10 +344,13 @@
         out_shape=[jax.ShapeDtypeStruct((slots, share), BF16)] * columns,
         in_specs=[VMEM] * (len(late) + 2),
         out_specs=[VMEM] * columns,
-        compiler_params=params(2 * columns * slots * (columns * units + 6 * share)),
+        scratch_shapes=[pltpu.VMEM((columns * slots, share), F32)],
+        compiler_params=params(2 * columns * slots * (columns * units + 8 * share)),
         name="down",
     )(*[hiddens[f] for f in late], begun, down)
-    results = swap_all(results, "ing")
+    results = [
+        lax.ppermute(results[s], "ing", [(a, (a + s) % columns) for a in range(columns)]) for s in range(1, columns)
+    ] + [results[0]]
 
     backs = pl.pallas_call(
         functools.partial(spread_kernel, groups, columns),

time: 46.2 us -> 45.8 us (level)
  waiting for transfers between devices: 11.7 us -> 10.9 us
    ppermute x0 -> x3, starting transfers between devices: none -> 4.92 us  [local(): lax.ppermute(results[s], 'ing', [(a, (a + s) % columns) for a in range(co...]
    ppermute x18 -> x15, starting transfers between devices: 22.7 us -> 18.2 us  [swap(): lax.ppermute(x, name, [(a, a ^ step) for a in range(lax.axis_size(name))])]
    ppermute x18 -> x15, waiting for transfers between devices: 11.7 us -> 9.25 us  [swap(): lax.ppermute(x, name, [(a, a ^ step) for a in range(lax.axis_size(name))])]
    ppermute x0 -> x3, waiting for transfers between devices: none -> 1.61 us  [local(): lax.ppermute(results[s], 'ing', [(a, (a + s) % columns) for a in range(co...]
where the time goes in v14:
time: 45.8 us; the launch traced here: 45.6 us
  starting transfers between devices  23.1 us (50%)
  Pallas kernels  11.5 us (25%)
  waiting for transfers between devices  10.9 us (24%)
    ppermute x15, starting transfers between devices, swap(): lax.ppermute(x, name, [(a, a ^ step) for a in range(lax.axis_size(name))])  18.2 us
    ppermute x15, waiting for transfers between devices, swap(): lax.ppermute(x, name, [(a, a ^ step) for a in range(lax.axis_size(name))])  9.25 us
    ppermute x3, starting transfers between devices, local(): lax.ppermute(results[s], 'ing', [(a, (a + s) % columns) for a in range(co...  4.92 us
    pallas_call x1, Pallas kernels, local(): pl.pallas_call(load_kernel, out_shape=[pltpu.VMEM(w.shape, BF16) for w in...  3.17 us
    pallas_call x1, Pallas kernels, local(): pl.pallas_call(functools.partial(prepare_kernel, groups), out_shape=[pltp...  2.13 us
    pallas_call x1, Pallas kernels, local(): pl.pallas_call(functools.partial(dispatch_kernel, groups, features // 2),...  1.79 us
    ppermute x3, waiting for transfers between devices, local(): lax.ppermute(results[s], 'ing', [(a, (a + s) % columns) for a in range(co...  1.61 us
    pallas_call x1, Pallas kernels, local(): pl.pallas_call(functools.partial(combine_kernel, groups, columns), out_sh...  1.49 us
  transfers between devices with their start and end apart: 18, of which 9 were waited for; matrix products, arithmetic and copies ran while one was open for 0% of the time, Pallas kernels for 14%

profile of v14, /device:TPU:0, one launch (start us, length us, event | category | flops | bytes accessed | tf_op | source)
XLA Modules:
  0.0 45.6 jit_solution(13614564767104860029)
XLA Ops:
  0.0 1.8 %dispatch.1 = (bf16[8,3712]{1,0:T(8,128)(2,1)S(1)}, bf16[8,3712]{1,0:T(8,128)(2,1)S(1)}, bf16[8,3712]{1,0:T(8,128)(2,1)S(1)}, bf16[8,3712]{1,0:T(8,128)(2,1)S(1)}) custom-call(s32[8,256]{1,0:T(8,128)} %bitcast.9, bf16[256,3584]{1,0:T(8,128)(2,1)} %tokens_ref.1), custom_call_target="tpu_custom_call" | custom-call | tf_op jit(solution)/shard_map/dispatch/pallas_call | solution.py:251
  1.8 2.4 %collective-permute-start = (bf16[8,3712]{1,0:T(8,128)(2,1)S(1)}, bf16[8,3712]{1,0:T(8,128)(2,1)S(1)}, u32[]{:S(2)}, u32[]{:S(2)}) collective-permute-start(bf16[8,3712]{1,0:T(8,128)(2,1)S(1)} %get-tuple-element.28), channel_id=1, source_target_pairs={{0,12},{4,8},{8,4},{12,0},{1,13},{5,9},{9,5},{13,1},{2,14},{6,10},... | collective-permute-start | bytes 178184 | tf_op jit(solution)/shard_map/ppermute | solution.py:234
  4.2 0.6 %collective-permute-start.1 = (bf16[8,3712]{1,0:T(8,128)(2,1)S(1)}, bf16[8,3712]{1,0:T(8,128)(2,1)S(1)}, u32[]{:S(2)}, u32[]{:S(2)}) collective-permute-start(bf16[8,3712]{1,0:T(8,128)(2,1)S(1)} %get-tuple-element.29), channel_id=1, source_target_pairs={{0,8},{4,12},{8,0},{12,4},{1,9},{5,13},{9,1},{13,5},{2,10},{6,14},... | collective-permute-start | bytes 178184 | tf_op jit(solution)/shard_map/ppermute | solution.py:234
  4.9 3.2 %load.1 = (bf16[3584,512]{1,0:T(8,128)(2,1)S(1)}, bf16[3584,512]{1,0:T(8,128)(2,1)S(1)}) custom-call(bf16[8,3712]{1,0:T(8,128)(2,1)S(1)} %get-tuple-element.26.after_ref.refs_3_, bf16[3584,512]{1,0:T(8,128)(2,1)} %bitcast.5, bf16[3584,512]{1,0:T(8,128)(2,1)} %bitcast.6), custom_call_target="tpu_custom_call" | custom-call | tf_op jit(solution)/shard_map/load/pallas_call | solution.py:269
  8.1 0.7 %collective-permute-done.1.refs_1_ = bf16[8,3712]{1,0:T(8,128)(2,1)S(1)} collective-permute-done((bf16[8,3712]{1,0:T(8,128)(2,1)S(1)}, bf16[8,3712]{1,0:T(8,128)(2,1)S(1)}, u32[]{:S(2)}, u32[]{:S(2)}) %collective-permute-start.1) | collective-permute-done | bytes 59424 | tf_op jit(solution)/shard_map/ppermute | solution.py:234
  8.8 0.3 compact.1
  9.1 2.7 %collective-permute-start.4 = (bf16[16,1792]{1,0:T(8,128)(2,1)S(1)}, bf16[16,1792]{1,0:T(8,128)(2,1)S(1)}, u32[]{:S(2)}, u32[]{:S(2)}) collective-permute-start(bf16[16,1792]{1,0:T(8,128)(2,1)S(1)} %get-tuple-element.31.refs_0_), channel_id=1, source_target_pairs={{0,2},{1,3},{2,0},{3,1},{4,6},{5,7},{6,4},{7,5},{8,10},{9,11},{10,... | collective-permute-start | bytes 172040 | tf_op jit(solution)/shard_map/ppermute | solution.py:234
  11.8 1.6 %collective-permute-start.6 = (bf16[16,1792]{1,0:T(8,128)(2,1)S(1)}, bf16[16,1792]{1,0:T(8,128)(2,1)S(1)}, u32[]{:S(2)}, u32[]{:S(2)}) collective-permute-start(bf16[16,1792]{1,0:T(8,128)(2,1)S(1)} %get-tuple-element.32.refs_0_), channel_id=1, source_target_pairs={{0,1},{1,0},{2,3},{3,2},{4,5},{5,4},{6,7},{7,6},{8,9},{9,8},{10,11... | collective-permute-start | bytes 172040 | tf_op jit(solution)/shard_map/ppermute | solution.py:234
  13.6 1.8 %collective-permute-start.8 = (bf16[16,1792]{1,0:T(8,128)(2,1)S(1)}, bf16[16,1792]{1,0:T(8,128)(2,1)S(1)}, u32[]{:S(2)}, u32[]{:S(2)}) collective-permute-start(bf16[16,1792]{1,0:T(8,128)(2,1)S(1)} %get-tuple-element.32.refs_0_), channel_id=1, source_target_pairs={{0,2},{1,3},{2,0},{3,1},{4,6},{5,7},{6,4},{7,5},{8,10},{9,11},{10,... | collective-permute-start | bytes 172040 | tf_op jit(solution)/shard_map/ppermute | solution.py:234
  15.3 2.5 %collective-permute-start.3 = (bf16[16,1792]{1,0:T(8,128)(2,1)S(1)}, bf16[16,1792]{1,0:T(8,128)(2,1)S(1)}, u32[]{:S(2)}, u32[]{:S(2)}) collective-permute-start(bf16[16,1792]{1,0:T(8,128)(2,1)S(1)} %get-tuple-element.31.refs_0_), channel_id=1, source_target_pairs={{0,1},{1,0},{2,3},{3,2},{4,5},{5,4},{6,7},{7,6},{8,9},{9,8},{10,11... | collective-permute-start | bytes 172040 | tf_op jit(solution)/shard_map/ppermute | solution.py:234
  17.8 2.2 %collective-permute-done.7.refs_2_ = bf16[16,1792]{1,0:T(8,128)(2,1)S(1)} collective-permute-done((bf16[16,1792]{1,0:T(8,128)(2,1)S(1)}, bf16[16,1792]{1,0:T(8,128)(2,1)S(1)}, u32[]{:S(2)}, u32[]{:S(2)}) %collective-permute-start.7) | collective-permute-done | bytes 57376 | tf_op jit(solution)/shard_map/ppermute | solution.py:234
  20.1 0.7 %ahead.1 = (f32[64,512]{1,0:T(8,128)S(1)}, f32[64,512]{1,0:T(8,128)S(1)}) custom-call(bf16[16,1792]{1,0:T(8,128)(2,1)S(1)} %get-tuple-element.32.refs_0_, bf16[16,1792]{1,0:T(8,128)(2,1)S(1)} %collective-permute-done.6.refs_1_, bf16[16,1792]{1,0:T(8,128)(2,1)S(1)} %collective-permute-done.7.refs_2_, bf16[16,1792]{1,0:T(8,128)(2,1)S(1)} %collective-permute-done.8.refs_3_, ...), custom_call_target="tpu_custom_call" | custom-call | tf_op jit(solution)/shard_map/ahead/pallas_call | solution.py:294
  20.8 0.3 collective-permute-done.3.refs_1_
  21.2 0.8 %collective-permute-done.5.refs_3_ = bf16[16,1792]{1,0:T(8,128)(2,1)S(1)} collective-permute-done((bf16[16,1792]{1,0:T(8,128)(2,1)S(1)}, bf16[16,1792]{1,0:T(8,128)(2,1)S(1)}, u32[]{:S(2)}, u32[]{:S(2)}) %collective-permute-start.5) | collective-permute-done | bytes 57376 | tf_op jit(solution)/shard_map/ppermute | solution.py:234
  22.0 0.8 %hidden.1.after_ref.refs_0_ = bf16[64,512]{1,0:T(8,128)(2,1)S(1)} custom-call(bf16[16,1792]{1,0:T(8,128)(2,1)S(1)} %get-tuple-element.31.refs_0_, bf16[16,1792]{1,0:T(8,128)(2,1)S(1)} %collective-permute-done.3.refs_1_, bf16[16,1792]{1,0:T(8,128)(2,1)S(1)} %collective-permute-done.4.refs_2_, bf16[16,1792]{1,0:T(8,128)(2,1)S(1)} %collective-permute-done.5.refs_3_, ...), custom_call_target="tpu_custom_call" | custom-call | tf_op jit(solution)/shard_map/hidden/pallas_call | solution.py:307
  22.8 3.4 %collective-permute-start.11 = (bf16[64,512]{1,0:T(8,128)(2,1)S(1)}, bf16[64,512]{1,0:T(8,128)(2,1)S(1)}, u32[]{:S(2)}, u32[]{:S(2)}) collective-permute-start(bf16[64,512]{1,0:T(8,128)(2,1)S(1)} %hidden.1.after_ref.refs_0_), channel_id=1, source_target_pairs={{0,3},{1,2},{2,1},{3,0},{4,7},{5,6},{6,5},{7,4},{8,11},{9,10},{10,... | collective-permute-start | bytes 196616 | tf_op jit(solution)/shard_map/ppermute | solution.py:234
  26.2 1.0 %collective-permute-start.9 = (bf16[64,512]{1,0:T(8,128)(2,1)S(1)}, bf16[64,512]{1,0:T(8,128)(2,1)S(1)}, u32[]{:S(2)}, u32[]{:S(2)}) collective-permute-start(bf16[64,512]{1,0:T(8,128)(2,1)S(1)} %hidden.1.after_ref.refs_0_), channel_id=1, source_target_pairs={{0,1},{1,0},{2,3},{3,2},{4,5},{5,4},{6,7},{7,6},{8,9},{9,8},{10,11... | collective-permute-start | bytes 196616 | tf_op jit(solution)/shard_map/ppermute | solution.py:234
  27.2 2.1 %prepare.1 = (bf16[2048,896]{1,0:T(8,128)(2,1)S(1)}, bf16[256,32]{1,0:T(8,128)(2,1)S(1)}) custom-call(bf16[64,512]{1,0:T(8,128)(2,1)S(1)} %hidden.1.after_ref.refs_0_, s32[8,256]{1,0:T(8,128)} %bitcast.10, f32[96,256]{1,0:T(8,128)} %bitcast.8, bf16[2048,896]{1,0:T(8,128)(2,1)} %bitcast.7), custom_call_target="tpu_custom_call" | custom-call | tf_op jit(solution)/shard_map/prepare/pallas_call | solution.py:315
  29.4 0.4 begin.1.refs_2_
  29.8 1.6 %collective-permute-done.10.refs_1_ = bf16[64,512]{1,0:T(8,128)(2,1)S(1)} collective-permute-done((bf16[64,512]{1,0:T(8,128)(2,1)S(1)}, bf16[64,512]{1,0:T(8,128)(2,1)S(1)}, u32[]{:S(2)}, u32[]{:S(2)}) %collective-permute-start.10) | collective-permute-done | bytes 65568 | tf_op jit(solution)/shard_map/ppermute | solution.py:234
  31.5 0.4 down.1
  31.9 0.5 %collective-permute-start.12 = (bf16[16,896]{1,0:T(8,128)(2,1)S(1)}, bf16[16,896]{1,0:T(8,128)(2,1)S(1)}, u32[]{:S(2)}, u32[]{:S(2)}) collective-permute-start(bf16[16,896]{1,0:T(8,128)(2,1)S(1)} %get-tuple-element.39), channel_id=1, source_target_pairs={{0,1},{1,2},{2,3},{3,0},{4,5},{5,6},{6,7},{7,4},{8,9},{9,10},{10,1... | collective-permute-start | bytes 86024 | tf_op jit(solution)/shard_map/ppermute | solution.py:352
  32.4 2.1 %collective-permute-start.13 = (bf16[16,896]{1,0:T(8,128)(2,1)S(1)}, bf16[16,896]{1,0:T(8,128)(2,1)S(1)}, u32[]{:S(2)}, u32[]{:S(2)}) collective-permute-start(bf16[16,896]{1,0:T(8,128)(2,1)S(1)} %get-tuple-element.40), channel_id=1, source_target_pairs={{0,2},{1,3},{2,0},{3,1},{4,6},{5,7},{6,4},{7,5},{8,10},{9,11},{10,... | collective-permute-start | bytes 86024 | tf_op jit(solution)/shard_map/ppermute | solution.py:352
  34.6 2.3 %collective-permute-start.14 = (bf16[16,896]{1,0:T(8,128)(2,1)S(1)}, bf16[16,896]{1,0:T(8,128)(2,1)S(1)}, u32[]{:S(2)}, u32[]{:S(2)}) collective-permute-start(bf16[16,896]{1,0:T(8,128)(2,1)S(1)} %get-tuple-element.41), channel_id=1, source_target_pairs={{0,3},{1,0},{2,1},{3,2},{4,7},{5,4},{6,5},{7,6},{8,11},{9,8},{10,9... | collective-permute-start | bytes 86024 | tf_op jit(solution)/shard_map/ppermute | solution.py:352
  36.8 0.9 %collective-permute-done.12.refs_0_ = bf16[16,896]{1,0:T(8,128)(2,1)S(1)} collective-permute-done((bf16[16,896]{1,0:T(8,128)(2,1)S(1)}, bf16[16,896]{1,0:T(8,128)(2,1)S(1)}, u32[]{:S(2)}, u32[]{:S(2)}) %collective-permute-start.12) | collective-permute-done | bytes 28704 | tf_op jit(solution)/shard_map/ppermute | solution.py:352
  37.8 0.7 %collective-permute-done.14.refs_2_ = bf16[16,896]{1,0:T(8,128)(2,1)S(1)} collective-permute-done((bf16[16,896]{1,0:T(8,128)(2,1)S(1)}, bf16[16,896]{1,0:T(8,128)(2,1)S(1)}, u32[]{:S(2)}, u32[]{:S(2)}) %collective-permute-start.14) | collective-permute-done | bytes 28704 | tf_op jit(solution)/shard_map/ppermute | solution.py:352
  38.4 0.2 spread.1
  38.7 1.6 %collective-permute-start.16 = (bf16[4,8,896]{2,1,0:T(8,128)(2,1)S(1)}, bf16[4,8,896]{2,1,0:T(8,128)(2,1)S(1)}, u32[]{:S(2)}, u32[]{:S(2)}) collective-permute-start(bf16[4,8,896]{2,1,0:T(8,128)(2,1)S(1)} %get-tuple-element.44), channel_id=1, source_target_pairs={{0,8},{4,12},{8,0},{12,4},{1,9},{5,13},{9,1},{13,5},{2,10},{6,14},... | collective-permute-start | bytes 172040 | tf_op jit(solution)/shard_map/ppermute | solution.py:234
  40.3 0.2 collective-permute-start.17
  40.6 2.3 %collective-permute-done.15.refs_0_ = bf16[4,8,896]{2,1,0:T(8,128)(2,1)S(1)} collective-permute-done((bf16[4,8,896]{2,1,0:T(8,128)(2,1)S(1)}, bf16[4,8,896]{2,1,0:T(8,128)(2,1)S(1)}, u32[]{:S(2)}, u32[]{:S(2)}) %collective-permute-start.15) | collective-permute-done | bytes 57376 | tf_op jit(solution)/shard_map/ppermute | solution.py:234
  42.8 1.3 %collective-permute-done.16.refs_1_ = bf16[4,8,896]{2,1,0:T(8,128)(2,1)S(1)} collective-permute-done((bf16[4,8,896]{2,1,0:T(8,128)(2,1)S(1)}, bf16[4,8,896]{2,1,0:T(8,128)(2,1)S(1)}, u32[]{:S(2)}, u32[]{:S(2)}) %collective-permute-start.16) | collective-permute-done | bytes 57376 | tf_op jit(solution)/shard_map/ppermute | solution.py:234
  44.1 1.5 %combine.1 = bf16[256,3584]{1,0:T(8,128)(2,1)} custom-call(bf16[256,32]{1,0:T(8,128)(2,1)S(1)} %get-tuple-element.36.mixing_ref, bf16[4,8,896]{2,1,0:T(8,128)(2,1)S(1)} %collective-permute-done.15.refs_0_, bf16[4,8,896]{2,1,0:T(8,128)(2,1)S(1)} %collective-permute-done.16.refs_1_, bf16[4,8,896]{2,1,0:T(8,128)(2,1)S(1)} %collective-permute-done.17.refs_2_, ...), custom_call_target="tpu_custom_call" | custom-call | tf_op jit(solution)/shard_map/combine/pallas_call | solution.py:370
  (14 shorter events, 0.4 us)
Async XLA Ops:
  1.8 6.3 %collective-permute-start = (bf16[8,3712]{1,0:T(8,128)(2,1)S(1)}, bf16[8,3712]{1,0:T(8,128)(2,1)S(1)}, u32[]{:S(2)}, u32[]{:S(2)}) collective-permute-start(bf16[8,3712]{1,0:T(8,128)(2,1)S(1)} %get-tuple-element.28), channel_id=1, source_target_pairs={{0,12},{4,8},{8,4},{12,0},{1,13},{5,9},{9,5},{13,1},{2,14},{6,10},... | collective-permute-start | bytes 178184 | tf_op jit(solution)/shard_map/ppermute | solution.py:234
  4.2 4.5 %collective-permute-start.1 = (bf16[8,3712]{1,0:T(8,128)(2,1)S(1)}, bf16[8,3712]{1,0:T(8,128)(2,1)S(1)}, u32[]{:S(2)}, u32[]{:S(2)}) collective-permute-start(bf16[8,3712]{1,0:T(8,128)(2,1)S(1)} %get-tuple-element.29), channel_id=1, source_target_pairs={{0,8},{4,12},{8,0},{12,4},{1,9},{5,13},{9,1},{13,5},{2,10},{6,14},... | collective-permute-start | bytes 178184 | tf_op jit(solution)/shard_map/ppermute | solution.py:234
  4.9 3.9 %collective-permute-start.2 = (bf16[8,3712]{1,0:T(8,128)(2,1)S(1)}, bf16[8,3712]{1,0:T(8,128)(2,1)S(1)}, u32[]{:S(2)}, u32[]{:S(2)}) collective-permute-start(bf16[8,3712]{1,0:T(8,128)(2,1)S(1)} %get-tuple-element.30), channel_id=1, source_target_pairs={{0,4},{4,0},{8,12},{12,8},{1,5},{5,1},{9,13},{13,9},{2,6},{6,2},{1... | collective-permute-start | bytes 178184 | tf_op jit(solution)/shard_map/ppermute | solution.py:234
  9.1 8.7 %collective-permute-start.4 = (bf16[16,1792]{1,0:T(8,128)(2,1)S(1)}, bf16[16,1792]{1,0:T(8,128)(2,1)S(1)}, u32[]{:S(2)}, u32[]{:S(2)}) collective-permute-start(bf16[16,1792]{1,0:T(8,128)(2,1)S(1)} %get-tuple-element.31.refs_0_), channel_id=1, source_target_pairs={{0,2},{1,3},{2,0},{3,1},{4,6},{5,7},{6,4},{7,5},{8,10},{9,11},{10,... | collective-permute-start | bytes 172040 | tf_op jit(solution)/shard_map/ppermute | solution.py:234
  11.8 6.0 %collective-permute-start.6 = (bf16[16,1792]{1,0:T(8,128)(2,1)S(1)}, bf16[16,1792]{1,0:T(8,128)(2,1)S(1)}, u32[]{:S(2)}, u32[]{:S(2)}) collective-permute-start(bf16[16,1792]{1,0:T(8,128)(2,1)S(1)} %get-tuple-element.32.refs_0_), channel_id=1, source_target_pairs={{0,1},{1,0},{2,3},{3,2},{4,5},{5,4},{6,7},{7,6},{8,9},{9,8},{10,11... | collective-permute-start | bytes 172040 | tf_op jit(solution)/shard_map/ppermute | solution.py:234
  13.4 6.7 %collective-permute-start.7 = (bf16[16,1792]{1,0:T(8,128)(2,1)S(1)}, bf16[16,1792]{1,0:T(8,128)(2,1)S(1)}, u32[]{:S(2)}, u32[]{:S(2)}) collective-permute-start(bf16[16,1792]{1,0:T(8,128)(2,1)S(1)} %get-tuple-element.32.refs_0_), channel_id=1, source_target_pairs={{0,3},{1,2},{2,1},{3,0},{4,7},{5,6},{6,5},{7,4},{8,11},{9,10},{10,... | collective-permute-start | bytes 172040 | tf_op jit(solution)/shard_map/ppermute | solution.py:234
  13.6 6.5 %collective-permute-start.8 = (bf16[16,1792]{1,0:T(8,128)(2,1)S(1)}, bf16[16,1792]{1,0:T(8,128)(2,1)S(1)}, u32[]{:S(2)}, u32[]{:S(2)}) collective-permute-start(bf16[16,1792]{1,0:T(8,128)(2,1)S(1)} %get-tuple-element.32.refs_0_), channel_id=1, source_target_pairs={{0,2},{1,3},{2,0},{3,1},{4,6},{5,7},{6,4},{7,5},{8,10},{9,11},{10,... | collective-permute-start | bytes 172040 | tf_op jit(solution)/shard_map/ppermute | solution.py:234
  15.3 5.8 %collective-permute-start.3 = (bf16[16,1792]{1,0:T(8,128)(2,1)S(1)}, bf16[16,1792]{1,0:T(8,128)(2,1)S(1)}, u32[]{:S(2)}, u32[]{:S(2)}) collective-permute-start(bf16[16,1792]{1,0:T(8,128)(2,1)S(1)} %get-tuple-element.31.refs_0_), channel_id=1, source_target_pairs={{0,1},{1,0},{2,3},{3,2},{4,5},{5,4},{6,7},{7,6},{8,9},{9,8},{10,11... | collective-permute-start | bytes 172040 | tf_op jit(solution)/shard_map/ppermute | solution.py:234
  17.8 4.2 %collective-permute-start.5 = (bf16[16,1792]{1,0:T(8,128)(2,1)S(1)}, bf16[16,1792]{1,0:T(8,128)(2,1)S(1)}, u32[]{:S(2)}, u32[]{:S(2)}) collective-permute-start(bf16[16,1792]{1,0:T(8,128)(2,1)S(1)} %collective-permute-done.4.refs_2_), channel_id=1, source_target_pairs={{0,1},{1,0},{2,3},{3,2},{4,5},{5,4},{6,7},{7,6},{8,9},{9,8},{10,11... | collective-permute-start | bytes 172040 | tf_op jit(solution)/shard_map/ppermute | solution.py:234
  22.8 6.6 %collective-permute-start.11 = (bf16[64,512]{1,0:T(8,128)(2,1)S(1)}, bf16[64,512]{1,0:T(8,128)(2,1)S(1)}, u32[]{:S(2)}, u32[]{:S(2)}) collective-permute-start(bf16[64,512]{1,0:T(8,128)(2,1)S(1)} %hidden.1.after_ref.refs_0_), channel_id=1, source_target_pairs={{0,3},{1,2},{2,1},{3,0},{4,7},{5,6},{6,5},{7,4},{8,11},{9,10},{10,... | collective-permute-start | bytes 196616 | tf_op jit(solution)/shard_map/ppermute | solution.py:234
  26.2 5.2 %collective-permute-start.10 = (bf16[64,512]{1,0:T(8,128)(2,1)S(1)}, bf16[64,512]{1,0:T(8,128)(2,1)S(1)}, u32[]{:S(2)}, u32[]{:S(2)}) collective-permute-start(bf16[64,512]{1,0:T(8,128)(2,1)S(1)} %hidden.1.after_ref.refs_0_), channel_id=1, source_target_pairs={{0,2},{1,3},{2,0},{3,1},{4,6},{5,7},{6,4},{7,5},{8,10},{9,11},{10,... | collective-permute-start | bytes 196616 | tf_op jit(solution)/shard_map/ppermute | solution.py:234
  26.2 5.2 %collective-permute-start.9 = (bf16[64,512]{1,0:T(8,128)(2,1)S(1)}, bf16[64,512]{1,0:T(8,128)(2,1)S(1)}, u32[]{:S(2)}, u32[]{:S(2)}) collective-permute-start(bf16[64,512]{1,0:T(8,128)(2,1)S(1)} %hidden.1.after_ref.refs_0_), channel_id=1, source_target_pairs={{0,1},{1,0},{2,3},{3,2},{4,5},{5,4},{6,7},{7,6},{8,9},{9,8},{10,11... | collective-permute-start | bytes 196616 | tf_op jit(solution)/shard_map/ppermute | solution.py:234
  31.9 5.8 %collective-permute-start.12 = (bf16[16,896]{1,0:T(8,128)(2,1)S(1)}, bf16[16,896]{1,0:T(8,128)(2,1)S(1)}, u32[]{:S(2)}, u32[]{:S(2)}) collective-permute-start(bf16[16,896]{1,0:T(8,128)(2,1)S(1)} %get-tuple-element.39), channel_id=1, source_target_pairs={{0,1},{1,2},{2,3},{3,0},{4,5},{5,6},{6,7},{7,4},{8,9},{9,10},{10,1... | collective-permute-start | bytes 86024 | tf_op jit(solution)/shard_map/ppermute | solution.py:352
  32.4 5.3 %collective-permute-start.13 = (bf16[16,896]{1,0:T(8,128)(2,1)S(1)}, bf16[16,896]{1,0:T(8,128)(2,1)S(1)}, u32[]{:S(2)}, u32[]{:S(2)}) collective-permute-start(bf16[16,896]{1,0:T(8,128)(2,1)S(1)} %get-tuple-element.40), channel_id=1, source_target_pairs={{0,2},{1,3},{2,0},{3,1},{4,6},{5,7},{6,4},{7,5},{8,10},{9,11},{10,... | collective-permute-start | bytes 86024 | tf_op jit(solution)/shard_map/ppermute | solution.py:352
  34.6 3.9 %collective-permute-start.14 = (bf16[16,896]{1,0:T(8,128)(2,1)S(1)}, bf16[16,896]{1,0:T(8,128)(2,1)S(1)}, u32[]{:S(2)}, u32[]{:S(2)}) collective-permute-start(bf16[16,896]{1,0:T(8,128)(2,1)S(1)} %get-tuple-element.41), channel_id=1, source_target_pairs={{0,3},{1,0},{2,1},{3,2},{4,7},{5,4},{6,5},{7,6},{8,11},{9,8},{10,9... | collective-permute-start | bytes 86024 | tf_op jit(solution)/shard_map/ppermute | solution.py:352
  38.6 4.2 %collective-permute-start.15 = (bf16[4,8,896]{2,1,0:T(8,128)(2,1)S(1)}, bf16[4,8,896]{2,1,0:T(8,128)(2,1)S(1)}, u32[]{:S(2)}, u32[]{:S(2)}) collective-permute-start(bf16[4,8,896]{2,1,0:T(8,128)(2,1)S(1)} %get-tuple-element.43), channel_id=1, source_target_pairs={{0,12},{4,8},{8,4},{12,0},{1,13},{5,9},{9,5},{13,1},{2,14},{6,10},... | collective-permute-start | bytes 172040 | tf_op jit(solution)/shard_map/ppermute | solution.py:234
  38.7 5.4 %collective-permute-start.16 = (bf16[4,8,896]{2,1,0:T(8,128)(2,1)S(1)}, bf16[4,8,896]{2,1,0:T(8,128)(2,1)S(1)}, u32[]{:S(2)}, u32[]{:S(2)}) collective-permute-start(bf16[4,8,896]{2,1,0:T(8,128)(2,1)S(1)} %get-tuple-element.44), channel_id=1, source_target_pairs={{0,8},{4,12},{8,0},{12,4},{1,9},{5,13},{9,1},{13,5},{2,10},{6,14},... | collective-permute-start | bytes 172040 | tf_op jit(solution)/shard_map/ppermute | solution.py:234
  40.3 3.8 %collective-permute-start.17 = (bf16[4,8,896]{2,1,0:T(8,128)(2,1)S(1)}, bf16[4,8,896]{2,1,0:T(8,128)(2,1)S(1)}, u32[]{:S(2)}, u32[]{:S(2)}) collective-permute-start(bf16[4,8,896]{2,1,0:T(8,128)(2,1)S(1)} %get-tuple-element.45), channel_id=1, source_target_pairs={{0,4},{4,0},{8,12},{12,8},{1,5},{5,1},{9,13},{13,9},{2,6},{6,2},{1... | collective-permute-start | bytes 172040 | tf_op jit(solution)/shard_map/ppermute | solution.py:234

commit v15 on v14

--- a/solution.py
+++ b/solution.py
@@ -48,15 +48,16 @@
     return jnp.concatenate(place, axis=0), rank[:, count - 1 :]
 
 
-def dispatch_kernel(groups, width, ids_ref, tokens_ref, *refs):
+def dispatch_kernel(groups, cut, ids_ref, tokens_ref, *refs):
     outs, (ids_held, staged, before_ref, sems) = refs[:groups], refs[groups:]
     me = lax.axis_index("grp")
     features = tokens_ref.shape[1]
-    first = pltpu.make_async_copy(ids_ref, ids_held, sems.at[features // width])
+    first = pltpu.make_async_copy(ids_ref, ids_held, sems.at[2])
     first.start()
     copies = []
-    for c in range(features // width):
-        part = pl.ds(c * width, width)
+    parts = (0, cut), (cut, features)
+    for c, (begin, end) in enumerate(parts):
+        part = pl.ds(begin, end - begin)
         copies.append(pltpu.make_async_copy(tokens_ref.at[:, part], staged.at[:, part], sems.at[c]))
         copies[-1].start()
     before_ref[...] = upto(tokens_ref.shape[0])
@@ -67,9 +68,9 @@
     for d in range(groups):
         live = slot < jnp.broadcast_to(counts[d : d + 1, :], (CAP, LANES))
         outs[d][:, features:] = jnp.where(live, 1.0, 0.0).astype(BF16)
-    for c in range(features // width):
-        copies[c].wait()
-        part = slice(c * width, (c + 1) * width)
+    for copy, (begin, end) in zip(copies, parts):
+        copy.wait()
+        part = slice(begin, end)
         rows = jnp.dot(place, staged[:, part], preferred_element_type=F32)
         for d in range(groups):
             outs[d][:, part] = rows[d * CAP : (d + 1) * CAP].astype(BF16)
@@ -249,7 +250,7 @@
     logits = pltpu.with_memory_space_constraint(router_logits.T, pltpu.HBM)
 
     outbound = pl.pallas_call(
-        functools.partial(dispatch_kernel, groups, features // 2),
+        functools.partial(dispatch_kernel, groups, features * 5 // 7),
         out_shape=[jax.ShapeDtypeStruct((CAP, wide), BF16)] * groups,
         in_specs=[ANY, ANY],
         out_specs=[VMEM] * groups,

time: 45.8 us -> 45.9 us (level)
  no operation moved by 1% of the time
where the time goes in v15:
time: 45.9 us; the launch traced here: 45.7 us
  starting transfers between devices  23.1 us (50%)
  Pallas kernels  11.6 us (25%)
  waiting for transfers between devices  10.9 us (24%)
    ppermute x15, starting transfers between devices, swap(): lax.ppermute(x, name, [(a, a ^ step) for a in range(lax.axis_size(name))])  18.2 us
    ppermute x15, waiting for transfers between devices, swap(): lax.ppermute(x, name, [(a, a ^ step) for a in range(lax.axis_size(name))])  9.24 us
    ppermute x3, starting transfers between devices, local(): lax.ppermute(results[s], 'ing', [(a, (a + s) % columns) for a in range(co...  4.92 us
    pallas_call x1, Pallas kernels, local(): pl.pallas_call(load_kernel, out_shape=[pltpu.VMEM(w.shape, BF16) for w in...  3.17 us
    pallas_call x1, Pallas kernels, local(): pl.pallas_call(functools.partial(prepare_kernel, groups), out_shape=[pltp...  2.13 us
    pallas_call x1, Pallas kernels, local(): pl.pallas_call(functools.partial(dispatch_kernel, groups, features * 5 //...  1.92 us
    ppermute x3, waiting for transfers between devices, local(): lax.ppermute(results[s], 'ing', [(a, (a + s) % columns) for a in range(co...  1.61 us
    pallas_call x1, Pallas kernels, local(): pl.pallas_call(functools.partial(combine_kernel, groups, columns), out_sh...  1.48 us
  transfers between devices with their start and end apart: 18, of which 9 were waited for; matrix products, arithmetic and copies ran while one was open for 0% of the time, Pallas kernels for 14%

profile of v15, /device:TPU:0, one launch (start us, length us, event | category | flops | bytes accessed | tf_op | source)
XLA Modules:
  0.0 45.7 jit_solution(3581816201911036299)
XLA Ops:
  0.0 1.9 %dispatch.1 = (bf16[8,3712]{1,0:T(8,128)(2,1)S(1)}, bf16[8,3712]{1,0:T(8,128)(2,1)S(1)}, bf16[8,3712]{1,0:T(8,128)(2,1)S(1)}, bf16[8,3712]{1,0:T(8,128)(2,1)S(1)}) custom-call(s32[8,256]{1,0:T(8,128)} %bitcast.9, bf16[256,3584]{1,0:T(8,128)(2,1)} %tokens_ref.1), custom_call_target="tpu_custom_call" | custom-call | tf_op jit(solution)/shard_map/dispatch/pallas_call | solution.py:252
  1.9 2.4 %collective-permute-start = (bf16[8,3712]{1,0:T(8,128)(2,1)S(1)}, bf16[8,3712]{1,0:T(8,128)(2,1)S(1)}, u32[]{:S(2)}, u32[]{:S(2)}) collective-permute-start(bf16[8,3712]{1,0:T(8,128)(2,1)S(1)} %get-tuple-element.28), channel_id=1, source_target_pairs={{0,12},{4,8},{8,4},{12,0},{1,13},{5,9},{9,5},{13,1},{2,14},{6,10},... | collective-permute-start | bytes 178184 | tf_op jit(solution)/shard_map/ppermute | solution.py:235
  4.4 0.6 %collective-permute-start.1 = (bf16[8,3712]{1,0:T(8,128)(2,1)S(1)}, bf16[8,3712]{1,0:T(8,128)(2,1)S(1)}, u32[]{:S(2)}, u32[]{:S(2)}) collective-permute-start(bf16[8,3712]{1,0:T(8,128)(2,1)S(1)} %get-tuple-element.29), channel_id=1, source_target_pairs={{0,8},{4,12},{8,0},{12,4},{1,9},{5,13},{9,1},{13,5},{2,10},{6,14},... | collective-permute-start | bytes 178184 | tf_op jit(solution)/shard_map/ppermute | solution.py:235
  5.1 3.2 %load.1 = (bf16[3584,512]{1,0:T(8,128)(2,1)S(1)}, bf16[3584,512]{1,0:T(8,128)(2,1)S(1)}) custom-call(bf16[8,3712]{1,0:T(8,128)(2,1)S(1)} %get-tuple-element.26.after_ref.refs_3_, bf16[3584,512]{1,0:T(8,128)(2,1)} %bitcast.5, bf16[3584,512]{1,0:T(8,128)(2,1)} %bitcast.6), custom_call_target="tpu_custom_call" | custom-call | tf_op jit(solution)/shard_map/load/pallas_call | solution.py:270
  8.2 0.7 %collective-permute-done.1.refs_1_ = bf16[8,3712]{1,0:T(8,128)(2,1)S(1)} collective-permute-done((bf16[8,3712]{1,0:T(8,128)(2,1)S(1)}, bf16[8,3712]{1,0:T(8,128)(2,1)S(1)}, u32[]{:S(2)}, u32[]{:S(2)}) %collective-permute-start.1) | collective-permute-done | bytes 59424 | tf_op jit(solution)/shard_map/ppermute | solution.py:235
  8.9 0.3 compact.1
  9.3 2.7 %collective-permute-start.4 = (bf16[16,1792]{1,0:T(8,128)(2,1)S(1)}, bf16[16,1792]{1,0:T(8,128)(2,1)S(1)}, u32[]{:S(2)}, u32[]{:S(2)}) collective-permute-start(bf16[16,1792]{1,0:T(8,128)(2,1)S(1)} %get-tuple-element.31.refs_0_), channel_id=1, source_target_pairs={{0,2},{1,3},{2,0},{3,1},{4,6},{5,7},{6,4},{7,5},{8,10},{9,11},{10,... | collective-permute-start | bytes 172040 | tf_op jit(solution)/shard_map/ppermute | solution.py:235
  12.0 1.6 %collective-permute-start.6 = (bf16[16,1792]{1,0:T(8,128)(2,1)S(1)}, bf16[16,1792]{1,0:T(8,128)(2,1)S(1)}, u32[]{:S(2)}, u32[]{:S(2)}) collective-permute-start(bf16[16,1792]{1,0:T(8,128)(2,1)S(1)} %get-tuple-element.32.refs_0_), channel_id=1, source_target_pairs={{0,1},{1,0},{2,3},{3,2},{4,5},{5,4},{6,7},{7,6},{8,9},{9,8},{10,11... | collective-permute-start | bytes 172040 | tf_op jit(solution)/shard_map/ppermute | solution.py:235
  13.7 1.8 %collective-permute-start.8 = (bf16[16,1792]{1,0:T(8,128)(2,1)S(1)}, bf16[16,1792]{1,0:T(8,128)(2,1)S(1)}, u32[]{:S(2)}, u32[]{:S(2)}) collective-permute-start(bf16[16,1792]{1,0:T(8,128)(2,1)S(1)} %get-tuple-element.32.refs_0_), channel_id=1, source_target_pairs={{0,2},{1,3},{2,0},{3,1},{4,6},{5,7},{6,4},{7,5},{8,10},{9,11},{10,... | collective-permute-start | bytes 172040 | tf_op jit(solution)/shard_map/ppermute | solution.py:235
  15.5 2.5 %collective-permute-start.3 = (bf16[16,1792]{1,0:T(8,128)(2,1)S(1)}, bf16[16,1792]{1,0:T(8,128)(2,1)S(1)}, u32[]{:S(2)}, u32[]{:S(2)}) collective-permute-start(bf16[16,1792]{1,0:T(8,128)(2,1)S(1)} %get-tuple-element.31.refs_0_), channel_id=1, source_target_pairs={{0,1},{1,0},{2,3},{3,2},{4,5},{5,4},{6,7},{7,6},{8,9},{9,8},{10,11... | collective-permute-start | bytes 172040 | tf_op jit(solution)/shard_map/ppermute | solution.py:235
  18.0 2.2 %collective-permute-done.7.refs_2_ = bf16[16,1792]{1,0:T(8,128)(2,1)S(1)} collective-permute-done((bf16[16,1792]{1,0:T(8,128)(2,1)S(1)}, bf16[16,1792]{1,0:T(8,128)(2,1)S(1)}, u32[]{:S(2)}, u32[]{:S(2)}) %collective-permute-start.7) | collective-permute-done | bytes 57376 | tf_op jit(solution)/shard_map/ppermute | solution.py:235
  20.2 0.7 %ahead.1 = (f32[64,512]{1,0:T(8,128)S(1)}, f32[64,512]{1,0:T(8,128)S(1)}) custom-call(bf16[16,1792]{1,0:T(8,128)(2,1)S(1)} %get-tuple-element.32.refs_0_, bf16[16,1792]{1,0:T(8,128)(2,1)S(1)} %collective-permute-done.6.refs_1_, bf16[16,1792]{1,0:T(8,128)(2,1)S(1)} %collective-permute-done.7.refs_2_, bf16[16,1792]{1,0:T(8,128)(2,1)S(1)} %collective-permute-done.8.refs_3_, ...), custom_call_target="tpu_custom_call" | custom-call | tf_op jit(solution)/shard_map/ahead/pallas_call | solution.py:295
  21.0 0.3 collective-permute-done.3.refs_1_
  21.3 0.8 %collective-permute-done.5.refs_3_ = bf16[16,1792]{1,0:T(8,128)(2,1)S(1)} collective-permute-done((bf16[16,1792]{1,0:T(8,128)(2,1)S(1)}, bf16[16,1792]{1,0:T(8,128)(2,1)S(1)}, u32[]{:S(2)}, u32[]{:S(2)}) %collective-permute-start.5) | collective-permute-done | bytes 57376 | tf_op jit(solution)/shard_map/ppermute | solution.py:235
  22.1 0.8 %hidden.1.after_ref.refs_0_ = bf16[64,512]{1,0:T(8,128)(2,1)S(1)} custom-call(bf16[16,1792]{1,0:T(8,128)(2,1)S(1)} %get-tuple-element.31.refs_0_, bf16[16,1792]{1,0:T(8,128)(2,1)S(1)} %collective-permute-done.3.refs_1_, bf16[16,1792]{1,0:T(8,128)(2,1)S(1)} %collective-permute-done.4.refs_2_, bf16[16,1792]{1,0:T(8,128)(2,1)S(1)} %collective-permute-done.5.refs_3_, ...), custom_call_target="tpu_custom_call" | custom-call | tf_op jit(solution)/shard_map/hidden/pallas_call | solution.py:308
  22.9 3.4 %collective-permute-start.11 = (bf16[64,512]{1,0:T(8,128)(2,1)S(1)}, bf16[64,512]{1,0:T(8,128)(2,1)S(1)}, u32[]{:S(2)}, u32[]{:S(2)}) collective-permute-start(bf16[64,512]{1,0:T(8,128)(2,1)S(1)} %hidden.1.after_ref.refs_0_), channel_id=1, source_target_pairs={{0,3},{1,2},{2,1},{3,0},{4,7},{5,6},{6,5},{7,4},{8,11},{9,10},{10,... | collective-permute-start | bytes 196616 | tf_op jit(solution)/shard_map/ppermute | solution.py:235
  26.3 1.0 %collective-permute-start.9 = (bf16[64,512]{1,0:T(8,128)(2,1)S(1)}, bf16[64,512]{1,0:T(8,128)(2,1)S(1)}, u32[]{:S(2)}, u32[]{:S(2)}) collective-permute-start(bf16[64,512]{1,0:T(8,128)(2,1)S(1)} %hidden.1.after_ref.refs_0_), channel_id=1, source_target_pairs={{0,1},{1,0},{2,3},{3,2},{4,5},{5,4},{6,7},{7,6},{8,9},{9,8},{10,11... | collective-permute-start | bytes 196616 | tf_op jit(solution)/shard_map/ppermute | solution.py:235
  27.3 2.1 %prepare.1 = (bf16[2048,896]{1,0:T(8,128)(2,1)S(1)}, bf16[256,32]{1,0:T(8,128)(2,1)S(1)}) custom-call(bf16[64,512]{1,0:T(8,128)(2,1)S(1)} %hidden.1.after_ref.refs_0_, s32[8,256]{1,0:T(8,128)} %bitcast.10, f32[96,256]{1,0:T(8,128)} %bitcast.8, bf16[2048,896]{1,0:T(8,128)(2,1)} %bitcast.7), custom_call_target="tpu_custom_call" | custom-call | tf_op jit(solution)/shard_map/prepare/pallas_call | solution.py:316
  29.5 0.4 begin.1.refs_2_
  29.9 1.6 %collective-permute-done.10.refs_1_ = bf16[64,512]{1,0:T(8,128)(2,1)S(1)} collective-permute-done((bf16[64,512]{1,0:T(8,128)(2,1)S(1)}, bf16[64,512]{1,0:T(8,128)(2,1)S(1)}, u32[]{:S(2)}, u32[]{:S(2)}) %collective-permute-start.10) | collective-permute-done | bytes 65568 | tf_op jit(solution)/shard_map/ppermute | solution.py:235
  31.6 0.4 down.1
  32.0 0.5 %collective-permute-start.12 = (bf16[16,896]{1,0:T(8,128)(2,1)S(1)}, bf16[16,896]{1,0:T(8,128)(2,1)S(1)}, u32[]{:S(2)}, u32[]{:S(2)}) collective-permute-start(bf16[16,896]{1,0:T(8,128)(2,1)S(1)} %get-tuple-element.39), channel_id=1, source_target_pairs={{0,1},{1,2},{2,3},{3,0},{4,5},{5,6},{6,7},{7,4},{8,9},{9,10},{10,1... | collective-permute-start | bytes 86024 | tf_op jit(solution)/shard_map/ppermute | solution.py:353
  32.6 2.1 %collective-permute-start.13 = (bf16[16,896]{1,0:T(8,128)(2,1)S(1)}, bf16[16,896]{1,0:T(8,128)(2,1)S(1)}, u32[]{:S(2)}, u32[]{:S(2)}) collective-permute-start(bf16[16,896]{1,0:T(8,128)(2,1)S(1)} %get-tuple-element.40), channel_id=1, source_target_pairs={{0,2},{1,3},{2,0},{3,1},{4,6},{5,7},{6,4},{7,5},{8,10},{9,11},{10,... | collective-permute-start | bytes 86024 | tf_op jit(solution)/shard_map/ppermute | solution.py:353
  34.7 2.3 %collective-permute-start.14 = (bf16[16,896]{1,0:T(8,128)(2,1)S(1)}, bf16[16,896]{1,0:T(8,128)(2,1)S(1)}, u32[]{:S(2)}, u32[]{:S(2)}) collective-permute-start(bf16[16,896]{1,0:T(8,128)(2,1)S(1)} %get-tuple-element.41), channel_id=1, source_target_pairs={{0,3},{1,0},{2,1},{3,2},{4,7},{5,4},{6,5},{7,6},{8,11},{9,8},{10,9... | collective-permute-start | bytes 86024 | tf_op jit(solution)/shard_map/ppermute | solution.py:353
  37.0 0.9 %collective-permute-done.12.refs_0_ = bf16[16,896]{1,0:T(8,128)(2,1)S(1)} collective-permute-done((bf16[16,896]{1,0:T(8,128)(2,1)S(1)}, bf16[16,896]{1,0:T(8,128)(2,1)S(1)}, u32[]{:S(2)}, u32[]{:S(2)}) %collective-permute-start.12) | collective-permute-done | bytes 28704 | tf_op jit(solution)/shard_map/ppermute | solution.py:353
  37.9 0.7 %collective-permute-done.14.refs_2_ = bf16[16,896]{1,0:T(8,128)(2,1)S(1)} collective-permute-done((bf16[16,896]{1,0:T(8,128)(2,1)S(1)}, bf16[16,896]{1,0:T(8,128)(2,1)S(1)}, u32[]{:S(2)}, u32[]{:S(2)}) %collective-permute-start.14) | collective-permute-done | bytes 28704 | tf_op jit(solution)/shard_map/ppermute | solution.py:353
  38.6 0.2 spread.1
  38.8 1.6 %collective-permute-start.16 = (bf16[4,8,896]{2,1,0:T(8,128)(2,1)S(1)}, bf16[4,8,896]{2,1,0:T(8,128)(2,1)S(1)}, u32[]{:S(2)}, u32[]{:S(2)}) collective-permute-start(bf16[4,8,896]{2,1,0:T(8,128)(2,1)S(1)} %get-tuple-element.44), channel_id=1, source_target_pairs={{0,8},{4,12},{8,0},{12,4},{1,9},{5,13},{9,1},{13,5},{2,10},{6,14},... | collective-permute-start | bytes 172040 | tf_op jit(solution)/shard_map/ppermute | solution.py:235
  40.4 0.2 collective-permute-start.17
  40.7 2.3 %collective-permute-done.15.refs_0_ = bf16[4,8,896]{2,1,0:T(8,128)(2,1)S(1)} collective-permute-done((bf16[4,8,896]{2,1,0:T(8,128)(2,1)S(1)}, bf16[4,8,896]{2,1,0:T(8,128)(2,1)S(1)}, u32[]{:S(2)}, u32[]{:S(2)}) %collective-permute-start.15) | collective-permute-done | bytes 57376 | tf_op jit(solution)/shard_map/ppermute | solution.py:235
  42.9 1.3 %collective-permute-done.16.refs_1_ = bf16[4,8,896]{2,1,0:T(8,128)(2,1)S(1)} collective-permute-done((bf16[4,8,896]{2,1,0:T(8,128)(2,1)S(1)}, bf16[4,8,896]{2,1,0:T(8,128)(2,1)S(1)}, u32[]{:S(2)}, u32[]{:S(2)}) %collective-permute-start.16) | collective-permute-done | bytes 57376 | tf_op jit(solution)/shard_map/ppermute | solution.py:235
  44.2 1.5 %combine.1 = bf16[256,3584]{1,0:T(8,128)(2,1)} custom-call(bf16[256,32]{1,0:T(8,128)(2,1)S(1)} %get-tuple-element.36.mixing_ref, bf16[4,8,896]{2,1,0:T(8,128)(2,1)S(1)} %collective-permute-done.15.refs_0_, bf16[4,8,896]{2,1,0:T(8,128)(2,1)S(1)} %collective-permute-done.16.refs_1_, bf16[4,8,896]{2,1,0:T(8,128)(2,1)S(1)} %collective-permute-done.17.refs_2_, ...), custom_call_target="tpu_custom_call" | custom-call | tf_op jit(solution)/shard_map/combine/pallas_call | solution.py:371
  (14 shorter events, 0.4 us)
Async XLA Ops:
  1.9 6.3 %collective-permute-start = (bf16[8,3712]{1,0:T(8,128)(2,1)S(1)}, bf16[8,3712]{1,0:T(8,128)(2,1)S(1)}, u32[]{:S(2)}, u32[]{:S(2)}) collective-permute-start(bf16[8,3712]{1,0:T(8,128)(2,1)S(1)} %get-tuple-element.28), channel_id=1, source_target_pairs={{0,12},{4,8},{8,4},{12,0},{1,13},{5,9},{9,5},{13,1},{2,14},{6,10},... | collective-permute-start | bytes 178184 | tf_op jit(solution)/shard_map/ppermute | solution.py:235
  4.4 4.5 %collective-permute-start.1 = (bf16[8,3712]{1,0:T(8,128)(2,1)S(1)}, bf16[8,3712]{1,0:T(8,128)(2,1)S(1)}, u32[]{:S(2)}, u32[]{:S(2)}) collective-permute-start(bf16[8,3712]{1,0:T(8,128)(2,1)S(1)} %get-tuple-element.29), channel_id=1, source_target_pairs={{0,8},{4,12},{8,0},{12,4},{1,9},{5,13},{9,1},{13,5},{2,10},{6,14},... | collective-permute-start | bytes 178184 | tf_op jit(solution)/shard_map/ppermute | solution.py:235
  5.0 3.9 %collective-permute-start.2 = (bf16[8,3712]{1,0:T(8,128)(2,1)S(1)}, bf16[8,3712]{1,0:T(8,128)(2,1)S(1)}, u32[]{:S(2)}, u32[]{:S(2)}) collective-permute-start(bf16[8,3712]{1,0:T(8,128)(2,1)S(1)} %get-tuple-element.30), channel_id=1, source_target_pairs={{0,4},{4,0},{8,12},{12,8},{1,5},{5,1},{9,13},{13,9},{2,6},{6,2},{1... | collective-permute-start | bytes 178184 | tf_op jit(solution)/shard_map/ppermute | solution.py:235
  9.3 8.7 %collective-permute-start.4 = (bf16[16,1792]{1,0:T(8,128)(2,1)S(1)}, bf16[16,1792]{1,0:T(8,128)(2,1)S(1)}, u32[]{:S(2)}, u32[]{:S(2)}) collective-permute-start(bf16[16,1792]{1,0:T(8,128)(2,1)S(1)} %get-tuple-element.31.refs_0_), channel_id=1, source_target_pairs={{0,2},{1,3},{2,0},{3,1},{4,6},{5,7},{6,4},{7,5},{8,10},{9,11},{10,... | collective-permute-start | bytes 172040 | tf_op jit(solution)/shard_map/ppermute | solution.py:235
  12.0 6.0 %collective-permute-start.6 = (bf16[16,1792]{1,0:T(8,128)(2,1)S(1)}, bf16[16,1792]{1,0:T(8,128)(2,1)S(1)}, u32[]{:S(2)}, u32[]{:S(2)}) collective-permute-start(bf16[16,1792]{1,0:T(8,128)(2,1)S(1)} %get-tuple-element.32.refs_0_), channel_id=1, source_target_pairs={{0,1},{1,0},{2,3},{3,2},{4,5},{5,4},{6,7},{7,6},{8,9},{9,8},{10,11... | collective-permute-start | bytes 172040 | tf_op jit(solution)/shard_map/ppermute | solution.py:235
  13.5 6.7 %collective-permute-start.7 = (bf16[16,1792]{1,0:T(8,128)(2,1)S(1)}, bf16[16,1792]{1,0:T(8,128)(2,1)S(1)}, u32[]{:S(2)}, u32[]{:S(2)}) collective-permute-start(bf16[16,1792]{1,0:T(8,128)(2,1)S(1)} %get-tuple-element.32.refs_0_), channel_id=1, source_target_pairs={{0,3},{1,2},{2,1},{3,0},{4,7},{5,6},{6,5},{7,4},{8,11},{9,10},{10,... | collective-permute-start | bytes 172040 | tf_op jit(solution)/shard_map/ppermute | solution.py:235
  13.7 6.5 %collective-permute-start.8 = (bf16[16,1792]{1,0:T(8,128)(2,1)S(1)}, bf16[16,1792]{1,0:T(8,128)(2,1)S(1)}, u32[]{:S(2)}, u32[]{:S(2)}) collective-permute-start(bf16[16,1792]{1,0:T(8,128)(2,1)S(1)} %get-tuple-element.32.refs_0_), channel_id=1, source_target_pairs={{0,2},{1,3},{2,0},{3,1},{4,6},{5,7},{6,4},{7,5},{8,10},{9,11},{10,... | collective-permute-start | bytes 172040 | tf_op jit(solution)/shard_map/ppermute | solution.py:235
  15.5 5.8 %collective-permute-start.3 = (bf16[16,1792]{1,0:T(8,128)(2,1)S(1)}, bf16[16,1792]{1,0:T(8,128)(2,1)S(1)}, u32[]{:S(2)}, u32[]{:S(2)}) collective-permute-start(bf16[16,1792]{1,0:T(8,128)(2,1)S(1)} %get-tuple-element.31.refs_0_), channel_id=1, source_target_pairs={{0,1},{1,0},{2,3},{3,2},{4,5},{5,4},{6,7},{7,6},{8,9},{9,8},{10,11... | collective-permute-start | bytes 172040 | tf_op jit(solution)/shard_map/ppermute | solution.py:235
  17.9 4.2 %collective-permute-start.5 = (bf16[16,1792]{1,0:T(8,128)(2,1)S(1)}, bf16[16,1792]{1,0:T(8,128)(2,1)S(1)}, u32[]{:S(2)}, u32[]{:S(2)}) collective-permute-start(bf16[16,1792]{1,0:T(8,128)(2,1)S(1)} %collective-permute-done.4.refs_2_), channel_id=1, source_target_pairs={{0,1},{1,0},{2,3},{3,2},{4,5},{5,4},{6,7},{7,6},{8,9},{9,8},{10,11... | collective-permute-start | bytes 172040 | tf_op jit(solution)/shard_map/ppermute | solution.py:235
  22.9 6.6 %collective-permute-start.11 = (bf16[64,512]{1,0:T(8,128)(2,1)S(1)}, bf16[64,512]{1,0:T(8,128)(2,1)S(1)}, u32[]{:S(2)}, u32[]{:S(2)}) collective-permute-start(bf16[64,512]{1,0:T(8,128)(2,1)S(1)} %hidden.1.after_ref.refs_0_), channel_id=1, source_target_pairs={{0,3},{1,2},{2,1},{3,0},{4,7},{5,6},{6,5},{7,4},{8,11},{9,10},{10,... | collective-permute-start | bytes 196616 | tf_op jit(solution)/shard_map/ppermute | solution.py:235
  26.3 5.2 %collective-permute-start.10 = (bf16[64,512]{1,0:T(8,128)(2,1)S(1)}, bf16[64,512]{1,0:T(8,128)(2,1)S(1)}, u32[]{:S(2)}, u32[]{:S(2)}) collective-permute-start(bf16[64,512]{1,0:T(8,128)(2,1)S(1)} %hidden.1.after_ref.refs_0_), channel_id=1, source_target_pairs={{0,2},{1,3},{2,0},{3,1},{4,6},{5,7},{6,4},{7,5},{8,10},{9,11},{10,... | collective-permute-start | bytes 196616 | tf_op jit(solution)/shard_map/ppermute | solution.py:235
  26.3 5.2 %collective-permute-start.9 = (bf16[64,512]{1,0:T(8,128)(2,1)S(1)}, bf16[64,512]{1,0:T(8,128)(2,1)S(1)}, u32[]{:S(2)}, u32[]{:S(2)}) collective-permute-start(bf16[64,512]{1,0:T(8,128)(2,1)S(1)} %hidden.1.after_ref.refs_0_), channel_id=1, source_target_pairs={{0,1},{1,0},{2,3},{3,2},{4,5},{5,4},{6,7},{7,6},{8,9},{9,8},{10,11... | collective-permute-start | bytes 196616 | tf_op jit(solution)/shard_map/ppermute | solution.py:235
  32.0 5.8 %collective-permute-start.12 = (bf16[16,896]{1,0:T(8,128)(2,1)S(1)}, bf16[16,896]{1,0:T(8,128)(2,1)S(1)}, u32[]{:S(2)}, u32[]{:S(2)}) collective-permute-start(bf16[16,896]{1,0:T(8,128)(2,1)S(1)} %get-tuple-element.39), channel_id=1, source_target_pairs={{0,1},{1,2},{2,3},{3,0},{4,5},{5,6},{6,7},{7,4},{8,9},{9,10},{10,1... | collective-permute-start | bytes 86024 | tf_op jit(solution)/shard_map/ppermute | solution.py:353
  32.6 5.3 %collective-permute-start.13 = (bf16[16,896]{1,0:T(8,128)(2,1)S(1)}, bf16[16,896]{1,0:T(8,128)(2,1)S(1)}, u32[]{:S(2)}, u32[]{:S(2)}) collective-permute-start(bf16[16,896]{1,0:T(8,128)(2,1)S(1)} %get-tuple-element.40), channel_id=1, source_target_pairs={{0,2},{1,3},{2,0},{3,1},{4,6},{5,7},{6,4},{7,5},{8,10},{9,11},{10,... | collective-permute-start | bytes 86024 | tf_op jit(solution)/shard_map/ppermute | solution.py:353
  34.7 3.9 %collective-permute-start.14 = (bf16[16,896]{1,0:T(8,128)(2,1)S(1)}, bf16[16,896]{1,0:T(8,128)(2,1)S(1)}, u32[]{:S(2)}, u32[]{:S(2)}) collective-permute-start(bf16[16,896]{1,0:T(8,128)(2,1)S(1)} %get-tuple-element.41), channel_id=1, source_target_pairs={{0,3},{1,0},{2,1},{3,2},{4,7},{5,4},{6,5},{7,6},{8,11},{9,8},{10,9... | collective-permute-start | bytes 86024 | tf_op jit(solution)/shard_map/ppermute | solution.py:353
  38.8 4.2 %collective-permute-start.15 = (bf16[4,8,896]{2,1,0:T(8,128)(2,1)S(1)}, bf16[4,8,896]{2,1,0:T(8,128)(2,1)S(1)}, u32[]{:S(2)}, u32[]{:S(2)}) collective-permute-start(bf16[4,8,896]{2,1,0:T(8,128)(2,1)S(1)} %get-tuple-element.43), channel_id=1, source_target_pairs={{0,12},{4,8},{8,4},{12,0},{1,13},{5,9},{9,5},{13,1},{2,14},{6,10},... | collective-permute-start | bytes 172040 | tf_op jit(solution)/shard_map/ppermute | solution.py:235
  38.8 5.4 %collective-permute-start.16 = (bf16[4,8,896]{2,1,0:T(8,128)(2,1)S(1)}, bf16[4,8,896]{2,1,0:T(8,128)(2,1)S(1)}, u32[]{:S(2)}, u32[]{:S(2)}) collective-permute-start(bf16[4,8,896]{2,1,0:T(8,128)(2,1)S(1)} %get-tuple-element.44), channel_id=1, source_target_pairs={{0,8},{4,12},{8,0},{12,4},{1,9},{5,13},{9,1},{13,5},{2,10},{6,14},... | collective-permute-start | bytes 172040 | tf_op jit(solution)/shard_map/ppermute | solution.py:235
  40.4 3.8 %collective-permute-start.17 = (bf16[4,8,896]{2,1,0:T(8,128)(2,1)S(1)}, bf16[4,8,896]{2,1,0:T(8,128)(2,1)S(1)}, u32[]{:S(2)}, u32[]{:S(2)}) collective-permute-start(bf16[4,8,896]{2,1,0:T(8,128)(2,1)S(1)} %get-tuple-element.45), channel_id=1, source_target_pairs={{0,4},{4,0},{8,12},{12,8},{1,5},{5,1},{9,13},{13,9},{2,6},{6,2},{1... | collective-permute-start | bytes 172040 | tf_op jit(solution)/shard_map/ppermute | solution.py:235

commit v16 on v14

--- a/solution.py
+++ b/solution.py
@@ -249,7 +249,7 @@
     logits = pltpu.with_memory_space_constraint(router_logits.T, pltpu.HBM)
 
     outbound = pl.pallas_call(
-        functools.partial(dispatch_kernel, groups, features // 2),
+        functools.partial(dispatch_kernel, groups, features // 4),
         out_shape=[jax.ShapeDtypeStruct((CAP, wide), BF16)] * groups,
         in_specs=[ANY, ANY],
         out_specs=[VMEM] * groups,
@@ -257,7 +257,7 @@
             pltpu.VMEM(ids.shape, jnp.int32),
             pltpu.VMEM((count, features), BF16),
             pltpu.VMEM((count, count), BF16),
-            pltpu.SemaphoreType.DMA((3,)),
+            pltpu.SemaphoreType.DMA((5,)),
         ],
         compiler_params=params(2 * count * features),
         name="dispatch",

time: 45.8 us -> 45.9 us (level)
  no operation moved by 1% of the time
where the time goes in v16:
time: 45.9 us; the launch traced here: 45.7 us
  starting transfers between devices  23.1 us (50%)
  Pallas kernels  11.6 us (25%)
  waiting for transfers between devices  10.9 us (24%)
    ppermute x15, starting transfers between devices, swap(): lax.ppermute(x, name, [(a, a ^ step) for a in range(lax.axis_size(name))])  18.2 us
    ppermute x15, waiting for transfers between devices, swap(): lax.ppermute(x, name, [(a, a ^ step) for a in range(lax.axis_size(name))])  9.25 us
    ppermute x3, starting transfers between devices, local(): lax.ppermute(results[s], 'ing', [(a, (a + s) % columns) for a in range(co...  4.92 us
    pallas_call x1, Pallas kernels, local(): pl.pallas_call(load_kernel, out_shape=[pltpu.VMEM(w.shape, BF16) for w in...  3.17 us
    pallas_call x1, Pallas kernels, local(): pl.pallas_call(functools.partial(prepare_kernel, groups), out_shape=[pltp...  2.13 us
    pallas_call x1, Pallas kernels, local(): pl.pallas_call(functools.partial(dispatch_kernel, groups, features // 4),...  1.88 us
    ppermute x3, waiting for transfers between devices, local(): lax.ppermute(results[s], 'ing', [(a, (a + s) % columns) for a in range(co...  1.61 us
    pallas_call x1, Pallas kernels, local(): pl.pallas_call(functools.partial(combine_kernel, groups, columns), out_sh...  1.49 us
  transfers between devices with their start and end apart: 18, of which 9 were waited for; matrix products, arithmetic and copies ran while one was open for 0% of the time, Pallas kernels for 14%

profile of v16, /device:TPU:0, one launch (start us, length us, event | category | flops | bytes accessed | tf_op | source)
XLA Modules:
  0.0 45.7 jit_solution(7573040485270685191)
XLA Ops:
  0.0 1.9 %dispatch.1 = (bf16[8,3712]{1,0:T(8,128)(2,1)S(1)}, bf16[8,3712]{1,0:T(8,128)(2,1)S(1)}, bf16[8,3712]{1,0:T(8,128)(2,1)S(1)}, bf16[8,3712]{1,0:T(8,128)(2,1)S(1)}) custom-call(s32[8,256]{1,0:T(8,128)} %bitcast.9, bf16[256,3584]{1,0:T(8,128)(2,1)} %tokens_ref.1), custom_call_target="tpu_custom_call" | custom-call | tf_op jit(solution)/shard_map/dispatch/pallas_call | solution.py:251
  1.9 2.4 %collective-permute-start = (bf16[8,3712]{1,0:T(8,128)(2,1)S(1)}, bf16[8,3712]{1,0:T(8,128)(2,1)S(1)}, u32[]{:S(2)}, u32[]{:S(2)}) collective-permute-start(bf16[8,3712]{1,0:T(8,128)(2,1)S(1)} %get-tuple-element.28), channel_id=1, source_target_pairs={{0,12},{4,8},{8,4},{12,0},{1,13},{5,9},{9,5},{13,1},{2,14},{6,10},... | collective-permute-start | bytes 178184 | tf_op jit(solution)/shard_map/ppermute | solution.py:234
  4.3 0.6 %collective-permute-start.1 = (bf16[8,3712]{1,0:T(8,128)(2,1)S(1)}, bf16[8,3712]{1,0:T(8,128)(2,1)S(1)}, u32[]{:S(2)}, u32[]{:S(2)}) collective-permute-start(bf16[8,3712]{1,0:T(8,128)(2,1)S(1)} %get-tuple-element.29), channel_id=1, source_target_pairs={{0,8},{4,12},{8,0},{12,4},{1,9},{5,13},{9,1},{13,5},{2,10},{6,14},... | collective-permute-start | bytes 178184 | tf_op jit(solution)/shard_map/ppermute | solution.py:234
  5.0 3.2 %load.1 = (bf16[3584,512]{1,0:T(8,128)(2,1)S(1)}, bf16[3584,512]{1,0:T(8,128)(2,1)S(1)}) custom-call(bf16[8,3712]{1,0:T(8,128)(2,1)S(1)} %get-tuple-element.26.after_ref.refs_3_, bf16[3584,512]{1,0:T(8,128)(2,1)} %bitcast.5, bf16[3584,512]{1,0:T(8,128)(2,1)} %bitcast.6), custom_call_target="tpu_custom_call" | custom-call | tf_op jit(solution)/shard_map/load/pallas_call | solution.py:269
  8.2 0.7 %collective-permute-done.1.refs_1_ = bf16[8,3712]{1,0:T(8,128)(2,1)S(1)} collective-permute-done((bf16[8,3712]{1,0:T(8,128)(2,1)S(1)}, bf16[8,3712]{1,0:T(8,128)(2,1)S(1)}, u32[]{:S(2)}, u32[]{:S(2)}) %collective-permute-start.1) | collective-permute-done | bytes 59424 | tf_op jit(solution)/shard_map/ppermute | solution.py:234
  8.9 0.3 compact.1
  9.2 2.7 %collective-permute-start.4 = (bf16[16,1792]{1,0:T(8,128)(2,1)S(1)}, bf16[16,1792]{1,0:T(8,128)(2,1)S(1)}, u32[]{:S(2)}, u32[]{:S(2)}) collective-permute-start(bf16[16,1792]{1,0:T(8,128)(2,1)S(1)} %get-tuple-element.31.refs_0_), channel_id=1, source_target_pairs={{0,2},{1,3},{2,0},{3,1},{4,6},{5,7},{6,4},{7,5},{8,10},{9,11},{10,... | collective-permute-start | bytes 172040 | tf_op jit(solution)/shard_map/ppermute | solution.py:234
  11.9 1.6 %collective-permute-start.6 = (bf16[16,1792]{1,0:T(8,128)(2,1)S(1)}, bf16[16,1792]{1,0:T(8,128)(2,1)S(1)}, u32[]{:S(2)}, u32[]{:S(2)}) collective-permute-start(bf16[16,1792]{1,0:T(8,128)(2,1)S(1)} %get-tuple-element.32.refs_0_), channel_id=1, source_target_pairs={{0,1},{1,0},{2,3},{3,2},{4,5},{5,4},{6,7},{7,6},{8,9},{9,8},{10,11... | collective-permute-start | bytes 172040 | tf_op jit(solution)/shard_map/ppermute | solution.py:234
  13.7 1.8 %collective-permute-start.8 = (bf16[16,1792]{1,0:T(8,128)(2,1)S(1)}, bf16[16,1792]{1,0:T(8,128)(2,1)S(1)}, u32[]{:S(2)}, u32[]{:S(2)}) collective-permute-start(bf16[16,1792]{1,0:T(8,128)(2,1)S(1)} %get-tuple-element.32.refs_0_), channel_id=1, source_target_pairs={{0,2},{1,3},{2,0},{3,1},{4,6},{5,7},{6,4},{7,5},{8,10},{9,11},{10,... | collective-permute-start | bytes 172040 | tf_op jit(solution)/shard_map/ppermute | solution.py:234
  15.4 2.5 %collective-permute-start.3 = (bf16[16,1792]{1,0:T(8,128)(2,1)S(1)}, bf16[16,1792]{1,0:T(8,128)(2,1)S(1)}, u32[]{:S(2)}, u32[]{:S(2)}) collective-permute-start(bf16[16,1792]{1,0:T(8,128)(2,1)S(1)} %get-tuple-element.31.refs_0_), channel_id=1, source_target_pairs={{0,1},{1,0},{2,3},{3,2},{4,5},{5,4},{6,7},{7,6},{8,9},{9,8},{10,11... | collective-permute-start | bytes 172040 | tf_op jit(solution)/shard_map/ppermute | solution.py:234
  17.9 2.2 %collective-permute-done.7.refs_2_ = bf16[16,1792]{1,0:T(8,128)(2,1)S(1)} collective-permute-done((bf16[16,1792]{1,0:T(8,128)(2,1)S(1)}, bf16[16,1792]{1,0:T(8,128)(2,1)S(1)}, u32[]{:S(2)}, u32[]{:S(2)}) %collective-permute-start.7) | collective-permute-done | bytes 57376 | tf_op jit(solution)/shard_map/ppermute | solution.py:234
  20.2 0.7 %ahead.1 = (f32[64,512]{1,0:T(8,128)S(1)}, f32[64,512]{1,0:T(8,128)S(1)}) custom-call(bf16[16,1792]{1,0:T(8,128)(2,1)S(1)} %get-tuple-element.32.refs_0_, bf16[16,1792]{1,0:T(8,128)(2,1)S(1)} %collective-permute-done.6.refs_1_, bf16[16,1792]{1,0:T(8,128)(2,1)S(1)} %collective-permute-done.7.refs_2_, bf16[16,1792]{1,0:T(8,128)(2,1)S(1)} %collective-permute-done.8.refs_3_, ...), custom_call_target="tpu_custom_call" | custom-call | tf_op jit(solution)/shard_map/ahead/pallas_call | solution.py:294
  20.9 0.3 collective-permute-done.3.refs_1_
  21.3 0.8 %collective-permute-done.5.refs_3_ = bf16[16,1792]{1,0:T(8,128)(2,1)S(1)} collective-permute-done((bf16[16,1792]{1,0:T(8,128)(2,1)S(1)}, bf16[16,1792]{1,0:T(8,128)(2,1)S(1)}, u32[]{:S(2)}, u32[]{:S(2)}) %collective-permute-start.5) | collective-permute-done | bytes 57376 | tf_op jit(solution)/shard_map/ppermute | solution.py:234
  22.1 0.8 %hidden.1.after_ref.refs_0_ = bf16[64,512]{1,0:T(8,128)(2,1)S(1)} custom-call(bf16[16,1792]{1,0:T(8,128)(2,1)S(1)} %get-tuple-element.31.refs_0_, bf16[16,1792]{1,0:T(8,128)(2,1)S(1)} %collective-permute-done.3.refs_1_, bf16[16,1792]{1,0:T(8,128)(2,1)S(1)} %collective-permute-done.4.refs_2_, bf16[16,1792]{1,0:T(8,128)(2,1)S(1)} %collective-permute-done.5.refs_3_, ...), custom_call_target="tpu_custom_call" | custom-call | tf_op jit(solution)/shard_map/hidden/pallas_call | solution.py:307
  22.9 3.4 %collective-permute-start.11 = (bf16[64,512]{1,0:T(8,128)(2,1)S(1)}, bf16[64,512]{1,0:T(8,128)(2,1)S(1)}, u32[]{:S(2)}, u32[]{:S(2)}) collective-permute-start(bf16[64,512]{1,0:T(8,128)(2,1)S(1)} %hidden.1.after_ref.refs_0_), channel_id=1, source_target_pairs={{0,3},{1,2},{2,1},{3,0},{4,7},{5,6},{6,5},{7,4},{8,11},{9,10},{10,... | collective-permute-start | bytes 196616 | tf_op jit(solution)/shard_map/ppermute | solution.py:234
  26.3 1.0 %collective-permute-start.9 = (bf16[64,512]{1,0:T(8,128)(2,1)S(1)}, bf16[64,512]{1,0:T(8,128)(2,1)S(1)}, u32[]{:S(2)}, u32[]{:S(2)}) collective-permute-start(bf16[64,512]{1,0:T(8,128)(2,1)S(1)} %hidden.1.after_ref.refs_0_), channel_id=1, source_target_pairs={{0,1},{1,0},{2,3},{3,2},{4,5},{5,4},{6,7},{7,6},{8,9},{9,8},{10,11... | collective-permute-start | bytes 196616 | tf_op jit(solution)/shard_map/ppermute | solution.py:234
  27.3 2.1 %prepare.1 = (bf16[2048,896]{1,0:T(8,128)(2,1)S(1)}, bf16[256,32]{1,0:T(8,128)(2,1)S(1)}) custom-call(bf16[64,512]{1,0:T(8,128)(2,1)S(1)} %hidden.1.after_ref.refs_0_, s32[8,256]{1,0:T(8,128)} %bitcast.10, f32[96,256]{1,0:T(8,128)} %bitcast.8, bf16[2048,896]{1,0:T(8,128)(2,1)} %bitcast.7), custom_call_target="tpu_custom_call" | custom-call | tf_op jit(solution)/shard_map/prepare/pallas_call | solution.py:315
  29.5 0.4 begin.1.refs_2_
  29.9 1.6 %collective-permute-done.10.refs_1_ = bf16[64,512]{1,0:T(8,128)(2,1)S(1)} collective-permute-done((bf16[64,512]{1,0:T(8,128)(2,1)S(1)}, bf16[64,512]{1,0:T(8,128)(2,1)S(1)}, u32[]{:S(2)}, u32[]{:S(2)}) %collective-permute-start.10) | collective-permute-done | bytes 65568 | tf_op jit(solution)/shard_map/ppermute | solution.py:234
  31.5 0.4 down.1
  32.0 0.5 %collective-permute-start.12 = (bf16[16,896]{1,0:T(8,128)(2,1)S(1)}, bf16[16,896]{1,0:T(8,128)(2,1)S(1)}, u32[]{:S(2)}, u32[]{:S(2)}) collective-permute-start(bf16[16,896]{1,0:T(8,128)(2,1)S(1)} %get-tuple-element.39), channel_id=1, source_target_pairs={{0,1},{1,2},{2,3},{3,0},{4,5},{5,6},{6,7},{7,4},{8,9},{9,10},{10,1... | collective-permute-start | bytes 86024 | tf_op jit(solution)/shard_map/ppermute | solution.py:352
  32.5 2.1 %collective-permute-start.13 = (bf16[16,896]{1,0:T(8,128)(2,1)S(1)}, bf16[16,896]{1,0:T(8,128)(2,1)S(1)}, u32[]{:S(2)}, u32[]{:S(2)}) collective-permute-start(bf16[16,896]{1,0:T(8,128)(2,1)S(1)} %get-tuple-element.40), channel_id=1, source_target_pairs={{0,2},{1,3},{2,0},{3,1},{4,6},{5,7},{6,4},{7,5},{8,10},{9,11},{10,... | collective-permute-start | bytes 86024 | tf_op jit(solution)/shard_map/ppermute | solution.py:352
  34.7 2.3 %collective-permute-start.14 = (bf16[16,896]{1,0:T(8,128)(2,1)S(1)}, bf16[16,896]{1,0:T(8,128)(2,1)S(1)}, u32[]{:S(2)}, u32[]{:S(2)}) collective-permute-start(bf16[16,896]{1,0:T(8,128)(2,1)S(1)} %get-tuple-element.41), channel_id=1, source_target_pairs={{0,3},{1,0},{2,1},{3,2},{4,7},{5,4},{6,5},{7,6},{8,11},{9,8},{10,9... | collective-permute-start | bytes 86024 | tf_op jit(solution)/shard_map/ppermute | solution.py:352
  36.9 0.9 %collective-permute-done.12.refs_0_ = bf16[16,896]{1,0:T(8,128)(2,1)S(1)} collective-permute-done((bf16[16,896]{1,0:T(8,128)(2,1)S(1)}, bf16[16,896]{1,0:T(8,128)(2,1)S(1)}, u32[]{:S(2)}, u32[]{:S(2)}) %collective-permute-start.12) | collective-permute-done | bytes 28704 | tf_op jit(solution)/shard_map/ppermute | solution.py:352
  37.9 0.7 %collective-permute-done.14.refs_2_ = bf16[16,896]{1,0:T(8,128)(2,1)S(1)} collective-permute-done((bf16[16,896]{1,0:T(8,128)(2,1)S(1)}, bf16[16,896]{1,0:T(8,128)(2,1)S(1)}, u32[]{:S(2)}, u32[]{:S(2)}) %collective-permute-start.14) | collective-permute-done | bytes 28704 | tf_op jit(solution)/shard_map/ppermute | solution.py:352
  38.5 0.2 spread.1
  38.8 1.6 %collective-permute-start.16 = (bf16[4,8,896]{2,1,0:T(8,128)(2,1)S(1)}, bf16[4,8,896]{2,1,0:T(8,128)(2,1)S(1)}, u32[]{:S(2)}, u32[]{:S(2)}) collective-permute-start(bf16[4,8,896]{2,1,0:T(8,128)(2,1)S(1)} %get-tuple-element.44), channel_id=1, source_target_pairs={{0,8},{4,12},{8,0},{12,4},{1,9},{5,13},{9,1},{13,5},{2,10},{6,14},... | collective-permute-start | bytes 172040 | tf_op jit(solution)/shard_map/ppermute | solution.py:234
  40.4 0.2 collective-permute-start.17
  40.6 2.3 %collective-permute-done.15.refs_0_ = bf16[4,8,896]{2,1,0:T(8,128)(2,1)S(1)} collective-permute-done((bf16[4,8,896]{2,1,0:T(8,128)(2,1)S(1)}, bf16[4,8,896]{2,1,0:T(8,128)(2,1)S(1)}, u32[]{:S(2)}, u32[]{:S(2)}) %collective-permute-start.15) | collective-permute-done | bytes 57376 | tf_op jit(solution)/shard_map/ppermute | solution.py:234
  42.9 1.3 %collective-permute-done.16.refs_1_ = bf16[4,8,896]{2,1,0:T(8,128)(2,1)S(1)} collective-permute-done((bf16[4,8,896]{2,1,0:T(8,128)(2,1)S(1)}, bf16[4,8,896]{2,1,0:T(8,128)(2,1)S(1)}, u32[]{:S(2)}, u32[]{:S(2)}) %collective-permute-start.16) | collective-permute-done | bytes 57376 | tf_op jit(solution)/shard_map/ppermute | solution.py:234
  44.2 1.5 %combine.1 = bf16[256,3584]{1,0:T(8,128)(2,1)} custom-call(bf16[256,32]{1,0:T(8,128)(2,1)S(1)} %get-tuple-element.36.mixing_ref, bf16[4,8,896]{2,1,0:T(8,128)(2,1)S(1)} %collective-permute-done.15.refs_0_, bf16[4,8,896]{2,1,0:T(8,128)(2,1)S(1)} %collective-permute-done.16.refs_1_, bf16[4,8,896]{2,1,0:T(8,128)(2,1)S(1)} %collective-permute-done.17.refs_2_, ...), custom_call_target="tpu_custom_call" | custom-call | tf_op jit(solution)/shard_map/combine/pallas_call | solution.py:370
  (14 shorter events, 0.4 us)
Async XLA Ops:
  1.9 6.3 %collective-permute-start = (bf16[8,3712]{1,0:T(8,128)(2,1)S(1)}, bf16[8,3712]{1,0:T(8,128)(2,1)S(1)}, u32[]{:S(2)}, u32[]{:S(2)}) collective-permute-start(bf16[8,3712]{1,0:T(8,128)(2,1)S(1)} %get-tuple-element.28), channel_id=1, source_target_pairs={{0,12},{4,8},{8,4},{12,0},{1,13},{5,9},{9,5},{13,1},{2,14},{6,10},... | collective-permute-start | bytes 178184 | tf_op jit(solution)/shard_map/ppermute | solution.py:234
  4.3 4.5 %collective-permute-start.1 = (bf16[8,3712]{1,0:T(8,128)(2,1)S(1)}, bf16[8,3712]{1,0:T(8,128)(2,1)S(1)}, u32[]{:S(2)}, u32[]{:S(2)}) collective-permute-start(bf16[8,3712]{1,0:T(8,128)(2,1)S(1)} %get-tuple-element.29), channel_id=1, source_target_pairs={{0,8},{4,12},{8,0},{12,4},{1,9},{5,13},{9,1},{13,5},{2,10},{6,14},... | collective-permute-start | bytes 178184 | tf_op jit(solution)/shard_map/ppermute | solution.py:234
  5.0 3.9 %collective-permute-start.2 = (bf16[8,3712]{1,0:T(8,128)(2,1)S(1)}, bf16[8,3712]{1,0:T(8,128)(2,1)S(1)}, u32[]{:S(2)}, u32[]{:S(2)}) collective-permute-start(bf16[8,3712]{1,0:T(8,128)(2,1)S(1)} %get-tuple-element.30), channel_id=1, source_target_pairs={{0,4},{4,0},{8,12},{12,8},{1,5},{5,1},{9,13},{13,9},{2,6},{6,2},{1... | collective-permute-start | bytes 178184 | tf_op jit(solution)/shard_map/ppermute | solution.py:234
  9.2 8.7 %collective-permute-start.4 = (bf16[16,1792]{1,0:T(8,128)(2,1)S(1)}, bf16[16,1792]{1,0:T(8,128)(2,1)S(1)}, u32[]{:S(2)}, u32[]{:S(2)}) collective-permute-start(bf16[16,1792]{1,0:T(8,128)(2,1)S(1)} %get-tuple-element.31.refs_0_), channel_id=1, source_target_pairs={{0,2},{1,3},{2,0},{3,1},{4,6},{5,7},{6,4},{7,5},{8,10},{9,11},{10,... | collective-permute-start | bytes 172040 | tf_op jit(solution)/shard_map/ppermute | solution.py:234
  11.9 6.0 %collective-permute-start.6 = (bf16[16,1792]{1,0:T(8,128)(2,1)S(1)}, bf16[16,1792]{1,0:T(8,128)(2,1)S(1)}, u32[]{:S(2)}, u32[]{:S(2)}) collective-permute-start(bf16[16,1792]{1,0:T(8,128)(2,1)S(1)} %get-tuple-element.32.refs_0_), channel_id=1, source_target_pairs={{0,1},{1,0},{2,3},{3,2},{4,5},{5,4},{6,7},{7,6},{8,9},{9,8},{10,11... | collective-permute-start | bytes 172040 | tf_op jit(solution)/shard_map/ppermute | solution.py:234
  13.5 6.7 %collective-permute-start.7 = (bf16[16,1792]{1,0:T(8,128)(2,1)S(1)}, bf16[16,1792]{1,0:T(8,128)(2,1)S(1)}, u32[]{:S(2)}, u32[]{:S(2)}) collective-permute-start(bf16[16,1792]{1,0:T(8,128)(2,1)S(1)} %get-tuple-element.32.refs_0_), channel_id=1, source_target_pairs={{0,3},{1,2},{2,1},{3,0},{4,7},{5,6},{6,5},{7,4},{8,11},{9,10},{10,... | collective-permute-start | bytes 172040 | tf_op jit(solution)/shard_map/ppermute | solution.py:234
  13.7 6.5 %collective-permute-start.8 = (bf16[16,1792]{1,0:T(8,128)(2,1)S(1)}, bf16[16,1792]{1,0:T(8,128)(2,1)S(1)}, u32[]{:S(2)}, u32[]{:S(2)}) collective-permute-start(bf16[16,1792]{1,0:T(8,128)(2,1)S(1)} %get-tuple-element.32.refs_0_), channel_id=1, source_target_pairs={{0,2},{1,3},{2,0},{3,1},{4,6},{5,7},{6,4},{7,5},{8,10},{9,11},{10,... | collective-permute-start | bytes 172040 | tf_op jit(solution)/shard_map/ppermute | solution.py:234
  15.4 5.8 %collective-permute-start.3 = (bf16[16,1792]{1,0:T(8,128)(2,1)S(1)}, bf16[16,1792]{1,0:T(8,128)(2,1)S(1)}, u32[]{:S(2)}, u32[]{:S(2)}) collective-permute-start(bf16[16,1792]{1,0:T(8,128)(2,1)S(1)} %get-tuple-element.31.refs_0_), channel_id=1, source_target_pairs={{0,1},{1,0},{2,3},{3,2},{4,5},{5,4},{6,7},{7,6},{8,9},{9,8},{10,11... | collective-permute-start | bytes 172040 | tf_op jit(solution)/shard_map/ppermute | solution.py:234
  17.9 4.2 %collective-permute-start.5 = (bf16[16,1792]{1,0:T(8,128)(2,1)S(1)}, bf16[16,1792]{1,0:T(8,128)(2,1)S(1)}, u32[]{:S(2)}, u32[]{:S(2)}) collective-permute-start(bf16[16,1792]{1,0:T(8,128)(2,1)S(1)} %collective-permute-done.4.refs_2_), channel_id=1, source_target_pairs={{0,1},{1,0},{2,3},{3,2},{4,5},{5,4},{6,7},{7,6},{8,9},{9,8},{10,11... | collective-permute-start | bytes 172040 | tf_op jit(solution)/shard_map/ppermute | solution.py:234
  22.9 6.6 %collective-permute-start.11 = (bf16[64,512]{1,0:T(8,128)(2,1)S(1)}, bf16[64,512]{1,0:T(8,128)(2,1)S(1)}, u32[]{:S(2)}, u32[]{:S(2)}) collective-permute-start(bf16[64,512]{1,0:T(8,128)(2,1)S(1)} %hidden.1.after_ref.refs_0_), channel_id=1, source_target_pairs={{0,3},{1,2},{2,1},{3,0},{4,7},{5,6},{6,5},{7,4},{8,11},{9,10},{10,... | collective-permute-start | bytes 196616 | tf_op jit(solution)/shard_map/ppermute | solution.py:234
  26.3 5.2 %collective-permute-start.10 = (bf16[64,512]{1,0:T(8,128)(2,1)S(1)}, bf16[64,512]{1,0:T(8,128)(2,1)S(1)}, u32[]{:S(2)}, u32[]{:S(2)}) collective-permute-start(bf16[64,512]{1,0:T(8,128)(2,1)S(1)} %hidden.1.after_ref.refs_0_), channel_id=1, source_target_pairs={{0,2},{1,3},{2,0},{3,1},{4,6},{5,7},{6,4},{7,5},{8,10},{9,11},{10,... | collective-permute-start | bytes 196616 | tf_op jit(solution)/shard_map/ppermute | solution.py:234
  26.3 5.2 %collective-permute-start.9 = (bf16[64,512]{1,0:T(8,128)(2,1)S(1)}, bf16[64,512]{1,0:T(8,128)(2,1)S(1)}, u32[]{:S(2)}, u32[]{:S(2)}) collective-permute-start(bf16[64,512]{1,0:T(8,128)(2,1)S(1)} %hidden.1.after_ref.refs_0_), channel_id=1, source_target_pairs={{0,1},{1,0},{2,3},{3,2},{4,5},{5,4},{6,7},{7,6},{8,9},{9,8},{10,11... | collective-permute-start | bytes 196616 | tf_op jit(solution)/shard_map/ppermute | solution.py:234
  32.0 5.8 %collective-permute-start.12 = (bf16[16,896]{1,0:T(8,128)(2,1)S(1)}, bf16[16,896]{1,0:T(8,128)(2,1)S(1)}, u32[]{:S(2)}, u32[]{:S(2)}) collective-permute-start(bf16[16,896]{1,0:T(8,128)(2,1)S(1)} %get-tuple-element.39), channel_id=1, source_target_pairs={{0,1},{1,2},{2,3},{3,0},{4,5},{5,6},{6,7},{7,4},{8,9},{9,10},{10,1... | collective-permute-start | bytes 86024 | tf_op jit(solution)/shard_map/ppermute | solution.py:352
  32.5 5.3 %collective-permute-start.13 = (bf16[16,896]{1,0:T(8,128)(2,1)S(1)}, bf16[16,896]{1,0:T(8,128)(2,1)S(1)}, u32[]{:S(2)}, u32[]{:S(2)}) collective-permute-start(bf16[16,896]{1,0:T(8,128)(2,1)S(1)} %get-tuple-element.40), channel_id=1, source_target_pairs={{0,2},{1,3},{2,0},{3,1},{4,6},{5,7},{6,4},{7,5},{8,10},{9,11},{10,... | collective-permute-start | bytes 86024 | tf_op jit(solution)/shard_map/ppermute | solution.py:352
  34.7 3.9 %collective-permute-start.14 = (bf16[16,896]{1,0:T(8,128)(2,1)S(1)}, bf16[16,896]{1,0:T(8,128)(2,1)S(1)}, u32[]{:S(2)}, u32[]{:S(2)}) collective-permute-start(bf16[16,896]{1,0:T(8,128)(2,1)S(1)} %get-tuple-element.41), channel_id=1, source_target_pairs={{0,3},{1,0},{2,1},{3,2},{4,7},{5,4},{6,5},{7,6},{8,11},{9,8},{10,9... | collective-permute-start | bytes 86024 | tf_op jit(solution)/shard_map/ppermute | solution.py:352
  38.7 4.2 %collective-permute-start.15 = (bf16[4,8,896]{2,1,0:T(8,128)(2,1)S(1)}, bf16[4,8,896]{2,1,0:T(8,128)(2,1)S(1)}, u32[]{:S(2)}, u32[]{:S(2)}) collective-permute-start(bf16[4,8,896]{2,1,0:T(8,128)(2,1)S(1)} %get-tuple-element.43), channel_id=1, source_target_pairs={{0,12},{4,8},{8,4},{12,0},{1,13},{5,9},{9,5},{13,1},{2,14},{6,10},... | collective-permute-start | bytes 172040 | tf_op jit(solution)/shard_map/ppermute | solution.py:234
  38.8 5.4 %collective-permute-start.16 = (bf16[4,8,896]{2,1,0:T(8,128)(2,1)S(1)}, bf16[4,8,896]{2,1,0:T(8,128)(2,1)S(1)}, u32[]{:S(2)}, u32[]{:S(2)}) collective-permute-start(bf16[4,8,896]{2,1,0:T(8,128)(2,1)S(1)} %get-tuple-element.44), channel_id=1, source_target_pairs={{0,8},{4,12},{8,0},{12,4},{1,9},{5,13},{9,1},{13,5},{2,10},{6,14},... | collective-permute-start | bytes 172040 | tf_op jit(solution)/shard_map/ppermute | solution.py:234
  40.4 3.8 %collective-permute-start.17 = (bf16[4,8,896]{2,1,0:T(8,128)(2,1)S(1)}, bf16[4,8,896]{2,1,0:T(8,128)(2,1)S(1)}, u32[]{:S(2)}, u32[]{:S(2)}) collective-permute-start(bf16[4,8,896]{2,1,0:T(8,128)(2,1)S(1)} %get-tuple-element.45), channel_id=1, source_target_pairs={{0,4},{4,0},{8,12},{12,8},{1,5},{5,1},{9,13},{13,9},{2,6},{6,2},{1... | collective-permute-start | bytes 172040 | tf_op jit(solution)/shard_map/ppermute | solution.py:234

commit v17 on v16

--- a/solution.py
+++ b/solution.py
@@ -144,7 +144,7 @@
 def ahead_kernel(first, order, *refs):
     blocks, (gate_ref, up_ref, gate_sum, up_sum) = [refs[k] for k in order], refs[len(order) :]
     rows = jnp.concatenate([block[...] for block in blocks], axis=0)
-    step = min(256, gate_ref.shape[1])
+    step = min(512, gate_ref.shape[1])
     for c in range(gate_ref.shape[1] // step):
         part = slice(c * step, (c + 1) * step)
         gate_sum[:, part] = jnp.dot(rows, gate_ref[first:, part], preferred_element_type=F32)
@@ -155,7 +155,7 @@
     blocks, sums, (gate_ref, up_ref, hidden_ref) = refs[:count], refs[count:-3], refs[-3:]
     units = gate_ref.shape[1]
     rows = jnp.concatenate([block[...] for block in blocks], axis=0)
-    step = min(256, units)
+    step = min(512, units)
     for c in range(units // step):
         part = slice(c * step, (c + 1) * step)
         gate = jnp.dot(rows, gate_ref[:last, part], preferred_element_type=F32)

time: 45.9 us -> 45.9 us (level)
  no operation moved by 1% of the time
where the time goes in v17:
time: 45.9 us; the launch traced here: 45.6 us
  starting transfers between devices  23.1 us (50%)
  Pallas kernels  11.5 us (25%)
  waiting for transfers between devices  10.9 us (24%)
    ppermute x15, starting transfers between devices, swap(): lax.ppermute(x, name, [(a, a ^ step) for a in range(lax.axis_size(name))])  18.2 us
    ppermute x15, waiting for transfers between devices, swap(): lax.ppermute(x, name, [(a, a ^ step) for a in range(lax.axis_size(name))])  9.26 us
    ppermute x3, starting transfers between devices, local(): lax.ppermute(results[s], 'ing', [(a, (a + s) % columns) for a in range(co...  4.92 us
    pallas_call x1, Pallas kernels, local(): pl.pallas_call(load_kernel, out_shape=[pltpu.VMEM(w.shape, BF16) for w in...  3.17 us
    pallas_call x1, Pallas kernels, local(): pl.pallas_call(functools.partial(prepare_kernel, groups), out_shape=[pltp...  2.13 us
    pallas_call x1, Pallas kernels, local(): pl.pallas_call(functools.partial(dispatch_kernel, groups, features // 4),...  1.88 us
    ppermute x3, waiting for transfers between devices, local(): lax.ppermute(results[s], 'ing', [(a, (a + s) % columns) for a in range(co...  1.61 us
    pallas_call x1, Pallas kernels, local(): pl.pallas_call(functools.partial(combine_kernel, groups, columns), out_sh...  1.49 us
  transfers between devices with their start and end apart: 18, of which 9 were waited for; matrix products, arithmetic and copies ran while one was open for 0% of the time, Pallas kernels for 14%

profile of v17, /device:TPU:0, one launch (start us, length us, event | category | flops | bytes accessed | tf_op | source)
XLA Modules:
  0.0 45.6 jit_solution(5515079228879196273)
XLA Ops:
  0.0 1.9 %dispatch.1 = (bf16[8,3712]{1,0:T(8,128)(2,1)S(1)}, bf16[8,3712]{1,0:T(8,128)(2,1)S(1)}, bf16[8,3712]{1,0:T(8,128)(2,1)S(1)}, bf16[8,3712]{1,0:T(8,128)(2,1)S(1)}) custom-call(s32[8,256]{1,0:T(8,128)} %bitcast.9, bf16[256,3584]{1,0:T(8,128)(2,1)} %tokens_ref.1), custom_call_target="tpu_custom_call" | custom-call | tf_op jit(solution)/shard_map/dispatch/pallas_call | solution.py:251
  1.9 2.4 %collective-permute-start = (bf16[8,3712]{1,0:T(8,128)(2,1)S(1)}, bf16[8,3712]{1,0:T(8,128)(2,1)S(1)}, u32[]{:S(2)}, u32[]{:S(2)}) collective-permute-start(bf16[8,3712]{1,0:T(8,128)(2,1)S(1)} %get-tuple-element.28), channel_id=1, source_target_pairs={{0,12},{4,8},{8,4},{12,0},{1,13},{5,9},{9,5},{13,1},{2,14},{6,10},... | collective-permute-start | bytes 178184 | tf_op jit(solution)/shard_map/ppermute | solution.py:234
  4.3 0.6 %collective-permute-start.1 = (bf16[8,3712]{1,0:T(8,128)(2,1)S(1)}, bf16[8,3712]{1,0:T(8,128)(2,1)S(1)}, u32[]{:S(2)}, u32[]{:S(2)}) collective-permute-start(bf16[8,3712]{1,0:T(8,128)(2,1)S(1)} %get-tuple-element.29), channel_id=1, source_target_pairs={{0,8},{4,12},{8,0},{12,4},{1,9},{5,13},{9,1},{13,5},{2,10},{6,14},... | collective-permute-start | bytes 178184 | tf_op jit(solution)/shard_map/ppermute | solution.py:234
  5.0 3.2 %load.1 = (bf16[3584,512]{1,0:T(8,128)(2,1)S(1)}, bf16[3584,512]{1,0:T(8,128)(2,1)S(1)}) custom-call(bf16[8,3712]{1,0:T(8,128)(2,1)S(1)} %get-tuple-element.26.after_ref.refs_3_, bf16[3584,512]{1,0:T(8,128)(2,1)} %bitcast.5, bf16[3584,512]{1,0:T(8,128)(2,1)} %bitcast.6), custom_call_target="tpu_custom_call" | custom-call | tf_op jit(solution)/shard_map/load/pallas_call | solution.py:269
  8.2 0.7 %collective-permute-done.1.refs_1_ = bf16[8,3712]{1,0:T(8,128)(2,1)S(1)} collective-permute-done((bf16[8,3712]{1,0:T(8,128)(2,1)S(1)}, bf16[8,3712]{1,0:T(8,128)(2,1)S(1)}, u32[]{:S(2)}, u32[]{:S(2)}) %collective-permute-start.1) | collective-permute-done | bytes 59424 | tf_op jit(solution)/shard_map/ppermute | solution.py:234
  8.9 0.3 compact.1
  9.2 2.7 %collective-permute-start.4 = (bf16[16,1792]{1,0:T(8,128)(2,1)S(1)}, bf16[16,1792]{1,0:T(8,128)(2,1)S(1)}, u32[]{:S(2)}, u32[]{:S(2)}) collective-permute-start(bf16[16,1792]{1,0:T(8,128)(2,1)S(1)} %get-tuple-element.31.refs_0_), channel_id=1, source_target_pairs={{0,2},{1,3},{2,0},{3,1},{4,6},{5,7},{6,4},{7,5},{8,10},{9,11},{10,... | collective-permute-start | bytes 172040 | tf_op jit(solution)/shard_map/ppermute | solution.py:234
  11.9 1.6 %collective-permute-start.6 = (bf16[16,1792]{1,0:T(8,128)(2,1)S(1)}, bf16[16,1792]{1,0:T(8,128)(2,1)S(1)}, u32[]{:S(2)}, u32[]{:S(2)}) collective-permute-start(bf16[16,1792]{1,0:T(8,128)(2,1)S(1)} %get-tuple-element.32.refs_0_), channel_id=1, source_target_pairs={{0,1},{1,0},{2,3},{3,2},{4,5},{5,4},{6,7},{7,6},{8,9},{9,8},{10,11... | collective-permute-start | bytes 172040 | tf_op jit(solution)/shard_map/ppermute | solution.py:234
  13.7 1.8 %collective-permute-start.8 = (bf16[16,1792]{1,0:T(8,128)(2,1)S(1)}, bf16[16,1792]{1,0:T(8,128)(2,1)S(1)}, u32[]{:S(2)}, u32[]{:S(2)}) collective-permute-start(bf16[16,1792]{1,0:T(8,128)(2,1)S(1)} %get-tuple-element.32.refs_0_), channel_id=1, source_target_pairs={{0,2},{1,3},{2,0},{3,1},{4,6},{5,7},{6,4},{7,5},{8,10},{9,11},{10,... | collective-permute-start | bytes 172040 | tf_op jit(solution)/shard_map/ppermute | solution.py:234
  15.4 2.5 %collective-permute-start.3 = (bf16[16,1792]{1,0:T(8,128)(2,1)S(1)}, bf16[16,1792]{1,0:T(8,128)(2,1)S(1)}, u32[]{:S(2)}, u32[]{:S(2)}) collective-permute-start(bf16[16,1792]{1,0:T(8,128)(2,1)S(1)} %get-tuple-element.31.refs_0_), channel_id=1, source_target_pairs={{0,1},{1,0},{2,3},{3,2},{4,5},{5,4},{6,7},{7,6},{8,9},{9,8},{10,11... | collective-permute-start | bytes 172040 | tf_op jit(solution)/shard_map/ppermute | solution.py:234
  17.9 2.2 %collective-permute-done.7.refs_2_ = bf16[16,1792]{1,0:T(8,128)(2,1)S(1)} collective-permute-done((bf16[16,1792]{1,0:T(8,128)(2,1)S(1)}, bf16[16,1792]{1,0:T(8,128)(2,1)S(1)}, u32[]{:S(2)}, u32[]{:S(2)}) %collective-permute-start.7) | collective-permute-done | bytes 57376 | tf_op jit(solution)/shard_map/ppermute | solution.py:234
  20.2 0.7 %ahead.1 = (f32[64,512]{1,0:T(8,128)S(1)}, f32[64,512]{1,0:T(8,128)S(1)}) custom-call(bf16[16,1792]{1,0:T(8,128)(2,1)S(1)} %get-tuple-element.32.refs_0_, bf16[16,1792]{1,0:T(8,128)(2,1)S(1)} %collective-permute-done.6.refs_1_, bf16[16,1792]{1,0:T(8,128)(2,1)S(1)} %collective-permute-done.7.refs_2_, bf16[16,1792]{1,0:T(8,128)(2,1)S(1)} %collective-permute-done.8.refs_3_, ...), custom_call_target="tpu_custom_call" | custom-call | tf_op jit(solution)/shard_map/ahead/pallas_call | solution.py:294
  20.9 0.3 collective-permute-done.3.refs_1_
  21.3 0.8 %collective-permute-done.5.refs_3_ = bf16[16,1792]{1,0:T(8,128)(2,1)S(1)} collective-permute-done((bf16[16,1792]{1,0:T(8,128)(2,1)S(1)}, bf16[16,1792]{1,0:T(8,128)(2,1)S(1)}, u32[]{:S(2)}, u32[]{:S(2)}) %collective-permute-start.5) | collective-permute-done | bytes 57376 | tf_op jit(solution)/shard_map/ppermute | solution.py:234
  22.1 0.7 %hidden.1.after_ref.refs_0_ = bf16[64,512]{1,0:T(8,128)(2,1)S(1)} custom-call(bf16[16,1792]{1,0:T(8,128)(2,1)S(1)} %get-tuple-element.31.refs_0_, bf16[16,1792]{1,0:T(8,128)(2,1)S(1)} %collective-permute-done.3.refs_1_, bf16[16,1792]{1,0:T(8,128)(2,1)S(1)} %collective-permute-done.4.refs_2_, bf16[16,1792]{1,0:T(8,128)(2,1)S(1)} %collective-permute-done.5.refs_3_, ...), custom_call_target="tpu_custom_call" | custom-call | tf_op jit(solution)/shard_map/hidden/pallas_call | solution.py:307
  22.8 3.4 %collective-permute-start.11 = (bf16[64,512]{1,0:T(8,128)(2,1)S(1)}, bf16[64,512]{1,0:T(8,128)(2,1)S(1)}, u32[]{:S(2)}, u32[]{:S(2)}) collective-permute-start(bf16[64,512]{1,0:T(8,128)(2,1)S(1)} %hidden.1.after_ref.refs_0_), channel_id=1, source_target_pairs={{0,3},{1,2},{2,1},{3,0},{4,7},{5,6},{6,5},{7,4},{8,11},{9,10},{10,... | collective-permute-start | bytes 196616 | tf_op jit(solution)/shard_map/ppermute | solution.py:234
  26.3 1.0 %collective-permute-start.9 = (bf16[64,512]{1,0:T(8,128)(2,1)S(1)}, bf16[64,512]{1,0:T(8,128)(2,1)S(1)}, u32[]{:S(2)}, u32[]{:S(2)}) collective-permute-start(bf16[64,512]{1,0:T(8,128)(2,1)S(1)} %hidden.1.after_ref.refs_0_), channel_id=1, source_target_pairs={{0,1},{1,0},{2,3},{3,2},{4,5},{5,4},{6,7},{7,6},{8,9},{9,8},{10,11... | collective-permute-start | bytes 196616 | tf_op jit(solution)/shard_map/ppermute | solution.py:234
  27.3 2.1 %prepare.1 = (bf16[2048,896]{1,0:T(8,128)(2,1)S(1)}, bf16[256,32]{1,0:T(8,128)(2,1)S(1)}) custom-call(bf16[64,512]{1,0:T(8,128)(2,1)S(1)} %hidden.1.after_ref.refs_0_, s32[8,256]{1,0:T(8,128)} %bitcast.10, f32[96,256]{1,0:T(8,128)} %bitcast.8, bf16[2048,896]{1,0:T(8,128)(2,1)} %bitcast.7), custom_call_target="tpu_custom_call" | custom-call | tf_op jit(solution)/shard_map/prepare/pallas_call | solution.py:315
  29.4 0.4 begin.1.refs_2_
  29.9 1.6 %collective-permute-done.10.refs_1_ = bf16[64,512]{1,0:T(8,128)(2,1)S(1)} collective-permute-done((bf16[64,512]{1,0:T(8,128)(2,1)S(1)}, bf16[64,512]{1,0:T(8,128)(2,1)S(1)}, u32[]{:S(2)}, u32[]{:S(2)}) %collective-permute-start.10) | collective-permute-done | bytes 65568 | tf_op jit(solution)/shard_map/ppermute | solution.py:234
  31.5 0.4 down.1
  32.0 0.5 %collective-permute-start.12 = (bf16[16,896]{1,0:T(8,128)(2,1)S(1)}, bf16[16,896]{1,0:T(8,128)(2,1)S(1)}, u32[]{:S(2)}, u32[]{:S(2)}) collective-permute-start(bf16[16,896]{1,0:T(8,128)(2,1)S(1)} %get-tuple-element.39), channel_id=1, source_target_pairs={{0,1},{1,2},{2,3},{3,0},{4,5},{5,6},{6,7},{7,4},{8,9},{9,10},{10,1... | collective-permute-start | bytes 86024 | tf_op jit(solution)/shard_map/ppermute | solution.py:352
  32.5 2.1 %collective-permute-start.13 = (bf16[16,896]{1,0:T(8,128)(2,1)S(1)}, bf16[16,896]{1,0:T(8,128)(2,1)S(1)}, u32[]{:S(2)}, u32[]{:S(2)}) collective-permute-start(bf16[16,896]{1,0:T(8,128)(2,1)S(1)} %get-tuple-element.40), channel_id=1, source_target_pairs={{0,2},{1,3},{2,0},{3,1},{4,6},{5,7},{6,4},{7,5},{8,10},{9,11},{10,... | collective-permute-start | bytes 86024 | tf_op jit(solution)/shard_map/ppermute | solution.py:352
  34.6 2.3 %collective-permute-start.14 = (bf16[16,896]{1,0:T(8,128)(2,1)S(1)}, bf16[16,896]{1,0:T(8,128)(2,1)S(1)}, u32[]{:S(2)}, u32[]{:S(2)}) collective-permute-start(bf16[16,896]{1,0:T(8,128)(2,1)S(1)} %get-tuple-element.41), channel_id=1, source_target_pairs={{0,3},{1,0},{2,1},{3,2},{4,7},{5,4},{6,5},{7,6},{8,11},{9,8},{10,9... | collective-permute-start | bytes 86024 | tf_op jit(solution)/shard_map/ppermute | solution.py:352
  36.9 0.9 %collective-permute-done.12.refs_0_ = bf16[16,896]{1,0:T(8,128)(2,1)S(1)} collective-permute-done((bf16[16,896]{1,0:T(8,128)(2,1)S(1)}, bf16[16,896]{1,0:T(8,128)(2,1)S(1)}, u32[]{:S(2)}, u32[]{:S(2)}) %collective-permute-start.12) | collective-permute-done | bytes 28704 | tf_op jit(solution)/shard_map/ppermute | solution.py:352
  37.8 0.7 %collective-permute-done.14.refs_2_ = bf16[16,896]{1,0:T(8,128)(2,1)S(1)} collective-permute-done((bf16[16,896]{1,0:T(8,128)(2,1)S(1)}, bf16[16,896]{1,0:T(8,128)(2,1)S(1)}, u32[]{:S(2)}, u32[]{:S(2)}) %collective-permute-start.14) | collective-permute-done | bytes 28704 | tf_op jit(solution)/shard_map/ppermute | solution.py:352
  38.5 0.2 spread.1
  38.8 1.6 %collective-permute-start.16 = (bf16[4,8,896]{2,1,0:T(8,128)(2,1)S(1)}, bf16[4,8,896]{2,1,0:T(8,128)(2,1)S(1)}, u32[]{:S(2)}, u32[]{:S(2)}) collective-permute-start(bf16[4,8,896]{2,1,0:T(8,128)(2,1)S(1)} %get-tuple-element.44), channel_id=1, source_target_pairs={{0,8},{4,12},{8,0},{12,4},{1,9},{5,13},{9,1},{13,5},{2,10},{6,14},... | collective-permute-start | bytes 172040 | tf_op jit(solution)/shard_map/ppermute | solution.py:234
  40.4 0.2 collective-permute-start.17
  40.6 2.3 %collective-permute-done.15.refs_0_ = bf16[4,8,896]{2,1,0:T(8,128)(2,1)S(1)} collective-permute-done((bf16[4,8,896]{2,1,0:T(8,128)(2,1)S(1)}, bf16[4,8,896]{2,1,0:T(8,128)(2,1)S(1)}, u32[]{:S(2)}, u32[]{:S(2)}) %collective-permute-start.15) | collective-permute-done | bytes 57376 | tf_op jit(solution)/shard_map/ppermute | solution.py:234
  42.9 1.3 %collective-permute-done.16.refs_1_ = bf16[4,8,896]{2,1,0:T(8,128)(2,1)S(1)} collective-permute-done((bf16[4,8,896]{2,1,0:T(8,128)(2,1)S(1)}, bf16[4,8,896]{2,1,0:T(8,128)(2,1)S(1)}, u32[]{:S(2)}, u32[]{:S(2)}) %collective-permute-start.16) | collective-permute-done | bytes 57376 | tf_op jit(solution)/shard_map/ppermute | solution.py:234
  44.2 1.5 %combine.1 = bf16[256,3584]{1,0:T(8,128)(2,1)} custom-call(bf16[256,32]{1,0:T(8,128)(2,1)S(1)} %get-tuple-element.36.mixing_ref, bf16[4,8,896]{2,1,0:T(8,128)(2,1)S(1)} %collective-permute-done.15.refs_0_, bf16[4,8,896]{2,1,0:T(8,128)(2,1)S(1)} %collective-permute-done.16.refs_1_, bf16[4,8,896]{2,1,0:T(8,128)(2,1)S(1)} %collective-permute-done.17.refs_2_, ...), custom_call_target="tpu_custom_call" | custom-call | tf_op jit(solution)/shard_map/combine/pallas_call | solution.py:370
  (14 shorter events, 0.4 us)
Async XLA Ops:
  1.9 6.3 %collective-permute-start = (bf16[8,3712]{1,0:T(8,128)(2,1)S(1)}, bf16[8,3712]{1,0:T(8,128)(2,1)S(1)}, u32[]{:S(2)}, u32[]{:S(2)}) collective-permute-start(bf16[8,3712]{1,0:T(8,128)(2,1)S(1)} %get-tuple-element.28), channel_id=1, source_target_pairs={{0,12},{4,8},{8,4},{12,0},{1,13},{5,9},{9,5},{13,1},{2,14},{6,10},... | collective-permute-start | bytes 178184 | tf_op jit(solution)/shard_map/ppermute | solution.py:234
  4.3 4.5 %collective-permute-start.1 = (bf16[8,3712]{1,0:T(8,128)(2,1)S(1)}, bf16[8,3712]{1,0:T(8,128)(2,1)S(1)}, u32[]{:S(2)}, u32[]{:S(2)}) collective-permute-start(bf16[8,3712]{1,0:T(8,128)(2,1)S(1)} %get-tuple-element.29), channel_id=1, source_target_pairs={{0,8},{4,12},{8,0},{12,4},{1,9},{5,13},{9,1},{13,5},{2,10},{6,14},... | collective-permute-start | bytes 178184 | tf_op jit(solution)/shard_map/ppermute | solution.py:234
  5.0 3.9 %collective-permute-start.2 = (bf16[8,3712]{1,0:T(8,128)(2,1)S(1)}, bf16[8,3712]{1,0:T(8,128)(2,1)S(1)}, u32[]{:S(2)}, u32[]{:S(2)}) collective-permute-start(bf16[8,3712]{1,0:T(8,128)(2,1)S(1)} %get-tuple-element.30), channel_id=1, source_target_pairs={{0,4},{4,0},{8,12},{12,8},{1,5},{5,1},{9,13},{13,9},{2,6},{6,2},{1... | collective-permute-start | bytes 178184 | tf_op jit(solution)/shard_map/ppermute | solution.py:234
  9.2 8.7 %collective-permute-start.4 = (bf16[16,1792]{1,0:T(8,128)(2,1)S(1)}, bf16[16,1792]{1,0:T(8,128)(2,1)S(1)}, u32[]{:S(2)}, u32[]{:S(2)}) collective-permute-start(bf16[16,1792]{1,0:T(8,128)(2,1)S(1)} %get-tuple-element.31.refs_0_), channel_id=1, source_target_pairs={{0,2},{1,3},{2,0},{3,1},{4,6},{5,7},{6,4},{7,5},{8,10},{9,11},{10,... | collective-permute-start | bytes 172040 | tf_op jit(solution)/shard_map/ppermute | solution.py:234
  11.9 6.0 %collective-permute-start.6 = (bf16[16,1792]{1,0:T(8,128)(2,1)S(1)}, bf16[16,1792]{1,0:T(8,128)(2,1)S(1)}, u32[]{:S(2)}, u32[]{:S(2)}) collective-permute-start(bf16[16,1792]{1,0:T(8,128)(2,1)S(1)} %get-tuple-element.32.refs_0_), channel_id=1, source_target_pairs={{0,1},{1,0},{2,3},{3,2},{4,5},{5,4},{6,7},{7,6},{8,9},{9,8},{10,11... | collective-permute-start | bytes 172040 | tf_op jit(solution)/shard_map/ppermute | solution.py:234
  13.5 6.7 %collective-permute-start.7 = (bf16[16,1792]{1,0:T(8,128)(2,1)S(1)}, bf16[16,1792]{1,0:T(8,128)(2,1)S(1)}, u32[]{:S(2)}, u32[]{:S(2)}) collective-permute-start(bf16[16,1792]{1,0:T(8,128)(2,1)S(1)} %get-tuple-element.32.refs_0_), channel_id=1, source_target_pairs={{0,3},{1,2},{2,1},{3,0},{4,7},{5,6},{6,5},{7,4},{8,11},{9,10},{10,... | collective-permute-start | bytes 172040 | tf_op jit(solution)/shard_map/ppermute | solution.py:234
  13.7 6.5 %collective-permute-start.8 = (bf16[16,1792]{1,0:T(8,128)(2,1)S(1)}, bf16[16,1792]{1,0:T(8,128)(2,1)S(1)}, u32[]{:S(2)}, u32[]{:S(2)}) collective-permute-start(bf16[16,1792]{1,0:T(8,128)(2,1)S(1)} %get-tuple-element.32.refs_0_), channel_id=1, source_target_pairs={{0,2},{1,3},{2,0},{3,1},{4,6},{5,7},{6,4},{7,5},{8,10},{9,11},{10,... | collective-permute-start | bytes 172040 | tf_op jit(solution)/shard_map/ppermute | solution.py:234
  15.4 5.8 %collective-permute-start.3 = (bf16[16,1792]{1,0:T(8,128)(2,1)S(1)}, bf16[16,1792]{1,0:T(8,128)(2,1)S(1)}, u32[]{:S(2)}, u32[]{:S(2)}) collective-permute-start(bf16[16,1792]{1,0:T(8,128)(2,1)S(1)} %get-tuple-element.31.refs_0_), channel_id=1, source_target_pairs={{0,1},{1,0},{2,3},{3,2},{4,5},{5,4},{6,7},{7,6},{8,9},{9,8},{10,11... | collective-permute-start | bytes 172040 | tf_op jit(solution)/shard_map/ppermute | solution.py:234
  17.9 4.2 %collective-permute-start.5 = (bf16[16,1792]{1,0:T(8,128)(2,1)S(1)}, bf16[16,1792]{1,0:T(8,128)(2,1)S(1)}, u32[]{:S(2)}, u32[]{:S(2)}) collective-permute-start(bf16[16,1792]{1,0:T(8,128)(2,1)S(1)} %collective-permute-done.4.refs_2_), channel_id=1, source_target_pairs={{0,1},{1,0},{2,3},{3,2},{4,5},{5,4},{6,7},{7,6},{8,9},{9,8},{10,11... | collective-permute-start | bytes 172040 | tf_op jit(solution)/shard_map/ppermute | solution.py:234
  22.8 6.6 %collective-permute-start.11 = (bf16[64,512]{1,0:T(8,128)(2,1)S(1)}, bf16[64,512]{1,0:T(8,128)(2,1)S(1)}, u32[]{:S(2)}, u32[]{:S(2)}) collective-permute-start(bf16[64,512]{1,0:T(8,128)(2,1)S(1)} %hidden.1.after_ref.refs_0_), channel_id=1, source_target_pairs={{0,3},{1,2},{2,1},{3,0},{4,7},{5,6},{6,5},{7,4},{8,11},{9,10},{10,... | collective-permute-start | bytes 196616 | tf_op jit(solution)/shard_map/ppermute | solution.py:234
  26.3 5.2 %collective-permute-start.10 = (bf16[64,512]{1,0:T(8,128)(2,1)S(1)}, bf16[64,512]{1,0:T(8,128)(2,1)S(1)}, u32[]{:S(2)}, u32[]{:S(2)}) collective-permute-start(bf16[64,512]{1,0:T(8,128)(2,1)S(1)} %hidden.1.after_ref.refs_0_), channel_id=1, source_target_pairs={{0,2},{1,3},{2,0},{3,1},{4,6},{5,7},{6,4},{7,5},{8,10},{9,11},{10,... | collective-permute-start | bytes 196616 | tf_op jit(solution)/shard_map/ppermute | solution.py:234
  26.3 5.2 %collective-permute-start.9 = (bf16[64,512]{1,0:T(8,128)(2,1)S(1)}, bf16[64,512]{1,0:T(8,128)(2,1)S(1)}, u32[]{:S(2)}, u32[]{:S(2)}) collective-permute-start(bf16[64,512]{1,0:T(8,128)(2,1)S(1)} %hidden.1.after_ref.refs_0_), channel_id=1, source_target_pairs={{0,1},{1,0},{2,3},{3,2},{4,5},{5,4},{6,7},{7,6},{8,9},{9,8},{10,11... | collective-permute-start | bytes 196616 | tf_op jit(solution)/shard_map/ppermute | solution.py:234
  32.0 5.8 %collective-permute-start.12 = (bf16[16,896]{1,0:T(8,128)(2,1)S(1)}, bf16[16,896]{1,0:T(8,128)(2,1)S(1)}, u32[]{:S(2)}, u32[]{:S(2)}) collective-permute-start(bf16[16,896]{1,0:T(8,128)(2,1)S(1)} %get-tuple-element.39), channel_id=1, source_target_pairs={{0,1},{1,2},{2,3},{3,0},{4,5},{5,6},{6,7},{7,4},{8,9},{9,10},{10,1... | collective-permute-start | bytes 86024 | tf_op jit(solution)/shard_map/ppermute | solution.py:352
  32.5 5.3 %collective-permute-start.13 = (bf16[16,896]{1,0:T(8,128)(2,1)S(1)}, bf16[16,896]{1,0:T(8,128)(2,1)S(1)}, u32[]{:S(2)}, u32[]{:S(2)}) collective-permute-start(bf16[16,896]{1,0:T(8,128)(2,1)S(1)} %get-tuple-element.40), channel_id=1, source_target_pairs={{0,2},{1,3},{2,0},{3,1},{4,6},{5,7},{6,4},{7,5},{8,10},{9,11},{10,... | collective-permute-start | bytes 86024 | tf_op jit(solution)/shard_map/ppermute | solution.py:352
  34.6 3.9 %collective-permute-start.14 = (bf16[16,896]{1,0:T(8,128)(2,1)S(1)}, bf16[16,896]{1,0:T(8,128)(2,1)S(1)}, u32[]{:S(2)}, u32[]{:S(2)}) collective-permute-start(bf16[16,896]{1,0:T(8,128)(2,1)S(1)} %get-tuple-element.41), channel_id=1, source_target_pairs={{0,3},{1,0},{2,1},{3,2},{4,7},{5,4},{6,5},{7,6},{8,11},{9,8},{10,9... | collective-permute-start | bytes 86024 | tf_op jit(solution)/shard_map/ppermute | solution.py:352
  38.7 4.2 %collective-permute-start.15 = (bf16[4,8,896]{2,1,0:T(8,128)(2,1)S(1)}, bf16[4,8,896]{2,1,0:T(8,128)(2,1)S(1)}, u32[]{:S(2)}, u32[]{:S(2)}) collective-permute-start(bf16[4,8,896]{2,1,0:T(8,128)(2,1)S(1)} %get-tuple-element.43), channel_id=1, source_target_pairs={{0,12},{4,8},{8,4},{12,0},{1,13},{5,9},{9,5},{13,1},{2,14},{6,10},... | collective-permute-start | bytes 172040 | tf_op jit(solution)/shard_map/ppermute | solution.py:234
  38.8 5.4 %collective-permute-start.16 = (bf16[4,8,896]{2,1,0:T(8,128)(2,1)S(1)}, bf16[4,8,896]{2,1,0:T(8,128)(2,1)S(1)}, u32[]{:S(2)}, u32[]{:S(2)}) collective-permute-start(bf16[4,8,896]{2,1,0:T(8,128)(2,1)S(1)} %get-tuple-element.44), channel_id=1, source_target_pairs={{0,8},{4,12},{8,0},{12,4},{1,9},{5,13},{9,1},{13,5},{2,10},{6,14},... | collective-permute-start | bytes 172040 | tf_op jit(solution)/shard_map/ppermute | solution.py:234
  40.4 3.8 %collective-permute-start.17 = (bf16[4,8,896]{2,1,0:T(8,128)(2,1)S(1)}, bf16[4,8,896]{2,1,0:T(8,128)(2,1)S(1)}, u32[]{:S(2)}, u32[]{:S(2)}) collective-permute-start(bf16[4,8,896]{2,1,0:T(8,128)(2,1)S(1)} %get-tuple-element.45), channel_id=1, source_target_pairs={{0,4},{4,0},{8,12},{12,8},{1,5},{5,1},{9,13},{13,9},{2,6},{6,2},{1... | collective-permute-start | bytes 172040 | tf_op jit(solution)/shard_map/ppermute | solution.py:234

commit v18 on v16

--- a/solution.py
+++ b/solution.py
@@ -196,24 +196,28 @@
 
 
 def spread_kernel(groups, columns, pick_ref, *refs):
-    blocks, outs = refs[:columns], refs[columns:]
-    me = lax.axis_index("ing")
+    blocks, outs, back_ref = refs[:columns], refs[columns:-1], refs[-1]
+    me, group = lax.axis_index("ing"), lax.axis_index("grp")
     for k in range(columns):
         block = blocks[k][...]
         place = lax.rem(me + columns - (k + 1), columns) ^ me
-        back = jnp.dot(pick_ref[:, : block.shape[0]], block, preferred_element_type=F32)
-        for d in range(groups):
-            outs[d][place] = back[d * CAP : (d + 1) * CAP].astype(BF16)
+        back_ref[...] = jnp.dot(pick_ref[:, : block.shape[0]], block, preferred_element_type=F32)
+        for s in range(groups):
+            at = pl.multiple_of((lax.rem(group + s, groups) ^ group) * CAP, CAP)
+            outs[s][place] = back_ref[pl.ds(at, CAP), :].astype(BF16)
 
 
 def combine_kernel(groups, columns, mixing_ref, *refs):
-    backs, (out_ref, held, sems) = refs[:groups][::-1], refs[groups:]
+    backs, (out_ref, rows_ref, held, sems) = refs[:groups], refs[groups:]
+    group = lax.axis_index("grp")
     me = lax.axis_index("ing")
     width, half = backs[0].shape[2], held.shape[0] // 2
     copies = []
     for e in range(columns):
-        rows = jnp.concatenate([backs[d][e].astype(F32) for d in range(groups)], axis=0)
-        rows = rows.astype(BF16)
+        for k in range(groups):
+            at = pl.multiple_of((lax.rem(group + groups - (k + 1), groups) ^ group) * CAP, CAP)
+            rows_ref[pl.ds(at, CAP), :] = backs[k][e].astype(F32)
+        rows = rows_ref[...].astype(BF16)
         part = pl.ds(e * width, width)
         there = pl.ds(pl.multiple_of((me ^ e) * width, width), width)
         for h in range(2):
@@ -357,14 +361,19 @@
         out_shape=[jax.ShapeDtypeStruct((columns, CAP, share), BF16)] * groups,
         in_specs=[VMEM] * (columns + 1),
         out_specs=[VMEM] * groups,
-        compiler_params=params(2 * (groups * CAP + slots) * features),
+        scratch_shapes=[pltpu.VMEM((groups * CAP, share), F32)],
+        compiler_params=params(2 * (groups * CAP + slots) * features + 4 * groups * CAP * share),
         name="spread",
     )(pick, *results)
-    backs = swap_all(backs, "grp")
+    backs = [
+        lax.ppermute(backs[s], "grp", [(a, (a + s) % groups) for a in range(groups)]) for s in range(1, groups)
+    ] + [backs[0]]
 
     if share % LANES:
         me = lax.axis_index("ing")
-        rows = jnp.stack(backs[::-1])[:, jnp.arange(columns) ^ me]
+        group = lax.axis_index("grp")
+        order = (group - 1 - (jnp.arange(groups) ^ group)) % groups
+        rows = jnp.stack(backs)[order][:, jnp.arange(columns) ^ me]
         rows = rows.transpose(0, 2, 1, 3).reshape(groups * CAP, features)
         return jnp.dot(mixing, rows, preferred_element_type=F32).astype(BF16)
     return pl.pallas_call(
@@ -372,7 +381,11 @@
         out_shape=jax.ShapeDtypeStruct((count, features), BF16),
         in_specs=[VMEM] * (1 + groups),
         out_specs=ANY,
-        scratch_shapes=[pltpu.VMEM((count, features), BF16), pltpu.SemaphoreType.DMA((2 * columns,))],
+        scratch_shapes=[
+            pltpu.VMEM((groups * CAP, share), F32),
+            pltpu.VMEM((count, features), BF16),
+            pltpu.SemaphoreType.DMA((2 * columns,)),
+        ],
         compiler_params=params(2 * (count + groups * CAP) * features),
         name="combine",
     )(mixing, *backs)

time: 45.9 us -> 45.5 us (level)
  waiting for transfers between devices: 10.9 us -> 9.16 us
  starting transfers between devices: 23.1 us -> 24.3 us
    ppermute x15 -> x12, waiting for transfers between devices: 9.25 us -> 5.72 us  [swap(): lax.ppermute(x, name, [(a, a ^ step) for a in range(lax.axis_size(name))])]
    ppermute x0 -> x3, starting transfers between devices: none -> 3.06 us  [local(): lax.ppermute(backs[s], 'grp', [(a, (a + s) % groups) for a in range(group...]
    ppermute x15 -> x12, starting transfers between devices: 18.2 us -> 16.3 us  [swap(): lax.ppermute(x, name, [(a, a ^ step) for a in range(lax.axis_size(name))])]
    ppermute x0 -> x3, waiting for transfers between devices: none -> 1.83 us  [local(): lax.ppermute(backs[s], 'grp', [(a, (a + s) % groups) for a in range(group...]
  transfers between devices with their start and end apart: 18 -> 18, of which waited for: 9 -> 10; matrix products, arithmetic and copies ran while one was open for 0% -> 0% of each run, Pallas kernels for 14% -> 14%
where the time goes in v18:
time: 45.5 us; the launch traced here: 45.1 us
  starting transfers between devices  24.3 us (53%)
  Pallas kernels  11.6 us (25%)
  waiting for transfers between devices  9.16 us (20%)
    ppermute x12, starting transfers between devices, swap(): lax.ppermute(x, name, [(a, a ^ step) for a in range(lax.axis_size(name))])  16.3 us
    ppermute x12, waiting for transfers between devices, swap(): lax.ppermute(x, name, [(a, a ^ step) for a in range(lax.axis_size(name))])  5.72 us
    ppermute x3, starting transfers between devices, local(): lax.ppermute(results[s], 'ing', [(a, (a + s) % columns) for a in range(co...  4.92 us
    pallas_call x1, Pallas kernels, local(): pl.pallas_call(load_kernel, out_shape=[pltpu.VMEM(w.shape, BF16) for w in...  3.17 us
    ppermute x3, starting transfers between devices, local(): lax.ppermute(backs[s], 'grp', [(a, (a + s) % groups) for a in range(group...  3.06 us
    pallas_call x1, Pallas kernels, local(): pl.pallas_call(functools.partial(prepare_kernel, groups), out_shape=[pltp...  2.13 us
    pallas_call x1, Pallas kernels, local(): pl.pallas_call(functools.partial(dispatch_kernel, groups, features // 4),...  1.88 us
    ppermute x3, waiting for transfers between devices, local(): lax.ppermute(backs[s], 'grp', [(a, (a + s) % groups) for a in range(group...  1.83 us
  transfers between devices with their start and end apart: 18, of which 10 were waited for; matrix products, arithmetic and copies ran while one was open for 0% of the time, Pallas kernels for 14%

profile of v18, /device:TPU:0, one launch (start us, length us, event | category | flops | bytes accessed | tf_op | source)
XLA Modules:
  0.0 45.1 jit_solution(4843038504537030616)
XLA Ops:
  0.0 1.9 %dispatch.1 = (bf16[8,3712]{1,0:T(8,128)(2,1)S(1)}, bf16[8,3712]{1,0:T(8,128)(2,1)S(1)}, bf16[8,3712]{1,0:T(8,128)(2,1)S(1)}, bf16[8,3712]{1,0:T(8,128)(2,1)S(1)}) custom-call(s32[8,256]{1,0:T(8,128)} %bitcast.9, bf16[256,3584]{1,0:T(8,128)(2,1)} %tokens_ref.1), custom_call_target="tpu_custom_call" | custom-call | tf_op jit(solution)/shard_map/dispatch/pallas_call | solution.py:255
  1.9 2.4 %collective-permute-start = (bf16[8,3712]{1,0:T(8,128)(2,1)S(1)}, bf16[8,3712]{1,0:T(8,128)(2,1)S(1)}, u32[]{:S(2)}, u32[]{:S(2)}) collective-permute-start(bf16[8,3712]{1,0:T(8,128)(2,1)S(1)} %get-tuple-element.28), channel_id=1, source_target_pairs={{0,12},{4,8},{8,4},{12,0},{1,13},{5,9},{9,5},{13,1},{2,14},{6,10},... | collective-permute-start | bytes 178184 | tf_op jit(solution)/shard_map/ppermute | solution.py:238
  4.3 0.6 %collective-permute-start.1 = (bf16[8,3712]{1,0:T(8,128)(2,1)S(1)}, bf16[8,3712]{1,0:T(8,128)(2,1)S(1)}, u32[]{:S(2)}, u32[]{:S(2)}) collective-permute-start(bf16[8,3712]{1,0:T(8,128)(2,1)S(1)} %get-tuple-element.29), channel_id=1, source_target_pairs={{0,8},{4,12},{8,0},{12,4},{1,9},{5,13},{9,1},{13,5},{2,10},{6,14},... | collective-permute-start | bytes 178184 | tf_op jit(solution)/shard_map/ppermute | solution.py:238
  5.0 3.2 %load.1 = (bf16[3584,512]{1,0:T(8,128)(2,1)S(1)}, bf16[3584,512]{1,0:T(8,128)(2,1)S(1)}) custom-call(bf16[8,3712]{1,0:T(8,128)(2,1)S(1)} %get-tuple-element.26.after_ref.refs_3_, bf16[3584,512]{1,0:T(8,128)(2,1)} %bitcast.5, bf16[3584,512]{1,0:T(8,128)(2,1)} %bitcast.6), custom_call_target="tpu_custom_call" | custom-call | tf_op jit(solution)/shard_map/load/pallas_call | solution.py:273
  8.2 0.7 %collective-permute-done.1.refs_1_ = bf16[8,3712]{1,0:T(8,128)(2,1)S(1)} collective-permute-done((bf16[8,3712]{1,0:T(8,128)(2,1)S(1)}, bf16[8,3712]{1,0:T(8,128)(2,1)S(1)}, u32[]{:S(2)}, u32[]{:S(2)}) %collective-permute-start.1) | collective-permute-done | bytes 59424 | tf_op jit(solution)/shard_map/ppermute | solution.py:238
  8.9 0.3 compact.1
  9.2 2.7 %collective-permute-start.4 = (bf16[16,1792]{1,0:T(8,128)(2,1)S(1)}, bf16[16,1792]{1,0:T(8,128)(2,1)S(1)}, u32[]{:S(2)}, u32[]{:S(2)}) collective-permute-start(bf16[16,1792]{1,0:T(8,128)(2,1)S(1)} %get-tuple-element.31.refs_0_), channel_id=1, source_target_pairs={{0,2},{1,3},{2,0},{3,1},{4,6},{5,7},{6,4},{7,5},{8,10},{9,11},{10,... | collective-permute-start | bytes 172040 | tf_op jit(solution)/shard_map/ppermute | solution.py:238
  11.9 1.6 %collective-permute-start.6 = (bf16[16,1792]{1,0:T(8,128)(2,1)S(1)}, bf16[16,1792]{1,0:T(8,128)(2,1)S(1)}, u32[]{:S(2)}, u32[]{:S(2)}) collective-permute-start(bf16[16,1792]{1,0:T(8,128)(2,1)S(1)} %get-tuple-element.32.refs_0_), channel_id=1, source_target_pairs={{0,1},{1,0},{2,3},{3,2},{4,5},{5,4},{6,7},{7,6},{8,9},{9,8},{10,11... | collective-permute-start | bytes 172040 | tf_op jit(solution)/shard_map/ppermute | solution.py:238
  13.7 1.8 %collective-permute-start.8 = (bf16[16,1792]{1,0:T(8,128)(2,1)S(1)}, bf16[16,1792]{1,0:T(8,128)(2,1)S(1)}, u32[]{:S(2)}, u32[]{:S(2)}) collective-permute-start(bf16[16,1792]{1,0:T(8,128)(2,1)S(1)} %get-tuple-element.32.refs_0_), channel_id=1, source_target_pairs={{0,2},{1,3},{2,0},{3,1},{4,6},{5,7},{6,4},{7,5},{8,10},{9,11},{10,... | collective-permute-start | bytes 172040 | tf_op jit(solution)/shard_map/ppermute | solution.py:238
  15.4 2.5 %collective-permute-start.3 = (bf16[16,1792]{1,0:T(8,128)(2,1)S(1)}, bf16[16,1792]{1,0:T(8,128)(2,1)S(1)}, u32[]{:S(2)}, u32[]{:S(2)}) collective-permute-start(bf16[16,1792]{1,0:T(8,128)(2,1)S(1)} %get-tuple-element.31.refs_0_), channel_id=1, source_target_pairs={{0,1},{1,0},{2,3},{3,2},{4,5},{5,4},{6,7},{7,6},{8,9},{9,8},{10,11... | collective-permute-start | bytes 172040 | tf_op jit(solution)/shard_map/ppermute | solution.py:238
  17.9 2.2 %collective-permute-done.7.refs_2_ = bf16[16,1792]{1,0:T(8,128)(2,1)S(1)} collective-permute-done((bf16[16,1792]{1,0:T(8,128)(2,1)S(1)}, bf16[16,1792]{1,0:T(8,128)(2,1)S(1)}, u32[]{:S(2)}, u32[]{:S(2)}) %collective-permute-start.7) | collective-permute-done | bytes 57376 | tf_op jit(solution)/shard_map/ppermute | solution.py:238
  20.2 0.7 %ahead.1 = (f32[64,512]{1,0:T(8,128)S(1)}, f32[64,512]{1,0:T(8,128)S(1)}) custom-call(bf16[16,1792]{1,0:T(8,128)(2,1)S(1)} %get-tuple-element.32.refs_0_, bf16[16,1792]{1,0:T(8,128)(2,1)S(1)} %collective-permute-done.6.refs_1_, bf16[16,1792]{1,0:T(8,128)(2,1)S(1)} %collective-permute-done.7.refs_2_, bf16[16,1792]{1,0:T(8,128)(2,1)S(1)} %collective-permute-done.8.refs_3_, ...), custom_call_target="tpu_custom_call" | custom-call | tf_op jit(solution)/shard_map/ahead/pallas_call | solution.py:298
  20.9 0.3 collective-permute-done.3.refs_1_
  21.3 0.8 %collective-permute-done.5.refs_3_ = bf16[16,1792]{1,0:T(8,128)(2,1)S(1)} collective-permute-done((bf16[16,1792]{1,0:T(8,128)(2,1)S(1)}, bf16[16,1792]{1,0:T(8,128)(2,1)S(1)}, u32[]{:S(2)}, u32[]{:S(2)}) %collective-permute-start.5) | collective-permute-done | bytes 57376 | tf_op jit(solution)/shard_map/ppermute | solution.py:238
  22.1 0.8 %hidden.1.after_ref.refs_0_ = bf16[64,512]{1,0:T(8,128)(2,1)S(1)} custom-call(bf16[16,1792]{1,0:T(8,128)(2,1)S(1)} %get-tuple-element.31.refs_0_, bf16[16,1792]{1,0:T(8,128)(2,1)S(1)} %collective-permute-done.3.refs_1_, bf16[16,1792]{1,0:T(8,128)(2,1)S(1)} %collective-permute-done.4.refs_2_, bf16[16,1792]{1,0:T(8,128)(2,1)S(1)} %collective-permute-done.5.refs_3_, ...), custom_call_target="tpu_custom_call" | custom-call | tf_op jit(solution)/shard_map/hidden/pallas_call | solution.py:311
  22.9 3.4 %collective-permute-start.11 = (bf16[64,512]{1,0:T(8,128)(2,1)S(1)}, bf16[64,512]{1,0:T(8,128)(2,1)S(1)}, u32[]{:S(2)}, u32[]{:S(2)}) collective-permute-start(bf16[64,512]{1,0:T(8,128)(2,1)S(1)} %hidden.1.after_ref.refs_0_), channel_id=1, source_target_pairs={{0,3},{1,2},{2,1},{3,0},{4,7},{5,6},{6,5},{7,4},{8,11},{9,10},{10,... | collective-permute-start | bytes 196616 | tf_op jit(solution)/shard_map/ppermute | solution.py:238
  26.3 1.0 %collective-permute-start.9 = (bf16[64,512]{1,0:T(8,128)(2,1)S(1)}, bf16[64,512]{1,0:T(8,128)(2,1)S(1)}, u32[]{:S(2)}, u32[]{:S(2)}) collective-permute-start(bf16[64,512]{1,0:T(8,128)(2,1)S(1)} %hidden.1.after_ref.refs_0_), channel_id=1, source_target_pairs={{0,1},{1,0},{2,3},{3,2},{4,5},{5,4},{6,7},{7,6},{8,9},{9,8},{10,11... | collective-permute-start | bytes 196616 | tf_op jit(solution)/shard_map/ppermute | solution.py:238
  27.3 2.1 %prepare.1 = (bf16[2048,896]{1,0:T(8,128)(2,1)S(1)}, bf16[256,32]{1,0:T(8,128)(2,1)S(1)}) custom-call(bf16[64,512]{1,0:T(8,128)(2,1)S(1)} %hidden.1.after_ref.refs_0_, s32[8,256]{1,0:T(8,128)} %bitcast.10, f32[96,256]{1,0:T(8,128)} %bitcast.8, bf16[2048,896]{1,0:T(8,128)(2,1)} %bitcast.7), custom_call_target="tpu_custom_call" | custom-call | tf_op jit(solution)/shard_map/prepare/pallas_call | solution.py:319
  29.5 0.4 begin.1.refs_2_
  29.9 1.6 %collective-permute-done.10.refs_1_ = bf16[64,512]{1,0:T(8,128)(2,1)S(1)} collective-permute-done((bf16[64,512]{1,0:T(8,128)(2,1)S(1)}, bf16[64,512]{1,0:T(8,128)(2,1)S(1)}, u32[]{:S(2)}, u32[]{:S(2)}) %collective-permute-start.10) | collective-permute-done | bytes 65568 | tf_op jit(solution)/shard_map/ppermute | solution.py:238
  31.5 0.4 down.1
  32.0 0.5 %collective-permute-start.12 = (bf16[16,896]{1,0:T(8,128)(2,1)S(1)}, bf16[16,896]{1,0:T(8,128)(2,1)S(1)}, u32[]{:S(2)}, u32[]{:S(2)}) collective-permute-start(bf16[16,896]{1,0:T(8,128)(2,1)S(1)} %get-tuple-element.39), channel_id=1, source_target_pairs={{0,1},{1,2},{2,3},{3,0},{4,5},{5,6},{6,7},{7,4},{8,9},{9,10},{10,1... | collective-permute-start | bytes 86024 | tf_op jit(solution)/shard_map/ppermute | solution.py:356
  32.5 2.1 %collective-permute-start.13 = (bf16[16,896]{1,0:T(8,128)(2,1)S(1)}, bf16[16,896]{1,0:T(8,128)(2,1)S(1)}, u32[]{:S(2)}, u32[]{:S(2)}) collective-permute-start(bf16[16,896]{1,0:T(8,128)(2,1)S(1)} %get-tuple-element.40), channel_id=1, source_target_pairs={{0,2},{1,3},{2,0},{3,1},{4,6},{5,7},{6,4},{7,5},{8,10},{9,11},{10,... | collective-permute-start | bytes 86024 | tf_op jit(solution)/shard_map/ppermute | solution.py:356
  34.7 2.3 %collective-permute-start.14 = (bf16[16,896]{1,0:T(8,128)(2,1)S(1)}, bf16[16,896]{1,0:T(8,128)(2,1)S(1)}, u32[]{:S(2)}, u32[]{:S(2)}) collective-permute-start(bf16[16,896]{1,0:T(8,128)(2,1)S(1)} %get-tuple-element.41), channel_id=1, source_target_pairs={{0,3},{1,0},{2,1},{3,2},{4,7},{5,4},{6,5},{7,6},{8,11},{9,8},{10,9... | collective-permute-start | bytes 86024 | tf_op jit(solution)/shard_map/ppermute | solution.py:356
  36.9 0.9 %collective-permute-done.12.refs_0_ = bf16[16,896]{1,0:T(8,128)(2,1)S(1)} collective-permute-done((bf16[16,896]{1,0:T(8,128)(2,1)S(1)}, bf16[16,896]{1,0:T(8,128)(2,1)S(1)}, u32[]{:S(2)}, u32[]{:S(2)}) %collective-permute-start.12) | collective-permute-done | bytes 28704 | tf_op jit(solution)/shard_map/ppermute | solution.py:356
  37.9 0.7 %collective-permute-done.14.refs_2_ = bf16[16,896]{1,0:T(8,128)(2,1)S(1)} collective-permute-done((bf16[16,896]{1,0:T(8,128)(2,1)S(1)}, bf16[16,896]{1,0:T(8,128)(2,1)S(1)}, u32[]{:S(2)}, u32[]{:S(2)}) %collective-permute-start.14) | collective-permute-done | bytes 28704 | tf_op jit(solution)/shard_map/ppermute | solution.py:356
  38.8 1.6 %collective-permute-start.16 = (bf16[4,8,896]{2,1,0:T(8,128)(2,1)S(1)}, bf16[4,8,896]{2,1,0:T(8,128)(2,1)S(1)}, u32[]{:S(2)}, u32[]{:S(2)}) collective-permute-start(bf16[4,8,896]{2,1,0:T(8,128)(2,1)S(1)} %get-tuple-element.44), channel_id=1, source_target_pairs={{0,8},{4,12},{8,0},{12,4},{1,9},{5,13},{9,1},{13,5},{2,10},{6,14},... | collective-permute-start | bytes 172040 | tf_op jit(solution)/shard_map/ppermute | solution.py:369
  40.4 1.4 %collective-permute-start.17 = (bf16[4,8,896]{2,1,0:T(8,128)(2,1)S(1)}, bf16[4,8,896]{2,1,0:T(8,128)(2,1)S(1)}, u32[]{:S(2)}, u32[]{:S(2)}) collective-permute-start(bf16[4,8,896]{2,1,0:T(8,128)(2,1)S(1)} %get-tuple-element.45), channel_id=1, source_target_pairs={{0,12},{4,0},{8,4},{12,8},{1,13},{5,1},{9,5},{13,9},{2,14},{6,2},{... | collective-permute-start | bytes 172040 | tf_op jit(solution)/shard_map/ppermute | solution.py:369
  41.8 0.6 %collective-permute-done.15.refs_0_ = bf16[4,8,896]{2,1,0:T(8,128)(2,1)S(1)} collective-permute-done((bf16[4,8,896]{2,1,0:T(8,128)(2,1)S(1)}, bf16[4,8,896]{2,1,0:T(8,128)(2,1)S(1)}, u32[]{:S(2)}, u32[]{:S(2)}) %collective-permute-start.15) | collective-permute-done | bytes 57376 | tf_op jit(solution)/shard_map/ppermute | solution.py:369
  42.4 0.7 %collective-permute-done.16.refs_1_ = bf16[4,8,896]{2,1,0:T(8,128)(2,1)S(1)} collective-permute-done((bf16[4,8,896]{2,1,0:T(8,128)(2,1)S(1)}, bf16[4,8,896]{2,1,0:T(8,128)(2,1)S(1)}, u32[]{:S(2)}, u32[]{:S(2)}) %collective-permute-start.16) | collective-permute-done | bytes 57376 | tf_op jit(solution)/shard_map/ppermute | solution.py:369
  43.0 0.6 %collective-permute-done.17.refs_2_ = bf16[4,8,896]{2,1,0:T(8,128)(2,1)S(1)} collective-permute-done((bf16[4,8,896]{2,1,0:T(8,128)(2,1)S(1)}, bf16[4,8,896]{2,1,0:T(8,128)(2,1)S(1)}, u32[]{:S(2)}, u32[]{:S(2)}) %collective-permute-start.17) | collective-permute-done | bytes 57376 | tf_op jit(solution)/shard_map/ppermute | solution.py:369
  43.6 1.5 %combine.1 = bf16[256,3584]{1,0:T(8,128)(2,1)} custom-call(bf16[256,32]{1,0:T(8,128)(2,1)S(1)} %get-tuple-element.36.mixing_ref, bf16[4,8,896]{2,1,0:T(8,128)(2,1)S(1)} %collective-permute-done.15.refs_0_, bf16[4,8,896]{2,1,0:T(8,128)(2,1)S(1)} %collective-permute-done.16.refs_1_, bf16[4,8,896]{2,1,0:T(8,128)(2,1)S(1)} %collective-permute-done.17.refs_2_, ...), custom_call_target="tpu_custom_call" | custom-call | tf_op jit(solution)/shard_map/combine/pallas_call | solution.py:379
  (14 shorter events, 0.5 us)
Async XLA Ops:
  1.9 6.3 %collective-permute-start = (bf16[8,3712]{1,0:T(8,128)(2,1)S(1)}, bf16[8,3712]{1,0:T(8,128)(2,1)S(1)}, u32[]{:S(2)}, u32[]{:S(2)}) collective-permute-start(bf16[8,3712]{1,0:T(8,128)(2,1)S(1)} %get-tuple-element.28), channel_id=1, source_target_pairs={{0,12},{4,8},{8,4},{12,0},{1,13},{5,9},{9,5},{13,1},{2,14},{6,10},... | collective-permute-start | bytes 178184 | tf_op jit(solution)/shard_map/ppermute | solution.py:238
  4.3 4.5 %collective-permute-start.1 = (bf16[8,3712]{1,0:T(8,128)(2,1)S(1)}, bf16[8,3712]{1,0:T(8,128)(2,1)S(1)}, u32[]{:S(2)}, u32[]{:S(2)}) collective-permute-start(bf16[8,3712]{1,0:T(8,128)(2,1)S(1)} %get-tuple-element.29), channel_id=1, source_target_pairs={{0,8},{4,12},{8,0},{12,4},{1,9},{5,13},{9,1},{13,5},{2,10},{6,14},... | collective-permute-start | bytes 178184 | tf_op jit(solution)/shard_map/ppermute | solution.py:238
  5.0 3.9 %collective-permute-start.2 = (bf16[8,3712]{1,0:T(8,128)(2,1)S(1)}, bf16[8,3712]{1,0:T(8,128)(2,1)S(1)}, u32[]{:S(2)}, u32[]{:S(2)}) collective-permute-start(bf16[8,3712]{1,0:T(8,128)(2,1)S(1)} %get-tuple-element.30), channel_id=1, source_target_pairs={{0,4},{4,0},{8,12},{12,8},{1,5},{5,1},{9,13},{13,9},{2,6},{6,2},{1... | collective-permute-start | bytes 178184 | tf_op jit(solution)/shard_map/ppermute | solution.py:238
  9.2 8.7 %collective-permute-start.4 = (bf16[16,1792]{1,0:T(8,128)(2,1)S(1)}, bf16[16,1792]{1,0:T(8,128)(2,1)S(1)}, u32[]{:S(2)}, u32[]{:S(2)}) collective-permute-start(bf16[16,1792]{1,0:T(8,128)(2,1)S(1)} %get-tuple-element.31.refs_0_), channel_id=1, source_target_pairs={{0,2},{1,3},{2,0},{3,1},{4,6},{5,7},{6,4},{7,5},{8,10},{9,11},{10,... | collective-permute-start | bytes 172040 | tf_op jit(solution)/shard_map/ppermute | solution.py:238
  11.9 6.0 %collective-permute-start.6 = (bf16[16,1792]{1,0:T(8,128)(2,1)S(1)}, bf16[16,1792]{1,0:T(8,128)(2,1)S(1)}, u32[]{:S(2)}, u32[]{:S(2)}) collective-permute-start(bf16[16,1792]{1,0:T(8,128)(2,1)S(1)} %get-tuple-element.32.refs_0_), channel_id=1, source_target_pairs={{0,1},{1,0},{2,3},{3,2},{4,5},{5,4},{6,7},{7,6},{8,9},{9,8},{10,11... | collective-permute-start | bytes 172040 | tf_op jit(solution)/shard_map/ppermute | solution.py:238
  13.5 6.7 %collective-permute-start.7 = (bf16[16,1792]{1,0:T(8,128)(2,1)S(1)}, bf16[16,1792]{1,0:T(8,128)(2,1)S(1)}, u32[]{:S(2)}, u32[]{:S(2)}) collective-permute-start(bf16[16,1792]{1,0:T(8,128)(2,1)S(1)} %get-tuple-element.32.refs_0_), channel_id=1, source_target_pairs={{0,3},{1,2},{2,1},{3,0},{4,7},{5,6},{6,5},{7,4},{8,11},{9,10},{10,... | collective-permute-start | bytes 172040 | tf_op jit(solution)/shard_map/ppermute | solution.py:238
  13.7 6.5 %collective-permute-start.8 = (bf16[16,1792]{1,0:T(8,128)(2,1)S(1)}, bf16[16,1792]{1,0:T(8,128)(2,1)S(1)}, u32[]{:S(2)}, u32[]{:S(2)}) collective-permute-start(bf16[16,1792]{1,0:T(8,128)(2,1)S(1)} %get-tuple-element.32.refs_0_), channel_id=1, source_target_pairs={{0,2},{1,3},{2,0},{3,1},{4,6},{5,7},{6,4},{7,5},{8,10},{9,11},{10,... | collective-permute-start | bytes 172040 | tf_op jit(solution)/shard_map/ppermute | solution.py:238
  15.4 5.8 %collective-permute-start.3 = (bf16[16,1792]{1,0:T(8,128)(2,1)S(1)}, bf16[16,1792]{1,0:T(8,128)(2,1)S(1)}, u32[]{:S(2)}, u32[]{:S(2)}) collective-permute-start(bf16[16,1792]{1,0:T(8,128)(2,1)S(1)} %get-tuple-element.31.refs_0_), channel_id=1, source_target_pairs={{0,1},{1,0},{2,3},{3,2},{4,5},{5,4},{6,7},{7,6},{8,9},{9,8},{10,11... | collective-permute-start | bytes 172040 | tf_op jit(solution)/shard_map/ppermute | solution.py:238
  17.9 4.2 %collective-permute-start.5 = (bf16[16,1792]{1,0:T(8,128)(2,1)S(1)}, bf16[16,1792]{1,0:T(8,128)(2,1)S(1)}, u32[]{:S(2)}, u32[]{:S(2)}) collective-permute-start(bf16[16,1792]{1,0:T(8,128)(2,1)S(1)} %collective-permute-done.4.refs_2_), channel_id=1, source_target_pairs={{0,1},{1,0},{2,3},{3,2},{4,5},{5,4},{6,7},{7,6},{8,9},{9,8},{10,11... | collective-permute-start | bytes 172040 | tf_op jit(solution)/shard_map/ppermute | solution.py:238
  22.9 6.6 %collective-permute-start.11 = (bf16[64,512]{1,0:T(8,128)(2,1)S(1)}, bf16[64,512]{1,0:T(8,128)(2,1)S(1)}, u32[]{:S(2)}, u32[]{:S(2)}) collective-permute-start(bf16[64,512]{1,0:T(8,128)(2,1)S(1)} %hidden.1.after_ref.refs_0_), channel_id=1, source_target_pairs={{0,3},{1,2},{2,1},{3,0},{4,7},{5,6},{6,5},{7,4},{8,11},{9,10},{10,... | collective-permute-start | bytes 196616 | tf_op jit(solution)/shard_map/ppermute | solution.py:238
  26.3 5.2 %collective-permute-start.10 = (bf16[64,512]{1,0:T(8,128)(2,1)S(1)}, bf16[64,512]{1,0:T(8,128)(2,1)S(1)}, u32[]{:S(2)}, u32[]{:S(2)}) collective-permute-start(bf16[64,512]{1,0:T(8,128)(2,1)S(1)} %hidden.1.after_ref.refs_0_), channel_id=1, source_target_pairs={{0,2},{1,3},{2,0},{3,1},{4,6},{5,7},{6,4},{7,5},{8,10},{9,11},{10,... | collective-permute-start | bytes 196616 | tf_op jit(solution)/shard_map/ppermute | solution.py:238
  26.3 5.2 %collective-permute-start.9 = (bf16[64,512]{1,0:T(8,128)(2,1)S(1)}, bf16[64,512]{1,0:T(8,128)(2,1)S(1)}, u32[]{:S(2)}, u32[]{:S(2)}) collective-permute-start(bf16[64,512]{1,0:T(8,128)(2,1)S(1)} %hidden.1.after_ref.refs_0_), channel_id=1, source_target_pairs={{0,1},{1,0},{2,3},{3,2},{4,5},{5,4},{6,7},{7,6},{8,9},{9,8},{10,11... | collective-permute-start | bytes 196616 | tf_op jit(solution)/shard_map/ppermute | solution.py:238
  32.0 5.8 %collective-permute-start.12 = (bf16[16,896]{1,0:T(8,128)(2,1)S(1)}, bf16[16,896]{1,0:T(8,128)(2,1)S(1)}, u32[]{:S(2)}, u32[]{:S(2)}) collective-permute-start(bf16[16,896]{1,0:T(8,128)(2,1)S(1)} %get-tuple-element.39), channel_id=1, source_target_pairs={{0,1},{1,2},{2,3},{3,0},{4,5},{5,6},{6,7},{7,4},{8,9},{9,10},{10,1... | collective-permute-start | bytes 86024 | tf_op jit(solution)/shard_map/ppermute | solution.py:356
  32.5 5.3 %collective-permute-start.13 = (bf16[16,896]{1,0:T(8,128)(2,1)S(1)}, bf16[16,896]{1,0:T(8,128)(2,1)S(1)}, u32[]{:S(2)}, u32[]{:S(2)}) collective-permute-start(bf16[16,896]{1,0:T(8,128)(2,1)S(1)} %get-tuple-element.40), channel_id=1, source_target_pairs={{0,2},{1,3},{2,0},{3,1},{4,6},{5,7},{6,4},{7,5},{8,10},{9,11},{10,... | collective-permute-start | bytes 86024 | tf_op jit(solution)/shard_map/ppermute | solution.py:356
  34.7 3.9 %collective-permute-start.14 = (bf16[16,896]{1,0:T(8,128)(2,1)S(1)}, bf16[16,896]{1,0:T(8,128)(2,1)S(1)}, u32[]{:S(2)}, u32[]{:S(2)}) collective-permute-start(bf16[16,896]{1,0:T(8,128)(2,1)S(1)} %get-tuple-element.41), channel_id=1, source_target_pairs={{0,3},{1,0},{2,1},{3,2},{4,7},{5,4},{6,5},{7,6},{8,11},{9,8},{10,9... | collective-permute-start | bytes 86024 | tf_op jit(solution)/shard_map/ppermute | solution.py:356
  38.7 3.7 %collective-permute-start.15 = (bf16[4,8,896]{2,1,0:T(8,128)(2,1)S(1)}, bf16[4,8,896]{2,1,0:T(8,128)(2,1)S(1)}, u32[]{:S(2)}, u32[]{:S(2)}) collective-permute-start(bf16[4,8,896]{2,1,0:T(8,128)(2,1)S(1)} %get-tuple-element.43), channel_id=1, source_target_pairs={{0,4},{4,8},{8,12},{12,0},{1,5},{5,9},{9,13},{13,1},{2,6},{6,10},{... | collective-permute-start | bytes 172040 | tf_op jit(solution)/shard_map/ppermute | solution.py:369
  38.8 4.2 %collective-permute-start.16 = (bf16[4,8,896]{2,1,0:T(8,128)(2,1)S(1)}, bf16[4,8,896]{2,1,0:T(8,128)(2,1)S(1)}, u32[]{:S(2)}, u32[]{:S(2)}) collective-permute-start(bf16[4,8,896]{2,1,0:T(8,128)(2,1)S(1)} %get-tuple-element.44), channel_id=1, source_target_pairs={{0,8},{4,12},{8,0},{12,4},{1,9},{5,13},{9,1},{13,5},{2,10},{6,14},... | collective-permute-start | bytes 172040 | tf_op jit(solution)/shard_map/ppermute | solution.py:369
  40.4 3.2 %collective-permute-start.17 = (bf16[4,8,896]{2,1,0:T(8,128)(2,1)S(1)}, bf16[4,8,896]{2,1,0:T(8,128)(2,1)S(1)}, u32[]{:S(2)}, u32[]{:S(2)}) collective-permute-start(bf16[4,8,896]{2,1,0:T(8,128)(2,1)S(1)} %get-tuple-element.45), channel_id=1, source_target_pairs={{0,12},{4,0},{8,4},{12,8},{1,13},{5,1},{9,5},{13,9},{2,14},{6,2},{... | collective-permute-start | bytes 172040 | tf_op jit(solution)/shard_map/ppermute | solution.py:369

commit v19 on v18

--- a/solution.py
+++ b/solution.py
@@ -253,7 +253,7 @@
     logits = pltpu.with_memory_space_constraint(router_logits.T, pltpu.HBM)
 
     outbound = pl.pallas_call(
-        functools.partial(dispatch_kernel, groups, features // 4),
+        functools.partial(dispatch_kernel, groups, features // 2),
         out_shape=[jax.ShapeDtypeStruct((CAP, wide), BF16)] * groups,
         in_specs=[ANY, ANY],
         out_specs=[VMEM] * groups,

time: 45.5 us -> 45.5 us (level)
  no operation moved by 1% of the time
where the time goes in v19:
time: 45.5 us; the launch traced here: 45.1 us
  starting transfers between devices  24.3 us (53%)
  Pallas kernels  11.5 us (25%)
  waiting for transfers between devices  9.17 us (20%)
    ppermute x12, starting transfers between devices, swap(): lax.ppermute(x, name, [(a, a ^ step) for a in range(lax.axis_size(name))])  16.3 us
    ppermute x12, waiting for transfers between devices, swap(): lax.ppermute(x, name, [(a, a ^ step) for a in range(lax.axis_size(name))])  5.73 us
    ppermute x3, starting transfers between devices, local(): lax.ppermute(results[s], 'ing', [(a, (a + s) % columns) for a in range(co...  4.92 us
    pallas_call x1, Pallas kernels, local(): pl.pallas_call(load_kernel, out_shape=[pltpu.VMEM(w.shape, BF16) for w in...  3.17 us
    ppermute x3, starting transfers between devices, local(): lax.ppermute(backs[s], 'grp', [(a, (a + s) % groups) for a in range(group...  3.06 us
    pallas_call x1, Pallas kernels, local(): pl.pallas_call(functools.partial(prepare_kernel, groups), out_shape=[pltp...  2.13 us
    ppermute x3, waiting for transfers between devices, local(): lax.ppermute(backs[s], 'grp', [(a, (a + s) % groups) for a in range(group...  1.83 us
    pallas_call x1, Pallas kernels, local(): pl.pallas_call(functools.partial(dispatch_kernel, groups, features // 2),...  1.81 us
  transfers between devices with their start and end apart: 18, of which 10 were waited for; matrix products, arithmetic and copies ran while one was open for 0% of the time, Pallas kernels for 14%

profile of v19, /device:TPU:0, one launch (start us, length us, event | category | flops | bytes accessed | tf_op | source)
XLA Modules:
  0.0 45.1 jit_solution(16596719883400275781)
XLA Ops:
  0.0 1.8 %dispatch.1 = (bf16[8,3712]{1,0:T(8,128)(2,1)S(1)}, bf16[8,3712]{1,0:T(8,128)(2,1)S(1)}, bf16[8,3712]{1,0:T(8,128)(2,1)S(1)}, bf16[8,3712]{1,0:T(8,128)(2,1)S(1)}) custom-call(s32[8,256]{1,0:T(8,128)} %bitcast.9, bf16[256,3584]{1,0:T(8,128)(2,1)} %tokens_ref.1), custom_call_target="tpu_custom_call" | custom-call | tf_op jit(solution)/shard_map/dispatch/pallas_call | solution.py:255
  1.8 2.4 %collective-permute-start = (bf16[8,3712]{1,0:T(8,128)(2,1)S(1)}, bf16[8,3712]{1,0:T(8,128)(2,1)S(1)}, u32[]{:S(2)}, u32[]{:S(2)}) collective-permute-start(bf16[8,3712]{1,0:T(8,128)(2,1)S(1)} %get-tuple-element.28), channel_id=1, source_target_pairs={{0,12},{4,8},{8,4},{12,0},{1,13},{5,9},{9,5},{13,1},{2,14},{6,10},... | collective-permute-start | bytes 178184 | tf_op jit(solution)/shard_map/ppermute | solution.py:238
  4.3 0.6 %collective-permute-start.1 = (bf16[8,3712]{1,0:T(8,128)(2,1)S(1)}, bf16[8,3712]{1,0:T(8,128)(2,1)S(1)}, u32[]{:S(2)}, u32[]{:S(2)}) collective-permute-start(bf16[8,3712]{1,0:T(8,128)(2,1)S(1)} %get-tuple-element.29), channel_id=1, source_target_pairs={{0,8},{4,12},{8,0},{12,4},{1,9},{5,13},{9,1},{13,5},{2,10},{6,14},... | collective-permute-start | bytes 178184 | tf_op jit(solution)/shard_map/ppermute | solution.py:238
  4.9 3.2 %load.1 = (bf16[3584,512]{1,0:T(8,128)(2,1)S(1)}, bf16[3584,512]{1,0:T(8,128)(2,1)S(1)}) custom-call(bf16[8,3712]{1,0:T(8,128)(2,1)S(1)} %get-tuple-element.26.after_ref.refs_3_, bf16[3584,512]{1,0:T(8,128)(2,1)} %bitcast.5, bf16[3584,512]{1,0:T(8,128)(2,1)} %bitcast.6), custom_call_target="tpu_custom_call" | custom-call | tf_op jit(solution)/shard_map/load/pallas_call | solution.py:273
  8.1 0.7 %collective-permute-done.1.refs_1_ = bf16[8,3712]{1,0:T(8,128)(2,1)S(1)} collective-permute-done((bf16[8,3712]{1,0:T(8,128)(2,1)S(1)}, bf16[8,3712]{1,0:T(8,128)(2,1)S(1)}, u32[]{:S(2)}, u32[]{:S(2)}) %collective-permute-start.1) | collective-permute-done | bytes 59424 | tf_op jit(solution)/shard_map/ppermute | solution.py:238
  8.8 0.3 compact.1
  9.1 2.7 %collective-permute-start.4 = (bf16[16,1792]{1,0:T(8,128)(2,1)S(1)}, bf16[16,1792]{1,0:T(8,128)(2,1)S(1)}, u32[]{:S(2)}, u32[]{:S(2)}) collective-permute-start(bf16[16,1792]{1,0:T(8,128)(2,1)S(1)} %get-tuple-element.31.refs_0_), channel_id=1, source_target_pairs={{0,2},{1,3},{2,0},{3,1},{4,6},{5,7},{6,4},{7,5},{8,10},{9,11},{10,... | collective-permute-start | bytes 172040 | tf_op jit(solution)/shard_map/ppermute | solution.py:238
  11.9 1.6 %collective-permute-start.6 = (bf16[16,1792]{1,0:T(8,128)(2,1)S(1)}, bf16[16,1792]{1,0:T(8,128)(2,1)S(1)}, u32[]{:S(2)}, u32[]{:S(2)}) collective-permute-start(bf16[16,1792]{1,0:T(8,128)(2,1)S(1)} %get-tuple-element.32.refs_0_), channel_id=1, source_target_pairs={{0,1},{1,0},{2,3},{3,2},{4,5},{5,4},{6,7},{7,6},{8,9},{9,8},{10,11... | collective-permute-start | bytes 172040 | tf_op jit(solution)/shard_map/ppermute | solution.py:238
  13.6 1.8 %collective-permute-start.8 = (bf16[16,1792]{1,0:T(8,128)(2,1)S(1)}, bf16[16,1792]{1,0:T(8,128)(2,1)S(1)}, u32[]{:S(2)}, u32[]{:S(2)}) collective-permute-start(bf16[16,1792]{1,0:T(8,128)(2,1)S(1)} %get-tuple-element.32.refs_0_), channel_id=1, source_target_pairs={{0,2},{1,3},{2,0},{3,1},{4,6},{5,7},{6,4},{7,5},{8,10},{9,11},{10,... | collective-permute-start | bytes 172040 | tf_op jit(solution)/shard_map/ppermute | solution.py:238
  15.3 2.5 %collective-permute-start.3 = (bf16[16,1792]{1,0:T(8,128)(2,1)S(1)}, bf16[16,1792]{1,0:T(8,128)(2,1)S(1)}, u32[]{:S(2)}, u32[]{:S(2)}) collective-permute-start(bf16[16,1792]{1,0:T(8,128)(2,1)S(1)} %get-tuple-element.31.refs_0_), channel_id=1, source_target_pairs={{0,1},{1,0},{2,3},{3,2},{4,5},{5,4},{6,7},{7,6},{8,9},{9,8},{10,11... | collective-permute-start | bytes 172040 | tf_op jit(solution)/shard_map/ppermute | solution.py:238
  17.9 2.2 %collective-permute-done.7.refs_2_ = bf16[16,1792]{1,0:T(8,128)(2,1)S(1)} collective-permute-done((bf16[16,1792]{1,0:T(8,128)(2,1)S(1)}, bf16[16,1792]{1,0:T(8,128)(2,1)S(1)}, u32[]{:S(2)}, u32[]{:S(2)}) %collective-permute-start.7) | collective-permute-done | bytes 57376 | tf_op jit(solution)/shard_map/ppermute | solution.py:238
  20.1 0.7 %ahead.1 = (f32[64,512]{1,0:T(8,128)S(1)}, f32[64,512]{1,0:T(8,128)S(1)}) custom-call(bf16[16,1792]{1,0:T(8,128)(2,1)S(1)} %get-tuple-element.32.refs_0_, bf16[16,1792]{1,0:T(8,128)(2,1)S(1)} %collective-permute-done.6.refs_1_, bf16[16,1792]{1,0:T(8,128)(2,1)S(1)} %collective-permute-done.7.refs_2_, bf16[16,1792]{1,0:T(8,128)(2,1)S(1)} %collective-permute-done.8.refs_3_, ...), custom_call_target="tpu_custom_call" | custom-call | tf_op jit(solution)/shard_map/ahead/pallas_call | solution.py:298
  20.8 0.3 collective-permute-done.3.refs_1_
  21.2 0.8 %collective-permute-done.5.refs_3_ = bf16[16,1792]{1,0:T(8,128)(2,1)S(1)} collective-permute-done((bf16[16,1792]{1,0:T(8,128)(2,1)S(1)}, bf16[16,1792]{1,0:T(8,128)(2,1)S(1)}, u32[]{:S(2)}, u32[]{:S(2)}) %collective-permute-start.5) | collective-permute-done | bytes 57376 | tf_op jit(solution)/shard_map/ppermute | solution.py:238
  22.0 0.8 %hidden.1.after_ref.refs_0_ = bf16[64,512]{1,0:T(8,128)(2,1)S(1)} custom-call(bf16[16,1792]{1,0:T(8,128)(2,1)S(1)} %get-tuple-element.31.refs_0_, bf16[16,1792]{1,0:T(8,128)(2,1)S(1)} %collective-permute-done.3.refs_1_, bf16[16,1792]{1,0:T(8,128)(2,1)S(1)} %collective-permute-done.4.refs_2_, bf16[16,1792]{1,0:T(8,128)(2,1)S(1)} %collective-permute-done.5.refs_3_, ...), custom_call_target="tpu_custom_call" | custom-call | tf_op jit(solution)/shard_map/hidden/pallas_call | solution.py:311
  22.8 3.4 %collective-permute-start.11 = (bf16[64,512]{1,0:T(8,128)(2,1)S(1)}, bf16[64,512]{1,0:T(8,128)(2,1)S(1)}, u32[]{:S(2)}, u32[]{:S(2)}) collective-permute-start(bf16[64,512]{1,0:T(8,128)(2,1)S(1)} %hidden.1.after_ref.refs_0_), channel_id=1, source_target_pairs={{0,3},{1,2},{2,1},{3,0},{4,7},{5,6},{6,5},{7,4},{8,11},{9,10},{10,... | collective-permute-start | bytes 196616 | tf_op jit(solution)/shard_map/ppermute | solution.py:238
  26.2 1.0 %collective-permute-start.9 = (bf16[64,512]{1,0:T(8,128)(2,1)S(1)}, bf16[64,512]{1,0:T(8,128)(2,1)S(1)}, u32[]{:S(2)}, u32[]{:S(2)}) collective-permute-start(bf16[64,512]{1,0:T(8,128)(2,1)S(1)} %hidden.1.after_ref.refs_0_), channel_id=1, source_target_pairs={{0,1},{1,0},{2,3},{3,2},{4,5},{5,4},{6,7},{7,6},{8,9},{9,8},{10,11... | collective-permute-start | bytes 196616 | tf_op jit(solution)/shard_map/ppermute | solution.py:238
  27.2 2.1 %prepare.1 = (bf16[2048,896]{1,0:T(8,128)(2,1)S(1)}, bf16[256,32]{1,0:T(8,128)(2,1)S(1)}) custom-call(bf16[64,512]{1,0:T(8,128)(2,1)S(1)} %hidden.1.after_ref.refs_0_, s32[8,256]{1,0:T(8,128)} %bitcast.10, f32[96,256]{1,0:T(8,128)} %bitcast.8, bf16[2048,896]{1,0:T(8,128)(2,1)} %bitcast.7), custom_call_target="tpu_custom_call" | custom-call | tf_op jit(solution)/shard_map/prepare/pallas_call | solution.py:319
  29.4 0.4 begin.1.refs_2_
  29.8 1.6 %collective-permute-done.10.refs_1_ = bf16[64,512]{1,0:T(8,128)(2,1)S(1)} collective-permute-done((bf16[64,512]{1,0:T(8,128)(2,1)S(1)}, bf16[64,512]{1,0:T(8,128)(2,1)S(1)}, u32[]{:S(2)}, u32[]{:S(2)}) %collective-permute-start.10) | collective-permute-done | bytes 65568 | tf_op jit(solution)/shard_map/ppermute | solution.py:238
  31.5 0.4 down.1
  31.9 0.5 %collective-permute-start.12 = (bf16[16,896]{1,0:T(8,128)(2,1)S(1)}, bf16[16,896]{1,0:T(8,128)(2,1)S(1)}, u32[]{:S(2)}, u32[]{:S(2)}) collective-permute-start(bf16[16,896]{1,0:T(8,128)(2,1)S(1)} %get-tuple-element.39), channel_id=1, source_target_pairs={{0,1},{1,2},{2,3},{3,0},{4,5},{5,6},{6,7},{7,4},{8,9},{9,10},{10,1... | collective-permute-start | bytes 86024 | tf_op jit(solution)/shard_map/ppermute | solution.py:356
  32.4 2.1 %collective-permute-start.13 = (bf16[16,896]{1,0:T(8,128)(2,1)S(1)}, bf16[16,896]{1,0:T(8,128)(2,1)S(1)}, u32[]{:S(2)}, u32[]{:S(2)}) collective-permute-start(bf16[16,896]{1,0:T(8,128)(2,1)S(1)} %get-tuple-element.40), channel_id=1, source_target_pairs={{0,2},{1,3},{2,0},{3,1},{4,6},{5,7},{6,4},{7,5},{8,10},{9,11},{10,... | collective-permute-start | bytes 86024 | tf_op jit(solution)/shard_map/ppermute | solution.py:356
  34.6 2.3 %collective-permute-start.14 = (bf16[16,896]{1,0:T(8,128)(2,1)S(1)}, bf16[16,896]{1,0:T(8,128)(2,1)S(1)}, u32[]{:S(2)}, u32[]{:S(2)}) collective-permute-start(bf16[16,896]{1,0:T(8,128)(2,1)S(1)} %get-tuple-element.41), channel_id=1, source_target_pairs={{0,3},{1,0},{2,1},{3,2},{4,7},{5,4},{6,5},{7,6},{8,11},{9,8},{10,9... | collective-permute-start | bytes 86024 | tf_op jit(solution)/shard_map/ppermute | solution.py:356
  36.8 0.9 %collective-permute-done.12.refs_0_ = bf16[16,896]{1,0:T(8,128)(2,1)S(1)} collective-permute-done((bf16[16,896]{1,0:T(8,128)(2,1)S(1)}, bf16[16,896]{1,0:T(8,128)(2,1)S(1)}, u32[]{:S(2)}, u32[]{:S(2)}) %collective-permute-start.12) | collective-permute-done | bytes 28704 | tf_op jit(solution)/shard_map/ppermute | solution.py:356
  37.8 0.7 %collective-permute-done.14.refs_2_ = bf16[16,896]{1,0:T(8,128)(2,1)S(1)} collective-permute-done((bf16[16,896]{1,0:T(8,128)(2,1)S(1)}, bf16[16,896]{1,0:T(8,128)(2,1)S(1)}, u32[]{:S(2)}, u32[]{:S(2)}) %collective-permute-start.14) | collective-permute-done | bytes 28704 | tf_op jit(solution)/shard_map/ppermute | solution.py:356
  38.7 1.6 %collective-permute-start.16 = (bf16[4,8,896]{2,1,0:T(8,128)(2,1)S(1)}, bf16[4,8,896]{2,1,0:T(8,128)(2,1)S(1)}, u32[]{:S(2)}, u32[]{:S(2)}) collective-permute-start(bf16[4,8,896]{2,1,0:T(8,128)(2,1)S(1)} %get-tuple-element.44), channel_id=1, source_target_pairs={{0,8},{4,12},{8,0},{12,4},{1,9},{5,13},{9,1},{13,5},{2,10},{6,14},... | collective-permute-start | bytes 172040 | tf_op jit(solution)/shard_map/ppermute | solution.py:369
  40.3 1.4 %collective-permute-start.17 = (bf16[4,8,896]{2,1,0:T(8,128)(2,1)S(1)}, bf16[4,8,896]{2,1,0:T(8,128)(2,1)S(1)}, u32[]{:S(2)}, u32[]{:S(2)}) collective-permute-start(bf16[4,8,896]{2,1,0:T(8,128)(2,1)S(1)} %get-tuple-element.45), channel_id=1, source_target_pairs={{0,12},{4,0},{8,4},{12,8},{1,13},{5,1},{9,5},{13,9},{2,14},{6,2},{... | collective-permute-start | bytes 172040 | tf_op jit(solution)/shard_map/ppermute | solution.py:369
  41.7 0.6 %collective-permute-done.15.refs_0_ = bf16[4,8,896]{2,1,0:T(8,128)(2,1)S(1)} collective-permute-done((bf16[4,8,896]{2,1,0:T(8,128)(2,1)S(1)}, bf16[4,8,896]{2,1,0:T(8,128)(2,1)S(1)}, u32[]{:S(2)}, u32[]{:S(2)}) %collective-permute-start.15) | collective-permute-done | bytes 57376 | tf_op jit(solution)/shard_map/ppermute | solution.py:369
  42.3 0.7 %collective-permute-done.16.refs_1_ = bf16[4,8,896]{2,1,0:T(8,128)(2,1)S(1)} collective-permute-done((bf16[4,8,896]{2,1,0:T(8,128)(2,1)S(1)}, bf16[4,8,896]{2,1,0:T(8,128)(2,1)S(1)}, u32[]{:S(2)}, u32[]{:S(2)}) %collective-permute-start.16) | collective-permute-done | bytes 57376 | tf_op jit(solution)/shard_map/ppermute | solution.py:369
  43.0 0.6 %collective-permute-done.17.refs_2_ = bf16[4,8,896]{2,1,0:T(8,128)(2,1)S(1)} collective-permute-done((bf16[4,8,896]{2,1,0:T(8,128)(2,1)S(1)}, bf16[4,8,896]{2,1,0:T(8,128)(2,1)S(1)}, u32[]{:S(2)}, u32[]{:S(2)}) %collective-permute-start.17) | collective-permute-done | bytes 57376 | tf_op jit(solution)/shard_map/ppermute | solution.py:369
  43.6 1.5 %combine.1 = bf16[256,3584]{1,0:T(8,128)(2,1)} custom-call(bf16[256,32]{1,0:T(8,128)(2,1)S(1)} %get-tuple-element.36.mixing_ref, bf16[4,8,896]{2,1,0:T(8,128)(2,1)S(1)} %collective-permute-done.15.refs_0_, bf16[4,8,896]{2,1,0:T(8,128)(2,1)S(1)} %collective-permute-done.16.refs_1_, bf16[4,8,896]{2,1,0:T(8,128)(2,1)S(1)} %collective-permute-done.17.refs_2_, ...), custom_call_target="tpu_custom_call" | custom-call | tf_op jit(solution)/shard_map/combine/pallas_call | solution.py:379
  (14 shorter events, 0.6 us)
Async XLA Ops:
  1.8 6.3 %collective-permute-start = (bf16[8,3712]{1,0:T(8,128)(2,1)S(1)}, bf16[8,3712]{1,0:T(8,128)(2,1)S(1)}, u32[]{:S(2)}, u32[]{:S(2)}) collective-permute-start(bf16[8,3712]{1,0:T(8,128)(2,1)S(1)} %get-tuple-element.28), channel_id=1, source_target_pairs={{0,12},{4,8},{8,4},{12,0},{1,13},{5,9},{9,5},{13,1},{2,14},{6,10},... | collective-permute-start | bytes 178184 | tf_op jit(solution)/shard_map/ppermute | solution.py:238
  4.3 4.5 %collective-permute-start.1 = (bf16[8,3712]{1,0:T(8,128)(2,1)S(1)}, bf16[8,3712]{1,0:T(8,128)(2,1)S(1)}, u32[]{:S(2)}, u32[]{:S(2)}) collective-permute-start(bf16[8,3712]{1,0:T(8,128)(2,1)S(1)} %get-tuple-element.29), channel_id=1, source_target_pairs={{0,8},{4,12},{8,0},{12,4},{1,9},{5,13},{9,1},{13,5},{2,10},{6,14},... | collective-permute-start | bytes 178184 | tf_op jit(solution)/shard_map/ppermute | solution.py:238
  4.9 3.9 %collective-permute-start.2 = (bf16[8,3712]{1,0:T(8,128)(2,1)S(1)}, bf16[8,3712]{1,0:T(8,128)(2,1)S(1)}, u32[]{:S(2)}, u32[]{:S(2)}) collective-permute-start(bf16[8,3712]{1,0:T(8,128)(2,1)S(1)} %get-tuple-element.30), channel_id=1, source_target_pairs={{0,4},{4,0},{8,12},{12,8},{1,5},{5,1},{9,13},{13,9},{2,6},{6,2},{1... | collective-permute-start | bytes 178184 | tf_op jit(solution)/shard_map/ppermute | solution.py:238
  9.1 8.7 %collective-permute-start.4 = (bf16[16,1792]{1,0:T(8,128)(2,1)S(1)}, bf16[16,1792]{1,0:T(8,128)(2,1)S(1)}, u32[]{:S(2)}, u32[]{:S(2)}) collective-permute-start(bf16[16,1792]{1,0:T(8,128)(2,1)S(1)} %get-tuple-element.31.refs_0_), channel_id=1, source_target_pairs={{0,2},{1,3},{2,0},{3,1},{4,6},{5,7},{6,4},{7,5},{8,10},{9,11},{10,... | collective-permute-start | bytes 172040 | tf_op jit(solution)/shard_map/ppermute | solution.py:238
  11.9 6.0 %collective-permute-start.6 = (bf16[16,1792]{1,0:T(8,128)(2,1)S(1)}, bf16[16,1792]{1,0:T(8,128)(2,1)S(1)}, u32[]{:S(2)}, u32[]{:S(2)}) collective-permute-start(bf16[16,1792]{1,0:T(8,128)(2,1)S(1)} %get-tuple-element.32.refs_0_), channel_id=1, source_target_pairs={{0,1},{1,0},{2,3},{3,2},{4,5},{5,4},{6,7},{7,6},{8,9},{9,8},{10,11... | collective-permute-start | bytes 172040 | tf_op jit(solution)/shard_map/ppermute | solution.py:238
  13.4 6.7 %collective-permute-start.7 = (bf16[16,1792]{1,0:T(8,128)(2,1)S(1)}, bf16[16,1792]{1,0:T(8,128)(2,1)S(1)}, u32[]{:S(2)}, u32[]{:S(2)}) collective-permute-start(bf16[16,1792]{1,0:T(8,128)(2,1)S(1)} %get-tuple-element.32.refs_0_), channel_id=1, source_target_pairs={{0,3},{1,2},{2,1},{3,0},{4,7},{5,6},{6,5},{7,4},{8,11},{9,10},{10,... | collective-permute-start | bytes 172040 | tf_op jit(solution)/shard_map/ppermute | solution.py:238
  13.6 6.5 %collective-permute-start.8 = (bf16[16,1792]{1,0:T(8,128)(2,1)S(1)}, bf16[16,1792]{1,0:T(8,128)(2,1)S(1)}, u32[]{:S(2)}, u32[]{:S(2)}) collective-permute-start(bf16[16,1792]{1,0:T(8,128)(2,1)S(1)} %get-tuple-element.32.refs_0_), channel_id=1, source_target_pairs={{0,2},{1,3},{2,0},{3,1},{4,6},{5,7},{6,4},{7,5},{8,10},{9,11},{10,... | collective-permute-start | bytes 172040 | tf_op jit(solution)/shard_map/ppermute | solution.py:238
  15.3 5.8 %collective-permute-start.3 = (bf16[16,1792]{1,0:T(8,128)(2,1)S(1)}, bf16[16,1792]{1,0:T(8,128)(2,1)S(1)}, u32[]{:S(2)}, u32[]{:S(2)}) collective-permute-start(bf16[16,1792]{1,0:T(8,128)(2,1)S(1)} %get-tuple-element.31.refs_0_), channel_id=1, source_target_pairs={{0,1},{1,0},{2,3},{3,2},{4,5},{5,4},{6,7},{7,6},{8,9},{9,8},{10,11... | collective-permute-start | bytes 172040 | tf_op jit(solution)/shard_map/ppermute | solution.py:238
  17.8 4.2 %collective-permute-start.5 = (bf16[16,1792]{1,0:T(8,128)(2,1)S(1)}, bf16[16,1792]{1,0:T(8,128)(2,1)S(1)}, u32[]{:S(2)}, u32[]{:S(2)}) collective-permute-start(bf16[16,1792]{1,0:T(8,128)(2,1)S(1)} %collective-permute-done.4.refs_2_), channel_id=1, source_target_pairs={{0,1},{1,0},{2,3},{3,2},{4,5},{5,4},{6,7},{7,6},{8,9},{9,8},{10,11... | collective-permute-start | bytes 172040 | tf_op jit(solution)/shard_map/ppermute | solution.py:238
  22.8 6.6 %collective-permute-start.11 = (bf16[64,512]{1,0:T(8,128)(2,1)S(1)}, bf16[64,512]{1,0:T(8,128)(2,1)S(1)}, u32[]{:S(2)}, u32[]{:S(2)}) collective-permute-start(bf16[64,512]{1,0:T(8,128)(2,1)S(1)} %hidden.1.after_ref.refs_0_), channel_id=1, source_target_pairs={{0,3},{1,2},{2,1},{3,0},{4,7},{5,6},{6,5},{7,4},{8,11},{9,10},{10,... | collective-permute-start | bytes 196616 | tf_op jit(solution)/shard_map/ppermute | solution.py:238
  26.2 5.2 %collective-permute-start.10 = (bf16[64,512]{1,0:T(8,128)(2,1)S(1)}, bf16[64,512]{1,0:T(8,128)(2,1)S(1)}, u32[]{:S(2)}, u32[]{:S(2)}) collective-permute-start(bf16[64,512]{1,0:T(8,128)(2,1)S(1)} %hidden.1.after_ref.refs_0_), channel_id=1, source_target_pairs={{0,2},{1,3},{2,0},{3,1},{4,6},{5,7},{6,4},{7,5},{8,10},{9,11},{10,... | collective-permute-start | bytes 196616 | tf_op jit(solution)/shard_map/ppermute | solution.py:238
  26.2 5.2 %collective-permute-start.9 = (bf16[64,512]{1,0:T(8,128)(2,1)S(1)}, bf16[64,512]{1,0:T(8,128)(2,1)S(1)}, u32[]{:S(2)}, u32[]{:S(2)}) collective-permute-start(bf16[64,512]{1,0:T(8,128)(2,1)S(1)} %hidden.1.after_ref.refs_0_), channel_id=1, source_target_pairs={{0,1},{1,0},{2,3},{3,2},{4,5},{5,4},{6,7},{7,6},{8,9},{9,8},{10,11... | collective-permute-start | bytes 196616 | tf_op jit(solution)/shard_map/ppermute | solution.py:238
  31.9 5.8 %collective-permute-start.12 = (bf16[16,896]{1,0:T(8,128)(2,1)S(1)}, bf16[16,896]{1,0:T(8,128)(2,1)S(1)}, u32[]{:S(2)}, u32[]{:S(2)}) collective-permute-start(bf16[16,896]{1,0:T(8,128)(2,1)S(1)} %get-tuple-element.39), channel_id=1, source_target_pairs={{0,1},{1,2},{2,3},{3,0},{4,5},{5,6},{6,7},{7,4},{8,9},{9,10},{10,1... | collective-permute-start | bytes 86024 | tf_op jit(solution)/shard_map/ppermute | solution.py:356
  32.4 5.3 %collective-permute-start.13 = (bf16[16,896]{1,0:T(8,128)(2,1)S(1)}, bf16[16,896]{1,0:T(8,128)(2,1)S(1)}, u32[]{:S(2)}, u32[]{:S(2)}) collective-permute-start(bf16[16,896]{1,0:T(8,128)(2,1)S(1)} %get-tuple-element.40), channel_id=1, source_target_pairs={{0,2},{1,3},{2,0},{3,1},{4,6},{5,7},{6,4},{7,5},{8,10},{9,11},{10,... | collective-permute-start | bytes 86024 | tf_op jit(solution)/shard_map/ppermute | solution.py:356
  34.6 3.9 %collective-permute-start.14 = (bf16[16,896]{1,0:T(8,128)(2,1)S(1)}, bf16[16,896]{1,0:T(8,128)(2,1)S(1)}, u32[]{:S(2)}, u32[]{:S(2)}) collective-permute-start(bf16[16,896]{1,0:T(8,128)(2,1)S(1)} %get-tuple-element.41), channel_id=1, source_target_pairs={{0,3},{1,0},{2,1},{3,2},{4,7},{5,4},{6,5},{7,6},{8,11},{9,8},{10,9... | collective-permute-start | bytes 86024 | tf_op jit(solution)/shard_map/ppermute | solution.py:356
  38.7 3.7 %collective-permute-start.15 = (bf16[4,8,896]{2,1,0:T(8,128)(2,1)S(1)}, bf16[4,8,896]{2,1,0:T(8,128)(2,1)S(1)}, u32[]{:S(2)}, u32[]{:S(2)}) collective-permute-start(bf16[4,8,896]{2,1,0:T(8,128)(2,1)S(1)} %get-tuple-element.43), channel_id=1, source_target_pairs={{0,4},{4,8},{8,12},{12,0},{1,5},{5,9},{9,13},{13,1},{2,6},{6,10},{... | collective-permute-start | bytes 172040 | tf_op jit(solution)/shard_map/ppermute | solution.py:369
  38.7 4.2 %collective-permute-start.16 = (bf16[4,8,896]{2,1,0:T(8,128)(2,1)S(1)}, bf16[4,8,896]{2,1,0:T(8,128)(2,1)S(1)}, u32[]{:S(2)}, u32[]{:S(2)}) collective-permute-start(bf16[4,8,896]{2,1,0:T(8,128)(2,1)S(1)} %get-tuple-element.44), channel_id=1, source_target_pairs={{0,8},{4,12},{8,0},{12,4},{1,9},{5,13},{9,1},{13,5},{2,10},{6,14},... | collective-permute-start | bytes 172040 | tf_op jit(solution)/shard_map/ppermute | solution.py:369
  40.3 3.2 %collective-permute-start.17 = (bf16[4,8,896]{2,1,0:T(8,128)(2,1)S(1)}, bf16[4,8,896]{2,1,0:T(8,128)(2,1)S(1)}, u32[]{:S(2)}, u32[]{:S(2)}) collective-permute-start(bf16[4,8,896]{2,1,0:T(8,128)(2,1)S(1)} %get-tuple-element.45), channel_id=1, source_target_pairs={{0,12},{4,0},{8,4},{12,8},{1,13},{5,1},{9,5},{13,9},{2,14},{6,2},{... | collective-permute-start | bytes 172040 | tf_op jit(solution)/shard_map/ppermute | solution.py:369
